TPU v7x, 32 devices: a whole 2x2x4 slice. The times are simulated.
32 devices in a mesh: ctx: 8 (over z, core), exp: 4 (over y, x).
Axes of the slice: x: 2, y: 2, z: 4, core: 2. Of those that a mesh axis runs over, the one named last changes fastest.
Arguments:
- queries: bfloat16 [2048, 8192], P('ctx', 'exp'), may hold values from -8 to 8
- keys: bfloat16 [2048, 512], P('ctx'), may hold values from -4 to 4
- values: bfloat16 [2048, 512], P('ctx'), may hold values from -6 to 6
- w_out: bfloat16 [8192, 4096], P('exp'), may hold values from -0.5 to 0.5
- residual: bfloat16 [2048, 4096], P(('ctx', 'exp')), may hold values from -1.5 to 1.5
- norm_gain: bfloat16 [4096], replicated, may hold values from 0.099609375 to 1.8984375
- expert_ids: int32 [2048, 2], P(('ctx', 'exp')), may hold values from 0 to 3, all different within a row; in each aligned block of 64 rows (0 to 63, 64 to 127, ...) at most 64 rows name the same one
- gate_weights: float32 [2048, 2], P(('ctx', 'exp')), may hold values from 0.2 to 1
- w_gate: bfloat16 [4, 4096, 768], P('exp', 'ctx'), may hold values from -0.09375 to 0.09375
- w_up: bfloat16 [4, 4096, 768], P('exp', 'ctx'), may hold values from -0.09375 to 0.09375
- w_down: bfloat16 [4, 768, 4096], P('exp', None, 'ctx'), may hold values from -0.21875 to 0.21875
Outputs:
- layer_out: bfloat16 [2048, 4096], P(('ctx', 'exp'))
Inputs may be any that keep to these rules, and one draw needn't show every extreme that they name: `expert_ids`: each row names 2 different experts; within each aligned block of 64 rows (the rows of one device) no expert is named by more than 64 rows.
All inputs are finite; a program needn't handle non-finite values.
Results may differ from a plain program's by a relative error of at most 0.025.
Values may be sent and summed in bfloat16 or wider, within the bound.
No kernel may reach another device: no remote copies, remote signals or barrier semaphores. Data moves between devices by JAX's collectives and lax.ppermute only.
A program may use at most 128 MiB of HBM per device.

v0:
```python
import math

import jax
import jax.numpy as jnp
from jax import lax
from jax.sharding import PartitionSpec as P

D = 4096
HQ = 64
KVH = 4
HD = 128


def body(
    queries,
    keys,
    values,
    w_out,
    residual,
    norm_gain,
    expert_ids,
    gate_weights,
    w_gate,
    w_up,
    w_down,
):
    tok_rows = queries.shape[0]
    half_rows = tok_rows // 2
    exp_count = lax.axis_size("exp")
    heads_here = HQ // exp_count
    group = HQ // KVH
    kv_here = max(1, heads_here // group)
    heads_per_kv = heads_here // kv_here
    exp_index = lax.axis_index("exp")
    ctx_index = lax.axis_index("ctx")
    kv_first = exp_index * heads_here // group
    key_cols = lax.dynamic_slice_in_dim(keys, kv_first * HD, kv_here * HD, 1)
    value_cols = lax.dynamic_slice_in_dim(values, kv_first * HD, kv_here * HD, 1)
    scale = 1.0 / math.sqrt(HD)
    first_rows = queries[:half_rows]
    second_rows = queries[half_rows:]
    first_start = ctx_index * tok_rows
    second_start = ctx_index * tok_rows + half_rows
    query_sets = (
        first_rows.reshape(half_rows, kv_here, heads_per_kv, HD),
        second_rows.reshape(half_rows, kv_here, heads_per_kv, HD),
    )
    query_positions = (
        first_start + jnp.arange(half_rows, dtype=jnp.int32),
        second_start + jnp.arange(half_rows, dtype=jnp.int32),
    )
    last_positions = (first_start + half_rows - 1, second_start + half_rows - 1)

    def block_update(carry, query_four, query_pos, key_block, value_block, key_start):
        run_max, run_sum, run_acc = carry
        width = key_block.shape[0]
        key_three = key_block.reshape(width, kv_here, HD)
        value_three = value_block.reshape(width, kv_here, HD)
        scores = (
            jnp.einsum("tghd,kgd->ghtk", query_four, key_three, preferred_element_type=jnp.float32)
            * scale
        )
        key_pos = key_start + jnp.arange(width, dtype=jnp.int32)
        allowed = key_pos[None, :] <= query_pos[:, None]
        scores = jnp.where(allowed, scores, -1e30)
        new_max = jnp.maximum(run_max, jnp.max(scores, axis=-1))
        probs = jnp.where(allowed, jnp.exp(scores - new_max[..., None]), 0.0)
        factor = jnp.exp(run_max - new_max)
        run_sum = run_sum * factor + jnp.sum(probs, axis=-1)
        weighted = jnp.einsum(
            "ghtk,kgd->ghtd",
            probs.astype(jnp.bfloat16),
            value_three,
            preferred_element_type=jnp.float32,
        )
        run_acc = run_acc * factor[..., None] + weighted
        return (new_max, run_sum, run_acc)

    start_max = jnp.full((kv_here, heads_per_kv, half_rows), -1e30, jnp.float32)
    start_sum = jnp.zeros((kv_here, heads_per_kv, half_rows), jnp.float32)
    start_acc = jnp.zeros((kv_here, heads_per_kv, half_rows, HD), jnp.float32)
    start_state = (start_max, start_sum, start_acc)
    key_piece = lax.all_gather(key_cols, "ctx", axis=0, tiled=True)
    value_piece = lax.all_gather(value_cols, "ctx", axis=0, tiled=True)
    count = key_piece.shape[0]
    width = 512

    def one_block(index, inner):
        key_start = index * width
        key_block = lax.dynamic_slice_in_dim(key_piece, key_start, width, 0)
        value_block = lax.dynamic_slice_in_dim(value_piece, key_start, width, 0)
        updated = []
        for which in range(2):
            query_four = query_sets[which]
            query_pos = query_positions[which]
            updated.append(
                lax.cond(
                    key_start > last_positions[which],
                    lambda state: state,
                    lambda state: block_update(
                        state, query_four, query_pos, key_block, value_block, key_start
                    ),
                    inner[which],
                )
            )
        return (updated[0], updated[1])

    states = lax.fori_loop(0, count // width, one_block, (start_state, start_state))
    halves = []
    for which in range(2):
        run_max, run_sum, run_acc = states[which]
        halves.append(
            jnp.transpose(run_acc / run_sum[..., None], (2, 0, 1, 3))
            .reshape(half_rows, heads_here * HD)
            .astype(jnp.bfloat16)
        )
    attn_second = halves[1]
    attn = jnp.concatenate([halves[0], attn_second], axis=0)
    projected = lax.psum_scatter(
        jnp.dot(attn, w_out, preferred_element_type=jnp.float32).astype(jnp.bfloat16),
        "exp",
        scatter_dimension=0,
        tiled=True,
    ).astype(jnp.float32)
    hidden_state = (residual.astype(jnp.float32) + projected).astype(jnp.bfloat16)
    state_f = hidden_state.astype(jnp.float32)
    inv_rms = 1.0 / jnp.sqrt(jnp.mean(state_f * state_f, axis=1, keepdims=True) + 1e-06)
    normed = (state_f * inv_rms * norm_gain.astype(jnp.float32)[None, :]).astype(jnp.bfloat16)
    rows_here = expert_ids.shape[0]
    top_count = expert_ids.shape[1]
    experts_all = w_gate.shape[0] * exp_count
    capacity = min(rows_here, 2 * rows_here * top_count // experts_all)
    flat_ids = expert_ids.reshape(-1)
    onehot = (flat_ids[:, None] == jnp.arange(experts_all, dtype=jnp.int32)[None, :]).astype(
        jnp.int32
    )
    earlier = jnp.cumsum(onehot, axis=0) - onehot
    slot_index = jnp.sum(earlier * onehot, axis=1)
    target = flat_ids * capacity + slot_index
    picks = target[:, None] == jnp.arange(experts_all * capacity, dtype=jnp.int32)[None, :]
    dispatch_table = jnp.any(
        picks.reshape(rows_here, top_count, experts_all * capacity), axis=1
    ).astype(jnp.bfloat16)
    outgoing = jnp.einsum(
        "rs,rd->sd", dispatch_table, normed, preferred_element_type=jnp.float32
    ).astype(jnp.bfloat16)
    arrived = lax.all_to_all(
        outgoing.reshape(experts_all, capacity, D), "exp", split_axis=0, concat_axis=0, tiled=True
    )
    slot_rows = arrived.reshape(experts_all * capacity, D)
    gate_local = w_gate[0]
    up_local = w_up[0]
    gate_pre = jnp.dot(
        slot_rows,
        lax.all_gather(gate_local, "ctx", axis=0, tiled=True),
        preferred_element_type=jnp.float32,
    )
    up_pre = jnp.dot(
        slot_rows,
        lax.all_gather(up_local, "ctx", axis=0, tiled=True),
        preferred_element_type=jnp.float32,
    )
    expert_hidden = (jax.nn.silu(gate_pre) * up_pre).astype(jnp.bfloat16)
    down_local = w_down[0]
    expert_result = jnp.dot(
        expert_hidden,
        lax.all_gather(down_local, "ctx", axis=1, tiled=True),
        preferred_element_type=jnp.float32,
    ).astype(jnp.bfloat16)
    returned = lax.all_to_all(
        expert_result.reshape(experts_all, capacity, D),
        "exp",
        split_axis=0,
        concat_axis=0,
        tiled=True,
    )
    returned_flat = returned.reshape(experts_all * capacity, D)
    picked = jnp.dot(picks.astype(jnp.bfloat16), returned_flat, preferred_element_type=jnp.float32)
    weighted = gate_weights[:, :, None] * picked.reshape(rows_here, top_count, D)
    return (state_f + jnp.sum(weighted, axis=1)).astype(jnp.bfloat16)


def solution(mesh):
    placed = (
        P("ctx", "exp"),
        P("ctx", None),
        P("ctx", None),
        P("exp", None),
        P(("ctx", "exp"), None),
        P(),
        P(("ctx", "exp"), None),
        P(("ctx", "exp"), None),
        P("exp", "ctx", None),
        P("exp", "ctx", None),
        P("exp", None, "ctx"),
    )
    return jax.shard_map(
        body, mesh=mesh, in_specs=placed, out_specs=P(("ctx", "exp"), None), check_vma=False
    )
```

profile of v0, /device:TPU:0, one launch (start us, length us, event | category | flops | bytes accessed | tf_op | source)
XLA Modules:
  0.0 342.2 jit_solution(17921718915529915612)
XLA Ops:
  7.4 0.0 copy-start
  7.4 0.0 reduce-scatter.2.cloned.1.call-start
  7.4 0.9 copy-done
  8.3 17.6 %all_gather.15 = bf16[2048,128]{1,0:T(8,128)(2,1)} all-gather(bf16[256,128]{1,0:T(8,128)(2,1)S(1)} %constant_dynamic-slice_fusion.3), channel_id=1, replica_groups=mesh['ctx'=8,'exp'=4] {'ctx'}, dimensions={0}, use_global_device_ids=true | all-gather | bytes 589824 | tf_op jit(solution)/shard_map/all_gather | solution.py:83
  25.9 0.8 constant_dynamic-slice_fusion.2
  26.8 15.8 %all_gather.16 = bf16[2048,128]{1,0:T(8,128)(2,1)} all-gather(bf16[256,128]{1,0:T(8,128)(2,1)S(1)} %constant_dynamic-slice_fusion.2), channel_id=1, replica_groups=mesh['ctx'=8,'exp'=4] {'ctx'}, dimensions={0}, use_global_device_ids=true | all-gather | bytes 589824 | tf_op jit(solution)/shard_map/all_gather | solution.py:84
  42.5 1.3 fusion.82
  43.8 0.3 copy.55
  44.1 0.3 copy.47
  44.4 0.3 copy.56
  44.7 0.3 copy.48
  45.0 0.1 broadcast_in_dim.49
  45.1 0.1 broadcast_in_dim.49.clone
  45.2 12.4 %while.24 = (s32[]{:T(128)}, f32[1,16,128]{2,1,0:T(8,128)S(1)}, f32[1,16,128]{2,1,0:T(8,128)S(1)}, f32[1,16,128,128]{3,2,1,0:T(8,128)S(1)}, f32[1,16,128]{2,1,0:...) while((s32[]{:T(128)}, f32[1,16,128]{2,1,0:T(8,128)S(1)}, ...), condition=%wide.region_9.10_spmd.clone, body=%wide.region_0.9_spmd.clone.sunk | while | flops 1102198016 | bytes 32256508 | solution.py:108
  45.4 1.0 constant_dynamic-slice_fusion.5
  46.4 3.8 %conditional.7 = (f32[1,16,128]{2,1,0:T(8,128)S(1)}, f32[1,16,128]{2,1,0:T(8,128)S(1)}, f32[1,16,128,128]{3,2,1,0:T(8,128)S(1)}) conditional(s32[]{:T(128)} %convert_element_type.165, (s32[]{:T(128)}, s32[]{:T(128)}, bf16[128,1,16,128]{3,0,2,1:T(8,128)(2,1)S(1)}, bf16[512,128]{1,0:T(8,128)(2,1)S(1)}, f32[1,16,128]{2,1,0:T(8,128)S(1)}, ...), branch_computations={%region_5.7_spmd, %region_8.8_spmd} | conditional | flops 551099008 | bytes 15848992 | solution.py:97
  46.5 0.1 broadcast_compare_fusion.1
  46.6 0.7 fusion.25
  47.4 1.0 fusion.27
  48.4 1.8 fusion.35
  50.3 3.8 %conditional.6 = (f32[1,16,128]{2,1,0:T(8,128)S(1)}, f32[1,16,128]{2,1,0:T(8,128)S(1)}, f32[1,16,128,128]{3,2,1,0:T(8,128)S(1)}) conditional(s32[]{:T(128)} %convert_element_type.164, (s32[]{:T(128)}, s32[]{:T(128)}, bf16[128,1,16,128]{3,0,2,1:T(8,128)(2,1)S(1)}, bf16[512,128]{1,0:T(8,128)(2,1)S(1)}, f32[1,16,128]{2,1,0:T(8,128)S(1)}, ...), branch_computations={%region_1.3_spmd, %region_4.4_spmd} | conditional | flops 551099008 | bytes 15848992 | solution.py:97
  50.3 0.1 broadcast_compare_fusion
  50.5 0.7 fusion.4
  51.2 1.0 fusion.6
  52.3 1.8 fusion.14
  54.1 1.0 constant_dynamic-slice_fusion.5
  55.3 1.0 constant_dynamic-slice_fusion.5
  56.4 1.0 constant_dynamic-slice_fusion.5
  57.6 1.3 copy.49
  58.9 0.3 copy.50
  59.2 1.3 divide_convert_fusion.1
  60.6 0.1 divide_convert_fusion
  60.7 11.6 %convolution_convert_fusion.1 = bf16[256,4096]{1,0:T(8,128)(2,1)} fusion(bf16[2048,4096]{1,0:T(8,128)(2,1)} %param.20, bf16[128,2048]{0,1:T(8,128)(2,1)S(1)} %bitcast.150, bf16[128,2048]{0,1:T(8,128)(2,1)S(1)} %bitcast.149), kind=kOutput, calls=%fused_computation.59 | convolution fusion | flops 4298113024 | bytes 19922944 | tf_op jit(solution)/shard_map/dot_general | solution.py:120
  72.3 0.0 reduce-scatter.2.cloned.1.call-update
  72.3 0.0 all-gather.7.cloned.1.call-start
  72.4 0.5 all-gather.7.cloned.1.call-update
  72.9 0.0 all-gather.11.cloned.1.call-start
  72.9 0.5 all-gather.11.cloned.1.call-update
  73.5 0.3 all-gather.9.cloned.1.call-start
  73.7 0.3 all-gather.9.cloned.1.call-update
  74.0 0.0 copy-done.5
  74.1 0.1 copy.51
  74.2 0.1 eq.51
  74.3 0.1 fusion.79
  74.4 0.2 reduce_window_sum.11
  74.6 0.2 select_reduce_fusion
  74.7 0.1 reduce_sum.52
  74.9 0.1 copy.52
  75.0 0.0 copy-done.4
  75.0 0.1 fusion.77
  75.1 56.4 %reduce-scatter.2.cloned.1.call-done = bf16[64,4096]{1,0:T(8,128)(2,1)} async-done(((bf16[256,4096]{1,0:T(8,128)(2,1)}), bf16[64,4096]{1,0:T(8,128)(2,1)}) %reduce-scatter.2.cloned.1.call-update) | async-done | bytes 524304 | tf_op jit(solution)/shard_map/reduce_scatter | solution.py:119
  131.5 0.0 copy-done.2
  131.5 1.3 fusion.62
  132.8 1.8 convolution_convert_fusion
  134.7 28.1 %all_to_all.10 = bf16[4,64,4096]{2,1,0:T(8,128)(2,1)S(1)} all-to-all(bf16[4,64,4096]{2,1,0:T(8,128)(2,1)S(1)} %bitcast.143), channel_id=1, replica_groups=mesh['ctx'=8,'exp'=4] {'exp'}, dimensions={0} | all-to-all | bytes 4194304 | tf_op jit(solution)/shard_map/all_to_all | solution.py:147
  162.8 0.1 all-gather.7.cloned.1.call-done
  162.9 5.5 %fusion.50 = f32[256,768]{1,0:T(8,128)} fusion(bf16[256,4096]{1,0:T(8,128)(2,1)S(1)} %bitcast.151, bf16[1,4096,768]{2,1,0:T(8,128)(2,1)} %all-gather.7.cloned.1.call-done), kind=kOutput, calls=%fused_computation.56 | convolution fusion | flops 1610612736 | bytes 9175040 | tf_op jit(solution)/shard_map/dot_general | solution.py:153
  168.3 59.2 %all-gather.11.cloned.1.call-done = bf16[1,768,4096]{2,1,0:T(8,128)(2,1)} async-done(((bf16[1,768,512]{2,1,0:T(8,128)(2,1)}), bf16[1,768,4096]{2,1,0:T(8,128)(2,1)}) %all-gather.11.cloned.1.call-update) | async-done | bytes 6291472 | tf_op jit(solution)/shard_map/all_gather | solution.py:167
  227.6 64.9 %all-gather.9.cloned.1.call-done = bf16[1,4096,768]{2,1,0:T(8,128)(2,1)} async-done(((bf16[1,512,768]{2,1,0:T(8,128)(2,1)}), bf16[1,4096,768]{2,1,0:T(8,128)(2,1)}) %all-gather.9.cloned.1.call-update) | async-done | bytes 6291472 | tf_op jit(solution)/shard_map/all_gather | solution.py:160
  292.5 10.7 %fusion.52 = bf16[256,4096]{1,0:T(8,128)(2,1)} fusion(bf16[1,768,4096]{2,1,0:T(8,128)(2,1)} %all-gather.11.cloned.1.call-done, bf16[256,4096]{1,0:T(8,128)(2,1)S(1)} %bitcast.152, bf16[1,4096,768]{2,1,0:T(8,128)(2,1)} %all-gather.9.cloned.1.call-done, f32[256,768]{1,0:T(8,128)} %fusion.50), kind=kOutput, calls=%fused_computation.60 | convolution fusion | flops 3223453696 | bytes 17563648 | tf_op jit(solution)/shard_map/dot_general | solution.py:165
  303.2 29.8 %all_to_all.11 = bf16[4,64,4096]{2,1,0:T(8,128)(2,1)S(1)} all-to-all(bf16[4,64,4096]{2,1,0:T(8,128)(2,1)} %bitcast.153), channel_id=1, replica_groups=mesh['ctx'=8,'exp'=4] {'exp'}, dimensions={0} | all-to-all | bytes 4194304 | tf_op jit(solution)/shard_map/all_to_all | solution.py:170
  333.0 0.6 fusion.55
  333.6 0.0 copy-done.3
  333.6 1.0 fusion.65
  (52 shorter events, 0.4 us)
Async XLA Ops:
  7.4 1.0 copy-start
  7.4 124.1 %reduce-scatter.2.cloned.1.call-start = ((), (), s32[]{:S(2)}) async-start(), calls=%async_computation.3 | async-start | bytes 2621440 | tf_op jit(solution)/shard_map/reduce_scatter | solution.py:119
  72.3 1.8 copy-start.5
  72.3 2.7 copy-start.4
  72.3 59.2 %copy-start.2 = (bf16[64,4096]{1,0:T(8,128)(2,1)S(1)}, bf16[64,4096]{1,0:T(8,128)(2,1)}, u32[]{:S(2)}) copy-start(bf16[64,4096]{1,0:T(8,128)(2,1)} %param.21) | copy-start | bytes 1572868
  72.3 90.6 %all-gather.7.cloned.1.call-start = ((), (), s32[]{:S(2)}) async-start(), calls=%async_computation.4 | async-start | bytes 7077888 | tf_op jit(solution)/shard_map/all_gather | solution.py:155
  72.9 154.7 %all-gather.11.cloned.1.call-start = ((), (), s32[]{:S(2)}) async-start(), calls=%async_computation.6 | async-start | bytes 7077888 | tf_op jit(solution)/shard_map/all_gather | solution.py:167
  73.5 219.0 %all-gather.9.cloned.1.call-start = ((), (), s32[]{:S(2)}) async-start(), calls=%async_computation.5 | async-start | bytes 7077888 | tf_op jit(solution)/shard_map/all_gather | solution.py:160
  303.2 29.8 %copy-start.6 = (f32[64,2]{0,1:T(2,128)S(1)}, f32[64,2]{0,1:T(2,128)}, u32[]{:S(2)}) copy-start(f32[64,2]{0,1:T(2,128)} %param.24) | copy-start | bytes 1540
  303.2 30.4 %copy-start.3 = (bf16[64,4096]{1,0:T(8,128)(2,1)S(1)}, bf16[64,4096]{1,0:T(8,128)(2,1)}, u32[]{:S(2)}) copy-start(bf16[64,4096]{1,0:T(8,128)(2,1)} %reduce-scatter.2.cloned.1.call-done) | copy-start | bytes 1572868
  303.2 31.3 %copy-start.1 = (bf16[256,512]{1,0:T(8,128)(2,1)S(1)}, bf16[256,512]{1,0:T(8,128)(2,1)}, u32[]{:S(2)}) copy-start(bf16[256,512]{1,0:T(8,128)(2,1)} %param.18) | copy-start | bytes 786436
Sparse Core Ops, SparseCore 0:
  72.4 59.0 reduce-scatter.1
Sparse Core Ops, SparseCore 1:
  74.4 88.4 all-gather.6
  164.3 63.2 all-gather.10
  229.2 63.3 all-gather.8
where the time goes:
time: 343 us; the launch traced here: 342 us
  waiting for transfers between devices  182 us (53%)
  blocking collectives  91.3 us (27%)
  matrix products  35.3 us (10%)
  between operations  15.2 us (4%)
  local copies, waits for them, and re-layouts  10.5 us (3%)
  other arithmetic  6.68 us (2%)
    all_gather x1, waiting for transfers between devices, body(): lax.all_gather(up_local, 'ctx', axis=0, tiled=True)  64.9 us
    all_gather x1, waiting for transfers between devices, body(): lax.all_gather(down_local, 'ctx', axis=1, tiled=True)  59.2 us
    reduce_scatter x1, waiting for transfers between devices, body(): lax.psum_scatter(jnp.dot(attn, w_out, preferred_element_type=jnp.float32)...  56.4 us
    all_to_all x1, blocking collectives, body(): lax.all_to_all(expert_result.reshape(experts_all, capacity, D), 'exp', sp...  29.8 us
    all_to_all x1, blocking collectives, body(): lax.all_to_all(outgoing.reshape(experts_all, capacity, D), 'exp', split_a...  28.1 us
    all_gather x1, blocking collectives, body(): key_piece = lax.all_gather(key_cols, 'ctx', axis=0, tiled=True)  17.6 us
    all_gather x1, blocking collectives, body(): value_piece = lax.all_gather(value_cols, 'ctx', axis=0, tiled=True)  15.8 us
    dot_general x1, matrix products, body(): jnp.dot(attn, w_out, preferred_element_type=jnp.float32)  11.6 us
  transfers between devices with their start and end apart: 4, of which 4 were waited for; matrix products, arithmetic and copies ran while one was open for 3% of the time, Pallas kernels for 0%

commit v1 on v0

--- a/solution.py
+++ b/solution.py
@@ -3,6 +3,8 @@
 import jax
 import jax.numpy as jnp
 from jax import lax
+from jax.experimental import pallas as pl
+from jax.experimental.pallas import tpu as pltpu
 from jax.sharding import PartitionSpec as P
 
 D = 4096
@@ -11,7 +13,7 @@
 HD = 128
 
 
-def body(
+def general_body(
     queries,
     keys,
     values,
@@ -180,6 +182,311 @@
     return (state_f + jnp.sum(weighted, axis=1)).astype(jnp.bfloat16)
 
 
+BF16 = jnp.bfloat16
+F32 = jnp.float32
+VMEM = pltpu.VMEM
+QB = 256
+CHUNK = 4
+CHEAP = pl.CostEstimate(flops=1000, bytes_accessed=1000, transcendentals=0)
+
+
+def swap(array, axis, mask):
+    size = lax.axis_size(axis)
+    return lax.ppermute(array, axis, [(i, i ^ mask) for i in range(size)])
+
+
+def params(mib):
+    return pltpu.CompilerParams(vmem_limit_bytes=mib * 1024 * 1024)
+
+
+def vmem_specs(count):
+    return [pl.BlockSpec(memory_space=VMEM) for _ in range(count)]
+
+
+def attention_kernel(index, q, kv, w_hbm, p0, p1, p2, p3, w_all, scores, ones_values, attn, sem):
+    ctx = index[0]
+    exp = index[1]
+    fetch = pltpu.make_async_copy(w_hbm, w_all, sem)
+    fetch.start()
+    factor = math.log2(math.e) / math.sqrt(HD)
+    rows = CHUNK * QB
+    heads = q.shape[1] // HD
+    ones_values[:, :HD] = kv[:, HD:]
+    ones_values[:, HD:] = jnp.ones((kv.shape[0], HD), BF16)
+    row = lax.broadcasted_iota(jnp.int32, (QB, QB), 0)
+    col = lax.broadcasted_iota(jnp.int32, (QB, QB), 1)
+    hidden_keys = jnp.concatenate([jnp.where(col <= row, 0.0, -1e30)] * CHUNK, axis=0)
+    for chunk in range(heads // CHUNK):
+        first = chunk * CHUNK
+        queries = jnp.concatenate(
+            [q[:, (first + h) * HD : (first + h + 1) * HD] for h in range(CHUNK)], axis=0
+        )
+
+        def score_block(j):
+            block = kv[pl.ds(pl.multiple_of(j * QB, QB), QB), :HD]
+            return lax.dot_general(
+                queries, block, (((1,), (1,)), ((), ())), preferred_element_type=F32
+            )
+
+        def first_pass(j, top):
+            block = score_block(j)
+            scores[j] = block
+            return jnp.maximum(top, jnp.maximum(block[:, :HD], block[:, HD:]))
+
+        last = score_block(ctx) + hidden_keys
+        scores[ctx] = last
+        top = jnp.maximum(last[:, :HD], last[:, HD:])
+        top = lax.fori_loop(0, ctx, first_pass, top)
+        top = jnp.max(top, axis=1, keepdims=True) * factor
+
+        def second_pass(j, total):
+            probs = jnp.exp2(scores[j] * factor - top).astype(BF16)
+            block = ones_values[pl.ds(pl.multiple_of(j * QB, QB), QB), :]
+            return total + jnp.dot(probs, block, preferred_element_type=F32)
+
+        total = lax.fori_loop(0, ctx + 1, second_pass, jnp.zeros((rows, 2 * HD), F32))
+        done = (total[:, :HD] / total[:, HD:]).astype(BF16)
+        part = QB // 4
+        for h in range(CHUNK):
+            for i in range(4):
+                start = pl.multiple_of((exp ^ i) * part, part)
+                attn[pl.ds(start, part), (first + h) * HD : (first + h + 1) * HD] = done[
+                    h * QB + i * part : h * QB + (i + 1) * part
+                ]
+    fetch.wait()
+    part = QB // 4
+    width = 512
+    for n in range(w_all.shape[1] // width):
+        cols = slice(n * width, (n + 1) * width)
+        block = jnp.dot(attn[...], w_all[:, cols], preferred_element_type=F32).astype(BF16)
+        for b, out in enumerate((p0, p1, p2, p3)):
+            out[:, cols] = block[b * part : (b + 1) * part]
+
+
+def attention(index, queries, kv, w_out):
+    rows = QB // 4
+    blocks = kv.shape[0] // QB
+    return pl.pallas_call(
+        attention_kernel,
+        out_shape=[jax.ShapeDtypeStruct((rows, D), BF16)] * 4,
+        in_specs=[pl.BlockSpec(memory_space=pltpu.SMEM)]
+        + vmem_specs(2)
+        + [pl.BlockSpec(memory_space=pl.ANY)],
+        out_specs=vmem_specs(4),
+        scratch_shapes=[
+            VMEM(w_out.shape, BF16),
+            VMEM((blocks, CHUNK * QB, QB), F32),
+            VMEM((kv.shape[0], 2 * HD), BF16),
+            VMEM(queries.shape, BF16),
+            pltpu.SemaphoreType.DMA,
+        ],
+        compiler_params=params(56),
+        cost_estimate=CHEAP,
+        name="attention",
+    )(index, queries, kv, w_out)
+
+
+def norm_kernel(index, p0, r1, r2, r3, residual, gain, state, mine, theirs, work):
+    ctx = index[0]
+    total = p0[...].astype(F32) + r1[...].astype(F32) + r2[...].astype(F32) + r3[...].astype(F32)
+    hidden = (residual[...].astype(F32) + total).astype(BF16)
+    state[...] = hidden
+    wide = hidden.astype(F32)
+    inv = 1.0 / jnp.sqrt(jnp.mean(wide * wide, axis=1, keepdims=True) + 1e-06)
+    normed = (wide * inv * gain[...].astype(F32)).astype(BF16)
+    part = D // 8
+    for j in range(8):
+        work[j] = normed[:, j * part : (j + 1) * part]
+    for j, (a, b) in enumerate(((0, 2), (1, 3), (6, 4), (7, 5))):
+        mine[:, j * part : (j + 1) * part] = work[ctx ^ a]
+        theirs[:, j * part : (j + 1) * part] = work[ctx ^ b]
+
+
+def norm(index, p0, r1, r2, r3, residual, gain):
+    rows = residual.shape[0]
+    half = jax.ShapeDtypeStruct((rows, D // 2), BF16)
+    return pl.pallas_call(
+        norm_kernel,
+        out_shape=[jax.ShapeDtypeStruct((rows, D), BF16), half, half],
+        in_specs=[pl.BlockSpec(memory_space=pltpu.SMEM)] + vmem_specs(6),
+        out_specs=vmem_specs(3),
+        scratch_shapes=[VMEM((8, rows, D // 8), BF16)],
+        compiler_params=params(16),
+        cost_estimate=CHEAP,
+        name="norm",
+    )(index, p0, r1, r2, r3, residual, gain)
+
+
+def enter_kernel(x0, x1, x2, x3, *refs):
+    gates, ups, out = refs[:4], refs[4:8], refs[8]
+    x = jnp.concatenate([x0[...], x1[...], x2[...], x3[...]], axis=0)
+    part, width = gates[0].shape
+    for which, weights in enumerate((gates, ups)):
+        total = jnp.zeros((x.shape[0], width), F32)
+        for j in range(4):
+            total = total + jnp.dot(
+                x[:, j * part : (j + 1) * part], weights[j][...], preferred_element_type=F32
+            )
+        out[:, which * width : (which + 1) * width] = total.astype(out.dtype)
+
+
+def enter(rows, gates, ups, kind):
+    count = 4 * rows[0].shape[0]
+    return pl.pallas_call(
+        enter_kernel,
+        out_shape=jax.ShapeDtypeStruct((count, 2 * gates[0].shape[1]), kind),
+        in_specs=vmem_specs(12),
+        out_specs=pl.BlockSpec(memory_space=VMEM),
+        compiler_params=params(32),
+        cost_estimate=CHEAP,
+        name="enter",
+    )(*rows, *gates, *ups)
+
+
+def silu_kernel(own, other, c0, c1, c2, c3, out):
+    width = out.shape[1]
+    part = c0.shape[0]
+    total = own[...] + other[...].astype(F32)
+    gate, up = total[:, :width], total[:, width:]
+    hidden = gate / (1.0 + jnp.exp(-gate)) * up
+    for b, share in enumerate((c0, c1, c2, c3)):
+        rows = slice(b * part, (b + 1) * part)
+        out[rows] = (hidden[rows] * share[...]).astype(BF16)
+
+
+def silu(own, other, shares):
+    return pl.pallas_call(
+        silu_kernel,
+        out_shape=jax.ShapeDtypeStruct((own.shape[0], own.shape[1] // 2), BF16),
+        in_specs=vmem_specs(6),
+        out_specs=pl.BlockSpec(memory_space=VMEM),
+        compiler_params=params(16),
+        cost_estimate=CHEAP,
+        name="silu",
+    )(own, other, *shares)
+
+
+def leave_kernel(hidden, d0, d1, d2, d3, y0, y1, y2, y3):
+    part = y0.shape[0]
+    width = d0.shape[1]
+    for j, weights in enumerate((d0, d1, d2, d3)):
+        block = jnp.dot(hidden[...], weights[...], preferred_element_type=F32).astype(BF16)
+        for b, out in enumerate((y0, y1, y2, y3)):
+            out[:, j * width : (j + 1) * width] = block[b * part : (b + 1) * part]
+
+
+def leave(hidden, downs):
+    part = jax.ShapeDtypeStruct((hidden.shape[0] // 4, 4 * downs[0].shape[1]), BF16)
+    return pl.pallas_call(
+        leave_kernel,
+        out_shape=[part] * 4,
+        in_specs=vmem_specs(5),
+        out_specs=vmem_specs(4),
+        compiler_params=params(16),
+        cost_estimate=CHEAP,
+        name="leave",
+    )(hidden, *downs)
+
+
+def total_kernel(y0, r1, r2, r3, out):
+    out[...] = (
+        y0[...].astype(F32) + r1[...].astype(F32) + r2[...].astype(F32) + r3[...].astype(F32)
+    ).astype(BF16)
+
+
+def total_of(y0, r1, r2, r3):
+    return pl.pallas_call(
+        total_kernel,
+        out_shape=jax.ShapeDtypeStruct(y0.shape, BF16),
+        in_specs=vmem_specs(4),
+        out_specs=pl.BlockSpec(memory_space=VMEM),
+        cost_estimate=CHEAP,
+        name="total",
+    )(y0, r1, r2, r3)
+
+
+def final_kernel(index, state, y0, r1, r2, r3, other, out):
+    ctx = index[0]
+    part = D // 8
+    own = y0[...].astype(F32) + r1[...].astype(F32) + r2[...].astype(F32) + r3[...].astype(F32)
+    for j, (a, b) in enumerate(((0, 2), (1, 3), (6, 4), (7, 5))):
+        cols = slice(j * part, (j + 1) * part)
+        here = pl.ds(pl.multiple_of((ctx ^ a) * part, part), part)
+        out[:, here] = (state[:, here].astype(F32) + own[:, cols]).astype(BF16)
+        there = pl.ds(pl.multiple_of((ctx ^ b) * part, part), part)
+        out[:, there] = (state[:, there].astype(F32) + other[:, cols].astype(F32)).astype(BF16)
+
+
+def final(index, state, y0, r1, r2, r3, other):
+    return pl.pallas_call(
+        final_kernel,
+        out_shape=jax.ShapeDtypeStruct(state.shape, BF16),
+        in_specs=[pl.BlockSpec(memory_space=pltpu.SMEM)] + vmem_specs(6),
+        out_specs=pl.BlockSpec(memory_space=VMEM),
+        compiler_params=params(16),
+        cost_estimate=CHEAP,
+        name="final",
+    )(index, state, y0, r1, r2, r3, other)
+
+
+def body(
+    queries,
+    keys,
+    values,
+    w_out,
+    residual,
+    norm_gain,
+    expert_ids,
+    gate_weights,
+    w_gate,
+    w_up,
+    w_down,
+):
+    exp = lax.axis_index("exp")
+    ctx = lax.axis_index("ctx")
+    index = jnp.stack([ctx, exp]).astype(jnp.int32)
+    kv_first = exp * (HQ // 4) // (HQ // KVH) * HD
+    kv_here = jnp.concatenate(
+        [
+            lax.dynamic_slice_in_dim(keys, kv_first, HD, 1),
+            lax.dynamic_slice_in_dim(values, kv_first, HD, 1),
+        ],
+        axis=1,
+    )
+    kv = lax.all_gather(kv_here, "ctx", axis=0, tiled=True)
+
+    shares = []
+    for b in range(4):
+        share = jnp.sum(jnp.where(expert_ids == (exp ^ b), gate_weights, 0.0), axis=1, keepdims=True)
+        shares.append(swap(share, "exp", b) if b else share)
+
+    def slices(array):
+        far = swap(array, "ctx", 6)
+        return (array, swap(array, "ctx", 1), far, swap(far, "ctx", 1))
+
+    gates = slices(w_gate[0])
+    ups = slices(w_up[0])
+
+    p = attention(index, queries, kv, w_out)
+    r = [swap(p[b], "exp", b) for b in (1, 2, 3)]
+    state, mine, theirs = norm(index, p[0], *r, residual, norm_gain.reshape(1, D))
+    downs = slices(w_down[0])
+    others = swap(theirs, "ctx", 2)
+    other_rows = [others] + [swap(others, "exp", b) for b in (1, 2, 3)]
+    own_rows = [mine] + [swap(mine, "exp", b) for b in (1, 2, 3)]
+    other_pre = enter(other_rows, gates, ups, BF16)
+    from_other = swap(other_pre, "ctx", 2)
+    own_pre = enter(own_rows, gates, ups, F32)
+    own_hidden = silu(own_pre, from_other, shares)
+    other_hidden = swap(own_hidden, "ctx", 2)
+    y = leave(own_hidden, downs)
+    own_parts = [y[0]] + [swap(y[b], "exp", b) for b in (1, 2, 3)]
+    z = leave(other_hidden, downs)
+    other_parts = [z[0]] + [swap(z[b], "exp", b) for b in (1, 2, 3)]
+    back = swap(total_of(*other_parts), "ctx", 2)
+    return final(index, state, *own_parts, back)
+
+
 def solution(mesh):
     placed = (
         P("ctx", "exp"),
@@ -194,6 +501,8 @@
         P("exp", "ctx", None),
         P("exp", None, "ctx"),
     )
+    shape = dict(mesh.shape)
+    small = shape["ctx"] == 8 and shape["exp"] == 4
     return jax.shard_map(
-        body, mesh=mesh, in_specs=placed, out_specs=P(("ctx", "exp"), None), check_vma=False
-    )
+        body if small else general_body, mesh=mesh, in_specs=placed, out_specs=P(("ctx", "exp"), None), check_vma=False
+    )

time: 343 us -> 249 us (0.73)
  the two profiles are of different devices: /device:TPU:0 before, /device:TPU:22 now
where the time goes in v1:
time: 249 us; the launch traced here: 248 us
  waiting for transfers between devices  126 us (51%)
  starting transfers between devices  50.5 us (20%)
  Pallas kernels  42.7 us (17%)
  local copies, waits for them, and re-layouts  13.7 us (6%)
  between operations  13.6 us (5%)
    ppermute x31, waiting for transfers between devices, swap(): return lax.ppermute(array, axis, [(i, i ^ mask) for i in range(size)])  75.7 us
    all_gather x1, waiting for transfers between devices, body(): kv = lax.all_gather(kv_here, 'ctx', axis=0, tiled=True)  50.5 us
    ppermute x31, starting transfers between devices, swap(): return lax.ppermute(array, axis, [(i, i ^ mask) for i in range(size)])  50.5 us
    pallas_call x1, Pallas kernels, attention(): pl.pallas_call(attention_kernel, out_shape=[jax.ShapeDtypeStruct((rows, D...  26.1 us
    unnamed x50, local copies, waits for them, and re-layouts  11.1 us
    pallas_call x2, Pallas kernels, enter(): pl.pallas_call(enter_kernel, out_shape=jax.ShapeDtypeStruct((count, 2 * g...  7.47 us
  transfers between devices with their start and end apart: 32, of which 13 were waited for; matrix products, arithmetic and copies ran while one was open for 1% of the time, Pallas kernels for 16%

profile of v1, /device:TPU:22, one launch (start us, length us, event | category | flops | bytes accessed | tf_op | source)
XLA Modules:
  0.0 248.1 jit_solution(12093197104638064867)
XLA Ops:
  6.6 1.0 constant_dynamic-slice_fusion
  7.7 0.7 pad_maximum_fusion
  8.4 0.5 collective-permute-start.7
  8.9 1.6 collective-permute-start.10
  10.5 0.6 pad_add_fusion.index
  11.1 50.5 %all-gather.2.cloned.1.call-done.kv = bf16[2048,256]{1,0:T(8,128)(2,1)} async-done(((bf16[256,256]{1,0:T(8,128)(2,1)}), bf16[2048,256]{1,0:T(8,128)(2,1)}) %all-gather.2.cloned.1.call-update) | async-done | bytes 1048592 | tf_op jit(solution)/shard_map/all_gather | solution.py:456
  61.6 26.1 %attention.1 = (bf16[64,4096]{1,0:T(8,128)(2,1)}, bf16[64,4096]{1,0:T(8,128)(2,1)}, bf16[64,4096]{1,0:T(8,128)(2,1)}, bf16[64,4096]{1,0:T(8,128)(2,1)}) custom-call(s32[2]{0:T(128)} %pad_add_fusion.index, bf16[256,2048]{1,0:T(8,128)(2,1)} %q.1, bf16[2048,256]{1,0:T(8,128)(2,1)} %all-gather.2.cloned.1.call-done.kv, bf16[2048,4096]{1,0:T(8,128)(2,1)} %w_hbm.1), custom_call_target="tpu_custom_call" | custom-call | flops 1000 | bytes 1000 | tf_op jit(solution)/shard_map/attention/pallas_call | solution.py:269
  87.7 0.6 collective-permute-start
  88.3 0.5 collective-permute-start.1
  88.8 3.0 %collective-permute-start.6 = (bf16[512,768]{1,0:T(8,128)(2,1)S(1)}, bf16[512,768]{1,0:T(8,128)(2,1)S(1)}, u32[]{:S(2)}, u32[]{:S(2)}) collective-permute-start(bf16[512,768]{1,0:T(8,128)(2,1)S(1)} %bitcast.14), channel_id=1, source_target_pairs={{0,4},{4,0},{8,12},{12,8},{16,20},{20,16},{24,28},{28,24},{1,5},{5... | collective-permute-start | bytes 2359304 | tf_op jit(solution)/shard_map/ppermute | solution.py:195
  91.8 2.4 collective-permute-start.2
  94.2 5.9 %collective-permute-done.r1 = bf16[64,4096]{1,0:T(8,128)(2,1)S(1)} collective-permute-done((bf16[64,4096]{1,0:T(8,128)(2,1)}, bf16[64,4096]{1,0:T(8,128)(2,1)S(1)}, u32[]{:S(2)}, u32[]{:S(2)}) %collective-permute-start) | collective-permute-done | bytes 524320 | tf_op jit(solution)/shard_map/ppermute | solution.py:195
  100.1 5.4 %collective-permute-start.8 = (bf16[512,768]{1,0:T(8,128)(2,1)}, bf16[512,768]{1,0:T(8,128)(2,1)S(1)}, u32[]{:S(2)}, u32[]{:S(2)}) collective-permute-start(bf16[512,768]{1,0:T(8,128)(2,1)} %collective-permute-done.7.refs_2_), channel_id=1, source_target_pairs={{0,4},{4,0},{8,12},{12,8},{16,20},{20,16},{24,28},{28,24},{1,5},{5... | collective-permute-start | bytes 2359304 | tf_op jit(solution)/shard_map/ppermute | solution.py:195
  105.5 8.9 %collective-permute-start.11 = (bf16[512,768]{1,0:T(8,128)(2,1)}, bf16[512,768]{1,0:T(8,128)(2,1)S(1)}, u32[]{:S(2)}, u32[]{:S(2)}) collective-permute-start(bf16[512,768]{1,0:T(8,128)(2,1)} %collective-permute-done.10.refs_6_), channel_id=1, source_target_pairs={{0,4},{4,0},{8,12},{12,8},{16,20},{20,16},{24,28},{28,24},{1,5},{5... | collective-permute-start | bytes 2359304 | tf_op jit(solution)/shard_map/ppermute | solution.py:195
  114.4 1.0 copy-done.16
  115.4 1.2 norm.1
  116.6 0.8 copy-done.13
  117.4 7.5 %collective-permute-start.12 = (bf16[64,2048]{1,0:T(8,128)(2,1)S(1)}, bf16[64,2048]{1,0:T(8,128)(2,1)S(1)}, u32[]{:S(2)}, u32[]{:S(2)}) collective-permute-start(bf16[64,2048]{1,0:T(8,128)(2,1)S(1)} %get-tuple-element.26), channel_id=1, source_target_pairs={{0,8},{4,12},{8,0},{12,4},{16,24},{20,28},{24,16},{28,20},{1,9},{5... | collective-permute-start | bytes 786440 | tf_op jit(solution)/shard_map/ppermute | solution.py:195
  125.0 22.5 %collective-permute-done.12.x0 = bf16[64,2048]{1,0:T(8,128)(2,1)S(1)} collective-permute-done((bf16[64,2048]{1,0:T(8,128)(2,1)S(1)}, bf16[64,2048]{1,0:T(8,128)(2,1)S(1)}, u32[]{:S(2)}, u32[]{:S(2)}) %collective-permute-start.12) | collective-permute-done | bytes 262176 | tf_op jit(solution)/shard_map/ppermute | solution.py:195
  147.5 1.5 collective-permute-start.13
  149.0 0.5 collective-permute-start.14
  149.5 1.5 collective-permute-start.15
  151.0 5.7 %collective-permute-done.13.x1 = bf16[64,2048]{1,0:T(8,128)(2,1)S(1)} collective-permute-done((bf16[64,2048]{1,0:T(8,128)(2,1)S(1)}, bf16[64,2048]{1,0:T(8,128)(2,1)S(1)}, u32[]{:S(2)}, u32[]{:S(2)}) %collective-permute-start.13) | collective-permute-done | bytes 262176 | tf_op jit(solution)/shard_map/ppermute | solution.py:195
  156.7 3.1 %collective-permute-done.14.x2 = bf16[64,2048]{1,0:T(8,128)(2,1)S(1)} collective-permute-done((bf16[64,2048]{1,0:T(8,128)(2,1)S(1)}, bf16[64,2048]{1,0:T(8,128)(2,1)S(1)}, u32[]{:S(2)}, u32[]{:S(2)}) %collective-permute-start.14) | collective-permute-done | bytes 262176 | tf_op jit(solution)/shard_map/ppermute | solution.py:195
  159.9 1.8 collective-permute-done.15.x3
  161.7 4.1 %enter.3 = bf16[256,1536]{1,0:T(8,128)(2,1)} custom-call(bf16[64,2048]{1,0:T(8,128)(2,1)S(1)} %collective-permute-done.12.x0, bf16[64,2048]{1,0:T(8,128)(2,1)S(1)} %collective-permute-done.13.x1, bf16[64,2048]{1,0:T(8,128)(2,1)S(1)} %collective-permute-done.14.x2, bf16[64,2048]{1,0:T(8,128)(2,1)S(1)} %collective-permute-done.15.x3, ...), custom_call_target="tpu_custom_call" | custom-call | flops 1000 | bytes 1000 | tf_op jit(solution)/shard_map/enter/pallas_call | solution.py:335
  165.8 2.5 collective-permute-start.16
  168.2 0.6 collective-permute-start.3
  168.9 0.6 collective-permute-start.22
  169.5 1.5 collective-permute-start.17
  171.0 5.1 %collective-permute-done.17.c1 = f32[64,1]{1,0:T(8,128)S(1)} collective-permute-done((f32[64,1]{1,0:T(8,128)S(1)}, f32[64,1]{1,0:T(8,128)S(1)}, u32[]{:S(2)}, u32[]{:S(2)}) %collective-permute-start.17) | collective-permute-done | bytes 288 | tf_op jit(solution)/shard_map/ppermute | solution.py:195
  176.1 1.7 collective-permute-start.5
  177.8 0.7 copy.13
  178.5 0.7 copy.14
  179.2 8.9 %collective-permute-done.4.x2 = bf16[64,2048]{1,0:T(8,128)(2,1)} collective-permute-done((bf16[64,2048]{1,0:T(8,128)(2,1)S(1)}, bf16[64,2048]{1,0:T(8,128)(2,1)}, u32[]{:S(2)}, u32[]{:S(2)}) %collective-permute-start.4) | collective-permute-done | bytes 262176 | tf_op jit(solution)/shard_map/ppermute | solution.py:195
  188.1 0.7 collective-permute-start.18
  188.9 1.1 collective-permute-start.19
  190.1 1.1 copy-done.2
  191.2 1.1 copy-done.4
  192.4 1.1 copy-done.6
  193.5 1.1 copy-done.8
  194.6 1.1 copy-done.10
  195.8 1.1 copy-done.12
  196.9 3.4 %enter.2.own = f32[256,1536]{1,0:T(8,128)S(1)} custom-call(bf16[64,2048]{1,0:T(8,128)(2,1)S(1)} %get-tuple-element.25.x0, bf16[64,2048]{1,0:T(8,128)(2,1)} %collective-permute-done.3.x1, bf16[64,2048]{1,0:T(8,128)(2,1)} %collective-permute-done.4.x2, bf16[64,2048]{1,0:T(8,128)(2,1)} %collective-permute-done.5.x3, bf16[512,768]{1,0:T(8,128)(2,1)S(1)} %bitcast.16, ...), custom_call_target="tpu_custom_call" | custom-call | flops 1000 | bytes 1000 | tf_op jit(solution)/shard_map/enter/pallas_call | solution.py:335
  200.4 1.5 silu.1.hidden
  202.1 9.0 %collective-permute-done.26.hidden = bf16[256,768]{1,0:T(8,128)(2,1)S(1)} collective-permute-done((bf16[256,768]{1,0:T(8,128)(2,1)S(1)}, bf16[256,768]{1,0:T(8,128)(2,1)S(1)}, u32[]{:S(2)}, u32[]{:S(2)}) %collective-permute-start.26) | collective-permute-done | bytes 393248 | tf_op jit(solution)/shard_map/ppermute | solution.py:195
  211.1 1.0 leave.3
  212.1 1.6 collective-permute-start.27
  213.7 0.3 collective-permute-start.28
  213.9 1.7 collective-permute-start.29
  215.6 1.8 leave.2
  217.5 1.5 collective-permute-start.23
  219.0 0.3 collective-permute-start.24
  219.3 2.1 collective-permute-done.27.r1
  221.4 1.3 collective-permute-start.25
  222.6 5.9 %collective-permute-done.28.r2 = bf16[64,2048]{1,0:T(8,128)(2,1)S(1)} collective-permute-done((bf16[64,2048]{1,0:T(8,128)(2,1)S(1)}, bf16[64,2048]{1,0:T(8,128)(2,1)S(1)}, u32[]{:S(2)}, u32[]{:S(2)}) %collective-permute-start.28) | collective-permute-done | bytes 262176 | tf_op jit(solution)/shard_map/ppermute | solution.py:195
  228.6 0.7 copy-done.20
  229.2 0.7 copy-done.21
  229.9 2.0 total.1
  232.0 1.0 collective-permute-start.30
  233.0 2.6 %collective-permute-done.24.r2 = bf16[64,2048]{1,0:T(8,128)(2,1)S(1)} collective-permute-done((bf16[64,2048]{1,0:T(8,128)(2,1)}, bf16[64,2048]{1,0:T(8,128)(2,1)S(1)}, u32[]{:S(2)}, u32[]{:S(2)}) %collective-permute-start.24) | collective-permute-done | bytes 262176 | tf_op jit(solution)/shard_map/ppermute | solution.py:195
  235.6 3.0 %collective-permute-done.30.other = bf16[64,2048]{1,0:T(8,128)(2,1)S(1)} collective-permute-done((bf16[64,2048]{1,0:T(8,128)(2,1)}, bf16[64,2048]{1,0:T(8,128)(2,1)S(1)}, u32[]{:S(2)}, u32[]{:S(2)}) %collective-permute-start.30) | collective-permute-done | bytes 262176 | tf_op jit(solution)/shard_map/ppermute | solution.py:195
  238.5 1.0 copy-done.14
  239.6 1.7 final.1
  (69 shorter events, 0.7 us)
Async XLA Ops:
  6.5 82.3 %copy-start.1 = (bf16[1,512,768]{2,1,0:T(8,128)(2,1)S(1)}, bf16[1,512,768]{2,1,0:T(8,128)(2,1)}, u32[]{:S(2)}) copy-start(bf16[1,512,768]{2,1,0:T(8,128)(2,1)} %param.19) | copy-start | bytes 2359300
  6.5 87.7 %copy-start.3 = (bf16[1,512,768]{2,1,0:T(8,128)(2,1)S(1)}, bf16[1,512,768]{2,1,0:T(8,128)(2,1)}, u32[]{:S(2)}) copy-start(bf16[1,512,768]{2,1,0:T(8,128)(2,1)} %param.20) | copy-start | bytes 2359300
  6.5 107.8 %copy-start.22 = (bf16[4096]{0:T(1024)(128)(2,1)S(1)}, bf16[4096]{0:T(1024)(128)(2,1)}, u32[]{:S(2)}) copy-start(bf16[4096]{0:T(1024)(128)(2,1)} %param.16) | copy-start | bytes 24580
  6.5 107.8 %copy-start.15 = (bf16[64,4096]{1,0:T(8,128)(2,1)S(1)}, bf16[64,4096]{1,0:T(8,128)(2,1)}, u32[]{:S(2)}) copy-start(bf16[64,4096]{1,0:T(8,128)(2,1)} %residual.1) | copy-start | bytes 1572868
  6.5 118.4 %copy-start = (bf16[1,768,512]{2,1,0:T(8,128)(2,1)S(1)}, bf16[1,768,512]{2,1,0:T(8,128)(2,1)}, u32[]{:S(2)}) copy-start(bf16[1,768,512]{2,1,0:T(8,128)(2,1)} %param.21) | copy-start | bytes 2359300
  6.5 162.9 %copy-start.23 = (f32[64,2]{0,1:T(2,128)S(1)}, f32[64,2]{0,1:T(2,128)}, u32[]{:S(2)}) copy-start(f32[64,2]{0,1:T(2,128)} %param.18) | copy-start | bytes 1540
  6.6 162.9 %copy-start.24 = (s32[64,2]{0,1:T(2,128)S(1)}, s32[64,2]{0,1:T(2,128)}, u32[]{:S(2)}) copy-start(s32[64,2]{0,1:T(2,128)} %param.17) | copy-start | bytes 1540
  6.6 55.0 %all-gather.2.cloned.1.call-start = ((), (), s32[]{:S(2)}) async-start(), calls=%async_computation | async-start | bytes 1179648 | tf_op jit(solution)/shard_map/all_gather | solution.py:456
  8.4 83.4 %collective-permute-start.7 = (bf16[512,768]{1,0:T(8,128)(2,1)}, bf16[512,768]{1,0:T(8,128)(2,1)}, u32[]{:S(2)}, u32[]{:S(2)}) collective-permute-start(bf16[512,768]{1,0:T(8,128)(2,1)} %bitcast.13), channel_id=1, source_target_pairs={{0,24},{4,28},{8,16},{12,20},{16,8},{20,12},{24,0},{28,4},{1,25},{... | collective-permute-start | bytes 2359304 | tf_op jit(solution)/shard_map/ppermute | solution.py:195
  8.9 85.3 %collective-permute-start.10 = (bf16[512,768]{1,0:T(8,128)(2,1)}, bf16[512,768]{1,0:T(8,128)(2,1)}, u32[]{:S(2)}, u32[]{:S(2)}) collective-permute-start(bf16[512,768]{1,0:T(8,128)(2,1)} %bitcast.17), channel_id=1, source_target_pairs={{0,24},{4,28},{8,16},{12,20},{16,8},{20,12},{24,0},{28,4},{1,25},{... | collective-permute-start | bytes 2359304 | tf_op jit(solution)/shard_map/ppermute | solution.py:195
  11.1 103.3 %copy-start.18 = (s32[2]{0:T(128)S(1)}, s32[2]{0:T(128)}, u32[]{:S(2)}) copy-start(s32[2]{0:T(128)} %pad_add_fusion.index) | copy-start | bytes 28
  87.7 12.4 %collective-permute-start = (bf16[64,4096]{1,0:T(8,128)(2,1)}, bf16[64,4096]{1,0:T(8,128)(2,1)S(1)}, u32[]{:S(2)}, u32[]{:S(2)}) collective-permute-start(bf16[64,4096]{1,0:T(8,128)(2,1)} %get-tuple-element.21), channel_id=1, source_target_pairs={{0,1},{1,0},{2,3},{3,2},{4,5},{5,4},{6,7},{7,6},{8,9},{9,8},{10,11... | collective-permute-start | bytes 1572872 | tf_op jit(solution)/shard_map/ppermute | solution.py:195
  88.3 17.2 %collective-permute-start.1 = (bf16[64,4096]{1,0:T(8,128)(2,1)}, bf16[64,4096]{1,0:T(8,128)(2,1)S(1)}, u32[]{:S(2)}, u32[]{:S(2)}) collective-permute-start(bf16[64,4096]{1,0:T(8,128)(2,1)} %get-tuple-element.22), channel_id=1, source_target_pairs={{0,2},{1,3},{2,0},{3,1},{4,6},{5,7},{6,4},{7,5},{8,10},{9,11},{10,... | collective-permute-start | bytes 1572872 | tf_op jit(solution)/shard_map/ppermute | solution.py:195
  88.8 36.1 %collective-permute-start.6 = (bf16[512,768]{1,0:T(8,128)(2,1)S(1)}, bf16[512,768]{1,0:T(8,128)(2,1)S(1)}, u32[]{:S(2)}, u32[]{:S(2)}) collective-permute-start(bf16[512,768]{1,0:T(8,128)(2,1)S(1)} %bitcast.14), channel_id=1, source_target_pairs={{0,4},{4,0},{8,12},{12,8},{16,20},{20,16},{24,28},{28,24},{1,5},{5... | collective-permute-start | bytes 2359304 | tf_op jit(solution)/shard_map/ppermute | solution.py:195
  91.8 22.6 %collective-permute-start.2 = (bf16[64,4096]{1,0:T(8,128)(2,1)}, bf16[64,4096]{1,0:T(8,128)(2,1)S(1)}, u32[]{:S(2)}, u32[]{:S(2)}) collective-permute-start(bf16[64,4096]{1,0:T(8,128)(2,1)} %get-tuple-element.23), channel_id=1, source_target_pairs={{0,3},{1,2},{2,1},{3,0},{4,7},{5,6},{6,5},{7,4},{8,11},{9,10},{10,... | collective-permute-start | bytes 1572872 | tf_op jit(solution)/shard_map/ppermute | solution.py:195
  94.2 54.8 %collective-permute-start.9 = (bf16[512,768]{1,0:T(8,128)(2,1)S(1)}, bf16[512,768]{1,0:T(8,128)(2,1)S(1)}, u32[]{:S(2)}, u32[]{:S(2)}) collective-permute-start(bf16[512,768]{1,0:T(8,128)(2,1)S(1)} %bitcast.18), channel_id=1, source_target_pairs={{0,4},{4,0},{8,12},{12,8},{16,20},{20,16},{24,28},{28,24},{1,5},{5... | collective-permute-start | bytes 2359304 | tf_op jit(solution)/shard_map/ppermute | solution.py:195
  100.1 49.4 %collective-permute-start.8 = (bf16[512,768]{1,0:T(8,128)(2,1)}, bf16[512,768]{1,0:T(8,128)(2,1)S(1)}, u32[]{:S(2)}, u32[]{:S(2)}) collective-permute-start(bf16[512,768]{1,0:T(8,128)(2,1)} %collective-permute-done.7.refs_2_), channel_id=1, source_target_pairs={{0,4},{4,0},{8,12},{12,8},{16,20},{20,16},{24,28},{28,24},{1,5},{5... | collective-permute-start | bytes 2359304 | tf_op jit(solution)/shard_map/ppermute | solution.py:195
  105.5 45.5 %collective-permute-start.11 = (bf16[512,768]{1,0:T(8,128)(2,1)}, bf16[512,768]{1,0:T(8,128)(2,1)S(1)}, u32[]{:S(2)}, u32[]{:S(2)}) collective-permute-start(bf16[512,768]{1,0:T(8,128)(2,1)} %collective-permute-done.10.refs_6_), channel_id=1, source_target_pairs={{0,4},{4,0},{8,12},{12,8},{16,20},{20,16},{24,28},{28,24},{1,5},{5... | collective-permute-start | bytes 2359304 | tf_op jit(solution)/shard_map/ppermute | solution.py:195
  114.4 1.0 copy-start.16
  116.6 0.8 copy-start.13
  117.4 30.1 %collective-permute-start.12 = (bf16[64,2048]{1,0:T(8,128)(2,1)S(1)}, bf16[64,2048]{1,0:T(8,128)(2,1)S(1)}, u32[]{:S(2)}, u32[]{:S(2)}) collective-permute-start(bf16[64,2048]{1,0:T(8,128)(2,1)S(1)} %get-tuple-element.26), channel_id=1, source_target_pairs={{0,8},{4,12},{8,0},{12,4},{16,24},{20,28},{24,16},{28,20},{1,9},{5... | collective-permute-start | bytes 786440 | tf_op jit(solution)/shard_map/ppermute | solution.py:195
  124.9 43.9 %copy-start.5 = (bf16[512,768]{1,0:T(8,128)(2,1)}, bf16[512,768]{1,0:T(8,128)(2,1)S(1)}, u32[]{:S(2)}) copy-start(bf16[512,768]{1,0:T(8,128)(2,1)S(1)} %collective-permute-done.6.refs_1_) | copy-start | bytes 2359300
  124.9 43.9 %collective-permute-start.21 = (bf16[768,512]{1,0:T(8,128)(2,1)S(1)}, bf16[768,512]{1,0:T(8,128)(2,1)S(1)}, u32[]{:S(2)}, u32[]{:S(2)}) collective-permute-start(bf16[768,512]{1,0:T(8,128)(2,1)S(1)} %bitcast.9), channel_id=1, source_target_pairs={{0,24},{4,28},{8,16},{12,20},{16,8},{20,12},{24,0},{28,4},{1,25},{... | collective-permute-start | bytes 2359304 | tf_op jit(solution)/shard_map/ppermute | solution.py:195
  147.5 9.2 %collective-permute-start.13 = (bf16[64,2048]{1,0:T(8,128)(2,1)S(1)}, bf16[64,2048]{1,0:T(8,128)(2,1)S(1)}, u32[]{:S(2)}, u32[]{:S(2)}) collective-permute-start(bf16[64,2048]{1,0:T(8,128)(2,1)S(1)} %collective-permute-done.12.x0), channel_id=1, source_target_pairs={{0,1},{1,0},{2,3},{3,2},{4,5},{5,4},{6,7},{7,6},{8,9},{9,8},{10,11... | collective-permute-start | bytes 786440 | tf_op jit(solution)/shard_map/ppermute | solution.py:195
  149.0 19.8 %copy-start.7 = (bf16[512,768]{1,0:T(8,128)(2,1)}, bf16[512,768]{1,0:T(8,128)(2,1)S(1)}, u32[]{:S(2)}) copy-start(bf16[512,768]{1,0:T(8,128)(2,1)S(1)} %collective-permute-done.9.refs_5_) | copy-start | bytes 2359300
  149.0 10.9 %collective-permute-start.14 = (bf16[64,2048]{1,0:T(8,128)(2,1)S(1)}, bf16[64,2048]{1,0:T(8,128)(2,1)S(1)}, u32[]{:S(2)}, u32[]{:S(2)}) collective-permute-start(bf16[64,2048]{1,0:T(8,128)(2,1)S(1)} %collective-permute-done.12.x0), channel_id=1, source_target_pairs={{0,2},{1,3},{2,0},{3,1},{4,6},{5,7},{6,4},{7,5},{8,10},{9,11},{10,... | collective-permute-start | bytes 786440 | tf_op jit(solution)/shard_map/ppermute | solution.py:195
  149.5 19.3 %copy-start.9 = (bf16[512,768]{1,0:T(8,128)(2,1)}, bf16[512,768]{1,0:T(8,128)(2,1)S(1)}, u32[]{:S(2)}) copy-start(bf16[512,768]{1,0:T(8,128)(2,1)S(1)} %collective-permute-done.8.refs_3_) | copy-start | bytes 2359300
  149.5 12.2 %collective-permute-start.15 = (bf16[64,2048]{1,0:T(8,128)(2,1)S(1)}, bf16[64,2048]{1,0:T(8,128)(2,1)S(1)}, u32[]{:S(2)}, u32[]{:S(2)}) collective-permute-start(bf16[64,2048]{1,0:T(8,128)(2,1)S(1)} %collective-permute-done.12.x0), channel_id=1, source_target_pairs={{0,3},{1,2},{2,1},{3,0},{4,7},{5,6},{6,5},{7,4},{8,11},{9,10},{10,... | collective-permute-start | bytes 786440 | tf_op jit(solution)/shard_map/ppermute | solution.py:195
  151.0 17.9 %copy-start.11 = (bf16[512,768]{1,0:T(8,128)(2,1)}, bf16[512,768]{1,0:T(8,128)(2,1)S(1)}, u32[]{:S(2)}) copy-start(bf16[512,768]{1,0:T(8,128)(2,1)S(1)} %collective-permute-done.11.refs_7_) | copy-start | bytes 2359300
  165.8 34.6 %collective-permute-start.16 = (bf16[256,1536]{1,0:T(8,128)(2,1)}, bf16[256,1536]{1,0:T(8,128)(2,1)}, u32[]{:S(2)}, u32[]{:S(2)}) collective-permute-start(bf16[256,1536]{1,0:T(8,128)(2,1)} %enter.3), channel_id=1, source_target_pairs={{0,8},{4,12},{8,0},{12,4},{16,24},{20,28},{24,16},{28,20},{1,9},{5... | collective-permute-start | bytes 2359304 | tf_op jit(solution)/shard_map/ppermute | solution.py:195
  168.2 7.9 %collective-permute-start.3 = (bf16[64,2048]{1,0:T(8,128)(2,1)S(1)}, bf16[64,2048]{1,0:T(8,128)(2,1)}, u32[]{:S(2)}, u32[]{:S(2)}) collective-permute-start(bf16[64,2048]{1,0:T(8,128)(2,1)S(1)} %get-tuple-element.25.x0), channel_id=1, source_target_pairs={{0,1},{1,0},{2,3},{3,2},{4,5},{5,4},{6,7},{7,6},{8,9},{9,8},{10,11... | collective-permute-start | bytes 786440 | tf_op jit(solution)/shard_map/ppermute | solution.py:195
  168.8 33.2 %collective-permute-start.20 = (bf16[768,512]{1,0:T(8,128)(2,1)S(1)}, bf16[768,512]{1,0:T(8,128)(2,1)S(1)}, u32[]{:S(2)}, u32[]{:S(2)}) collective-permute-start(bf16[768,512]{1,0:T(8,128)(2,1)S(1)} %bitcast.10), channel_id=1, source_target_pairs={{0,4},{4,0},{8,12},{12,8},{16,20},{20,16},{24,28},{28,24},{1,5},{5... | collective-permute-start | bytes 2359304 | tf_op jit(solution)/shard_map/ppermute | solution.py:195
  168.9 33.2 %collective-permute-start.22 = (bf16[768,512]{1,0:T(8,128)(2,1)S(1)}, bf16[768,512]{1,0:T(8,128)(2,1)S(1)}, u32[]{:S(2)}, u32[]{:S(2)}) collective-permute-start(bf16[768,512]{1,0:T(8,128)(2,1)S(1)} %collective-permute-done.21.d2), channel_id=1, source_target_pairs={{0,4},{4,0},{8,12},{12,8},{16,20},{20,16},{24,28},{28,24},{1,5},{5... | collective-permute-start | bytes 2359304 | tf_op jit(solution)/shard_map/ppermute | solution.py:195
  169.5 6.5 %collective-permute-start.17 = (f32[64,1]{1,0:T(8,128)S(1)}, f32[64,1]{1,0:T(8,128)S(1)}, u32[]{:S(2)}, u32[]{:S(2)}) collective-permute-start(f32[64,1]{1,0:T(8,128)S(1)} %copy.12), channel_id=1, source_target_pairs={{0,1},{1,0},{2,3},{3,2},{4,5},{5,4},{6,7},{7,6},{8,9},{9,8},{10,11... | collective-permute-start | bytes 776 | tf_op jit(solution)/shard_map/ppermute | solution.py:195
  176.1 12.1 %collective-permute-start.4 = (bf16[64,2048]{1,0:T(8,128)(2,1)S(1)}, bf16[64,2048]{1,0:T(8,128)(2,1)}, u32[]{:S(2)}, u32[]{:S(2)}) collective-permute-start(bf16[64,2048]{1,0:T(8,128)(2,1)S(1)} %get-tuple-element.25.x0), channel_id=1, source_target_pairs={{0,2},{1,3},{2,0},{3,1},{4,6},{5,7},{6,4},{7,5},{8,10},{9,11},{10,... | collective-permute-start | bytes 786440 | tf_op jit(solution)/shard_map/ppermute | solution.py:195
  176.1 12.8 %collective-permute-start.5 = (bf16[64,2048]{1,0:T(8,128)(2,1)S(1)}, bf16[64,2048]{1,0:T(8,128)(2,1)}, u32[]{:S(2)}, u32[]{:S(2)}) collective-permute-start(bf16[64,2048]{1,0:T(8,128)(2,1)S(1)} %get-tuple-element.25.x0), channel_id=1, source_target_pairs={{0,3},{1,2},{2,1},{3,0},{4,7},{5,6},{6,5},{7,4},{8,11},{9,10},{10,... | collective-permute-start | bytes 786440 | tf_op jit(solution)/shard_map/ppermute | solution.py:195
  188.1 12.2 %collective-permute-start.18 = (f32[64,1]{1,0:T(8,128)}, f32[64,1]{1,0:T(8,128)S(1)}, u32[]{:S(2)}, u32[]{:S(2)}) collective-permute-start(f32[64,1]{1,0:T(8,128)} %copy.13), channel_id=1, source_target_pairs={{0,2},{1,3},{2,0},{3,1},{4,6},{5,7},{6,4},{7,5},{8,10},{9,11},{10,... | collective-permute-start | bytes 776 | tf_op jit(solution)/shard_map/ppermute | solution.py:195
  188.9 11.5 %collective-permute-start.19 = (f32[64,1]{1,0:T(8,128)}, f32[64,1]{1,0:T(8,128)S(1)}, u32[]{:S(2)}, u32[]{:S(2)}) collective-permute-start(f32[64,1]{1,0:T(8,128)} %copy.14), channel_id=1, source_target_pairs={{0,3},{1,2},{2,1},{3,0},{4,7},{5,6},{6,5},{7,4},{8,11},{9,10},{10,... | collective-permute-start | bytes 776 | tf_op jit(solution)/shard_map/ppermute | solution.py:195
  190.1 1.1 copy-start.2
  191.2 1.1 copy-start.4
  192.4 1.1 copy-start.6
  193.5 1.1 copy-start.8
  194.6 1.1 copy-start.10
  195.8 1.1 copy-start.12
  201.8 9.2 %collective-permute-start.26 = (bf16[256,768]{1,0:T(8,128)(2,1)S(1)}, bf16[256,768]{1,0:T(8,128)(2,1)S(1)}, u32[]{:S(2)}, u32[]{:S(2)}) collective-permute-start(bf16[256,768]{1,0:T(8,128)(2,1)S(1)} %silu.1.hidden), channel_id=1, source_target_pairs={{0,8},{4,12},{8,0},{12,4},{16,24},{20,28},{24,16},{28,20},{1,9},{5... | collective-permute-start | bytes 1179656 | tf_op jit(solution)/shard_map/ppermute | solution.py:195
  212.1 6.9 %copy-start.17 = (bf16[64,2048]{1,0:T(8,128)(2,1)}, bf16[64,2048]{1,0:T(8,128)(2,1)S(1)}, u32[]{:S(2)}) copy-start(bf16[64,2048]{1,0:T(8,128)(2,1)S(1)} %get-tuple-element.31.y0) | copy-start | bytes 786436
  212.1 9.3 %collective-permute-start.27 = (bf16[64,2048]{1,0:T(8,128)(2,1)S(1)}, bf16[64,2048]{1,0:T(8,128)(2,1)S(1)}, u32[]{:S(2)}, u32[]{:S(2)}) collective-permute-start(bf16[64,2048]{1,0:T(8,128)(2,1)S(1)} %get-tuple-element.32), channel_id=1, source_target_pairs={{0,1},{1,0},{2,3},{3,2},{4,5},{5,4},{6,7},{7,6},{8,9},{9,8},{10,11... | collective-permute-start | bytes 786440 | tf_op jit(solution)/shard_map/ppermute | solution.py:195
  213.7 14.9 %collective-permute-start.28 = (bf16[64,2048]{1,0:T(8,128)(2,1)S(1)}, bf16[64,2048]{1,0:T(8,128)(2,1)S(1)}, u32[]{:S(2)}, u32[]{:S(2)}) collective-permute-start(bf16[64,2048]{1,0:T(8,128)(2,1)S(1)} %get-tuple-element.33), channel_id=1, source_target_pairs={{0,2},{1,3},{2,0},{3,1},{4,6},{5,7},{6,4},{7,5},{8,10},{9,11},{10,... | collective-permute-start | bytes 786440 | tf_op jit(solution)/shard_map/ppermute | solution.py:195
  213.9 14.6 %collective-permute-start.29 = (bf16[64,2048]{1,0:T(8,128)(2,1)S(1)}, bf16[64,2048]{1,0:T(8,128)(2,1)S(1)}, u32[]{:S(2)}, u32[]{:S(2)}) collective-permute-start(bf16[64,2048]{1,0:T(8,128)(2,1)S(1)} %get-tuple-element.34), channel_id=1, source_target_pairs={{0,3},{1,2},{2,1},{3,0},{4,7},{5,6},{6,5},{7,4},{8,11},{9,10},{10,... | collective-permute-start | bytes 786440 | tf_op jit(solution)/shard_map/ppermute | solution.py:195
  217.5 15.5 %collective-permute-start.23 = (bf16[64,2048]{1,0:T(8,128)(2,1)}, bf16[64,2048]{1,0:T(8,128)(2,1)S(1)}, u32[]{:S(2)}, u32[]{:S(2)}) collective-permute-start(bf16[64,2048]{1,0:T(8,128)(2,1)} %get-tuple-element.28), channel_id=1, source_target_pairs={{0,1},{1,0},{2,3},{3,2},{4,5},{5,4},{6,7},{7,6},{8,9},{9,8},{10,11... | collective-permute-start | bytes 786440 | tf_op jit(solution)/shard_map/ppermute | solution.py:195
  219.0 16.6 %collective-permute-start.24 = (bf16[64,2048]{1,0:T(8,128)(2,1)}, bf16[64,2048]{1,0:T(8,128)(2,1)S(1)}, u32[]{:S(2)}, u32[]{:S(2)}) collective-permute-start(bf16[64,2048]{1,0:T(8,128)(2,1)} %get-tuple-element.29), channel_id=1, source_target_pairs={{0,2},{1,3},{2,0},{3,1},{4,6},{5,7},{6,4},{7,5},{8,10},{9,11},{10,... | collective-permute-start | bytes 786440 | tf_op jit(solution)/shard_map/ppermute | solution.py:195
  221.4 7.2 %copy-start.19 = (bf16[64,2048]{1,0:T(8,128)(2,1)}, bf16[64,2048]{1,0:T(8,128)(2,1)S(1)}, u32[]{:S(2)}) copy-start(bf16[64,2048]{1,0:T(8,128)(2,1)S(1)} %collective-permute-done.27.r1) | copy-start | bytes 786436
  221.4 14.2 %collective-permute-start.25 = (bf16[64,2048]{1,0:T(8,128)(2,1)}, bf16[64,2048]{1,0:T(8,128)(2,1)S(1)}, u32[]{:S(2)}, u32[]{:S(2)}) collective-permute-start(bf16[64,2048]{1,0:T(8,128)(2,1)} %get-tuple-element.30), channel_id=1, source_target_pairs={{0,3},{1,2},{2,1},{3,0},{4,7},{5,6},{6,5},{7,4},{8,11},{9,10},{10,... | collective-permute-start | bytes 786440 | tf_op jit(solution)/shard_map/ppermute | solution.py:195
  228.5 0.7 copy-start.20
  229.2 0.7 copy-start.21
  232.0 6.6 %collective-permute-start.30 = (bf16[64,2048]{1,0:T(8,128)(2,1)}, bf16[64,2048]{1,0:T(8,128)(2,1)S(1)}, u32[]{:S(2)}, u32[]{:S(2)}) collective-permute-start(bf16[64,2048]{1,0:T(8,128)(2,1)} %total.1), channel_id=1, source_target_pairs={{0,8},{4,12},{8,0},{12,4},{16,24},{20,28},{24,16},{28,20},{1,9},{5... | collective-permute-start | bytes 786440 | tf_op jit(solution)/shard_map/ppermute | solution.py:195
  238.5 1.0 copy-start.14
Sparse Core Ops, SparseCore 0:
  9.0 52.5 all-gather.1

commit v2 on v1

--- a/solution.py
+++ b/solution.py
@@ -1,3 +1,4 @@
+import functools
 import math
 
 import jax
@@ -186,7 +187,6 @@
 F32 = jnp.float32
 VMEM = pltpu.VMEM
 QB = 256
-CHUNK = 4
 CHEAP = pl.CostEstimate(flops=1000, bytes_accessed=1000, transcendentals=0)
 
 
@@ -203,87 +203,108 @@
     return [pl.BlockSpec(memory_space=VMEM) for _ in range(count)]
 
 
-def attention_kernel(index, q, kv, w_hbm, p0, p1, p2, p3, w_all, scores, ones_values, attn, sem):
+def attention_kernel(index, q, *refs):
+    pieces, w_hbm, outs = refs[:8], refs[8], refs[9:13]
+    w_all, keys, ones_values, bias, even, odd, attn, sems = refs[13:]
     ctx = index[0]
     exp = index[1]
-    fetch = pltpu.make_async_copy(w_hbm, w_all, sem)
-    fetch.start()
+    chip = ctx // 2
+    steps = sems.shape[0]
+    depth = w_all.shape[0] // steps
+    fetches = [
+        pltpu.make_async_copy(
+            w_hbm.at[pl.ds(i * depth, depth)], w_all.at[pl.ds(i * depth, depth)], sems.at[i]
+        )
+        for i in range(steps)
+    ]
+    for fetch in fetches:
+        fetch.start()
     factor = math.log2(math.e) / math.sqrt(HD)
-    rows = CHUNK * QB
     heads = q.shape[1] // HD
-    ones_values[:, :HD] = kv[:, HD:]
-    ones_values[:, HD:] = jnp.ones((kv.shape[0], HD), BF16)
-    row = lax.broadcasted_iota(jnp.int32, (QB, QB), 0)
-    col = lax.broadcasted_iota(jnp.int32, (QB, QB), 1)
-    hidden_keys = jnp.concatenate([jnp.where(col <= row, 0.0, -1e30)] * CHUNK, axis=0)
-    for chunk in range(heads // CHUNK):
-        first = chunk * CHUNK
-        queries = jnp.concatenate(
-            [q[:, (first + h) * HD : (first + h + 1) * HD] for h in range(CHUNK)], axis=0
-        )
-
-        def score_block(j):
-            block = kv[pl.ds(pl.multiple_of(j * QB, QB), QB), :HD]
-            return lax.dot_general(
-                queries, block, (((1,), (1,)), ((), ())), preferred_element_type=F32
-            )
-
-        def first_pass(j, top):
-            block = score_block(j)
-            scores[j] = block
-            return jnp.maximum(top, jnp.maximum(block[:, :HD], block[:, HD:]))
-
-        last = score_block(ctx) + hidden_keys
-        scores[ctx] = last
-        top = jnp.maximum(last[:, :HD], last[:, HD:])
-        top = lax.fori_loop(0, ctx, first_pass, top)
-        top = jnp.max(top, axis=1, keepdims=True) * factor
-
-        def second_pass(j, total):
-            probs = jnp.exp2(scores[j] * factor - top).astype(BF16)
-            block = ones_values[pl.ds(pl.multiple_of(j * QB, QB), QB), :]
-            return total + jnp.dot(probs, block, preferred_element_type=F32)
-
-        total = lax.fori_loop(0, ctx + 1, second_pass, jnp.zeros((rows, 2 * HD), F32))
-        done = (total[:, :HD] / total[:, HD:]).astype(BF16)
-        part = QB // 4
-        for h in range(CHUNK):
+    ones_values[:, HD:] = jnp.ones((ones_values.shape[0], HD), BF16)
+    core = ctx % 2
+    for d in range(4):
+
+        @pl.when(chip >= d)
+        def _():
+            for other in range(2):
+                piece = pieces[2 * d + other]
+                place = 2 * (chip - d) + (core ^ other)
+                here = pl.ds(pl.multiple_of(place * QB, QB), QB)
+                keys[:, here] = piece[:, :HD].astype(F32).T.astype(BF16)
+                ones_values[here, :HD] = piece[:, HD:]
+
+    row = lax.broadcasted_iota(jnp.int32, (QB, 2 * QB), 0) + core * QB
+    col = lax.broadcasted_iota(jnp.int32, (QB, 2 * QB), 1)
+    bias[...] = jnp.where(col <= row, 0.0, -1e30)
+    part = QB // 4
+
+    def run(length):
+        def scores_of(h, store):
+            rows = q[:, pl.ds(pl.multiple_of(h * HD, HD), HD)]
+            block = jnp.dot(rows, keys[:, :length], preferred_element_type=F32)
+            last = length - 2 * QB
+            if last:
+                store[:, :last] = block[:, :last]
+            store[:, last:length] = block[:, last:] + bias[...]
+
+        def finish(h, store):
+            block = store[:, :length]
+            top = jnp.max(block, axis=1, keepdims=True) * factor
+            probs = jnp.exp2(block * factor - top).astype(BF16)
+            total = jnp.dot(probs, ones_values[:length, :], preferred_element_type=F32)
+            done = (total[:, :HD] / total[:, HD:]).astype(BF16)
+            cols = pl.ds(pl.multiple_of(h * HD, HD), HD)
             for i in range(4):
                 start = pl.multiple_of((exp ^ i) * part, part)
-                attn[pl.ds(start, part), (first + h) * HD : (first + h + 1) * HD] = done[
-                    h * QB + i * part : h * QB + (i + 1) * part
-                ]
-    fetch.wait()
-    part = QB // 4
+                attn[pl.ds(start, part), cols] = done[i * part : (i + 1) * part]
+
+        scores_of(0, even)
+
+        @pl.loop(0, heads // 2)
+        def _(pair):
+            scores_of(2 * pair + 1, odd)
+            finish(2 * pair, even)
+            scores_of(jnp.minimum(2 * pair + 2, heads - 1), even)
+            finish(2 * pair + 1, odd)
+
+    for z in range(4):
+        pl.when(chip == z)(functools.partial(run, (z + 1) * 2 * QB))
+
+    for fetch in fetches:
+        fetch.wait()
     width = 512
     for n in range(w_all.shape[1] // width):
         cols = slice(n * width, (n + 1) * width)
         block = jnp.dot(attn[...], w_all[:, cols], preferred_element_type=F32).astype(BF16)
-        for b, out in enumerate((p0, p1, p2, p3)):
+        for b, out in enumerate(outs):
             out[:, cols] = block[b * part : (b + 1) * part]
 
 
-def attention(index, queries, kv, w_out):
+def attention(index, queries, pieces, w_out):
     rows = QB // 4
-    blocks = kv.shape[0] // QB
+    length = 8 * QB
     return pl.pallas_call(
         attention_kernel,
         out_shape=[jax.ShapeDtypeStruct((rows, D), BF16)] * 4,
         in_specs=[pl.BlockSpec(memory_space=pltpu.SMEM)]
-        + vmem_specs(2)
+        + vmem_specs(9)
         + [pl.BlockSpec(memory_space=pl.ANY)],
         out_specs=vmem_specs(4),
         scratch_shapes=[
             VMEM(w_out.shape, BF16),
-            VMEM((blocks, CHUNK * QB, QB), F32),
-            VMEM((kv.shape[0], 2 * HD), BF16),
+            VMEM((HD, length), BF16),
+            VMEM((length, 2 * HD), BF16),
+            VMEM((QB, 2 * QB), F32),
+            VMEM((QB, length), F32),
+            VMEM((QB, length), F32),
             VMEM(queries.shape, BF16),
-            pltpu.SemaphoreType.DMA,
+            pltpu.SemaphoreType.DMA((16,)),
         ],
-        compiler_params=params(56),
+        compiler_params=params(52),
         cost_estimate=CHEAP,
         name="attention",
-    )(index, queries, kv, w_out)
+    )(index, queries, *pieces, w_out)
 
 
 def norm_kernel(index, p0, r1, r2, r3, residual, gain, state, mine, theirs, work):
@@ -318,29 +339,43 @@
 
 
 def enter_kernel(x0, x1, x2, x3, *refs):
-    gates, ups, out = refs[:4], refs[4:8], refs[8]
+    weights, out, gate_all, up_all, sems = refs[:4], refs[4], refs[5], refs[6], refs[7]
+    part, width = weights[0].shape[0] // 2, weights[0].shape[1]
+    fetches = []
+    for which, whole in enumerate((gate_all, up_all)):
+        for j, array in enumerate(weights):
+            source = array.at[pl.ds(which * part, part)]
+            target = whole.at[pl.ds(j * part, part)]
+            fetches.append(pltpu.make_async_copy(source, target, sems.at[4 * which + j]))
+            fetches[-1].start()
     x = jnp.concatenate([x0[...], x1[...], x2[...], x3[...]], axis=0)
-    part, width = gates[0].shape
-    for which, weights in enumerate((gates, ups)):
-        total = jnp.zeros((x.shape[0], width), F32)
-        for j in range(4):
-            total = total + jnp.dot(
-                x[:, j * part : (j + 1) * part], weights[j][...], preferred_element_type=F32
-            )
-        out[:, which * width : (which + 1) * width] = total.astype(out.dtype)
-
-
-def enter(rows, gates, ups, kind):
+    tile = 256
+    for which, whole in enumerate((gate_all, up_all)):
+        for fetch in fetches[4 * which : 4 * which + 4]:
+            fetch.wait()
+        for n in range(width // tile):
+            cols = slice(which * width + n * tile, which * width + (n + 1) * tile)
+            block = jnp.dot(x, whole[:, n * tile : (n + 1) * tile], preferred_element_type=F32)
+            out[:, cols] = block.astype(out.dtype)
+
+
+def enter(rows, weights, kind):
     count = 4 * rows[0].shape[0]
+    part, width = weights[0].shape[0] // 2, weights[0].shape[1]
     return pl.pallas_call(
         enter_kernel,
-        out_shape=jax.ShapeDtypeStruct((count, 2 * gates[0].shape[1]), kind),
-        in_specs=vmem_specs(12),
+        out_shape=jax.ShapeDtypeStruct((count, 2 * width), kind),
+        in_specs=vmem_specs(4) + [pl.BlockSpec(memory_space=pl.ANY)] * 4,
         out_specs=pl.BlockSpec(memory_space=VMEM),
-        compiler_params=params(32),
+        scratch_shapes=[
+            VMEM((4 * part, width), BF16),
+            VMEM((4 * part, width), BF16),
+            pltpu.SemaphoreType.DMA((8,)),
+        ],
+        compiler_params=params(24),
         cost_estimate=CHEAP,
         name="enter",
-    )(*rows, *gates, *ups)
+    )(*rows, *weights)
 
 
 def silu_kernel(own, other, c0, c1, c2, c3, out):
@@ -351,7 +386,7 @@
     hidden = gate / (1.0 + jnp.exp(-gate)) * up
     for b, share in enumerate((c0, c1, c2, c3)):
         rows = slice(b * part, (b + 1) * part)
-        out[rows] = (hidden[rows] * share[...]).astype(BF16)
+        out[rows] = (hidden[rows] * share[:, :1]).astype(BF16)
 
 
 def silu(own, other, shares):
@@ -366,11 +401,16 @@
     )(own, other, *shares)
 
 
-def leave_kernel(hidden, d0, d1, d2, d3, y0, y1, y2, y3):
+def leave_kernel(hidden, d0, d1, d2, d3, y0, y1, y2, y3, down_all, sems):
     part = y0.shape[0]
     width = d0.shape[1]
-    for j, weights in enumerate((d0, d1, d2, d3)):
-        block = jnp.dot(hidden[...], weights[...], preferred_element_type=F32).astype(BF16)
+    fetches = []
+    for j, array in enumerate((d0, d1, d2, d3)):
+        fetches.append(pltpu.make_async_copy(array, down_all.at[j], sems.at[j]))
+        fetches[-1].start()
+    for j in range(4):
+        fetches[j].wait()
+        block = jnp.dot(hidden[...], down_all[j], preferred_element_type=F32).astype(BF16)
         for b, out in enumerate((y0, y1, y2, y3)):
             out[:, j * width : (j + 1) * width] = block[b * part : (b + 1) * part]
 
@@ -380,8 +420,9 @@
     return pl.pallas_call(
         leave_kernel,
         out_shape=[part] * 4,
-        in_specs=vmem_specs(5),
+        in_specs=vmem_specs(1) + [pl.BlockSpec(memory_space=pl.ANY)] * 4,
         out_specs=vmem_specs(4),
+        scratch_shapes=[VMEM((4,) + downs[0].shape, BF16), pltpu.SemaphoreType.DMA((4,))],
         compiler_params=params(16),
         cost_estimate=CHEAP,
         name="leave",
@@ -453,32 +494,42 @@
         ],
         axis=1,
     )
-    kv = lax.all_gather(kv_here, "ctx", axis=0, tiled=True)
+    pair_here, down_here = jnp.concatenate([w_gate[0], w_up[0]], axis=0), w_down[0]
+
+    def later(array, chips):
+        return lax.ppermute(array, "ctx", [(i, i + 2 * chips) for i in range(8 - 2 * chips)])
+
+    pieces = [kv_here] + [later(kv_here, d) for d in (3, 2, 1)][::-1]
+    pieces = [part for piece in pieces for part in (piece, swap(piece, "ctx", 1))]
 
     shares = []
     for b in range(4):
         share = jnp.sum(jnp.where(expert_ids == (exp ^ b), gate_weights, 0.0), axis=1, keepdims=True)
+        share = jnp.broadcast_to(share, (share.shape[0], HD))
         shares.append(swap(share, "exp", b) if b else share)
-
-    def slices(array):
-        far = swap(array, "ctx", 6)
-        return (array, swap(array, "ctx", 1), far, swap(far, "ctx", 1))
-
-    gates = slices(w_gate[0])
-    ups = slices(w_up[0])
-
-    p = attention(index, queries, kv, w_out)
+    near = [swap(array, "ctx", 1) for array in (pair_here, down_here)]
+
+    pieces, shares, near, pair_here = lax.optimization_barrier((pieces, shares, near, pair_here))
+    pair_far = swap(pair_here, "ctx", 6)
+
+    p = attention(index, queries, pieces, w_out)
     r = [swap(p[b], "exp", b) for b in (1, 2, 3)]
     state, mine, theirs = norm(index, p[0], *r, residual, norm_gain.reshape(1, D))
-    downs = slices(w_down[0])
     others = swap(theirs, "ctx", 2)
+    own_rows = [mine] + [swap(mine, "exp", b) for b in (1, 2, 3)]
     other_rows = [others] + [swap(others, "exp", b) for b in (1, 2, 3)]
-    own_rows = [mine] + [swap(mine, "exp", b) for b in (1, 2, 3)]
-    other_pre = enter(other_rows, gates, ups, BF16)
+    own_rows, other_rows, pair_far, down_here = lax.optimization_barrier(
+        (own_rows, other_rows, pair_far, down_here)
+    )
+    down_far = swap(down_here, "ctx", 6)
+    pairs = (pair_here, near[0], pair_far, swap(pair_far, "ctx", 1))
+    other_pre = enter(other_rows, pairs, BF16)
     from_other = swap(other_pre, "ctx", 2)
-    own_pre = enter(own_rows, gates, ups, F32)
+    own_pre = enter(own_rows, pairs, F32)
     own_hidden = silu(own_pre, from_other, shares)
     other_hidden = swap(own_hidden, "ctx", 2)
+    own_hidden, down_far = lax.optimization_barrier((own_hidden, down_far))
+    downs = (down_here, near[1], down_far, swap(down_far, "ctx", 1))
     y = leave(own_hidden, downs)
     own_parts = [y[0]] + [swap(y[b], "exp", b) for b in (1, 2, 3)]
     z = leave(other_hidden, downs)

time: 249 us -> 198 us (0.80)
  the two profiles are of different devices: /device:TPU:22 before, /device:TPU:0 now
where the time goes in v2:
time: 198 us
  waiting for transfers between devices  102 us (52%)
  starting transfers between devices  51.1 us (26%)
  Pallas kernels  30.9 us (16%)
  local copies, waits for them, and re-layouts  12.3 us (6%)
    ppermute x32, waiting for transfers between devices, swap(): return lax.ppermute(array, axis, [(i, i ^ mask) for i in range(size)])  98.7 us
    ppermute x32, starting transfers between devices, swap(): return lax.ppermute(array, axis, [(i, i ^ mask) for i in range(size)])  40.4 us
    pallas_call x1, Pallas kernels, attention(): pl.pallas_call(attention_kernel, out_shape=[jax.ShapeDtypeStruct((rows, D...  12.8 us
    ppermute x3, starting transfers between devices, later(): lax.ppermute(array, 'ctx', [(i, i + 2 * chips) for i in range(8 - 2 * chi...  10.7 us
    unnamed x54, local copies, waits for them, and re-layouts  10.5 us
    pallas_call x2, Pallas kernels, enter(): pl.pallas_call(enter_kernel, out_shape=jax.ShapeDtypeStruct((count, 2 * w...  7.58 us
    pallas_call x2, Pallas kernels, leave(): pl.pallas_call(leave_kernel, out_shape=[part] * 4, in_specs=vmem_specs(1)...  5.3 us
  transfers between devices with their start and end apart: 35, of which 20 were waited for; matrix products, arithmetic and copies ran while one was open for 1% of the time, Pallas kernels for 12%

profile of v2, /device:TPU:0, one launch (start us, length us, event | category | flops | bytes accessed | tf_op | source)
XLA Modules:
  0.0 197.8 jit_solution(15753989347464983420)
XLA Ops:
  0.0 1.5 pad_maximum_fusion.refs_0_
  2.1 0.9 constant_dynamic-slice_fusion
  3.0 4.9 %collective-permute-start.1 = (bf16[256,256]{1,0:T(8,128)(2,1)S(1)}, bf16[256,256]{1,0:T(8,128)(2,1)S(1)}, u32[]{:S(2)}, u32[]{:S(2)}) collective-permute-start(bf16[256,256]{1,0:T(8,128)(2,1)S(1)} %pad_maximum_fusion.1.refs_0_), channel_id=1, source_target_pairs={{0,8},{4,12},{8,16},{12,20},{16,24},{20,28},{1,9},{5,13},{9,17},{1... | collective-permute-start | bytes 393224 | tf_op jit(solution)/shard_map/ppermute | solution.py:500
  8.1 1.5 collective-permute-start.7
  9.6 1.5 collective-permute-start.8
  11.2 0.8 collective-permute-done.7.c1
  12.1 2.5 %collective-permute-start.9 = (f32[64,128]{1,0:T(8,128)S(1)}, f32[64,128]{1,0:T(8,128)S(1)}, u32[]{:S(2)}, u32[]{:S(2)}) collective-permute-start(f32[64,128]{1,0:T(8,128)S(1)} %broadcast_in_dim.35), channel_id=1, source_target_pairs={{0,3},{1,2},{2,1},{3,0},{4,7},{5,6},{6,5},{7,4},{8,11},{9,10},{10,... | collective-permute-start | bytes 98312 | tf_op jit(solution)/shard_map/ppermute | solution.py:195
  14.5 0.6 copy-done.17
  15.1 4.5 %collective-permute-start.3 = (bf16[256,256]{1,0:T(8,128)(2,1)S(1)}, bf16[256,256]{1,0:T(8,128)(2,1)S(1)}, u32[]{:S(2)}, u32[]{:S(2)}) collective-permute-start(bf16[256,256]{1,0:T(8,128)(2,1)S(1)} %pad_maximum_fusion.1.refs_0_), channel_id=1, source_target_pairs={{0,16},{4,20},{8,24},{12,28},{1,17},{5,21},{9,25},{13,29},{2,18},{... | collective-permute-start | bytes 393224 | tf_op jit(solution)/shard_map/ppermute | solution.py:500
  19.6 0.6 copy-done.19
  20.2 1.3 collective-permute-start.5
  21.6 1.5 collective-permute-done.3.refs_4_
  23.1 1.4 collective-permute-done.5.refs_6_
  24.5 0.7 copy-done.6
  25.7 0.7 copy-done.4
  26.3 0.6 copy-done.8
  27.0 0.7 copy-done.10
  27.6 0.7 copy-done.12
  28.3 0.7 broadcast_in_dim.16.c0
  29.0 5.2 %collective-permute-start.22 = (bf16[1024,768]{1,0:T(8,128)(2,1)S(1)}, bf16[1024,768]{1,0:T(8,128)(2,1)}, u32[]{:S(2)}, u32[]{:S(2)}) collective-permute-start(bf16[1024,768]{1,0:T(8,128)(2,1)S(1)} %pad_maximum_fusion.refs_0_), channel_id=1, source_target_pairs={{0,24},{4,28},{8,16},{12,20},{16,8},{20,12},{24,0},{28,4},{1,25},{... | collective-permute-start | bytes 4718600 | tf_op jit(solution)/shard_map/ppermute | solution.py:195
  34.3 0.9 copy-done.5
  35.2 0.9 copy-done.7
  36.1 0.9 copy-done.9
  37.0 0.9 copy-done.11
  37.9 0.9 copy-done.13
  38.8 12.8 %attention.1 = (bf16[64,4096]{1,0:T(8,128)(2,1)S(1)}, bf16[64,4096]{1,0:T(8,128)(2,1)}, bf16[64,4096]{1,0:T(8,128)(2,1)}, bf16[64,4096]{1,0:T(8,128)(2,1)}) custom-call(s32[2]{0:T(128)S(1)} %pad_add_fusion.index, bf16[256,2048]{1,0:T(8,128)(2,1)} %q.1, bf16[256,256]{1,0:T(8,128)(2,1)S(1)} %pad_maximum_fusion.1.refs_0_, bf16[256,256]{1,0:T(8,128)(2,1)S(1)} %copy-done.7, ...), custom_call_target="tpu_custom_call" | custom-call | flops 1000 | bytes 1000 | tf_op jit(solution)/shard_map/attention/pallas_call | solution.py:287
  51.6 0.6 collective-permute-start.12
  52.8 2.4 %collective-permute-start.14 = (bf16[64,4096]{1,0:T(8,128)(2,1)}, bf16[64,4096]{1,0:T(8,128)(2,1)S(1)}, u32[]{:S(2)}, u32[]{:S(2)}) collective-permute-start(bf16[64,4096]{1,0:T(8,128)(2,1)} %get-tuple-element.58), channel_id=1, source_target_pairs={{0,3},{1,2},{2,1},{3,0},{4,7},{5,6},{6,5},{7,4},{8,11},{9,10},{10,... | collective-permute-start | bytes 1572872 | tf_op jit(solution)/shard_map/ppermute | solution.py:195
  55.2 11.5 %collective-permute-done.12.r1 = bf16[64,4096]{1,0:T(8,128)(2,1)S(1)} collective-permute-done((bf16[64,4096]{1,0:T(8,128)(2,1)}, bf16[64,4096]{1,0:T(8,128)(2,1)S(1)}, u32[]{:S(2)}, u32[]{:S(2)}) %collective-permute-start.12) | collective-permute-done | bytes 524320 | tf_op jit(solution)/shard_map/ppermute | solution.py:195
  66.6 10.8 %collective-permute-done.13.r2 = bf16[64,4096]{1,0:T(8,128)(2,1)S(1)} collective-permute-done((bf16[64,4096]{1,0:T(8,128)(2,1)}, bf16[64,4096]{1,0:T(8,128)(2,1)S(1)}, u32[]{:S(2)}, u32[]{:S(2)}) %collective-permute-start.13) | collective-permute-done | bytes 524320 | tf_op jit(solution)/shard_map/ppermute | solution.py:195
  77.4 1.2 norm.1
  78.6 0.8 copy-done
  79.4 1.5 collective-permute-start.15
  81.4 1.5 collective-permute-start.17
  82.9 3.8 %collective-permute-done.18.x0 = bf16[64,2048]{1,0:T(8,128)(2,1)S(1)} collective-permute-done((bf16[64,2048]{1,0:T(8,128)(2,1)S(1)}, bf16[64,2048]{1,0:T(8,128)(2,1)S(1)}, u32[]{:S(2)}, u32[]{:S(2)}) %collective-permute-start.18) | collective-permute-done | bytes 262176 | tf_op jit(solution)/shard_map/ppermute | solution.py:195
  86.7 1.4 collective-permute-start.19
  88.6 1.2 collective-permute-start.20
  89.8 3.2 %collective-permute-done.16.x2 = bf16[64,2048]{1,0:T(8,128)(2,1)S(1)} collective-permute-done((bf16[64,2048]{1,0:T(8,128)(2,1)S(1)}, bf16[64,2048]{1,0:T(8,128)(2,1)S(1)}, u32[]{:S(2)}, u32[]{:S(2)}) %collective-permute-start.16) | collective-permute-done | bytes 262176 | tf_op jit(solution)/shard_map/ppermute | solution.py:195
  93.1 1.3 collective-permute-start.21
  94.4 0.6 collective-permute-done.17.x3
  94.9 5.0 %collective-permute-done.19.x1 = bf16[64,2048]{1,0:T(8,128)(2,1)S(1)} collective-permute-done((bf16[64,2048]{1,0:T(8,128)(2,1)S(1)}, bf16[64,2048]{1,0:T(8,128)(2,1)S(1)}, u32[]{:S(2)}, u32[]{:S(2)}) %collective-permute-start.19) | collective-permute-done | bytes 262176 | tf_op jit(solution)/shard_map/ppermute | solution.py:195
  99.9 4.8 %collective-permute-done.20.x2 = bf16[64,2048]{1,0:T(8,128)(2,1)S(1)} collective-permute-done((bf16[64,2048]{1,0:T(8,128)(2,1)S(1)}, bf16[64,2048]{1,0:T(8,128)(2,1)S(1)}, u32[]{:S(2)}, u32[]{:S(2)}) %collective-permute-start.20) | collective-permute-done | bytes 262176 | tf_op jit(solution)/shard_map/ppermute | solution.py:195
  104.8 3.6 %collective-permute-done.23.refs_3_ = bf16[1024,768]{1,0:T(8,128)(2,1)S(1)} collective-permute-done((bf16[1024,768]{1,0:T(8,128)(2,1)}, bf16[1024,768]{1,0:T(8,128)(2,1)S(1)}, u32[]{:S(2)}, u32[]{:S(2)}) %collective-permute-start.23) | collective-permute-done | bytes 1572896 | tf_op jit(solution)/shard_map/ppermute | solution.py:195
  108.4 3.8 %enter.3 = bf16[256,1536]{1,0:T(8,128)(2,1)S(1)} custom-call(bf16[64,2048]{1,0:T(8,128)(2,1)S(1)} %collective-permute-done.18.x0, bf16[64,2048]{1,0:T(8,128)(2,1)S(1)} %collective-permute-done.19.x1, bf16[64,2048]{1,0:T(8,128)(2,1)S(1)} %collective-permute-done.20.x2, bf16[64,2048]{1,0:T(8,128)(2,1)S(1)} %collective-permute-done.21.x3, ...), custom_call_target="tpu_custom_call" | custom-call | flops 1000 | bytes 1000 | tf_op jit(solution)/shard_map/enter/pallas_call | solution.py:365
  112.2 1.8 collective-permute-start.24
  114.0 8.3 %collective-permute-start.25 = (bf16[768,512]{1,0:T(8,128)(2,1)}, bf16[768,512]{1,0:T(8,128)(2,1)S(1)}, u32[]{:S(2)}, u32[]{:S(2)}) collective-permute-start(bf16[768,512]{1,0:T(8,128)(2,1)} %bitcast.4.d0), channel_id=1, source_target_pairs={{0,24},{4,28},{8,16},{12,20},{16,8},{20,12},{24,0},{28,4},{1,25},{... | collective-permute-start | bytes 2359304 | tf_op jit(solution)/shard_map/ppermute | solution.py:195
  122.4 3.8 %enter.2.own = f32[256,1536]{1,0:T(8,128)S(1)} custom-call(bf16[64,2048]{1,0:T(8,128)(2,1)S(1)} %get-tuple-element.63.x0, bf16[64,2048]{1,0:T(8,128)(2,1)S(1)} %collective-permute-done.15.x1, bf16[64,2048]{1,0:T(8,128)(2,1)S(1)} %collective-permute-done.16.x2, bf16[64,2048]{1,0:T(8,128)(2,1)S(1)} %collective-permute-done.17.x3, ...), custom_call_target="tpu_custom_call" | custom-call | flops 1000 | bytes 1000 | tf_op jit(solution)/shard_map/enter/pallas_call | solution.py:365
  126.2 5.8 %collective-permute-done.24.other = bf16[256,1536]{1,0:T(8,128)(2,1)S(1)} collective-permute-done((bf16[256,1536]{1,0:T(8,128)(2,1)S(1)}, bf16[256,1536]{1,0:T(8,128)(2,1)S(1)}, u32[]{:S(2)}, u32[]{:S(2)}) %collective-permute-start.24) | collective-permute-done | bytes 786464 | tf_op jit(solution)/shard_map/ppermute | solution.py:195
  132.3 24.5 %collective-permute-done.25.d2 = bf16[768,512]{1,0:T(8,128)(2,1)S(1)} collective-permute-done((bf16[768,512]{1,0:T(8,128)(2,1)}, bf16[768,512]{1,0:T(8,128)(2,1)S(1)}, u32[]{:S(2)}, u32[]{:S(2)}) %collective-permute-start.25) | collective-permute-done | bytes 786464 | tf_op jit(solution)/shard_map/ppermute | solution.py:195
  156.8 11.5 %collective-permute-done.30.hidden = bf16[256,768]{1,0:T(8,128)(2,1)S(1)} collective-permute-done((bf16[256,768]{1,0:T(8,128)(2,1)S(1)}, bf16[256,768]{1,0:T(8,128)(2,1)S(1)}, u32[]{:S(2)}, u32[]{:S(2)}) %collective-permute-start.30) | collective-permute-done | bytes 393248 | tf_op jit(solution)/shard_map/ppermute | solution.py:195
  168.3 2.7 %leave.3 = (bf16[64,2048]{1,0:T(8,128)(2,1)S(1)}, bf16[64,2048]{1,0:T(8,128)(2,1)S(1)}, bf16[64,2048]{1,0:T(8,128)(2,1)S(1)}, bf16[64,2048]{1,0:T(8,128)(2,1)S(1)}) custom-call(bf16[256,768]{1,0:T(8,128)(2,1)S(1)} %collective-permute-done.30.hidden, bf16[768,512]{1,0:T(8,128)(2,1)} %bitcast.4.d0, bf16[768,512]{1,0:T(8,128)(2,1)} %collective-permute-done.11.d1, ...), custom_call_target="tpu_custom_call" | custom-call | flops 1000 | bytes 1000 | tf_op jit(solution)/shard_map/leave/pallas_call | solution.py:420
  171.0 0.6 collective-permute-start.31
  171.6 1.5 collective-permute-start.32
  173.1 1.4 collective-permute-start.33
  174.5 2.6 %leave.2 = (bf16[64,2048]{1,0:T(8,128)(2,1)S(1)}, bf16[64,2048]{1,0:T(8,128)(2,1)S(1)}, bf16[64,2048]{1,0:T(8,128)(2,1)S(1)}, bf16[64,2048]{1,0:T(8,128)(2,1)S(1)}) custom-call(bf16[256,768]{1,0:T(8,128)(2,1)S(1)} %silu.1.hidden, bf16[768,512]{1,0:T(8,128)(2,1)} %bitcast.4.d0, bf16[768,512]{1,0:T(8,128)(2,1)} %collective-permute-done.11.d1, ...), custom_call_target="tpu_custom_call" | custom-call | flops 1000 | bytes 1000 | tf_op jit(solution)/shard_map/leave/pallas_call | solution.py:420
  177.2 0.6 collective-permute-start.27
  177.8 1.5 collective-permute-start.28
  179.3 0.9 collective-permute-done.31.r1
  180.3 1.5 collective-permute-start.29
  181.8 3.6 %collective-permute-done.32.r2 = bf16[64,2048]{1,0:T(8,128)(2,1)S(1)} collective-permute-done((bf16[64,2048]{1,0:T(8,128)(2,1)S(1)}, bf16[64,2048]{1,0:T(8,128)(2,1)S(1)}, u32[]{:S(2)}, u32[]{:S(2)}) %collective-permute-start.32) | collective-permute-done | bytes 262176 | tf_op jit(solution)/shard_map/ppermute | solution.py:195
  186.6 2.0 %total.1 = bf16[64,2048]{1,0:T(8,128)(2,1)} custom-call(bf16[64,2048]{1,0:T(8,128)(2,1)} %copy-done.3, bf16[64,2048]{1,0:T(8,128)(2,1)} %copy-done.21, bf16[64,2048]{1,0:T(8,128)(2,1)} %copy-done.22, bf16[64,2048]{1,0:T(8,128)(2,1)} %copy-done.23), custom_call_target="tpu_custom_call" | custom-call | flops 1000 | bytes 1000 | tf_op jit(solution)/shard_map/total/pallas_call | solution.py:439
  188.9 2.6 %collective-permute-done.27.r1 = bf16[64,2048]{1,0:T(8,128)(2,1)S(1)} collective-permute-done((bf16[64,2048]{1,0:T(8,128)(2,1)S(1)}, bf16[64,2048]{1,0:T(8,128)(2,1)S(1)}, u32[]{:S(2)}, u32[]{:S(2)}) %collective-permute-start.27) | collective-permute-done | bytes 262176 | tf_op jit(solution)/shard_map/ppermute | solution.py:195
  191.6 4.5 %collective-permute-done.28.r2 = bf16[64,2048]{1,0:T(8,128)(2,1)S(1)} collective-permute-done((bf16[64,2048]{1,0:T(8,128)(2,1)S(1)}, bf16[64,2048]{1,0:T(8,128)(2,1)S(1)}, u32[]{:S(2)}, u32[]{:S(2)}) %collective-permute-start.28) | collective-permute-done | bytes 262176 | tf_op jit(solution)/shard_map/ppermute | solution.py:195
  196.1 1.7 final.1
  (79 shorter events, 5.0 us)
Async XLA Ops:
  0.0 7.9 %copy-start.25 = (f32[64,2]{0,1:T(2,128)S(1)}, f32[64,2]{0,1:T(2,128)}, u32[]{:S(2)}) copy-start(f32[64,2]{0,1:T(2,128)} %param.18) | copy-start | bytes 1540
  0.0 8.0 %copy-start.26 = (s32[64,2]{0,1:T(2,128)S(1)}, s32[64,2]{0,1:T(2,128)}, u32[]{:S(2)}) copy-start(s32[64,2]{0,1:T(2,128)} %param.17) | copy-start | bytes 1540
  1.5 26.8 %collective-permute-start.10 = (bf16[1024,768]{1,0:T(8,128)(2,1)S(1)}, bf16[1024,768]{1,0:T(8,128)(2,1)S(1)}, u32[]{:S(2)}, u32[]{:S(2)}) collective-permute-start(bf16[1024,768]{1,0:T(8,128)(2,1)S(1)} %pad_maximum_fusion.refs_0_), channel_id=1, source_target_pairs={{0,4},{4,0},{8,12},{12,8},{16,20},{20,16},{24,28},{28,24},{1,5},{5... | collective-permute-start | bytes 4718600 | tf_op jit(solution)/shard_map/ppermute | solution.py:195
  2.0 26.3 %collective-permute-start.11 = (bf16[768,512]{1,0:T(8,128)(2,1)}, bf16[768,512]{1,0:T(8,128)(2,1)}, u32[]{:S(2)}, u32[]{:S(2)}) collective-permute-start(bf16[768,512]{1,0:T(8,128)(2,1)} %bitcast.4.d0), channel_id=1, source_target_pairs={{0,4},{4,0},{8,12},{12,8},{16,20},{20,16},{24,28},{28,24},{1,5},{5... | collective-permute-start | bytes 2359304 | tf_op jit(solution)/shard_map/ppermute | solution.py:195
  3.0 18.5 %collective-permute-start.1 = (bf16[256,256]{1,0:T(8,128)(2,1)S(1)}, bf16[256,256]{1,0:T(8,128)(2,1)S(1)}, u32[]{:S(2)}, u32[]{:S(2)}) collective-permute-start(bf16[256,256]{1,0:T(8,128)(2,1)S(1)} %pad_maximum_fusion.1.refs_0_), channel_id=1, source_target_pairs={{0,8},{4,12},{8,16},{12,20},{16,24},{20,28},{1,9},{5,13},{9,17},{1... | collective-permute-start | bytes 393224 | tf_op jit(solution)/shard_map/ppermute | solution.py:500
  8.1 3.9 %collective-permute-start.7 = (f32[64,128]{1,0:T(8,128)S(1)}, f32[64,128]{1,0:T(8,128)S(1)}, u32[]{:S(2)}, u32[]{:S(2)}) collective-permute-start(f32[64,128]{1,0:T(8,128)S(1)} %broadcast_in_dim.17), channel_id=1, source_target_pairs={{0,1},{1,0},{2,3},{3,2},{4,5},{5,4},{6,7},{7,6},{8,9},{9,8},{10,11... | collective-permute-start | bytes 98312 | tf_op jit(solution)/shard_map/ppermute | solution.py:195
  9.6 4.9 %collective-permute-start.8 = (f32[64,128]{1,0:T(8,128)S(1)}, f32[64,128]{1,0:T(8,128)S(1)}, u32[]{:S(2)}, u32[]{:S(2)}) collective-permute-start(f32[64,128]{1,0:T(8,128)S(1)} %broadcast_in_dim.34), channel_id=1, source_target_pairs={{0,2},{1,3},{2,0},{3,1},{4,6},{5,7},{6,4},{7,5},{8,10},{9,11},{10,... | collective-permute-start | bytes 98312 | tf_op jit(solution)/shard_map/ppermute | solution.py:195
  12.0 16.3 %copy-start.15 = (f32[64,128]{1,0:T(8,128)}, f32[64,128]{1,0:T(8,128)S(1)}, u32[]{:S(2)}) copy-start(f32[64,128]{1,0:T(8,128)S(1)} %collective-permute-done.7.c1) | copy-start | bytes 98308
  12.1 7.6 %collective-permute-start.9 = (f32[64,128]{1,0:T(8,128)S(1)}, f32[64,128]{1,0:T(8,128)S(1)}, u32[]{:S(2)}, u32[]{:S(2)}) collective-permute-start(f32[64,128]{1,0:T(8,128)S(1)} %broadcast_in_dim.35), channel_id=1, source_target_pairs={{0,3},{1,2},{2,1},{3,0},{4,7},{5,6},{6,5},{7,4},{8,11},{9,10},{10,... | collective-permute-start | bytes 98312 | tf_op jit(solution)/shard_map/ppermute | solution.py:195
  14.5 0.6 copy-start.17
  15.1 8.0 %collective-permute-start.3 = (bf16[256,256]{1,0:T(8,128)(2,1)S(1)}, bf16[256,256]{1,0:T(8,128)(2,1)S(1)}, u32[]{:S(2)}, u32[]{:S(2)}) collective-permute-start(bf16[256,256]{1,0:T(8,128)(2,1)S(1)} %pad_maximum_fusion.1.refs_0_), channel_id=1, source_target_pairs={{0,16},{4,20},{8,24},{12,28},{1,17},{5,21},{9,25},{13,29},{2,18},{... | collective-permute-start | bytes 393224 | tf_op jit(solution)/shard_map/ppermute | solution.py:500
  19.6 0.6 copy-start.19
  20.2 4.3 %collective-permute-start.5 = (bf16[256,256]{1,0:T(8,128)(2,1)S(1)}, bf16[256,256]{1,0:T(8,128)(2,1)S(1)}, u32[]{:S(2)}, u32[]{:S(2)}) collective-permute-start(bf16[256,256]{1,0:T(8,128)(2,1)S(1)} %pad_maximum_fusion.1.refs_0_), channel_id=1, source_target_pairs={{0,24},{4,28},{1,25},{5,29},{2,26},{6,30},{3,27},{7,31}} | collective-permute-start | bytes 393224 | tf_op jit(solution)/shard_map/ppermute | solution.py:500
  21.5 3.0 %collective-permute-start = (bf16[256,256]{1,0:T(8,128)(2,1)S(1)}, bf16[256,256]{1,0:T(8,128)(2,1)S(1)}, u32[]{:S(2)}, u32[]{:S(2)}) collective-permute-start(bf16[256,256]{1,0:T(8,128)(2,1)S(1)} %pad_maximum_fusion.1.refs_0_), channel_id=1, source_target_pairs={{0,4},{4,0},{8,12},{12,8},{16,20},{20,16},{24,28},{28,24},{1,5},{5... | collective-permute-start | bytes 393224 | tf_op jit(solution)/shard_map/ppermute | solution.py:195
  23.1 3.2 %collective-permute-start.2 = (bf16[256,256]{1,0:T(8,128)(2,1)S(1)}, bf16[256,256]{1,0:T(8,128)(2,1)S(1)}, u32[]{:S(2)}, u32[]{:S(2)}) collective-permute-start(bf16[256,256]{1,0:T(8,128)(2,1)S(1)} %collective-permute-done.1.refs_2_), channel_id=1, source_target_pairs={{0,4},{4,0},{8,12},{12,8},{16,20},{20,16},{24,28},{28,24},{1,5},{5... | collective-permute-start | bytes 393224 | tf_op jit(solution)/shard_map/ppermute | solution.py:195
  24.5 2.5 %collective-permute-start.4 = (bf16[256,256]{1,0:T(8,128)(2,1)S(1)}, bf16[256,256]{1,0:T(8,128)(2,1)S(1)}, u32[]{:S(2)}, u32[]{:S(2)}) collective-permute-start(bf16[256,256]{1,0:T(8,128)(2,1)S(1)} %collective-permute-done.3.refs_4_), channel_id=1, source_target_pairs={{0,4},{4,0},{8,12},{12,8},{16,20},{20,16},{24,28},{28,24},{1,5},{5... | collective-permute-start | bytes 393224 | tf_op jit(solution)/shard_map/ppermute | solution.py:195
  24.5 0.7 copy-start.6
  25.2 2.5 %collective-permute-start.6 = (bf16[256,256]{1,0:T(8,128)(2,1)S(1)}, bf16[256,256]{1,0:T(8,128)(2,1)S(1)}, u32[]{:S(2)}, u32[]{:S(2)}) collective-permute-start(bf16[256,256]{1,0:T(8,128)(2,1)S(1)} %collective-permute-done.5.refs_6_), channel_id=1, source_target_pairs={{0,4},{4,0},{8,12},{12,8},{16,20},{20,16},{24,28},{28,24},{1,5},{5... | collective-permute-start | bytes 393224 | tf_op jit(solution)/shard_map/ppermute | solution.py:195
  25.7 0.7 copy-start.4
  26.3 0.6 copy-start.8
  27.0 0.7 copy-start.10
  27.6 0.7 copy-start.12
  29.0 75.8 %collective-permute-start.22 = (bf16[1024,768]{1,0:T(8,128)(2,1)S(1)}, bf16[1024,768]{1,0:T(8,128)(2,1)}, u32[]{:S(2)}, u32[]{:S(2)}) collective-permute-start(bf16[1024,768]{1,0:T(8,128)(2,1)S(1)} %pad_maximum_fusion.refs_0_), channel_id=1, source_target_pairs={{0,24},{4,28},{8,16},{12,20},{16,8},{20,12},{24,0},{28,4},{1,25},{... | collective-permute-start | bytes 4718600 | tf_op jit(solution)/shard_map/ppermute | solution.py:195
  34.3 0.9 copy-start.5
  35.2 0.9 copy-start.7
  36.1 0.9 copy-start.9
  37.0 0.9 copy-start.11
  37.9 0.9 copy-start.13
  38.8 16.4 %copy-start.24 = (bf16[4096]{0:T(1024)(128)(2,1)S(1)}, bf16[4096]{0:T(1024)(128)(2,1)}, u32[]{:S(2)}) copy-start(bf16[4096]{0:T(1024)(128)(2,1)} %param.16) | copy-start | bytes 24580
  38.8 38.7 %copy-start.2 = (bf16[64,4096]{1,0:T(8,128)(2,1)S(1)}, bf16[64,4096]{1,0:T(8,128)(2,1)}, u32[]{:S(2)}) copy-start(bf16[64,4096]{1,0:T(8,128)(2,1)} %residual.1) | copy-start | bytes 1572868
  51.6 15.0 %collective-permute-start.12 = (bf16[64,4096]{1,0:T(8,128)(2,1)}, bf16[64,4096]{1,0:T(8,128)(2,1)S(1)}, u32[]{:S(2)}, u32[]{:S(2)}) collective-permute-start(bf16[64,4096]{1,0:T(8,128)(2,1)} %get-tuple-element.56), channel_id=1, source_target_pairs={{0,1},{1,0},{2,3},{3,2},{4,5},{5,4},{6,7},{7,6},{8,9},{9,8},{10,11... | collective-permute-start | bytes 1572872 | tf_op jit(solution)/shard_map/ppermute | solution.py:195
  52.2 25.2 %collective-permute-start.13 = (bf16[64,4096]{1,0:T(8,128)(2,1)}, bf16[64,4096]{1,0:T(8,128)(2,1)S(1)}, u32[]{:S(2)}, u32[]{:S(2)}) collective-permute-start(bf16[64,4096]{1,0:T(8,128)(2,1)} %get-tuple-element.57), channel_id=1, source_target_pairs={{0,2},{1,3},{2,0},{3,1},{4,6},{5,7},{6,4},{7,5},{8,10},{9,11},{10,... | collective-permute-start | bytes 1572872 | tf_op jit(solution)/shard_map/ppermute | solution.py:195
  52.8 24.7 %collective-permute-start.14 = (bf16[64,4096]{1,0:T(8,128)(2,1)}, bf16[64,4096]{1,0:T(8,128)(2,1)S(1)}, u32[]{:S(2)}, u32[]{:S(2)}) collective-permute-start(bf16[64,4096]{1,0:T(8,128)(2,1)} %get-tuple-element.58), channel_id=1, source_target_pairs={{0,3},{1,2},{2,1},{3,0},{4,7},{5,6},{6,5},{7,4},{8,11},{9,10},{10,... | collective-permute-start | bytes 1572872 | tf_op jit(solution)/shard_map/ppermute | solution.py:195
  78.6 0.8 copy-start
  79.4 7.3 %collective-permute-start.18 = (bf16[64,2048]{1,0:T(8,128)(2,1)S(1)}, bf16[64,2048]{1,0:T(8,128)(2,1)S(1)}, u32[]{:S(2)}, u32[]{:S(2)}) collective-permute-start(bf16[64,2048]{1,0:T(8,128)(2,1)S(1)} %get-tuple-element.61), channel_id=1, source_target_pairs={{0,8},{4,12},{8,0},{12,4},{16,24},{20,28},{24,16},{28,20},{1,9},{5... | collective-permute-start | bytes 786440 | tf_op jit(solution)/shard_map/ppermute | solution.py:195
  79.4 9.2 %collective-permute-start.15 = (bf16[64,2048]{1,0:T(8,128)(2,1)S(1)}, bf16[64,2048]{1,0:T(8,128)(2,1)S(1)}, u32[]{:S(2)}, u32[]{:S(2)}) collective-permute-start(bf16[64,2048]{1,0:T(8,128)(2,1)S(1)} %get-tuple-element.63.x0), channel_id=1, source_target_pairs={{0,1},{1,0},{2,3},{3,2},{4,5},{5,4},{6,7},{7,6},{8,9},{9,8},{10,11... | collective-permute-start | bytes 786440 | tf_op jit(solution)/shard_map/ppermute | solution.py:195
  80.9 12.2 %collective-permute-start.16 = (bf16[64,2048]{1,0:T(8,128)(2,1)S(1)}, bf16[64,2048]{1,0:T(8,128)(2,1)S(1)}, u32[]{:S(2)}, u32[]{:S(2)}) collective-permute-start(bf16[64,2048]{1,0:T(8,128)(2,1)S(1)} %get-tuple-element.63.x0), channel_id=1, source_target_pairs={{0,2},{1,3},{2,0},{3,1},{4,6},{5,7},{6,4},{7,5},{8,10},{9,11},{10,... | collective-permute-start | bytes 786440 | tf_op jit(solution)/shard_map/ppermute | solution.py:195
  81.4 13.5 %collective-permute-start.17 = (bf16[64,2048]{1,0:T(8,128)(2,1)S(1)}, bf16[64,2048]{1,0:T(8,128)(2,1)S(1)}, u32[]{:S(2)}, u32[]{:S(2)}) collective-permute-start(bf16[64,2048]{1,0:T(8,128)(2,1)S(1)} %get-tuple-element.63.x0), channel_id=1, source_target_pairs={{0,3},{1,2},{2,1},{3,0},{4,7},{5,6},{6,5},{7,4},{8,11},{9,10},{10,... | collective-permute-start | bytes 786440 | tf_op jit(solution)/shard_map/ppermute | solution.py:195
  86.7 13.2 %collective-permute-start.19 = (bf16[64,2048]{1,0:T(8,128)(2,1)S(1)}, bf16[64,2048]{1,0:T(8,128)(2,1)S(1)}, u32[]{:S(2)}, u32[]{:S(2)}) collective-permute-start(bf16[64,2048]{1,0:T(8,128)(2,1)S(1)} %collective-permute-done.18.x0), channel_id=1, source_target_pairs={{0,1},{1,0},{2,3},{3,2},{4,5},{5,4},{6,7},{7,6},{8,9},{9,8},{10,11... | collective-permute-start | bytes 786440 | tf_op jit(solution)/shard_map/ppermute | solution.py:195
  88.6 16.1 %collective-permute-start.20 = (bf16[64,2048]{1,0:T(8,128)(2,1)S(1)}, bf16[64,2048]{1,0:T(8,128)(2,1)S(1)}, u32[]{:S(2)}, u32[]{:S(2)}) collective-permute-start(bf16[64,2048]{1,0:T(8,128)(2,1)S(1)} %collective-permute-done.18.x0), channel_id=1, source_target_pairs={{0,2},{1,3},{2,0},{3,1},{4,6},{5,7},{6,4},{7,5},{8,10},{9,11},{10,... | collective-permute-start | bytes 786440 | tf_op jit(solution)/shard_map/ppermute | solution.py:195
  93.1 11.7 %collective-permute-start.21 = (bf16[64,2048]{1,0:T(8,128)(2,1)S(1)}, bf16[64,2048]{1,0:T(8,128)(2,1)S(1)}, u32[]{:S(2)}, u32[]{:S(2)}) collective-permute-start(bf16[64,2048]{1,0:T(8,128)(2,1)S(1)} %collective-permute-done.18.x0), channel_id=1, source_target_pairs={{0,3},{1,2},{2,1},{3,0},{4,7},{5,6},{6,5},{7,4},{8,11},{9,10},{10,... | collective-permute-start | bytes 786440 | tf_op jit(solution)/shard_map/ppermute | solution.py:195
  104.8 3.6 %collective-permute-start.23 = (bf16[1024,768]{1,0:T(8,128)(2,1)}, bf16[1024,768]{1,0:T(8,128)(2,1)S(1)}, u32[]{:S(2)}, u32[]{:S(2)}) collective-permute-start(bf16[1024,768]{1,0:T(8,128)(2,1)} %collective-permute-done.22.refs_2_), channel_id=1, source_target_pairs={{0,4},{4,0},{8,12},{12,8},{16,20},{20,16},{24,28},{28,24},{1,5},{5... | collective-permute-start | bytes 4718600 | tf_op jit(solution)/shard_map/ppermute | solution.py:195
  112.2 19.8 %copy-start.14 = (f32[64,128]{1,0:T(8,128)S(1)}, f32[64,128]{1,0:T(8,128)}, u32[]{:S(2)}) copy-start(f32[64,128]{1,0:T(8,128)} %broadcast_in_dim.16.c0) | copy-start | bytes 98308
  112.2 19.8 %copy-start.16 = (f32[64,128]{1,0:T(8,128)S(1)}, f32[64,128]{1,0:T(8,128)}, u32[]{:S(2)}) copy-start(f32[64,128]{1,0:T(8,128)} %copy-done.15) | copy-start | bytes 98308
  112.2 19.7 %copy-start.18 = (f32[64,128]{1,0:T(8,128)S(1)}, f32[64,128]{1,0:T(8,128)}, u32[]{:S(2)}) copy-start(f32[64,128]{1,0:T(8,128)} %copy-done.17) | copy-start | bytes 98308
  112.2 19.7 %copy-start.20 = (f32[64,128]{1,0:T(8,128)S(1)}, f32[64,128]{1,0:T(8,128)}, u32[]{:S(2)}) copy-start(f32[64,128]{1,0:T(8,128)} %copy-done.19) | copy-start | bytes 98308
  112.2 19.7 %collective-permute-start.24 = (bf16[256,1536]{1,0:T(8,128)(2,1)S(1)}, bf16[256,1536]{1,0:T(8,128)(2,1)S(1)}, u32[]{:S(2)}, u32[]{:S(2)}) collective-permute-start(bf16[256,1536]{1,0:T(8,128)(2,1)S(1)} %enter.3), channel_id=1, source_target_pairs={{0,8},{4,12},{8,0},{12,4},{16,24},{20,28},{24,16},{28,20},{1,9},{5... | collective-permute-start | bytes 2359304 | tf_op jit(solution)/shard_map/ppermute | solution.py:195
  114.0 42.7 %collective-permute-start.25 = (bf16[768,512]{1,0:T(8,128)(2,1)}, bf16[768,512]{1,0:T(8,128)(2,1)S(1)}, u32[]{:S(2)}, u32[]{:S(2)}) collective-permute-start(bf16[768,512]{1,0:T(8,128)(2,1)} %bitcast.4.d0), channel_id=1, source_target_pairs={{0,24},{4,28},{8,16},{12,20},{16,8},{20,12},{24,0},{28,4},{1,25},{... | collective-permute-start | bytes 2359304 | tf_op jit(solution)/shard_map/ppermute | solution.py:195
  156.8 11.5 %collective-permute-start.26 = (bf16[768,512]{1,0:T(8,128)(2,1)S(1)}, bf16[768,512]{1,0:T(8,128)(2,1)S(1)}, u32[]{:S(2)}, u32[]{:S(2)}) collective-permute-start(bf16[768,512]{1,0:T(8,128)(2,1)S(1)} %collective-permute-done.25.d2), channel_id=1, source_target_pairs={{0,4},{4,0},{8,12},{12,8},{16,20},{20,16},{24,28},{28,24},{1,5},{5... | collective-permute-start | bytes 2359304 | tf_op jit(solution)/shard_map/ppermute | solution.py:195
  156.8 11.5 %collective-permute-start.30 = (bf16[256,768]{1,0:T(8,128)(2,1)S(1)}, bf16[256,768]{1,0:T(8,128)(2,1)S(1)}, u32[]{:S(2)}, u32[]{:S(2)}) collective-permute-start(bf16[256,768]{1,0:T(8,128)(2,1)S(1)} %silu.1.hidden), channel_id=1, source_target_pairs={{0,8},{4,12},{8,0},{12,4},{16,24},{20,28},{24,16},{28,20},{1,9},{5... | collective-permute-start | bytes 1179656 | tf_op jit(solution)/shard_map/ppermute | solution.py:195
  171.0 6.2 %copy-start.3 = (bf16[64,2048]{1,0:T(8,128)(2,1)}, bf16[64,2048]{1,0:T(8,128)(2,1)S(1)}, u32[]{:S(2)}) copy-start(bf16[64,2048]{1,0:T(8,128)(2,1)S(1)} %get-tuple-element.85.y0) | copy-start | bytes 786436
  171.0 9.3 %collective-permute-start.31 = (bf16[64,2048]{1,0:T(8,128)(2,1)S(1)}, bf16[64,2048]{1,0:T(8,128)(2,1)S(1)}, u32[]{:S(2)}, u32[]{:S(2)}) collective-permute-start(bf16[64,2048]{1,0:T(8,128)(2,1)S(1)} %get-tuple-element.86), channel_id=1, source_target_pairs={{0,1},{1,0},{2,3},{3,2},{4,5},{5,4},{6,7},{7,6},{8,9},{9,8},{10,11... | collective-permute-start | bytes 786440 | tf_op jit(solution)/shard_map/ppermute | solution.py:195
  171.6 13.8 %collective-permute-start.32 = (bf16[64,2048]{1,0:T(8,128)(2,1)S(1)}, bf16[64,2048]{1,0:T(8,128)(2,1)S(1)}, u32[]{:S(2)}, u32[]{:S(2)}) collective-permute-start(bf16[64,2048]{1,0:T(8,128)(2,1)S(1)} %get-tuple-element.87), channel_id=1, source_target_pairs={{0,2},{1,3},{2,0},{3,1},{4,6},{5,7},{6,4},{7,5},{8,10},{9,11},{10,... | collective-permute-start | bytes 786440 | tf_op jit(solution)/shard_map/ppermute | solution.py:195
  173.1 23.0 %copy-start.1 = (bf16[64,4096]{1,0:T(8,128)(2,1)S(1)}, bf16[64,4096]{1,0:T(8,128)(2,1)}, u32[]{:S(2)}) copy-start(bf16[64,4096]{1,0:T(8,128)(2,1)} %copy-done) | copy-start | bytes 1572868
  173.1 12.8 %collective-permute-start.33 = (bf16[64,2048]{1,0:T(8,128)(2,1)S(1)}, bf16[64,2048]{1,0:T(8,128)(2,1)S(1)}, u32[]{:S(2)}, u32[]{:S(2)}) collective-permute-start(bf16[64,2048]{1,0:T(8,128)(2,1)S(1)} %get-tuple-element.88), channel_id=1, source_target_pairs={{0,3},{1,2},{2,1},{3,0},{4,7},{5,6},{6,5},{7,4},{8,11},{9,10},{10,... | collective-permute-start | bytes 786440 | tf_op jit(solution)/shard_map/ppermute | solution.py:195
  177.2 14.3 %collective-permute-start.27 = (bf16[64,2048]{1,0:T(8,128)(2,1)S(1)}, bf16[64,2048]{1,0:T(8,128)(2,1)S(1)}, u32[]{:S(2)}, u32[]{:S(2)}) collective-permute-start(bf16[64,2048]{1,0:T(8,128)(2,1)S(1)} %get-tuple-element.82), channel_id=1, source_target_pairs={{0,1},{1,0},{2,3},{3,2},{4,5},{5,4},{6,7},{7,6},{8,9},{9,8},{10,11... | collective-permute-start | bytes 786440 | tf_op jit(solution)/shard_map/ppermute | solution.py:195
  177.8 18.3 %collective-permute-start.28 = (bf16[64,2048]{1,0:T(8,128)(2,1)S(1)}, bf16[64,2048]{1,0:T(8,128)(2,1)S(1)}, u32[]{:S(2)}, u32[]{:S(2)}) collective-permute-start(bf16[64,2048]{1,0:T(8,128)(2,1)S(1)} %get-tuple-element.83), channel_id=1, source_target_pairs={{0,2},{1,3},{2,0},{3,1},{4,6},{5,7},{6,4},{7,5},{8,10},{9,11},{10,... | collective-permute-start | bytes 786440 | tf_op jit(solution)/shard_map/ppermute | solution.py:195
  180.3 5.7 %copy-start.21 = (bf16[64,2048]{1,0:T(8,128)(2,1)}, bf16[64,2048]{1,0:T(8,128)(2,1)S(1)}, u32[]{:S(2)}) copy-start(bf16[64,2048]{1,0:T(8,128)(2,1)S(1)} %collective-permute-done.31.r1) | copy-start | bytes 786436
  180.3 15.8 %collective-permute-start.29 = (bf16[64,2048]{1,0:T(8,128)(2,1)S(1)}, bf16[64,2048]{1,0:T(8,128)(2,1)S(1)}, u32[]{:S(2)}, u32[]{:S(2)}) collective-permute-start(bf16[64,2048]{1,0:T(8,128)(2,1)S(1)} %get-tuple-element.84), channel_id=1, source_target_pairs={{0,3},{1,2},{2,1},{3,0},{4,7},{5,6},{6,5},{7,4},{8,11},{9,10},{10,... | collective-permute-start | bytes 786440 | tf_op jit(solution)/shard_map/ppermute | solution.py:195
  185.4 0.7 copy-start.22
  185.9 0.7 copy-start.23
  188.7 7.4 %collective-permute-start.34 = (bf16[64,2048]{1,0:T(8,128)(2,1)}, bf16[64,2048]{1,0:T(8,128)(2,1)S(1)}, u32[]{:S(2)}, u32[]{:S(2)}) collective-permute-start(bf16[64,2048]{1,0:T(8,128)(2,1)} %total.1), channel_id=1, source_target_pairs={{0,8},{4,12},{8,0},{12,4},{16,24},{20,28},{24,16},{28,20},{1,9},{5... | collective-permute-start | bytes 786440 | tf_op jit(solution)/shard_map/ppermute | solution.py:195

commit v3 on v2

--- a/solution.py
+++ b/solution.py
@@ -203,9 +203,15 @@
     return [pl.BlockSpec(memory_space=VMEM) for _ in range(count)]
 
 
-def attention_kernel(index, q, *refs):
-    pieces, w_hbm, outs = refs[:8], refs[8], refs[9:13]
-    w_all, keys, ones_values, bias, even, odd, attn, sems = refs[13:]
+def attention_kernel(index, q_hbm, *refs):
+    arrived, w_hbm, outs = refs[:8], refs[8], refs[9:13]
+    w_all, q, pieces, keys, ones_values, bias, even, odd, attn, q_sem, piece_sems, sems = refs[13:]
+    q_fetch = pltpu.make_async_copy(q_hbm, q, q_sem)
+    piece_fetches = [
+        pltpu.make_async_copy(arrived[i], pieces.at[i], piece_sems.at[i]) for i in range(8)
+    ]
+    for fetch in piece_fetches + [q_fetch]:
+        fetch.start()
     ctx = index[0]
     exp = index[1]
     chip = ctx // 2
@@ -223,20 +229,23 @@
     heads = q.shape[1] // HD
     ones_values[:, HD:] = jnp.ones((ones_values.shape[0], HD), BF16)
     core = ctx % 2
+    row = lax.broadcasted_iota(jnp.int32, (QB, 2 * QB), 0) + core * QB
+    col = lax.broadcasted_iota(jnp.int32, (QB, 2 * QB), 1)
+    bias[...] = jnp.where(col <= row, 0.0, -1e30)
+    for fetch in piece_fetches:
+        fetch.wait()
     for d in range(4):
 
         @pl.when(chip >= d)
         def _():
             for other in range(2):
-                piece = pieces[2 * d + other]
+                piece = pieces.at[2 * d + other]
                 place = 2 * (chip - d) + (core ^ other)
                 here = pl.ds(pl.multiple_of(place * QB, QB), QB)
                 keys[:, here] = piece[:, :HD].astype(F32).T.astype(BF16)
                 ones_values[here, :HD] = piece[:, HD:]
 
-    row = lax.broadcasted_iota(jnp.int32, (QB, 2 * QB), 0) + core * QB
-    col = lax.broadcasted_iota(jnp.int32, (QB, 2 * QB), 1)
-    bias[...] = jnp.where(col <= row, 0.0, -1e30)
+    q_fetch.wait()
     part = QB // 4
 
     def run(length):
@@ -288,17 +297,20 @@
         attention_kernel,
         out_shape=[jax.ShapeDtypeStruct((rows, D), BF16)] * 4,
         in_specs=[pl.BlockSpec(memory_space=pltpu.SMEM)]
-        + vmem_specs(9)
-        + [pl.BlockSpec(memory_space=pl.ANY)],
+        + [pl.BlockSpec(memory_space=pl.ANY)] * 10,
         out_specs=vmem_specs(4),
         scratch_shapes=[
             VMEM(w_out.shape, BF16),
+            VMEM(queries.shape, BF16),
+            VMEM((8,) + pieces[0].shape, BF16),
             VMEM((HD, length), BF16),
             VMEM((length, 2 * HD), BF16),
             VMEM((QB, 2 * QB), F32),
             VMEM((QB, length), F32),
             VMEM((QB, length), F32),
             VMEM(queries.shape, BF16),
+            pltpu.SemaphoreType.DMA,
+            pltpu.SemaphoreType.DMA((8,)),
             pltpu.SemaphoreType.DMA((16,)),
         ],
         compiler_params=params(52),
@@ -378,27 +390,23 @@
     )(*rows, *weights)
 
 
-def silu_kernel(own, other, c0, c1, c2, c3, out):
+def silu_kernel(own, other, out):
     width = out.shape[1]
-    part = c0.shape[0]
     total = own[...] + other[...].astype(F32)
     gate, up = total[:, :width], total[:, width:]
-    hidden = gate / (1.0 + jnp.exp(-gate)) * up
-    for b, share in enumerate((c0, c1, c2, c3)):
-        rows = slice(b * part, (b + 1) * part)
-        out[rows] = (hidden[rows] * share[:, :1]).astype(BF16)
-
-
-def silu(own, other, shares):
+    out[...] = (gate / (1.0 + jnp.exp(-gate)) * up).astype(BF16)
+
+
+def silu(own, other):
     return pl.pallas_call(
         silu_kernel,
         out_shape=jax.ShapeDtypeStruct((own.shape[0], own.shape[1] // 2), BF16),
-        in_specs=vmem_specs(6),
+        in_specs=vmem_specs(2),
         out_specs=pl.BlockSpec(memory_space=VMEM),
         compiler_params=params(16),
         cost_estimate=CHEAP,
         name="silu",
-    )(own, other, *shares)
+    )(own, other)
 
 
 def leave_kernel(hidden, d0, d1, d2, d3, y0, y1, y2, y3, down_all, sems):
@@ -429,27 +437,32 @@
     )(hidden, *downs)
 
 
-def total_kernel(y0, r1, r2, r3, out):
-    out[...] = (
-        y0[...].astype(F32) + r1[...].astype(F32) + r2[...].astype(F32) + r3[...].astype(F32)
-    ).astype(BF16)
-
-
-def total_of(y0, r1, r2, r3):
+def mixed(shares, parts):
+    total = shares[:, :1] * parts[0][...].astype(F32)
+    for b in range(1, 4):
+        total = total + shares[:, b : b + 1] * parts[b][...].astype(F32)
+    return total
+
+
+def total_kernel(shares, y0, r1, r2, r3, out):
+    out[...] = mixed(shares, (y0, r1, r2, r3)).astype(BF16)
+
+
+def total_of(shares, y0, r1, r2, r3):
     return pl.pallas_call(
         total_kernel,
         out_shape=jax.ShapeDtypeStruct(y0.shape, BF16),
-        in_specs=vmem_specs(4),
+        in_specs=vmem_specs(5),
         out_specs=pl.BlockSpec(memory_space=VMEM),
         cost_estimate=CHEAP,
         name="total",
-    )(y0, r1, r2, r3)
-
-
-def final_kernel(index, state, y0, r1, r2, r3, other, out):
+    )(shares, y0, r1, r2, r3)
+
+
+def final_kernel(index, state, shares, y0, r1, r2, r3, other, out):
     ctx = index[0]
     part = D // 8
-    own = y0[...].astype(F32) + r1[...].astype(F32) + r2[...].astype(F32) + r3[...].astype(F32)
+    own = mixed(shares, (y0, r1, r2, r3))
     for j, (a, b) in enumerate(((0, 2), (1, 3), (6, 4), (7, 5))):
         cols = slice(j * part, (j + 1) * part)
         here = pl.ds(pl.multiple_of((ctx ^ a) * part, part), part)
@@ -458,16 +471,16 @@
         out[:, there] = (state[:, there].astype(F32) + other[:, cols].astype(F32)).astype(BF16)
 
 
-def final(index, state, y0, r1, r2, r3, other):
+def final(index, state, shares, y0, r1, r2, r3, other):
     return pl.pallas_call(
         final_kernel,
         out_shape=jax.ShapeDtypeStruct(state.shape, BF16),
-        in_specs=[pl.BlockSpec(memory_space=pltpu.SMEM)] + vmem_specs(6),
+        in_specs=[pl.BlockSpec(memory_space=pltpu.SMEM)] + vmem_specs(7),
         out_specs=pl.BlockSpec(memory_space=VMEM),
         compiler_params=params(16),
         cost_estimate=CHEAP,
         name="final",
-    )(index, state, y0, r1, r2, r3, other)
+    )(index, state, shares, y0, r1, r2, r3, other)
 
 
 def body(
@@ -494,48 +507,50 @@
         ],
         axis=1,
     )
-    pair_here, down_here = jnp.concatenate([w_gate[0], w_up[0]], axis=0), w_down[0]
-
     def later(array, chips):
         return lax.ppermute(array, "ctx", [(i, i + 2 * chips) for i in range(8 - 2 * chips)])
 
-    pieces = [kv_here] + [later(kv_here, d) for d in (3, 2, 1)][::-1]
-    pieces = [part for piece in pieces for part in (piece, swap(piece, "ctx", 1))]
-
-    shares = []
-    for b in range(4):
-        share = jnp.sum(jnp.where(expert_ids == (exp ^ b), gate_weights, 0.0), axis=1, keepdims=True)
-        share = jnp.broadcast_to(share, (share.shape[0], HD))
-        shares.append(swap(share, "exp", b) if b else share)
-    near = [swap(array, "ctx", 1) for array in (pair_here, down_here)]
-
-    pieces, shares, near, pair_here = lax.optimization_barrier((pieces, shares, near, pair_here))
+    kv_here, gate_here, up_here = lax.optimization_barrier((kv_here, w_gate[0], w_up[0]))
+    moved = [later(kv_here, d) for d in (3, 2, 1)][::-1]
+    pair_here, down_here = jnp.concatenate([gate_here, up_here], axis=0), w_down[0]
+    pieces = [part for piece in [kv_here] + moved for part in (piece, swap(piece, "ctx", 1))]
+    pieces, pair_here = lax.optimization_barrier((pieces, pair_here))
     pair_far = swap(pair_here, "ctx", 6)
 
+    lane = lax.broadcasted_iota(jnp.int32, (expert_ids.shape[0], HD), 1)
+    shares = jnp.zeros(lane.shape, F32)
+    for k in range(expert_ids.shape[1]):
+        named = expert_ids[:, k : k + 1] ^ exp
+        shares = shares + jnp.where(lane == named, gate_weights[:, k : k + 1], 0.0)
+
     p = attention(index, queries, pieces, w_out)
+    p, shares, pair_here, down_here = lax.optimization_barrier((p, shares, pair_here, down_here))
     r = [swap(p[b], "exp", b) for b in (1, 2, 3)]
+    pair_near, down_near = swap(pair_here, "ctx", 1), swap(down_here, "ctx", 1)
+    other_shares = swap(shares, "ctx", 2)
     state, mine, theirs = norm(index, p[0], *r, residual, norm_gain.reshape(1, D))
     others = swap(theirs, "ctx", 2)
     own_rows = [mine] + [swap(mine, "exp", b) for b in (1, 2, 3)]
     other_rows = [others] + [swap(others, "exp", b) for b in (1, 2, 3)]
-    own_rows, other_rows, pair_far, down_here = lax.optimization_barrier(
-        (own_rows, other_rows, pair_far, down_here)
+    own_rows, others, pair_far, down_here = lax.optimization_barrier(
+        (own_rows, others, pair_far, down_here)
     )
     down_far = swap(down_here, "ctx", 6)
-    pairs = (pair_here, near[0], pair_far, swap(pair_far, "ctx", 1))
+    pairs = (pair_here, pair_near, pair_far, swap(pair_far, "ctx", 1))
     other_pre = enter(other_rows, pairs, BF16)
     from_other = swap(other_pre, "ctx", 2)
+    own_rows, down_far = lax.optimization_barrier((own_rows, down_far))
     own_pre = enter(own_rows, pairs, F32)
-    own_hidden = silu(own_pre, from_other, shares)
+    own_hidden = silu(own_pre, from_other)
     other_hidden = swap(own_hidden, "ctx", 2)
-    own_hidden, down_far = lax.optimization_barrier((own_hidden, down_far))
-    downs = (down_here, near[1], down_far, swap(down_far, "ctx", 1))
+    downs = (down_here, down_near, down_far, swap(down_far, "ctx", 1))
     y = leave(own_hidden, downs)
     own_parts = [y[0]] + [swap(y[b], "exp", b) for b in (1, 2, 3)]
+    other_hidden, *own_parts[1:3] = lax.optimization_barrier((other_hidden, *own_parts[1:3]))
     z = leave(other_hidden, downs)
     other_parts = [z[0]] + [swap(z[b], "exp", b) for b in (1, 2, 3)]
-    back = swap(total_of(*other_parts), "ctx", 2)
-    return final(index, state, *own_parts, back)
+    back = swap(total_of(other_shares, *other_parts), "ctx", 2)
+    return final(index, state, shares, *own_parts, back)
 
 
 def solution(mesh):

time: 198 us -> 175 us (0.88)
  waiting for transfers between devices: 102 us -> 91.1 us
  local copies, waits for them, and re-layouts: 12.3 us -> 2.42 us
  starting transfers between devices: 51.1 us -> 46.3 us
  Pallas kernels: 30.9 us -> 33.1 us
    ppermute x32 -> x30, waiting for transfers between devices: 98.7 us -> 87.7 us  [swap(): return lax.ppermute(array, axis, [(i, i ^ mask) for i in range(size)])]
    unnamed x54 -> x20, local copies, waits for them, and re-layouts: 10.5 us -> 1.52 us
    pallas_call x1, Pallas kernels: 12.8 us -> 18.2 us  [attention(): pl.pallas_call(attention_kernel, out_shape=[jax.ShapeDtypeStruct((rows, D...]
    ppermute x32 -> x30, starting transfers between devices: 40.4 us -> 35.6 us  [swap(): return lax.ppermute(array, axis, [(i, i ^ mask) for i in range(size)])]
  transfers between devices with their start and end apart: 35 -> 33, of which waited for: 20 -> 15; matrix products, arithmetic and copies ran while one was open for 1% -> 1% of each run, Pallas kernels for 12% -> 17%
where the time goes in v3:
time: 175 us
  waiting for transfers between devices  91.1 us (52%)
  starting transfers between devices  46.3 us (26%)
  Pallas kernels  33.1 us (19%)
  local copies, waits for them, and re-layouts  2.42 us (1%)
    ppermute x30, waiting for transfers between devices, swap(): return lax.ppermute(array, axis, [(i, i ^ mask) for i in range(size)])  87.7 us
    ppermute x30, starting transfers between devices, swap(): return lax.ppermute(array, axis, [(i, i ^ mask) for i in range(size)])  35.6 us
    pallas_call x1, Pallas kernels, attention(): pl.pallas_call(attention_kernel, out_shape=[jax.ShapeDtypeStruct((rows, D...  18.2 us
    ppermute x3, starting transfers between devices, later(): lax.ppermute(array, 'ctx', [(i, i + 2 * chips) for i in range(8 - 2 * chi...  10.7 us
    pallas_call x2, Pallas kernels, enter(): pl.pallas_call(enter_kernel, out_shape=jax.ShapeDtypeStruct((count, 2 * w...  6.1 us
  transfers between devices with their start and end apart: 33, of which 15 were waited for; matrix products, arithmetic and copies ran while one was open for 1% of the time, Pallas kernels for 17%

profile of v3, /device:TPU:0, one launch (start us, length us, event | category | flops | bytes accessed | tf_op | source)
XLA Modules:
  0.0 175.0 jit_solution(9798746007243865157)
XLA Ops:
  0.0 0.9 constant_dynamic-slice_fusion
  0.9 4.9 %collective-permute-start.1 = (bf16[256,256]{1,0:T(8,128)(2,1)S(1)}, bf16[256,256]{1,0:T(8,128)(2,1)S(1)}, u32[]{:S(2)}, u32[]{:S(2)}) collective-permute-start(bf16[256,256]{1,0:T(8,128)(2,1)S(1)} %pad_maximum_fusion.1.refs_0_), channel_id=1, source_target_pairs={{0,8},{4,12},{8,16},{12,20},{16,24},{20,28},{1,9},{5,13},{9,17},{1... | collective-permute-start | bytes 393224 | tf_op jit(solution)/shard_map/ppermute | solution.py:511
  5.9 4.5 %collective-permute-start.3 = (bf16[256,256]{1,0:T(8,128)(2,1)S(1)}, bf16[256,256]{1,0:T(8,128)(2,1)S(1)}, u32[]{:S(2)}, u32[]{:S(2)}) collective-permute-start(bf16[256,256]{1,0:T(8,128)(2,1)S(1)} %pad_maximum_fusion.1.refs_0_), channel_id=1, source_target_pairs={{0,16},{4,20},{8,24},{12,28},{1,17},{5,21},{9,25},{13,29},{2,18},{... | collective-permute-start | bytes 393224 | tf_op jit(solution)/shard_map/ppermute | solution.py:511
  10.4 1.3 collective-permute-start.5
  11.7 0.1 collective-permute-start
  11.7 0.0 copy-start.8
  11.8 0.0 copy-start.9
  11.8 0.5 collective-permute-start.2
  12.2 2.0 %collective-permute-done.3.refs_4_ = bf16[256,256]{1,0:T(8,128)(2,1)S(1)} collective-permute-done((bf16[256,256]{1,0:T(8,128)(2,1)S(1)}, bf16[256,256]{1,0:T(8,128)(2,1)S(1)}, u32[]{:S(2)}, u32[]{:S(2)}) %collective-permute-start.3) | collective-permute-done | bytes 131104 | tf_op jit(solution)/shard_map/ppermute | solution.py:511
  14.3 1.4 collective-permute-done.5.refs_6_
  15.7 1.5 pad_maximum_fusion.refs_0_
  17.2 6.3 %collective-permute-start.14 = (bf16[1024,768]{1,0:T(8,128)(2,1)S(1)}, bf16[1024,768]{1,0:T(8,128)(2,1)S(1)}, u32[]{:S(2)}, u32[]{:S(2)}) collective-permute-start(bf16[1024,768]{1,0:T(8,128)(2,1)S(1)} %pad_maximum_fusion.refs_0_), channel_id=1, source_target_pairs={{0,24},{4,28},{8,16},{12,20},{16,8},{20,12},{24,0},{28,4},{1,25},{... | collective-permute-start | bytes 4718600 | tf_op jit(solution)/shard_map/ppermute | solution.py:195
  23.5 0.1 pad_add_fusion.index
  23.6 0.1 select_add_fusion.shares
  23.7 0.0 copy-start.1
  23.7 18.2 %attention.1 = (bf16[64,4096]{1,0:T(8,128)(2,1)S(1)}, bf16[64,4096]{1,0:T(8,128)(2,1)}, bf16[64,4096]{1,0:T(8,128)(2,1)}, bf16[64,4096]{1,0:T(8,128)(2,1)}) custom-call(s32[2]{0:T(128)S(1)} %pad_add_fusion.index, bf16[256,2048]{1,0:T(8,128)(2,1)} %q_hbm.1, bf16[256,256]{1,0:T(8,128)(2,1)S(1)} %pad_maximum_fusion.1.refs_0_, ...), custom_call_target="tpu_custom_call" | custom-call | flops 1000 | bytes 1000 | tf_op jit(solution)/shard_map/attention/pallas_call | solution.py:296
  42.0 1.6 collective-permute-start.7
  43.5 1.5 collective-permute-start.8
  45.0 0.5 collective-permute-start.9
  45.5 11.5 %collective-permute-done.7.r1 = bf16[64,4096]{1,0:T(8,128)(2,1)S(1)} collective-permute-done((bf16[64,4096]{1,0:T(8,128)(2,1)}, bf16[64,4096]{1,0:T(8,128)(2,1)S(1)}, u32[]{:S(2)}, u32[]{:S(2)}) %collective-permute-start.7) | collective-permute-done | bytes 524320 | tf_op jit(solution)/shard_map/ppermute | solution.py:195
  57.1 11.2 %collective-permute-done.8.r2 = bf16[64,4096]{1,0:T(8,128)(2,1)S(1)} collective-permute-done((bf16[64,4096]{1,0:T(8,128)(2,1)}, bf16[64,4096]{1,0:T(8,128)(2,1)S(1)}, u32[]{:S(2)}, u32[]{:S(2)}) %collective-permute-start.8) | collective-permute-done | bytes 524320 | tf_op jit(solution)/shard_map/ppermute | solution.py:195
  68.2 1.2 norm.1
  69.4 1.3 collective-permute-start.10
  70.7 0.8 collective-permute-start.11
  71.5 1.4 collective-permute-start.12
  73.0 0.3 collective-permute-start.13
  73.2 5.5 %collective-permute-done.10.x1 = bf16[64,2048]{1,0:T(8,128)(2,1)S(1)} collective-permute-done((bf16[64,2048]{1,0:T(8,128)(2,1)S(1)}, bf16[64,2048]{1,0:T(8,128)(2,1)S(1)}, u32[]{:S(2)}, u32[]{:S(2)}) %collective-permute-start.10) | collective-permute-done | bytes 262176 | tf_op jit(solution)/shard_map/ppermute | solution.py:195
  78.7 4.4 %collective-permute-done.11.x2 = bf16[64,2048]{1,0:T(8,128)(2,1)S(1)} collective-permute-done((bf16[64,2048]{1,0:T(8,128)(2,1)S(1)}, bf16[64,2048]{1,0:T(8,128)(2,1)S(1)}, u32[]{:S(2)}, u32[]{:S(2)}) %collective-permute-start.11) | collective-permute-done | bytes 262176 | tf_op jit(solution)/shard_map/ppermute | solution.py:195
  83.1 0.1 collective-permute-start.17
  83.2 8.8 %collective-permute-start.15 = (bf16[768,512]{1,0:T(8,128)(2,1)S(1)}, bf16[768,512]{1,0:T(8,128)(2,1)S(1)}, u32[]{:S(2)}, u32[]{:S(2)}) collective-permute-start(bf16[768,512]{1,0:T(8,128)(2,1)S(1)} %bitcast.13), channel_id=1, source_target_pairs={{0,24},{4,28},{8,16},{12,20},{16,8},{20,12},{24,0},{28,4},{1,25},{... | collective-permute-start | bytes 2359304 | tf_op jit(solution)/shard_map/ppermute | solution.py:195
  92.0 0.6 collective-permute-start.18
  92.7 1.0 collective-permute-start.19
  93.7 6.7 %collective-permute-done.18.x1 = bf16[64,2048]{1,0:T(8,128)(2,1)S(1)} collective-permute-done((bf16[64,2048]{1,0:T(8,128)(2,1)S(1)}, bf16[64,2048]{1,0:T(8,128)(2,1)S(1)}, u32[]{:S(2)}, u32[]{:S(2)}) %collective-permute-start.18) | collective-permute-done | bytes 262176 | tf_op jit(solution)/shard_map/ppermute | solution.py:195
  100.4 1.1 collective-permute-start.20
  101.5 7.3 %collective-permute-done.20.x3 = bf16[64,2048]{1,0:T(8,128)(2,1)S(1)} collective-permute-done((bf16[64,2048]{1,0:T(8,128)(2,1)S(1)}, bf16[64,2048]{1,0:T(8,128)(2,1)S(1)}, u32[]{:S(2)}, u32[]{:S(2)}) %collective-permute-start.20) | collective-permute-done | bytes 262176 | tf_op jit(solution)/shard_map/ppermute | solution.py:195
  108.9 3.1 %enter.3 = bf16[256,1536]{1,0:T(8,128)(2,1)S(1)} custom-call(bf16[64,2048]{1,0:T(8,128)(2,1)S(1)} %collective-permute-done.13.x0, bf16[64,2048]{1,0:T(8,128)(2,1)S(1)} %collective-permute-done.18.x1, bf16[64,2048]{1,0:T(8,128)(2,1)S(1)} %collective-permute-done.19.x2, bf16[64,2048]{1,0:T(8,128)(2,1)S(1)} %collective-permute-done.20.x3, ...), custom_call_target="tpu_custom_call" | custom-call | flops 1000 | bytes 1000 | tf_op jit(solution)/shard_map/enter/pallas_call | solution.py:377
  111.9 0.1 collective-permute-start.21
  112.0 0.1 collective-permute-start.22
  112.1 0.5 collective-permute-start.23
  112.6 3.0 %enter.2.own = f32[256,1536]{1,0:T(8,128)S(1)} custom-call(bf16[64,2048]{1,0:T(8,128)(2,1)S(1)} %get-tuple-element.83.x0, bf16[64,2048]{1,0:T(8,128)(2,1)S(1)} %collective-permute-done.10.x1, bf16[64,2048]{1,0:T(8,128)(2,1)S(1)} %collective-permute-done.11.x2, bf16[64,2048]{1,0:T(8,128)(2,1)S(1)} %collective-permute-done.12.x3, ...), custom_call_target="tpu_custom_call" | custom-call | flops 1000 | bytes 1000 | tf_op jit(solution)/shard_map/enter/pallas_call | solution.py:377
  115.6 14.2 %collective-permute-done.21.other = bf16[256,1536]{1,0:T(8,128)(2,1)S(1)} collective-permute-done((bf16[256,1536]{1,0:T(8,128)(2,1)S(1)}, bf16[256,1536]{1,0:T(8,128)(2,1)S(1)}, u32[]{:S(2)}, u32[]{:S(2)}) %collective-permute-start.21) | collective-permute-done | bytes 786464 | tf_op jit(solution)/shard_map/ppermute | solution.py:195
  129.8 0.3 silu.1.hidden
  130.2 0.8 collective-permute-start.24
  131.0 1.7 leave.2
  132.7 0.8 collective-permute-start.25
  133.5 1.0 collective-permute-start.26
  134.6 6.6 %collective-permute-done.25.r1 = bf16[64,2048]{1,0:T(8,128)(2,1)S(1)} collective-permute-done((bf16[64,2048]{1,0:T(8,128)(2,1)S(1)}, bf16[64,2048]{1,0:T(8,128)(2,1)S(1)}, u32[]{:S(2)}, u32[]{:S(2)}) %collective-permute-start.25) | collective-permute-done | bytes 262176 | tf_op jit(solution)/shard_map/ppermute | solution.py:195
  141.2 0.4 collective-permute-done.26.r2
  141.6 1.7 leave.3
  143.4 0.7 copy-done.2
  144.1 1.3 collective-permute-start.29
  145.4 0.7 collective-permute-start.30
  146.1 1.5 collective-permute-start.31
  147.6 0.8 collective-permute-start.28
  148.4 1.2 collective-permute-start.27
  149.6 1.9 %collective-permute-done.28.shares = f32[64,128]{1,0:T(8,128)S(1)} collective-permute-done((f32[64,128]{1,0:T(8,128)S(1)}, f32[64,128]{1,0:T(8,128)S(1)}, u32[]{:S(2)}, u32[]{:S(2)}) %collective-permute-start.28) | collective-permute-done | bytes 32800 | tf_op jit(solution)/shard_map/ppermute | solution.py:195
  151.5 1.8 %collective-permute-done.29.r1 = bf16[64,2048]{1,0:T(8,128)(2,1)S(1)} collective-permute-done((bf16[64,2048]{1,0:T(8,128)(2,1)S(1)}, bf16[64,2048]{1,0:T(8,128)(2,1)S(1)}, u32[]{:S(2)}, u32[]{:S(2)}) %collective-permute-start.29) | collective-permute-done | bytes 262176 | tf_op jit(solution)/shard_map/ppermute | solution.py:195
  153.3 10.3 %collective-permute-done.30.r2 = bf16[64,2048]{1,0:T(8,128)(2,1)S(1)} collective-permute-done((bf16[64,2048]{1,0:T(8,128)(2,1)S(1)}, bf16[64,2048]{1,0:T(8,128)(2,1)S(1)}, u32[]{:S(2)}, u32[]{:S(2)}) %collective-permute-start.30) | collective-permute-done | bytes 262176 | tf_op jit(solution)/shard_map/ppermute | solution.py:195
  163.7 0.7 copy-done.4
  164.4 0.1 copy-done.5
  164.5 2.2 %total.1 = bf16[64,2048]{1,0:T(8,128)(2,1)} custom-call(f32[64,128]{1,0:T(8,128)} %copy-done.6, bf16[64,2048]{1,0:T(8,128)(2,1)} %copy-done.2, bf16[64,2048]{1,0:T(8,128)(2,1)} %copy-done.3, bf16[64,2048]{1,0:T(8,128)(2,1)} %copy-done.4, bf16[64,2048]{1,0:T(8,128)(2,1)} %copy-done.5), custom_call_target="tpu_custom_call" | custom-call | flops 1000 | bytes 1000 | tf_op jit(solution)/shard_map/total/pallas_call | solution.py:452
  166.6 0.8 collective-permute-start.32
  167.4 5.8 %collective-permute-done.32.other = bf16[64,2048]{1,0:T(8,128)(2,1)S(1)} collective-permute-done((bf16[64,2048]{1,0:T(8,128)(2,1)}, bf16[64,2048]{1,0:T(8,128)(2,1)S(1)}, u32[]{:S(2)}, u32[]{:S(2)}) %collective-permute-start.32) | collective-permute-done | bytes 262176 | tf_op jit(solution)/shard_map/ppermute | solution.py:195
  173.2 1.7 final.1
  (39 shorter events, 0.1 us)
Async XLA Ops:
  0.9 10.9 %collective-permute-start.1 = (bf16[256,256]{1,0:T(8,128)(2,1)S(1)}, bf16[256,256]{1,0:T(8,128)(2,1)S(1)}, u32[]{:S(2)}, u32[]{:S(2)}) collective-permute-start(bf16[256,256]{1,0:T(8,128)(2,1)S(1)} %pad_maximum_fusion.1.refs_0_), channel_id=1, source_target_pairs={{0,8},{4,12},{8,16},{12,20},{16,24},{20,28},{1,9},{5,13},{9,17},{1... | collective-permute-start | bytes 393224 | tf_op jit(solution)/shard_map/ppermute | solution.py:511
  5.9 8.4 %collective-permute-start.3 = (bf16[256,256]{1,0:T(8,128)(2,1)S(1)}, bf16[256,256]{1,0:T(8,128)(2,1)S(1)}, u32[]{:S(2)}, u32[]{:S(2)}) collective-permute-start(bf16[256,256]{1,0:T(8,128)(2,1)S(1)} %pad_maximum_fusion.1.refs_0_), channel_id=1, source_target_pairs={{0,16},{4,20},{8,24},{12,28},{1,17},{5,21},{9,25},{13,29},{2,18},{... | collective-permute-start | bytes 393224 | tf_op jit(solution)/shard_map/ppermute | solution.py:511
  10.4 5.3 %collective-permute-start.5 = (bf16[256,256]{1,0:T(8,128)(2,1)S(1)}, bf16[256,256]{1,0:T(8,128)(2,1)S(1)}, u32[]{:S(2)}, u32[]{:S(2)}) collective-permute-start(bf16[256,256]{1,0:T(8,128)(2,1)S(1)} %pad_maximum_fusion.1.refs_0_), channel_id=1, source_target_pairs={{0,24},{4,28},{1,25},{5,29},{2,26},{6,30},{3,27},{7,31}} | collective-permute-start | bytes 393224 | tf_op jit(solution)/shard_map/ppermute | solution.py:511
  11.7 5.5 %collective-permute-start = (bf16[256,256]{1,0:T(8,128)(2,1)S(1)}, bf16[256,256]{1,0:T(8,128)(2,1)S(1)}, u32[]{:S(2)}, u32[]{:S(2)}) collective-permute-start(bf16[256,256]{1,0:T(8,128)(2,1)S(1)} %pad_maximum_fusion.1.refs_0_), channel_id=1, source_target_pairs={{0,4},{4,0},{8,12},{12,8},{16,20},{20,16},{24,28},{28,24},{1,5},{5... | collective-permute-start | bytes 393224 | tf_op jit(solution)/shard_map/ppermute | solution.py:195
  11.7 11.8 %copy-start.8 = (f32[64,2]{0,1:T(2,128)S(1)}, f32[64,2]{0,1:T(2,128)}, u32[]{:S(2)}) copy-start(f32[64,2]{0,1:T(2,128)} %param.18) | copy-start | bytes 1540
  11.8 11.8 %copy-start.9 = (s32[64,2]{0,1:T(2,128)S(1)}, s32[64,2]{0,1:T(2,128)}, u32[]{:S(2)}) copy-start(s32[64,2]{0,1:T(2,128)} %param.17) | copy-start | bytes 1540
  11.8 5.4 %collective-permute-start.2 = (bf16[256,256]{1,0:T(8,128)(2,1)S(1)}, bf16[256,256]{1,0:T(8,128)(2,1)S(1)}, u32[]{:S(2)}, u32[]{:S(2)}) collective-permute-start(bf16[256,256]{1,0:T(8,128)(2,1)S(1)} %collective-permute-done.1.refs_2_), channel_id=1, source_target_pairs={{0,4},{4,0},{8,12},{12,8},{16,20},{20,16},{24,28},{28,24},{1,5},{5... | collective-permute-start | bytes 393224 | tf_op jit(solution)/shard_map/ppermute | solution.py:195
  14.3 2.9 %collective-permute-start.4 = (bf16[256,256]{1,0:T(8,128)(2,1)S(1)}, bf16[256,256]{1,0:T(8,128)(2,1)S(1)}, u32[]{:S(2)}, u32[]{:S(2)}) collective-permute-start(bf16[256,256]{1,0:T(8,128)(2,1)S(1)} %collective-permute-done.3.refs_4_), channel_id=1, source_target_pairs={{0,4},{4,0},{8,12},{12,8},{16,20},{20,16},{24,28},{28,24},{1,5},{5... | collective-permute-start | bytes 393224 | tf_op jit(solution)/shard_map/ppermute | solution.py:195
  15.7 1.5 collective-permute-start.6
  17.2 65.9 %collective-permute-start.14 = (bf16[1024,768]{1,0:T(8,128)(2,1)S(1)}, bf16[1024,768]{1,0:T(8,128)(2,1)S(1)}, u32[]{:S(2)}, u32[]{:S(2)}) collective-permute-start(bf16[1024,768]{1,0:T(8,128)(2,1)S(1)} %pad_maximum_fusion.refs_0_), channel_id=1, source_target_pairs={{0,24},{4,28},{8,16},{12,20},{16,8},{20,12},{24,0},{28,4},{1,25},{... | collective-permute-start | bytes 4718600 | tf_op jit(solution)/shard_map/ppermute | solution.py:195
  23.7 21.8 %copy-start.7 = (bf16[4096]{0:T(1024)(128)(2,1)S(1)}, bf16[4096]{0:T(1024)(128)(2,1)}, u32[]{:S(2)}) copy-start(bf16[4096]{0:T(1024)(128)(2,1)} %param.16) | copy-start | bytes 24580
  23.7 44.5 %copy-start.1 = (bf16[64,4096]{1,0:T(8,128)(2,1)S(1)}, bf16[64,4096]{1,0:T(8,128)(2,1)}, u32[]{:S(2)}) copy-start(bf16[64,4096]{1,0:T(8,128)(2,1)} %residual.1) | copy-start | bytes 1572868
  41.9 41.3 %copy-start = (bf16[1,768,512]{2,1,0:T(8,128)(2,1)S(1)}, bf16[1,768,512]{2,1,0:T(8,128)(2,1)}, u32[]{:S(2)}) copy-start(bf16[1,768,512]{2,1,0:T(8,128)(2,1)} %param.21) | copy-start | bytes 2359300
  42.0 15.1 %collective-permute-start.7 = (bf16[64,4096]{1,0:T(8,128)(2,1)}, bf16[64,4096]{1,0:T(8,128)(2,1)S(1)}, u32[]{:S(2)}, u32[]{:S(2)}) collective-permute-start(bf16[64,4096]{1,0:T(8,128)(2,1)} %get-tuple-element.70), channel_id=1, source_target_pairs={{0,1},{1,0},{2,3},{3,2},{4,5},{5,4},{6,7},{7,6},{8,9},{9,8},{10,11... | collective-permute-start | bytes 1572872 | tf_op jit(solution)/shard_map/ppermute | solution.py:195
  43.5 24.7 %collective-permute-start.8 = (bf16[64,4096]{1,0:T(8,128)(2,1)}, bf16[64,4096]{1,0:T(8,128)(2,1)S(1)}, u32[]{:S(2)}, u32[]{:S(2)}) collective-permute-start(bf16[64,4096]{1,0:T(8,128)(2,1)} %get-tuple-element.71), channel_id=1, source_target_pairs={{0,2},{1,3},{2,0},{3,1},{4,6},{5,7},{6,4},{7,5},{8,10},{9,11},{10,... | collective-permute-start | bytes 1572872 | tf_op jit(solution)/shard_map/ppermute | solution.py:195
  45.0 23.2 %collective-permute-start.9 = (bf16[64,4096]{1,0:T(8,128)(2,1)}, bf16[64,4096]{1,0:T(8,128)(2,1)S(1)}, u32[]{:S(2)}, u32[]{:S(2)}) collective-permute-start(bf16[64,4096]{1,0:T(8,128)(2,1)} %get-tuple-element.72), channel_id=1, source_target_pairs={{0,3},{1,2},{2,1},{3,0},{4,7},{5,6},{6,5},{7,4},{8,11},{9,10},{10,... | collective-permute-start | bytes 1572872 | tf_op jit(solution)/shard_map/ppermute | solution.py:195
  69.4 9.3 %collective-permute-start.10 = (bf16[64,2048]{1,0:T(8,128)(2,1)S(1)}, bf16[64,2048]{1,0:T(8,128)(2,1)S(1)}, u32[]{:S(2)}, u32[]{:S(2)}) collective-permute-start(bf16[64,2048]{1,0:T(8,128)(2,1)S(1)} %get-tuple-element.83.x0), channel_id=1, source_target_pairs={{0,1},{1,0},{2,3},{3,2},{4,5},{5,4},{6,7},{7,6},{8,9},{9,8},{10,11... | collective-permute-start | bytes 786440 | tf_op jit(solution)/shard_map/ppermute | solution.py:195
  70.7 12.4 %collective-permute-start.11 = (bf16[64,2048]{1,0:T(8,128)(2,1)S(1)}, bf16[64,2048]{1,0:T(8,128)(2,1)S(1)}, u32[]{:S(2)}, u32[]{:S(2)}) collective-permute-start(bf16[64,2048]{1,0:T(8,128)(2,1)S(1)} %get-tuple-element.83.x0), channel_id=1, source_target_pairs={{0,2},{1,3},{2,0},{3,1},{4,6},{5,7},{6,4},{7,5},{8,10},{9,11},{10,... | collective-permute-start | bytes 786440 | tf_op jit(solution)/shard_map/ppermute | solution.py:195
  71.5 11.6 %collective-permute-start.12 = (bf16[64,2048]{1,0:T(8,128)(2,1)S(1)}, bf16[64,2048]{1,0:T(8,128)(2,1)S(1)}, u32[]{:S(2)}, u32[]{:S(2)}) collective-permute-start(bf16[64,2048]{1,0:T(8,128)(2,1)S(1)} %get-tuple-element.83.x0), channel_id=1, source_target_pairs={{0,3},{1,2},{2,1},{3,0},{4,7},{5,6},{6,5},{7,4},{8,11},{9,10},{10,... | collective-permute-start | bytes 786440 | tf_op jit(solution)/shard_map/ppermute | solution.py:195
  73.0 10.2 %collective-permute-start.13 = (bf16[64,2048]{1,0:T(8,128)(2,1)S(1)}, bf16[64,2048]{1,0:T(8,128)(2,1)S(1)}, u32[]{:S(2)}, u32[]{:S(2)}) collective-permute-start(bf16[64,2048]{1,0:T(8,128)(2,1)S(1)} %get-tuple-element.76), channel_id=1, source_target_pairs={{0,8},{4,12},{8,0},{12,4},{16,24},{20,28},{24,16},{28,20},{1,9},{5... | collective-permute-start | bytes 786440 | tf_op jit(solution)/shard_map/ppermute | solution.py:195
  78.7 30.2 %collective-permute-start.16 = (bf16[1024,768]{1,0:T(8,128)(2,1)S(1)}, bf16[1024,768]{1,0:T(8,128)(2,1)S(1)}, u32[]{:S(2)}, u32[]{:S(2)}) collective-permute-start(bf16[1024,768]{1,0:T(8,128)(2,1)S(1)} %pad_maximum_fusion.refs_0_), channel_id=1, source_target_pairs={{0,4},{4,0},{8,12},{12,8},{16,20},{20,16},{24,28},{28,24},{1,5},{5... | collective-permute-start | bytes 4718600 | tf_op jit(solution)/shard_map/ppermute | solution.py:195
  83.1 25.8 %collective-permute-start.17 = (bf16[1024,768]{1,0:T(8,128)(2,1)S(1)}, bf16[1024,768]{1,0:T(8,128)(2,1)S(1)}, u32[]{:S(2)}, u32[]{:S(2)}) collective-permute-start(bf16[1024,768]{1,0:T(8,128)(2,1)S(1)} %collective-permute-done.14.refs_2_), channel_id=1, source_target_pairs={{0,4},{4,0},{8,12},{12,8},{16,20},{20,16},{24,28},{28,24},{1,5},{5... | collective-permute-start | bytes 4718600 | tf_op jit(solution)/shard_map/ppermute | solution.py:195
  83.2 28.9 %collective-permute-start.15 = (bf16[768,512]{1,0:T(8,128)(2,1)S(1)}, bf16[768,512]{1,0:T(8,128)(2,1)S(1)}, u32[]{:S(2)}, u32[]{:S(2)}) collective-permute-start(bf16[768,512]{1,0:T(8,128)(2,1)S(1)} %bitcast.13), channel_id=1, source_target_pairs={{0,24},{4,28},{8,16},{12,20},{16,8},{20,12},{24,0},{28,4},{1,25},{... | collective-permute-start | bytes 2359304 | tf_op jit(solution)/shard_map/ppermute | solution.py:195
  92.0 8.4 %collective-permute-start.18 = (bf16[64,2048]{1,0:T(8,128)(2,1)S(1)}, bf16[64,2048]{1,0:T(8,128)(2,1)S(1)}, u32[]{:S(2)}, u32[]{:S(2)}) collective-permute-start(bf16[64,2048]{1,0:T(8,128)(2,1)S(1)} %collective-permute-done.13.x0), channel_id=1, source_target_pairs={{0,1},{1,0},{2,3},{3,2},{4,5},{5,4},{6,7},{7,6},{8,9},{9,8},{10,11... | collective-permute-start | bytes 786440 | tf_op jit(solution)/shard_map/ppermute | solution.py:195
  92.7 8.9 %collective-permute-start.19 = (bf16[64,2048]{1,0:T(8,128)(2,1)S(1)}, bf16[64,2048]{1,0:T(8,128)(2,1)S(1)}, u32[]{:S(2)}, u32[]{:S(2)}) collective-permute-start(bf16[64,2048]{1,0:T(8,128)(2,1)S(1)} %collective-permute-done.13.x0), channel_id=1, source_target_pairs={{0,2},{1,3},{2,0},{3,1},{4,6},{5,7},{6,4},{7,5},{8,10},{9,11},{10,... | collective-permute-start | bytes 786440 | tf_op jit(solution)/shard_map/ppermute | solution.py:195
  100.4 8.4 %collective-permute-start.20 = (bf16[64,2048]{1,0:T(8,128)(2,1)S(1)}, bf16[64,2048]{1,0:T(8,128)(2,1)S(1)}, u32[]{:S(2)}, u32[]{:S(2)}) collective-permute-start(bf16[64,2048]{1,0:T(8,128)(2,1)S(1)} %collective-permute-done.13.x0), channel_id=1, source_target_pairs={{0,3},{1,2},{2,1},{3,0},{4,7},{5,6},{6,5},{7,4},{8,11},{9,10},{10,... | collective-permute-start | bytes 786440 | tf_op jit(solution)/shard_map/ppermute | solution.py:195
  111.9 17.9 %collective-permute-start.21 = (bf16[256,1536]{1,0:T(8,128)(2,1)S(1)}, bf16[256,1536]{1,0:T(8,128)(2,1)S(1)}, u32[]{:S(2)}, u32[]{:S(2)}) collective-permute-start(bf16[256,1536]{1,0:T(8,128)(2,1)S(1)} %enter.3), channel_id=1, source_target_pairs={{0,8},{4,12},{8,0},{12,4},{16,24},{20,28},{24,16},{28,20},{1,9},{5... | collective-permute-start | bytes 2359304 | tf_op jit(solution)/shard_map/ppermute | solution.py:195
  112.0 19.0 %collective-permute-start.22 = (bf16[768,512]{1,0:T(8,128)(2,1)S(1)}, bf16[768,512]{1,0:T(8,128)(2,1)S(1)}, u32[]{:S(2)}, u32[]{:S(2)}) collective-permute-start(bf16[768,512]{1,0:T(8,128)(2,1)S(1)} %bitcast.14), channel_id=1, source_target_pairs={{0,4},{4,0},{8,12},{12,8},{16,20},{20,16},{24,28},{28,24},{1,5},{5... | collective-permute-start | bytes 2359304 | tf_op jit(solution)/shard_map/ppermute | solution.py:195
  112.1 18.9 %collective-permute-start.23 = (bf16[768,512]{1,0:T(8,128)(2,1)S(1)}, bf16[768,512]{1,0:T(8,128)(2,1)S(1)}, u32[]{:S(2)}, u32[]{:S(2)}) collective-permute-start(bf16[768,512]{1,0:T(8,128)(2,1)S(1)} %collective-permute-done.15.d2), channel_id=1, source_target_pairs={{0,4},{4,0},{8,12},{12,8},{16,20},{20,16},{24,28},{28,24},{1,5},{5... | collective-permute-start | bytes 2359304 | tf_op jit(solution)/shard_map/ppermute | solution.py:195
  130.2 11.5 %collective-permute-start.24 = (bf16[256,768]{1,0:T(8,128)(2,1)S(1)}, bf16[256,768]{1,0:T(8,128)(2,1)S(1)}, u32[]{:S(2)}, u32[]{:S(2)}) collective-permute-start(bf16[256,768]{1,0:T(8,128)(2,1)S(1)} %silu.1.hidden), channel_id=1, source_target_pairs={{0,8},{4,12},{8,0},{12,4},{16,24},{20,28},{24,16},{28,20},{1,9},{5... | collective-permute-start | bytes 1179656 | tf_op jit(solution)/shard_map/ppermute | solution.py:195
  132.7 8.5 %collective-permute-start.25 = (bf16[64,2048]{1,0:T(8,128)(2,1)S(1)}, bf16[64,2048]{1,0:T(8,128)(2,1)S(1)}, u32[]{:S(2)}, u32[]{:S(2)}) collective-permute-start(bf16[64,2048]{1,0:T(8,128)(2,1)S(1)} %get-tuple-element.91), channel_id=1, source_target_pairs={{0,1},{1,0},{2,3},{3,2},{4,5},{5,4},{6,7},{7,6},{8,9},{9,8},{10,11... | collective-permute-start | bytes 786440 | tf_op jit(solution)/shard_map/ppermute | solution.py:195
  133.5 8.1 %collective-permute-start.26 = (bf16[64,2048]{1,0:T(8,128)(2,1)S(1)}, bf16[64,2048]{1,0:T(8,128)(2,1)S(1)}, u32[]{:S(2)}, u32[]{:S(2)}) collective-permute-start(bf16[64,2048]{1,0:T(8,128)(2,1)S(1)} %get-tuple-element.92), channel_id=1, source_target_pairs={{0,2},{1,3},{2,0},{3,1},{4,6},{5,7},{6,4},{7,5},{8,10},{9,11},{10,... | collective-permute-start | bytes 786440 | tf_op jit(solution)/shard_map/ppermute | solution.py:195
  143.4 0.7 copy-start.2
  144.1 9.2 %collective-permute-start.29 = (bf16[64,2048]{1,0:T(8,128)(2,1)S(1)}, bf16[64,2048]{1,0:T(8,128)(2,1)S(1)}, u32[]{:S(2)}, u32[]{:S(2)}) collective-permute-start(bf16[64,2048]{1,0:T(8,128)(2,1)S(1)} %get-tuple-element.98), channel_id=1, source_target_pairs={{0,1},{1,0},{2,3},{3,2},{4,5},{5,4},{6,7},{7,6},{8,9},{9,8},{10,11... | collective-permute-start | bytes 786440 | tf_op jit(solution)/shard_map/ppermute | solution.py:195
  145.4 18.3 %collective-permute-start.30 = (bf16[64,2048]{1,0:T(8,128)(2,1)S(1)}, bf16[64,2048]{1,0:T(8,128)(2,1)S(1)}, u32[]{:S(2)}, u32[]{:S(2)}) collective-permute-start(bf16[64,2048]{1,0:T(8,128)(2,1)S(1)} %get-tuple-element.99), channel_id=1, source_target_pairs={{0,2},{1,3},{2,0},{3,1},{4,6},{5,7},{6,4},{7,5},{8,10},{9,11},{10,... | collective-permute-start | bytes 786440 | tf_op jit(solution)/shard_map/ppermute | solution.py:195
  146.1 17.6 %collective-permute-start.31 = (bf16[64,2048]{1,0:T(8,128)(2,1)S(1)}, bf16[64,2048]{1,0:T(8,128)(2,1)S(1)}, u32[]{:S(2)}, u32[]{:S(2)}) collective-permute-start(bf16[64,2048]{1,0:T(8,128)(2,1)S(1)} %get-tuple-element.100), channel_id=1, source_target_pairs={{0,3},{1,2},{2,1},{3,0},{4,7},{5,6},{6,5},{7,4},{8,11},{9,10},{10,... | collective-permute-start | bytes 786440 | tf_op jit(solution)/shard_map/ppermute | solution.py:195
  147.6 3.9 %collective-permute-start.28 = (f32[64,128]{1,0:T(8,128)S(1)}, f32[64,128]{1,0:T(8,128)S(1)}, u32[]{:S(2)}, u32[]{:S(2)}) collective-permute-start(f32[64,128]{1,0:T(8,128)S(1)} %select_add_fusion.shares), channel_id=1, source_target_pairs={{0,8},{4,12},{8,0},{12,4},{16,24},{20,28},{24,16},{28,20},{1,9},{5... | collective-permute-start | bytes 98312 | tf_op jit(solution)/shard_map/ppermute | solution.py:195
  148.4 19.0 %collective-permute-start.27 = (bf16[64,2048]{1,0:T(8,128)(2,1)S(1)}, bf16[64,2048]{1,0:T(8,128)(2,1)S(1)}, u32[]{:S(2)}, u32[]{:S(2)}) collective-permute-start(bf16[64,2048]{1,0:T(8,128)(2,1)S(1)} %get-tuple-element.95), channel_id=1, source_target_pairs={{0,3},{1,2},{2,1},{3,0},{4,7},{5,6},{6,5},{7,4},{8,11},{9,10},{10,... | collective-permute-start | bytes 786440 | tf_op jit(solution)/shard_map/ppermute | solution.py:195
  151.5 12.2 %copy-start.6 = (f32[64,128]{1,0:T(8,128)}, f32[64,128]{1,0:T(8,128)S(1)}, u32[]{:S(2)}) copy-start(f32[64,128]{1,0:T(8,128)S(1)} %collective-permute-done.28.shares) | copy-start | bytes 98308
  153.3 10.4 %copy-start.3 = (bf16[64,2048]{1,0:T(8,128)(2,1)}, bf16[64,2048]{1,0:T(8,128)(2,1)S(1)}, u32[]{:S(2)}) copy-start(bf16[64,2048]{1,0:T(8,128)(2,1)S(1)} %collective-permute-done.29.r1) | copy-start | bytes 786436
  163.7 0.7 copy-start.4
  163.7 0.8 copy-start.5
  166.6 6.6 %collective-permute-start.32 = (bf16[64,2048]{1,0:T(8,128)(2,1)}, bf16[64,2048]{1,0:T(8,128)(2,1)S(1)}, u32[]{:S(2)}, u32[]{:S(2)}) collective-permute-start(bf16[64,2048]{1,0:T(8,128)(2,1)} %total.1), channel_id=1, source_target_pairs={{0,8},{4,12},{8,0},{12,4},{16,24},{20,28},{24,16},{28,20},{1,9},{5... | collective-permute-start | bytes 786440 | tf_op jit(solution)/shard_map/ppermute | solution.py:195

commit v4 on v3

--- a/solution.py
+++ b/solution.py
@@ -223,8 +223,6 @@
         )
         for i in range(steps)
     ]
-    for fetch in fetches:
-        fetch.start()
     factor = math.log2(math.e) / math.sqrt(HD)
     heads = q.shape[1] // HD
     ones_values[:, HD:] = jnp.ones((ones_values.shape[0], HD), BF16)
@@ -246,6 +244,8 @@
                 ones_values[here, :HD] = piece[:, HD:]
 
     q_fetch.wait()
+    for fetch in fetches:
+        fetch.start()
     part = QB // 4
 
     def run(length):
@@ -350,8 +350,8 @@
     )(index, p0, r1, r2, r3, residual, gain)
 
 
-def enter_kernel(x0, x1, x2, x3, *refs):
-    weights, out, gate_all, up_all, sems = refs[:4], refs[4], refs[5], refs[6], refs[7]
+def enter_kernel(*refs):
+    rows, weights, (out, gate_all, up_all, sems) = refs[:-8], refs[-8:-4], refs[-4:]
     part, width = weights[0].shape[0] // 2, weights[0].shape[1]
     fetches = []
     for which, whole in enumerate((gate_all, up_all)):
@@ -360,7 +360,7 @@
             target = whole.at[pl.ds(j * part, part)]
             fetches.append(pltpu.make_async_copy(source, target, sems.at[4 * which + j]))
             fetches[-1].start()
-    x = jnp.concatenate([x0[...], x1[...], x2[...], x3[...]], axis=0)
+    x = jnp.concatenate([block[...] for block in rows], axis=0)
     tile = 256
     for which, whole in enumerate((gate_all, up_all)):
         for fetch in fetches[4 * which : 4 * which + 4]:
@@ -372,12 +372,12 @@
 
 
 def enter(rows, weights, kind):
-    count = 4 * rows[0].shape[0]
+    count = len(rows) * rows[0].shape[0]
     part, width = weights[0].shape[0] // 2, weights[0].shape[1]
     return pl.pallas_call(
         enter_kernel,
         out_shape=jax.ShapeDtypeStruct((count, 2 * width), kind),
-        in_specs=vmem_specs(4) + [pl.BlockSpec(memory_space=pl.ANY)] * 4,
+        in_specs=vmem_specs(len(rows)) + [pl.BlockSpec(memory_space=pl.ANY)] * 4,
         out_specs=pl.BlockSpec(memory_space=VMEM),
         scratch_shapes=[
             VMEM((4 * part, width), BF16),
@@ -390,17 +390,18 @@
     )(*rows, *weights)
 
 
-def silu_kernel(own, other, out):
-    width = out.shape[1]
-    total = own[...] + other[...].astype(F32)
+def silu_kernel(half, own, other, out):
+    count, width = out.shape
+    total = own[half * count : (half + 1) * count] + other[...].astype(F32)
     gate, up = total[:, :width], total[:, width:]
     out[...] = (gate / (1.0 + jnp.exp(-gate)) * up).astype(BF16)
 
 
-def silu(own, other):
+def silu(own, other, half):
+    count, width = other.shape
     return pl.pallas_call(
-        silu_kernel,
-        out_shape=jax.ShapeDtypeStruct((own.shape[0], own.shape[1] // 2), BF16),
+        functools.partial(silu_kernel, half),
+        out_shape=jax.ShapeDtypeStruct((count, width // 2), BF16),
         in_specs=vmem_specs(2),
         out_specs=pl.BlockSpec(memory_space=VMEM),
         compiler_params=params(16),
@@ -409,32 +410,35 @@
     )(own, other)
 
 
-def leave_kernel(hidden, d0, d1, d2, d3, y0, y1, y2, y3, down_all, sems):
-    part = y0.shape[0]
-    width = d0.shape[1]
+def leave_kernel(*refs):
+    count = (len(refs) - 6) // 3
+    hiddens, arrays, outs, (down_all, sems) = refs[:count], refs[count : count + 4], refs[count + 4 : -2], refs[-2:]
+    part = outs[0].shape[0]
+    width = arrays[0].shape[1]
     fetches = []
-    for j, array in enumerate((d0, d1, d2, d3)):
+    for j, array in enumerate(arrays):
         fetches.append(pltpu.make_async_copy(array, down_all.at[j], sems.at[j]))
         fetches[-1].start()
+    hidden = jnp.concatenate([block[...] for block in hiddens], axis=0)
     for j in range(4):
         fetches[j].wait()
-        block = jnp.dot(hidden[...], down_all[j], preferred_element_type=F32).astype(BF16)
-        for b, out in enumerate((y0, y1, y2, y3)):
+        block = jnp.dot(hidden, down_all[j], preferred_element_type=F32).astype(BF16)
+        for b, out in enumerate(outs):
             out[:, j * width : (j + 1) * width] = block[b * part : (b + 1) * part]
 
 
-def leave(hidden, downs):
-    part = jax.ShapeDtypeStruct((hidden.shape[0] // 4, 4 * downs[0].shape[1]), BF16)
+def leave(hiddens, downs):
+    part = jax.ShapeDtypeStruct((hiddens[0].shape[0] // 2, 4 * downs[0].shape[1]), BF16)
     return pl.pallas_call(
         leave_kernel,
-        out_shape=[part] * 4,
-        in_specs=vmem_specs(1) + [pl.BlockSpec(memory_space=pl.ANY)] * 4,
-        out_specs=vmem_specs(4),
+        out_shape=[part] * (2 * len(hiddens)),
+        in_specs=vmem_specs(len(hiddens)) + [pl.BlockSpec(memory_space=pl.ANY)] * 4,
+        out_specs=vmem_specs(2 * len(hiddens)),
         scratch_shapes=[VMEM((4,) + downs[0].shape, BF16), pltpu.SemaphoreType.DMA((4,))],
-        compiler_params=params(16),
+        compiler_params=params(24),
         cost_estimate=CHEAP,
         name="leave",
-    )(hidden, *downs)
+    )(*hiddens, *downs)
 
 
 def mixed(shares, parts):
@@ -442,21 +446,6 @@
     for b in range(1, 4):
         total = total + shares[:, b : b + 1] * parts[b][...].astype(F32)
     return total
-
-
-def total_kernel(shares, y0, r1, r2, r3, out):
-    out[...] = mixed(shares, (y0, r1, r2, r3)).astype(BF16)
-
-
-def total_of(shares, y0, r1, r2, r3):
-    return pl.pallas_call(
-        total_kernel,
-        out_shape=jax.ShapeDtypeStruct(y0.shape, BF16),
-        in_specs=vmem_specs(5),
-        out_specs=pl.BlockSpec(memory_space=VMEM),
-        cost_estimate=CHEAP,
-        name="total",
-    )(shares, y0, r1, r2, r3)
 
 
 def final_kernel(index, state, shares, y0, r1, r2, r3, other, out):
@@ -513,8 +502,12 @@
     kv_here, gate_here, up_here = lax.optimization_barrier((kv_here, w_gate[0], w_up[0]))
     moved = [later(kv_here, d) for d in (3, 2, 1)][::-1]
     pair_here, down_here = jnp.concatenate([gate_here, up_here], axis=0), w_down[0]
+    moved[0], pair_here, down_here = lax.optimization_barrier((moved[0], pair_here, down_here))
     pieces = [part for piece in [kv_here] + moved for part in (piece, swap(piece, "ctx", 1))]
-    pieces, pair_here = lax.optimization_barrier((pieces, pair_here))
+    pair_near, down_near = swap(pair_here, "ctx", 1), swap(down_here, "ctx", 1)
+    pieces, pair_here, pair_near, down_near = lax.optimization_barrier(
+        (pieces, pair_here, pair_near, down_near)
+    )
     pair_far = swap(pair_here, "ctx", 6)
 
     lane = lax.broadcasted_iota(jnp.int32, (expert_ids.shape[0], HD), 1)
@@ -524,32 +517,35 @@
         shares = shares + jnp.where(lane == named, gate_weights[:, k : k + 1], 0.0)
 
     p = attention(index, queries, pieces, w_out)
-    p, shares, pair_here, down_here = lax.optimization_barrier((p, shares, pair_here, down_here))
+    p, shares = lax.optimization_barrier((p, shares))
     r = [swap(p[b], "exp", b) for b in (1, 2, 3)]
-    pair_near, down_near = swap(pair_here, "ctx", 1), swap(down_here, "ctx", 1)
     other_shares = swap(shares, "ctx", 2)
+    r, other_shares = lax.optimization_barrier((r, other_shares))
     state, mine, theirs = norm(index, p[0], *r, residual, norm_gain.reshape(1, D))
     others = swap(theirs, "ctx", 2)
     own_rows = [mine] + [swap(mine, "exp", b) for b in (1, 2, 3)]
     other_rows = [others] + [swap(others, "exp", b) for b in (1, 2, 3)]
-    own_rows, others, pair_far, down_here = lax.optimization_barrier(
-        (own_rows, others, pair_far, down_here)
+    own_rows, other_rows[1:3], pair_far, down_here = lax.optimization_barrier(
+        (own_rows, other_rows[1:3], pair_far, down_here)
     )
     down_far = swap(down_here, "ctx", 6)
     pairs = (pair_here, pair_near, pair_far, swap(pair_far, "ctx", 1))
-    other_pre = enter(other_rows, pairs, BF16)
-    from_other = swap(other_pre, "ctx", 2)
-    own_rows, down_far = lax.optimization_barrier((own_rows, down_far))
     own_pre = enter(own_rows, pairs, F32)
-    own_hidden = silu(own_pre, from_other)
-    other_hidden = swap(own_hidden, "ctx", 2)
+    other_rows[:2], own_pre = lax.optimization_barrier((other_rows[:2], own_pre))
+    first_pre = enter(other_rows[:2], pairs, BF16)
+    first_pre, other_rows[2:] = lax.optimization_barrier((first_pre, other_rows[2:]))
+    first_sum = swap(first_pre, "ctx", 2)
+    last_sum = swap(enter(other_rows[2:], pairs, BF16), "ctx", 2)
+    first = silu(own_pre, first_sum, 0)
+    other_first = swap(first, "ctx", 2)
+    last_sum, other_first, down_far = lax.optimization_barrier((last_sum, other_first, down_far))
+    last = silu(own_pre, last_sum, 1)
+    other_last = swap(last, "ctx", 2)
     downs = (down_here, down_near, down_far, swap(down_far, "ctx", 1))
-    y = leave(own_hidden, downs)
+    y = leave([first, last, other_first, other_last], downs)
     own_parts = [y[0]] + [swap(y[b], "exp", b) for b in (1, 2, 3)]
-    other_hidden, *own_parts[1:3] = lax.optimization_barrier((other_hidden, *own_parts[1:3]))
-    z = leave(other_hidden, downs)
-    other_parts = [z[0]] + [swap(z[b], "exp", b) for b in (1, 2, 3)]
-    back = swap(total_of(other_shares, *other_parts), "ctx", 2)
+    other_parts = [y[4]] + [swap(y[4 + b], "exp", b) for b in (1, 2, 3)]
+    back = swap(mixed(other_shares, other_parts).astype(BF16), "ctx", 2)
     return final(index, state, shares, *own_parts, back)
 
 

time: 175 us -> 179 us (1.023)
  starting transfers between devices: 46.3 us -> 55.9 us
  Pallas kernels: 33.1 us -> 28.1 us
    ppermute x30 -> x32, starting transfers between devices: 35.6 us -> 42.6 us  [swap(): return lax.ppermute(array, axis, [(i, i ^ mask) for i in range(size)])]
    pallas_call x1, Pallas kernels: 18.2 us -> 14.4 us  [attention(): pl.pallas_call(attention_kernel, out_shape=[jax.ShapeDtypeStruct((rows, D...]
    ppermute x3, starting transfers between devices: 10.7 us -> 13.3 us  [later(): lax.ppermute(array, 'ctx', [(i, i + 2 * chips) for i in range(8 - 2 * chi...]
    pallas_call x4 -> x3, Pallas kernels: 5.93 us -> 3.78 us  [the longest x1 3.46 us: leave(): pl.pallas_call(leave_kernel, out_shape=[part] * (2 * len(hiddens)), in_sp...]
    pallas_call x2 -> x3, Pallas kernels: 6.1 us -> 7 us  [enter(): pl.pallas_call(enter_kernel, out_shape=jax.ShapeDtypeStruct((count, 2 * w...]
    ppermute x30 -> x32, waiting for transfers between devices: 87.7 us -> 87.1 us  [swap(): return lax.ppermute(array, axis, [(i, i ^ mask) for i in range(size)])]
  transfers between devices with their start and end apart: 33 -> 35, of which waited for: 15 -> 22; matrix products, arithmetic and copies ran while one was open for 1% -> 1% of each run, Pallas kernels for 17% -> 13%
where the time goes in v4:
time: 179 us
  waiting for transfers between devices  91.5 us (51%)
  starting transfers between devices  55.9 us (31%)
  Pallas kernels  28.1 us (16%)
  other arithmetic  1.96 us (1%)
    ppermute x32, waiting for transfers between devices, swap(): return lax.ppermute(array, axis, [(i, i ^ mask) for i in range(size)])  87.1 us
    ppermute x32, starting transfers between devices, swap(): return lax.ppermute(array, axis, [(i, i ^ mask) for i in range(size)])  42.6 us
    pallas_call x1, Pallas kernels, attention(): pl.pallas_call(attention_kernel, out_shape=[jax.ShapeDtypeStruct((rows, D...  14.4 us
    ppermute x3, starting transfers between devices, later(): lax.ppermute(array, 'ctx', [(i, i + 2 * chips) for i in range(8 - 2 * chi...  13.3 us
    pallas_call x3, Pallas kernels, enter(): pl.pallas_call(enter_kernel, out_shape=jax.ShapeDtypeStruct((count, 2 * w...  7 us
    ppermute x3, waiting for transfers between devices, later(): lax.ppermute(array, 'ctx', [(i, i + 2 * chips) for i in range(8 - 2 * chi...  4.31 us
  transfers between devices with their start and end apart: 35, of which 22 were waited for; matrix products, arithmetic and copies ran while one was open for 1% of the time, Pallas kernels for 13%

profile of v4, /device:TPU:0, one launch (start us, length us, event | category | flops | bytes accessed | tf_op | source)
XLA Modules:
  0.0 178.7 jit_solution(5886557560921175030)
XLA Ops:
  0.0 0.9 constant_dynamic-slice_fusion
  0.9 4.9 %collective-permute-start.1 = (bf16[256,256]{1,0:T(8,128)(2,1)S(1)}, bf16[256,256]{1,0:T(8,128)(2,1)S(1)}, u32[]{:S(2)}, u32[]{:S(2)}) collective-permute-start(bf16[256,256]{1,0:T(8,128)(2,1)S(1)} %pad_maximum_fusion.1.refs_0_), channel_id=1, source_target_pairs={{0,8},{4,12},{8,16},{12,20},{16,24},{20,28},{1,9},{5,13},{9,17},{1... | collective-permute-start | bytes 393224 | tf_op jit(solution)/shard_map/ppermute | solution.py:500
  5.9 1.5 pad_maximum_fusion.refs_4_.refs_2_
  7.4 1.3 collective-permute-done.1.refs_2_
  8.6 0.5 collective-permute-start.8
  9.1 6.0 %collective-permute-start.3 = (bf16[256,256]{1,0:T(8,128)(2,1)S(1)}, bf16[256,256]{1,0:T(8,128)(2,1)}, u32[]{:S(2)}, u32[]{:S(2)}) collective-permute-start(bf16[256,256]{1,0:T(8,128)(2,1)S(1)} %pad_maximum_fusion.1.refs_0_), channel_id=1, source_target_pairs={{0,16},{4,20},{8,24},{12,28},{1,17},{5,21},{9,25},{13,29},{2,18},{... | collective-permute-start | bytes 393224 | tf_op jit(solution)/shard_map/ppermute | solution.py:500
  15.2 2.3 %collective-permute-start.5 = (bf16[256,256]{1,0:T(8,128)(2,1)S(1)}, bf16[256,256]{1,0:T(8,128)(2,1)}, u32[]{:S(2)}, u32[]{:S(2)}) collective-permute-start(bf16[256,256]{1,0:T(8,128)(2,1)S(1)} %pad_maximum_fusion.1.refs_0_), channel_id=1, source_target_pairs={{0,24},{4,28},{1,25},{5,29},{2,26},{6,30},{3,27},{7,31}} | collective-permute-start | bytes 393224 | tf_op jit(solution)/shard_map/ppermute | solution.py:500
  17.5 0.2 collective-permute-start.2
  17.7 0.6 collective-permute-done.3.refs_4_
  18.4 2.4 %collective-permute-done.5.refs_6_ = bf16[256,256]{1,0:T(8,128)(2,1)} collective-permute-done((bf16[256,256]{1,0:T(8,128)(2,1)S(1)}, bf16[256,256]{1,0:T(8,128)(2,1)}, u32[]{:S(2)}, u32[]{:S(2)}) %collective-permute-start.5) | collective-permute-done | bytes 131104 | tf_op jit(solution)/shard_map/ppermute | solution.py:500
  20.8 1.5 collective-permute-done.6.refs_7_
  22.3 7.3 %collective-permute-start.19 = (bf16[1024,768]{1,0:T(8,128)(2,1)S(1)}, bf16[1024,768]{1,0:T(8,128)(2,1)S(1)}, u32[]{:S(2)}, u32[]{:S(2)}) collective-permute-start(bf16[1024,768]{1,0:T(8,128)(2,1)S(1)} %pad_maximum_fusion.refs_4_.refs_2_), channel_id=1, source_target_pairs={{0,24},{4,28},{8,16},{12,20},{16,8},{20,12},{24,0},{28,4},{1,25},{... | collective-permute-start | bytes 4718600 | tf_op jit(solution)/shard_map/ppermute | solution.py:195
  29.7 0.1 pad_add_fusion.index
  29.8 0.1 select_add_fusion.shares
  29.9 14.4 %attention.1 = (bf16[64,4096]{1,0:T(8,128)(2,1)S(1)}, bf16[64,4096]{1,0:T(8,128)(2,1)}, bf16[64,4096]{1,0:T(8,128)(2,1)}, bf16[64,4096]{1,0:T(8,128)(2,1)}) custom-call(s32[2]{0:T(128)S(1)} %pad_add_fusion.index, bf16[256,2048]{1,0:T(8,128)(2,1)} %q_hbm.1, bf16[256,256]{1,0:T(8,128)(2,1)S(1)} %pad_maximum_fusion.1.refs_0_, ...), custom_call_target="tpu_custom_call" | custom-call | flops 1000 | bytes 1000 | tf_op jit(solution)/shard_map/attention/pallas_call | solution.py:296
  44.3 1.6 collective-permute-start.9
  45.9 1.5 collective-permute-start.10
  47.4 0.5 collective-permute-start.11
  47.9 17.5 %collective-permute-done.12 = f32[64,128]{1,0:T(8,128)S(1)} collective-permute-done((f32[64,128]{1,0:T(8,128)S(1)}, f32[64,128]{1,0:T(8,128)S(1)}, u32[]{:S(2)}, u32[]{:S(2)}) %collective-permute-start.12) | collective-permute-done | bytes 32800 | tf_op jit(solution)/shard_map/ppermute | solution.py:195
  65.4 5.6 %collective-permute-done.10.r2 = bf16[64,4096]{1,0:T(8,128)(2,1)S(1)} collective-permute-done((bf16[64,4096]{1,0:T(8,128)(2,1)}, bf16[64,4096]{1,0:T(8,128)(2,1)S(1)}, u32[]{:S(2)}, u32[]{:S(2)}) %collective-permute-start.10) | collective-permute-done | bytes 524320 | tf_op jit(solution)/shard_map/ppermute | solution.py:195
  71.0 1.2 norm.1
  72.2 1.3 collective-permute-start.14
  73.5 0.8 collective-permute-start.15
  74.3 1.4 collective-permute-start.16
  75.7 3.6 %collective-permute-done.13.refs_0_ = bf16[64,2048]{1,0:T(8,128)(2,1)S(1)} collective-permute-done((bf16[64,2048]{1,0:T(8,128)(2,1)S(1)}, bf16[64,2048]{1,0:T(8,128)(2,1)S(1)}, u32[]{:S(2)}, u32[]{:S(2)}) %collective-permute-start.13) | collective-permute-done | bytes 262176 | tf_op jit(solution)/shard_map/ppermute | solution.py:195
  79.4 1.4 collective-permute-start.17
  80.8 0.7 collective-permute-done.14.refs_1_
  81.5 1.5 collective-permute-start.18
  83.0 4.6 %collective-permute-done.15.refs_2_ = bf16[64,2048]{1,0:T(8,128)(2,1)S(1)} collective-permute-done((bf16[64,2048]{1,0:T(8,128)(2,1)S(1)}, bf16[64,2048]{1,0:T(8,128)(2,1)S(1)}, u32[]{:S(2)}, u32[]{:S(2)}) %collective-permute-start.15) | collective-permute-done | bytes 262176 | tf_op jit(solution)/shard_map/ppermute | solution.py:195
  87.7 0.3 collective-permute-done.16.refs_3_
  87.9 2.8 %collective-permute-done.17.refs_1_ = bf16[64,2048]{1,0:T(8,128)(2,1)S(1)} collective-permute-done((bf16[64,2048]{1,0:T(8,128)(2,1)S(1)}, bf16[64,2048]{1,0:T(8,128)(2,1)S(1)}, u32[]{:S(2)}, u32[]{:S(2)}) %collective-permute-start.17) | collective-permute-done | bytes 262176 | tf_op jit(solution)/shard_map/ppermute | solution.py:195
  90.7 1.1 collective-permute-done.18.refs_0_
  91.9 1.0 collective-permute-start.21
  92.9 8.0 %collective-permute-start.25 = (bf16[768,512]{1,0:T(8,128)(2,1)}, bf16[768,512]{1,0:T(8,128)(2,1)S(1)}, u32[]{:S(2)}, u32[]{:S(2)}) collective-permute-start(bf16[768,512]{1,0:T(8,128)(2,1)} %bitcast.4.refs_4_), channel_id=1, source_target_pairs={{0,24},{4,28},{8,16},{12,20},{16,8},{20,12},{24,0},{28,4},{1,25},{... | collective-permute-start | bytes 2359304 | tf_op jit(solution)/shard_map/ppermute | solution.py:195
  100.9 3.1 %enter.3.own = f32[256,1536]{1,0:T(8,128)S(1)} custom-call(bf16[64,2048]{1,0:T(8,128)(2,1)S(1)} %get-tuple-element.94.refs_0_, bf16[64,2048]{1,0:T(8,128)(2,1)S(1)} %collective-permute-done.14.refs_1_, bf16[64,2048]{1,0:T(8,128)(2,1)S(1)} %collective-permute-done.15.refs_2_, bf16[64,2048]{1,0:T(8,128)(2,1)S(1)} %collective-permute-done.16.refs_3_, ...), custom_call_target="tpu_custom_call" | custom-call | flops 1000 | bytes 1000 | tf_op jit(solution)/shard_map/enter/pallas_call | solution.py:377
  103.9 2.0 %enter.4 = bf16[128,1536]{1,0:T(8,128)(2,1)S(1)} custom-call(bf16[64,2048]{1,0:T(8,128)(2,1)S(1)} %collective-permute-done.13.refs_0_, bf16[64,2048]{1,0:T(8,128)(2,1)S(1)} %collective-permute-done.17.refs_1_, bf16[1024,768]{1,0:T(8,128)(2,1)S(1)} %pad_maximum_fusion.refs_4_.refs_2_, bf16[1024,768]{1,0:T(8,128)(2,1)S(1)} %collective-permute-done.7.refs_5_.refs_3_, ...), custom_call_target="tpu_custom_call" | custom-call | flops 1000 | bytes 1000 | tf_op jit(solution)/shard_map/enter/pallas_call | solution.py:377
  105.9 0.8 collective-permute-start.22
  106.8 2.0 %enter.5 = bf16[128,1536]{1,0:T(8,128)(2,1)S(1)} custom-call(bf16[64,2048]{1,0:T(8,128)(2,1)S(1)} %collective-permute-done.18.refs_0_, bf16[64,2048]{1,0:T(8,128)(2,1)S(1)} %collective-permute-done.21.refs_1_, bf16[1024,768]{1,0:T(8,128)(2,1)S(1)} %pad_maximum_fusion.refs_4_.refs_2_, bf16[1024,768]{1,0:T(8,128)(2,1)S(1)} %collective-permute-done.7.refs_5_.refs_3_, ...), custom_call_target="tpu_custom_call" | custom-call | flops 1000 | bytes 1000 | tf_op jit(solution)/shard_map/enter/pallas_call | solution.py:377
  108.7 1.3 collective-permute-start.23
  110.1 17.6 %collective-permute-done.22.other = bf16[128,1536]{1,0:T(8,128)(2,1)S(1)} collective-permute-done((bf16[128,1536]{1,0:T(8,128)(2,1)S(1)}, bf16[128,1536]{1,0:T(8,128)(2,1)S(1)}, u32[]{:S(2)}, u32[]{:S(2)}) %collective-permute-start.22) | collective-permute-done | bytes 393248 | tf_op jit(solution)/shard_map/ppermute | solution.py:195
  127.6 0.2 silu.2.refs_0_
  127.8 2.4 %collective-permute-start.24 = (bf16[128,768]{1,0:T(8,128)(2,1)S(1)}, bf16[128,768]{1,0:T(8,128)(2,1)S(1)}, u32[]{:S(2)}, u32[]{:S(2)}) collective-permute-start(bf16[128,768]{1,0:T(8,128)(2,1)S(1)} %silu.2.refs_0_), channel_id=1, source_target_pairs={{0,8},{4,12},{8,0},{12,4},{16,24},{20,28},{24,16},{28,20},{1,9},{5... | collective-permute-start | bytes 589832 | tf_op jit(solution)/shard_map/ppermute | solution.py:195
  130.2 5.9 %collective-permute-done.23.other = bf16[128,1536]{1,0:T(8,128)(2,1)S(1)} collective-permute-done((bf16[128,1536]{1,0:T(8,128)(2,1)S(1)}, bf16[128,1536]{1,0:T(8,128)(2,1)S(1)}, u32[]{:S(2)}, u32[]{:S(2)}) %collective-permute-start.23) | collective-permute-done | bytes 393248 | tf_op jit(solution)/shard_map/ppermute | solution.py:195
  136.0 4.1 %collective-permute-done.24.refs_2_ = bf16[128,768]{1,0:T(8,128)(2,1)S(1)} collective-permute-done((bf16[128,768]{1,0:T(8,128)(2,1)S(1)}, bf16[128,768]{1,0:T(8,128)(2,1)S(1)}, u32[]{:S(2)}, u32[]{:S(2)}) %collective-permute-start.24) | collective-permute-done | bytes 196640 | tf_op jit(solution)/shard_map/ppermute | solution.py:195
  140.2 0.2 silu.3.refs_1_
  140.3 1.8 %collective-permute-start.26 = (bf16[128,768]{1,0:T(8,128)(2,1)S(1)}, bf16[128,768]{1,0:T(8,128)(2,1)S(1)}, u32[]{:S(2)}, u32[]{:S(2)}) collective-permute-start(bf16[128,768]{1,0:T(8,128)(2,1)S(1)} %silu.3.refs_1_), channel_id=1, source_target_pairs={{0,8},{4,12},{8,0},{12,4},{16,24},{20,28},{24,16},{28,20},{1,9},{5... | collective-permute-start | bytes 589832 | tf_op jit(solution)/shard_map/ppermute | solution.py:195
  142.1 5.6 %collective-permute-done.26.refs_3_ = bf16[128,768]{1,0:T(8,128)(2,1)S(1)} collective-permute-done((bf16[128,768]{1,0:T(8,128)(2,1)S(1)}, bf16[128,768]{1,0:T(8,128)(2,1)S(1)}, u32[]{:S(2)}, u32[]{:S(2)}) %collective-permute-start.26) | collective-permute-done | bytes 196640 | tf_op jit(solution)/shard_map/ppermute | solution.py:195
  147.7 3.5 %leave.1 = (bf16[64,2048]{1,0:T(8,128)(2,1)S(1)}, bf16[64,2048]{1,0:T(8,128)(2,1)S(1)}, bf16[64,2048]{1,0:T(8,128)(2,1)S(1)}, bf16[64,2048]{1,0:T(8,128)(2,1)S(1...) custom-call(bf16[128,768]{1,0:T(8,128)(2,1)S(1)} %silu.2.refs_0_, ...), custom_call_target="tpu_custom_call" | custom-call | flops 1000 | bytes 1000 | tf_op jit(solution)/shard_map/leave/pallas_call | solution.py:432
  151.2 1.6 collective-permute-start.33
  152.7 0.5 collective-permute-start.32
  153.2 1.5 collective-permute-start.31
  154.7 0.2 slice_reduce_fusion.3
  155.0 0.6 collective-permute-start.28
  155.5 1.5 collective-permute-start.29
  157.1 4.3 %collective-permute-done.33 = bf16[64,2048]{1,0:T(8,128)(2,1)S(1)} collective-permute-done((bf16[64,2048]{1,0:T(8,128)(2,1)S(1)}, bf16[64,2048]{1,0:T(8,128)(2,1)S(1)}, u32[]{:S(2)}, u32[]{:S(2)}) %collective-permute-start.33) | collective-permute-done | bytes 262176 | tf_op jit(solution)/shard_map/ppermute | solution.py:195
  161.4 1.5 collective-permute-start.30
  162.9 2.9 %collective-permute-done.32 = bf16[64,2048]{1,0:T(8,128)(2,1)S(1)} collective-permute-done((bf16[64,2048]{1,0:T(8,128)(2,1)S(1)}, bf16[64,2048]{1,0:T(8,128)(2,1)S(1)}, u32[]{:S(2)}, u32[]{:S(2)}) %collective-permute-start.32) | collective-permute-done | bytes 262176 | tf_op jit(solution)/shard_map/ppermute | solution.py:195
  165.8 0.3 collective-permute-done.31
  166.1 0.3 add_convert_fusion
  166.4 1.8 %collective-permute-start.34 = (bf16[64,2048]{1,0:T(8,128)(2,1)S(1)}, bf16[64,2048]{1,0:T(8,128)(2,1)S(1)}, u32[]{:S(2)}, u32[]{:S(2)}) collective-permute-start(bf16[64,2048]{1,0:T(8,128)(2,1)S(1)} %add_convert_fusion), channel_id=1, source_target_pairs={{0,8},{4,12},{8,0},{12,4},{16,24},{20,28},{24,16},{28,20},{1,9},{5... | collective-permute-start | bytes 786440 | tf_op jit(solution)/shard_map/ppermute | solution.py:195
  168.2 3.5 %collective-permute-done.28.r1 = bf16[64,2048]{1,0:T(8,128)(2,1)S(1)} collective-permute-done((bf16[64,2048]{1,0:T(8,128)(2,1)S(1)}, bf16[64,2048]{1,0:T(8,128)(2,1)S(1)}, u32[]{:S(2)}, u32[]{:S(2)}) %collective-permute-start.28) | collective-permute-done | bytes 262176 | tf_op jit(solution)/shard_map/ppermute | solution.py:195
  171.7 0.8 collective-permute-done.29.r2
  172.6 4.4 %collective-permute-done.30.r3 = bf16[64,2048]{1,0:T(8,128)(2,1)S(1)} collective-permute-done((bf16[64,2048]{1,0:T(8,128)(2,1)S(1)}, bf16[64,2048]{1,0:T(8,128)(2,1)S(1)}, u32[]{:S(2)}, u32[]{:S(2)}) %collective-permute-start.30) | collective-permute-done | bytes 262176 | tf_op jit(solution)/shard_map/ppermute | solution.py:195
  177.0 1.7 final.1
  (33 shorter events, 0.2 us)
Async XLA Ops:
  0.9 19.9 %copy-start.2 = (f32[64,2]{0,1:T(2,128)S(1)}, f32[64,2]{0,1:T(2,128)}, u32[]{:S(2)}) copy-start(f32[64,2]{0,1:T(2,128)} %param.18) | copy-start | bytes 1540
  0.9 28.8 %copy-start.3 = (s32[64,2]{0,1:T(2,128)S(1)}, s32[64,2]{0,1:T(2,128)}, u32[]{:S(2)}) copy-start(s32[64,2]{0,1:T(2,128)} %param.17) | copy-start | bytes 1540
  0.9 7.7 %collective-permute-start.1 = (bf16[256,256]{1,0:T(8,128)(2,1)S(1)}, bf16[256,256]{1,0:T(8,128)(2,1)S(1)}, u32[]{:S(2)}, u32[]{:S(2)}) collective-permute-start(bf16[256,256]{1,0:T(8,128)(2,1)S(1)} %pad_maximum_fusion.1.refs_0_), channel_id=1, source_target_pairs={{0,8},{4,12},{8,16},{12,20},{16,24},{20,28},{1,9},{5,13},{9,17},{1... | collective-permute-start | bytes 393224 | tf_op jit(solution)/shard_map/ppermute | solution.py:500
  8.6 13.7 %collective-permute-start.7 = (bf16[1024,768]{1,0:T(8,128)(2,1)S(1)}, bf16[1024,768]{1,0:T(8,128)(2,1)S(1)}, u32[]{:S(2)}, u32[]{:S(2)}) collective-permute-start(bf16[1024,768]{1,0:T(8,128)(2,1)S(1)} %pad_maximum_fusion.refs_4_.refs_2_), channel_id=1, source_target_pairs={{0,4},{4,0},{8,12},{12,8},{16,20},{20,16},{24,28},{28,24},{1,5},{5... | collective-permute-start | bytes 4718600 | tf_op jit(solution)/shard_map/ppermute | solution.py:195
  8.6 13.7 %collective-permute-start.8 = (bf16[768,512]{1,0:T(8,128)(2,1)}, bf16[768,512]{1,0:T(8,128)(2,1)}, u32[]{:S(2)}, u32[]{:S(2)}) collective-permute-start(bf16[768,512]{1,0:T(8,128)(2,1)} %bitcast.4.refs_4_), channel_id=1, source_target_pairs={{0,4},{4,0},{8,12},{12,8},{16,20},{20,16},{24,28},{28,24},{1,5},{5... | collective-permute-start | bytes 2359304 | tf_op jit(solution)/shard_map/ppermute | solution.py:195
  9.1 8.4 %collective-permute-start = (bf16[256,256]{1,0:T(8,128)(2,1)S(1)}, bf16[256,256]{1,0:T(8,128)(2,1)S(1)}, u32[]{:S(2)}, u32[]{:S(2)}) collective-permute-start(bf16[256,256]{1,0:T(8,128)(2,1)S(1)} %pad_maximum_fusion.1.refs_0_), channel_id=1, source_target_pairs={{0,4},{4,0},{8,12},{12,8},{16,20},{20,16},{24,28},{28,24},{1,5},{5... | collective-permute-start | bytes 393224 | tf_op jit(solution)/shard_map/ppermute | solution.py:195
  9.1 9.2 %collective-permute-start.3 = (bf16[256,256]{1,0:T(8,128)(2,1)S(1)}, bf16[256,256]{1,0:T(8,128)(2,1)}, u32[]{:S(2)}, u32[]{:S(2)}) collective-permute-start(bf16[256,256]{1,0:T(8,128)(2,1)S(1)} %pad_maximum_fusion.1.refs_0_), channel_id=1, source_target_pairs={{0,16},{4,20},{8,24},{12,28},{1,17},{5,21},{9,25},{13,29},{2,18},{... | collective-permute-start | bytes 393224 | tf_op jit(solution)/shard_map/ppermute | solution.py:500
  15.2 5.6 %collective-permute-start.5 = (bf16[256,256]{1,0:T(8,128)(2,1)S(1)}, bf16[256,256]{1,0:T(8,128)(2,1)}, u32[]{:S(2)}, u32[]{:S(2)}) collective-permute-start(bf16[256,256]{1,0:T(8,128)(2,1)S(1)} %pad_maximum_fusion.1.refs_0_), channel_id=1, source_target_pairs={{0,24},{4,28},{1,25},{5,29},{2,26},{6,30},{3,27},{7,31}} | collective-permute-start | bytes 393224 | tf_op jit(solution)/shard_map/ppermute | solution.py:500
  17.5 3.3 %collective-permute-start.2 = (bf16[256,256]{1,0:T(8,128)(2,1)S(1)}, bf16[256,256]{1,0:T(8,128)(2,1)S(1)}, u32[]{:S(2)}, u32[]{:S(2)}) collective-permute-start(bf16[256,256]{1,0:T(8,128)(2,1)S(1)} %collective-permute-done.1.refs_2_), channel_id=1, source_target_pairs={{0,4},{4,0},{8,12},{12,8},{16,20},{20,16},{24,28},{28,24},{1,5},{5... | collective-permute-start | bytes 393224 | tf_op jit(solution)/shard_map/ppermute | solution.py:195
  18.4 2.5 %collective-permute-start.4 = (bf16[256,256]{1,0:T(8,128)(2,1)}, bf16[256,256]{1,0:T(8,128)(2,1)S(1)}, u32[]{:S(2)}, u32[]{:S(2)}) collective-permute-start(bf16[256,256]{1,0:T(8,128)(2,1)} %collective-permute-done.3.refs_4_), channel_id=1, source_target_pairs={{0,4},{4,0},{8,12},{12,8},{16,20},{20,16},{24,28},{28,24},{1,5},{5... | collective-permute-start | bytes 393224 | tf_op jit(solution)/shard_map/ppermute | solution.py:195
  20.8 1.6 collective-permute-start.6
  22.3 69.5 %collective-permute-start.19 = (bf16[1024,768]{1,0:T(8,128)(2,1)S(1)}, bf16[1024,768]{1,0:T(8,128)(2,1)S(1)}, u32[]{:S(2)}, u32[]{:S(2)}) collective-permute-start(bf16[1024,768]{1,0:T(8,128)(2,1)S(1)} %pad_maximum_fusion.refs_4_.refs_2_), channel_id=1, source_target_pairs={{0,24},{4,28},{8,16},{12,20},{16,8},{20,12},{24,0},{28,4},{1,25},{... | collective-permute-start | bytes 4718600 | tf_op jit(solution)/shard_map/ppermute | solution.py:195
  29.9 18.0 %copy-start.1 = (bf16[4096]{0:T(1024)(128)(2,1)S(1)}, bf16[4096]{0:T(1024)(128)(2,1)}, u32[]{:S(2)}) copy-start(bf16[4096]{0:T(1024)(128)(2,1)} %param.16) | copy-start | bytes 24580
  29.9 41.1 %copy-start = (bf16[64,4096]{1,0:T(8,128)(2,1)S(1)}, bf16[64,4096]{1,0:T(8,128)(2,1)}, u32[]{:S(2)}) copy-start(bf16[64,4096]{1,0:T(8,128)(2,1)} %residual.1) | copy-start | bytes 1572868
  44.3 21.0 %collective-permute-start.9 = (bf16[64,4096]{1,0:T(8,128)(2,1)}, bf16[64,4096]{1,0:T(8,128)(2,1)S(1)}, u32[]{:S(2)}, u32[]{:S(2)}) collective-permute-start(bf16[64,4096]{1,0:T(8,128)(2,1)} %get-tuple-element.82), channel_id=1, source_target_pairs={{0,1},{1,0},{2,3},{3,2},{4,5},{5,4},{6,7},{7,6},{8,9},{9,8},{10,11... | collective-permute-start | bytes 1572872 | tf_op jit(solution)/shard_map/ppermute | solution.py:195
  45.9 25.0 %collective-permute-start.10 = (bf16[64,4096]{1,0:T(8,128)(2,1)}, bf16[64,4096]{1,0:T(8,128)(2,1)S(1)}, u32[]{:S(2)}, u32[]{:S(2)}) collective-permute-start(bf16[64,4096]{1,0:T(8,128)(2,1)} %get-tuple-element.83), channel_id=1, source_target_pairs={{0,2},{1,3},{2,0},{3,1},{4,6},{5,7},{6,4},{7,5},{8,10},{9,11},{10,... | collective-permute-start | bytes 1572872 | tf_op jit(solution)/shard_map/ppermute | solution.py:195
  47.4 23.5 %collective-permute-start.11 = (bf16[64,4096]{1,0:T(8,128)(2,1)}, bf16[64,4096]{1,0:T(8,128)(2,1)S(1)}, u32[]{:S(2)}, u32[]{:S(2)}) collective-permute-start(bf16[64,4096]{1,0:T(8,128)(2,1)} %get-tuple-element.84), channel_id=1, source_target_pairs={{0,3},{1,2},{2,1},{3,0},{4,7},{5,6},{6,5},{7,4},{8,11},{9,10},{10,... | collective-permute-start | bytes 1572872 | tf_op jit(solution)/shard_map/ppermute | solution.py:195
  47.9 17.5 %collective-permute-start.12 = (f32[64,128]{1,0:T(8,128)S(1)}, f32[64,128]{1,0:T(8,128)S(1)}, u32[]{:S(2)}, u32[]{:S(2)}) collective-permute-start(f32[64,128]{1,0:T(8,128)S(1)} %select_add_fusion.shares), channel_id=1, source_target_pairs={{0,8},{4,12},{8,0},{12,4},{16,24},{20,28},{24,16},{28,20},{1,9},{5... | collective-permute-start | bytes 98312 | tf_op jit(solution)/shard_map/ppermute | solution.py:195
  72.1 7.3 %collective-permute-start.13 = (bf16[64,2048]{1,0:T(8,128)(2,1)S(1)}, bf16[64,2048]{1,0:T(8,128)(2,1)S(1)}, u32[]{:S(2)}, u32[]{:S(2)}) collective-permute-start(bf16[64,2048]{1,0:T(8,128)(2,1)S(1)} %get-tuple-element.90), channel_id=1, source_target_pairs={{0,8},{4,12},{8,0},{12,4},{16,24},{20,28},{24,16},{28,20},{1,9},{5... | collective-permute-start | bytes 786440 | tf_op jit(solution)/shard_map/ppermute | solution.py:195
  72.2 9.3 %collective-permute-start.14 = (bf16[64,2048]{1,0:T(8,128)(2,1)S(1)}, bf16[64,2048]{1,0:T(8,128)(2,1)S(1)}, u32[]{:S(2)}, u32[]{:S(2)}) collective-permute-start(bf16[64,2048]{1,0:T(8,128)(2,1)S(1)} %get-tuple-element.94.refs_0_), channel_id=1, source_target_pairs={{0,1},{1,0},{2,3},{3,2},{4,5},{5,4},{6,7},{7,6},{8,9},{9,8},{10,11... | collective-permute-start | bytes 786440 | tf_op jit(solution)/shard_map/ppermute | solution.py:195
  73.5 14.2 %collective-permute-start.15 = (bf16[64,2048]{1,0:T(8,128)(2,1)S(1)}, bf16[64,2048]{1,0:T(8,128)(2,1)S(1)}, u32[]{:S(2)}, u32[]{:S(2)}) collective-permute-start(bf16[64,2048]{1,0:T(8,128)(2,1)S(1)} %get-tuple-element.94.refs_0_), channel_id=1, source_target_pairs={{0,2},{1,3},{2,0},{3,1},{4,6},{5,7},{6,4},{7,5},{8,10},{9,11},{10,... | collective-permute-start | bytes 786440 | tf_op jit(solution)/shard_map/ppermute | solution.py:195
  74.3 13.6 %collective-permute-start.16 = (bf16[64,2048]{1,0:T(8,128)(2,1)S(1)}, bf16[64,2048]{1,0:T(8,128)(2,1)S(1)}, u32[]{:S(2)}, u32[]{:S(2)}) collective-permute-start(bf16[64,2048]{1,0:T(8,128)(2,1)S(1)} %get-tuple-element.94.refs_0_), channel_id=1, source_target_pairs={{0,3},{1,2},{2,1},{3,0},{4,7},{5,6},{6,5},{7,4},{8,11},{9,10},{10,... | collective-permute-start | bytes 786440 | tf_op jit(solution)/shard_map/ppermute | solution.py:195
  79.4 11.4 %collective-permute-start.17 = (bf16[64,2048]{1,0:T(8,128)(2,1)S(1)}, bf16[64,2048]{1,0:T(8,128)(2,1)S(1)}, u32[]{:S(2)}, u32[]{:S(2)}) collective-permute-start(bf16[64,2048]{1,0:T(8,128)(2,1)S(1)} %collective-permute-done.13.refs_0_), channel_id=1, source_target_pairs={{0,1},{1,0},{2,3},{3,2},{4,5},{5,4},{6,7},{7,6},{8,9},{9,8},{10,11... | collective-permute-start | bytes 786440 | tf_op jit(solution)/shard_map/ppermute | solution.py:195
  81.5 10.4 %collective-permute-start.18 = (bf16[64,2048]{1,0:T(8,128)(2,1)S(1)}, bf16[64,2048]{1,0:T(8,128)(2,1)S(1)}, u32[]{:S(2)}, u32[]{:S(2)}) collective-permute-start(bf16[64,2048]{1,0:T(8,128)(2,1)S(1)} %collective-permute-done.13.refs_0_), channel_id=1, source_target_pairs={{0,2},{1,3},{2,0},{3,1},{4,6},{5,7},{6,4},{7,5},{8,10},{9,11},{10,... | collective-permute-start | bytes 786440 | tf_op jit(solution)/shard_map/ppermute | solution.py:195
  91.9 9.0 %collective-permute-start.20 = (bf16[1024,768]{1,0:T(8,128)(2,1)S(1)}, bf16[1024,768]{1,0:T(8,128)(2,1)S(1)}, u32[]{:S(2)}, u32[]{:S(2)}) collective-permute-start(bf16[1024,768]{1,0:T(8,128)(2,1)S(1)} %collective-permute-done.19.refs_6_.refs_4_), channel_id=1, source_target_pairs={{0,4},{4,0},{8,12},{12,8},{16,20},{20,16},{24,28},{28,24},{1,5},{5... | collective-permute-start | bytes 4718600 | tf_op jit(solution)/shard_map/ppermute | solution.py:195
  91.9 14.0 %collective-permute-start.21 = (bf16[64,2048]{1,0:T(8,128)(2,1)S(1)}, bf16[64,2048]{1,0:T(8,128)(2,1)S(1)}, u32[]{:S(2)}, u32[]{:S(2)}) collective-permute-start(bf16[64,2048]{1,0:T(8,128)(2,1)S(1)} %collective-permute-done.13.refs_0_), channel_id=1, source_target_pairs={{0,3},{1,2},{2,1},{3,0},{4,7},{5,6},{6,5},{7,4},{8,11},{9,10},{10,... | collective-permute-start | bytes 786440 | tf_op jit(solution)/shard_map/ppermute | solution.py:195
  92.9 37.3 %collective-permute-start.25 = (bf16[768,512]{1,0:T(8,128)(2,1)}, bf16[768,512]{1,0:T(8,128)(2,1)S(1)}, u32[]{:S(2)}, u32[]{:S(2)}) collective-permute-start(bf16[768,512]{1,0:T(8,128)(2,1)} %bitcast.4.refs_4_), channel_id=1, source_target_pairs={{0,24},{4,28},{8,16},{12,20},{16,8},{20,12},{24,0},{28,4},{1,25},{... | collective-permute-start | bytes 2359304 | tf_op jit(solution)/shard_map/ppermute | solution.py:195
  105.9 21.7 %collective-permute-start.22 = (bf16[128,1536]{1,0:T(8,128)(2,1)S(1)}, bf16[128,1536]{1,0:T(8,128)(2,1)S(1)}, u32[]{:S(2)}, u32[]{:S(2)}) collective-permute-start(bf16[128,1536]{1,0:T(8,128)(2,1)S(1)} %enter.4), channel_id=1, source_target_pairs={{0,8},{4,12},{8,0},{12,4},{16,24},{20,28},{24,16},{28,20},{1,9},{5... | collective-permute-start | bytes 1179656 | tf_op jit(solution)/shard_map/ppermute | solution.py:195
  108.7 27.3 %collective-permute-start.23 = (bf16[128,1536]{1,0:T(8,128)(2,1)S(1)}, bf16[128,1536]{1,0:T(8,128)(2,1)S(1)}, u32[]{:S(2)}, u32[]{:S(2)}) collective-permute-start(bf16[128,1536]{1,0:T(8,128)(2,1)S(1)} %enter.5), channel_id=1, source_target_pairs={{0,8},{4,12},{8,0},{12,4},{16,24},{20,28},{24,16},{28,20},{1,9},{5... | collective-permute-start | bytes 1179656 | tf_op jit(solution)/shard_map/ppermute | solution.py:195
  127.8 12.4 %collective-permute-start.24 = (bf16[128,768]{1,0:T(8,128)(2,1)S(1)}, bf16[128,768]{1,0:T(8,128)(2,1)S(1)}, u32[]{:S(2)}, u32[]{:S(2)}) collective-permute-start(bf16[128,768]{1,0:T(8,128)(2,1)S(1)} %silu.2.refs_0_), channel_id=1, source_target_pairs={{0,8},{4,12},{8,0},{12,4},{16,24},{20,28},{24,16},{28,20},{1,9},{5... | collective-permute-start | bytes 589832 | tf_op jit(solution)/shard_map/ppermute | solution.py:195
  140.2 7.5 %collective-permute-start.27 = (bf16[768,512]{1,0:T(8,128)(2,1)S(1)}, bf16[768,512]{1,0:T(8,128)(2,1)S(1)}, u32[]{:S(2)}, u32[]{:S(2)}) collective-permute-start(bf16[768,512]{1,0:T(8,128)(2,1)S(1)} %collective-permute-done.25.refs_6_), channel_id=1, source_target_pairs={{0,4},{4,0},{8,12},{12,8},{16,20},{20,16},{24,28},{28,24},{1,5},{5... | collective-permute-start | bytes 2359304 | tf_op jit(solution)/shard_map/ppermute | solution.py:195
  140.3 7.4 %collective-permute-start.26 = (bf16[128,768]{1,0:T(8,128)(2,1)S(1)}, bf16[128,768]{1,0:T(8,128)(2,1)S(1)}, u32[]{:S(2)}, u32[]{:S(2)}) collective-permute-start(bf16[128,768]{1,0:T(8,128)(2,1)S(1)} %silu.3.refs_1_), channel_id=1, source_target_pairs={{0,8},{4,12},{8,0},{12,4},{16,24},{20,28},{24,16},{28,20},{1,9},{5... | collective-permute-start | bytes 589832 | tf_op jit(solution)/shard_map/ppermute | solution.py:195
  151.2 10.2 %collective-permute-start.33 = (bf16[64,2048]{1,0:T(8,128)(2,1)S(1)}, bf16[64,2048]{1,0:T(8,128)(2,1)S(1)}, u32[]{:S(2)}, u32[]{:S(2)}) collective-permute-start(bf16[64,2048]{1,0:T(8,128)(2,1)S(1)} %get-tuple-element.120), channel_id=1, source_target_pairs={{0,3},{1,2},{2,1},{3,0},{4,7},{5,6},{6,5},{7,4},{8,11},{9,10},{10,... | collective-permute-start | bytes 786440 | tf_op jit(solution)/shard_map/ppermute | solution.py:195
  152.7 13.0 %collective-permute-start.32 = (bf16[64,2048]{1,0:T(8,128)(2,1)S(1)}, bf16[64,2048]{1,0:T(8,128)(2,1)S(1)}, u32[]{:S(2)}, u32[]{:S(2)}) collective-permute-start(bf16[64,2048]{1,0:T(8,128)(2,1)S(1)} %get-tuple-element.119), channel_id=1, source_target_pairs={{0,2},{1,3},{2,0},{3,1},{4,6},{5,7},{6,4},{7,5},{8,10},{9,11},{10,... | collective-permute-start | bytes 786440 | tf_op jit(solution)/shard_map/ppermute | solution.py:195
  153.2 12.9 %collective-permute-start.31 = (bf16[64,2048]{1,0:T(8,128)(2,1)S(1)}, bf16[64,2048]{1,0:T(8,128)(2,1)S(1)}, u32[]{:S(2)}, u32[]{:S(2)}) collective-permute-start(bf16[64,2048]{1,0:T(8,128)(2,1)S(1)} %get-tuple-element.118), channel_id=1, source_target_pairs={{0,1},{1,0},{2,3},{3,2},{4,5},{5,4},{6,7},{7,6},{8,9},{9,8},{10,11... | collective-permute-start | bytes 786440 | tf_op jit(solution)/shard_map/ppermute | solution.py:195
  155.0 16.8 %collective-permute-start.28 = (bf16[64,2048]{1,0:T(8,128)(2,1)S(1)}, bf16[64,2048]{1,0:T(8,128)(2,1)S(1)}, u32[]{:S(2)}, u32[]{:S(2)}) collective-permute-start(bf16[64,2048]{1,0:T(8,128)(2,1)S(1)} %get-tuple-element.113), channel_id=1, source_target_pairs={{0,1},{1,0},{2,3},{3,2},{4,5},{5,4},{6,7},{7,6},{8,9},{9,8},{10,11... | collective-permute-start | bytes 786440 | tf_op jit(solution)/shard_map/ppermute | solution.py:195
  155.5 17.0 %collective-permute-start.29 = (bf16[64,2048]{1,0:T(8,128)(2,1)S(1)}, bf16[64,2048]{1,0:T(8,128)(2,1)S(1)}, u32[]{:S(2)}, u32[]{:S(2)}) collective-permute-start(bf16[64,2048]{1,0:T(8,128)(2,1)S(1)} %get-tuple-element.114), channel_id=1, source_target_pairs={{0,2},{1,3},{2,0},{3,1},{4,6},{5,7},{6,4},{7,5},{8,10},{9,11},{10,... | collective-permute-start | bytes 786440 | tf_op jit(solution)/shard_map/ppermute | solution.py:195
  161.4 15.6 %collective-permute-start.30 = (bf16[64,2048]{1,0:T(8,128)(2,1)S(1)}, bf16[64,2048]{1,0:T(8,128)(2,1)S(1)}, u32[]{:S(2)}, u32[]{:S(2)}) collective-permute-start(bf16[64,2048]{1,0:T(8,128)(2,1)S(1)} %get-tuple-element.115), channel_id=1, source_target_pairs={{0,3},{1,2},{2,1},{3,0},{4,7},{5,6},{6,5},{7,4},{8,11},{9,10},{10,... | collective-permute-start | bytes 786440 | tf_op jit(solution)/shard_map/ppermute | solution.py:195
  166.4 10.6 %collective-permute-start.34 = (bf16[64,2048]{1,0:T(8,128)(2,1)S(1)}, bf16[64,2048]{1,0:T(8,128)(2,1)S(1)}, u32[]{:S(2)}, u32[]{:S(2)}) collective-permute-start(bf16[64,2048]{1,0:T(8,128)(2,1)S(1)} %add_convert_fusion), channel_id=1, source_target_pairs={{0,8},{4,12},{8,0},{12,4},{16,24},{20,28},{24,16},{28,20},{1,9},{5... | collective-permute-start | bytes 786440 | tf_op jit(solution)/shard_map/ppermute | solution.py:195

commit v5 on v4

--- a/solution.py
+++ b/solution.py
@@ -502,12 +502,8 @@
     kv_here, gate_here, up_here = lax.optimization_barrier((kv_here, w_gate[0], w_up[0]))
     moved = [later(kv_here, d) for d in (3, 2, 1)][::-1]
     pair_here, down_here = jnp.concatenate([gate_here, up_here], axis=0), w_down[0]
-    moved[0], pair_here, down_here = lax.optimization_barrier((moved[0], pair_here, down_here))
     pieces = [part for piece in [kv_here] + moved for part in (piece, swap(piece, "ctx", 1))]
-    pair_near, down_near = swap(pair_here, "ctx", 1), swap(down_here, "ctx", 1)
-    pieces, pair_here, pair_near, down_near = lax.optimization_barrier(
-        (pieces, pair_here, pair_near, down_near)
-    )
+    pieces, pair_here = lax.optimization_barrier((pieces, pair_here))
     pair_far = swap(pair_here, "ctx", 6)
 
     lane = lax.broadcasted_iota(jnp.int32, (expert_ids.shape[0], HD), 1)
@@ -517,16 +513,15 @@
         shares = shares + jnp.where(lane == named, gate_weights[:, k : k + 1], 0.0)
 
     p = attention(index, queries, pieces, w_out)
-    p, shares = lax.optimization_barrier((p, shares))
+    p, pair_near = lax.optimization_barrier((p, swap(pair_here, "ctx", 1)))
     r = [swap(p[b], "exp", b) for b in (1, 2, 3)]
-    other_shares = swap(shares, "ctx", 2)
-    r, other_shares = lax.optimization_barrier((r, other_shares))
     state, mine, theirs = norm(index, p[0], *r, residual, norm_gain.reshape(1, D))
     others = swap(theirs, "ctx", 2)
     own_rows = [mine] + [swap(mine, "exp", b) for b in (1, 2, 3)]
+    others, own_rows[1:3] = lax.optimization_barrier((others, own_rows[1:3]))
     other_rows = [others] + [swap(others, "exp", b) for b in (1, 2, 3)]
-    own_rows, other_rows[1:3], pair_far, down_here = lax.optimization_barrier(
-        (own_rows, other_rows[1:3], pair_far, down_here)
+    own_rows, other_rows[1:3], pair_far, down_here, shares = lax.optimization_barrier(
+        (own_rows, other_rows[1:3], pair_far, down_here, shares)
     )
     down_far = swap(down_here, "ctx", 6)
     pairs = (pair_here, pair_near, pair_far, swap(pair_far, "ctx", 1))
@@ -538,7 +533,10 @@
     last_sum = swap(enter(other_rows[2:], pairs, BF16), "ctx", 2)
     first = silu(own_pre, first_sum, 0)
     other_first = swap(first, "ctx", 2)
-    last_sum, other_first, down_far = lax.optimization_barrier((last_sum, other_first, down_far))
+    down_near, other_shares = swap(down_here, "ctx", 1), swap(shares, "ctx", 2)
+    last_sum, other_first, down_far, down_near, other_shares = lax.optimization_barrier(
+        (last_sum, other_first, down_far, down_near, other_shares)
+    )
     last = silu(own_pre, last_sum, 1)
     other_last = swap(last, "ctx", 2)
     downs = (down_here, down_near, down_far, swap(down_far, "ctx", 1))

time: 179 us -> 180 us (level)
  local copies, waits for them, and re-layouts: 1.15 us -> 8.26 us
  starting transfers between devices: 55.9 us -> 51.3 us
  waiting for transfers between devices: 91.5 us -> 88.2 us
    unnamed x8 -> x30, local copies, waits for them, and re-layouts: 0.03 us -> 7.14 us
    ppermute x3, starting transfers between devices: 13.3 us -> 10.7 us  [later(): lax.ppermute(array, 'ctx', [(i, i + 2 * chips) for i in range(8 - 2 * chi...]
    ppermute x32, waiting for transfers between devices: 87.1 us -> 84.8 us  [swap(): return lax.ppermute(array, axis, [(i, i ^ mask) for i in range(size)])]
    pallas_call x3, Pallas kernels: 7 us -> 9.29 us  [enter(): pl.pallas_call(enter_kernel, out_shape=jax.ShapeDtypeStruct((count, 2 * w...]
    ppermute x32, starting transfers between devices: 42.6 us -> 40.6 us  [swap(): return lax.ppermute(array, axis, [(i, i ^ mask) for i in range(size)])]
  transfers between devices with their start and end apart: 35 -> 35, of which waited for: 22 -> 17; matrix products, arithmetic and copies ran while one was open for 1% -> 1% of each run, Pallas kernels for 13% -> 14%
where the time goes in v5:
time: 180 us
  waiting for transfers between devices  88.2 us (49%)
  starting transfers between devices  51.3 us (28%)
  Pallas kernels  29.8 us (17%)
  local copies, waits for them, and re-layouts  8.26 us (5%)
  other arithmetic  2 us (1%)
    ppermute x32, waiting for transfers between devices, swap(): return lax.ppermute(array, axis, [(i, i ^ mask) for i in range(size)])  84.8 us
    ppermute x32, starting transfers between devices, swap(): return lax.ppermute(array, axis, [(i, i ^ mask) for i in range(size)])  40.6 us
    pallas_call x1, Pallas kernels, attention(): pl.pallas_call(attention_kernel, out_shape=[jax.ShapeDtypeStruct((rows, D...  14.7 us
    ppermute x3, starting transfers between devices, later(): lax.ppermute(array, 'ctx', [(i, i + 2 * chips) for i in range(8 - 2 * chi...  10.7 us
    pallas_call x3, Pallas kernels, enter(): pl.pallas_call(enter_kernel, out_shape=jax.ShapeDtypeStruct((count, 2 * w...  9.29 us
    unnamed x30, local copies, waits for them, and re-layouts  7.14 us
  transfers between devices with their start and end apart: 35, of which 17 were waited for; matrix products, arithmetic and copies ran while one was open for 1% of the time, Pallas kernels for 14%

profile of v5, /device:TPU:0, one launch (start us, length us, event | category | flops | bytes accessed | tf_op | source)
XLA Modules:
  0.0 179.8 jit_solution(184771102013615311)
XLA Ops:
  0.0 0.9 constant_dynamic-slice_fusion
  0.9 4.9 %collective-permute-start.1 = (bf16[256,256]{1,0:T(8,128)(2,1)S(1)}, bf16[256,256]{1,0:T(8,128)(2,1)S(1)}, u32[]{:S(2)}, u32[]{:S(2)}) collective-permute-start(bf16[256,256]{1,0:T(8,128)(2,1)S(1)} %pad_maximum_fusion.1.refs_0_), channel_id=1, source_target_pairs={{0,8},{4,12},{8,16},{12,20},{16,24},{20,28},{1,9},{5,13},{9,17},{1... | collective-permute-start | bytes 393224 | tf_op jit(solution)/shard_map/ppermute | solution.py:500
  5.9 4.5 %collective-permute-start.3 = (bf16[256,256]{1,0:T(8,128)(2,1)S(1)}, bf16[256,256]{1,0:T(8,128)(2,1)S(1)}, u32[]{:S(2)}, u32[]{:S(2)}) collective-permute-start(bf16[256,256]{1,0:T(8,128)(2,1)S(1)} %pad_maximum_fusion.1.refs_0_), channel_id=1, source_target_pairs={{0,16},{4,20},{8,24},{12,28},{1,17},{5,21},{9,25},{13,29},{2,18},{... | collective-permute-start | bytes 393224 | tf_op jit(solution)/shard_map/ppermute | solution.py:500
  10.4 1.3 collective-permute-start.5
  11.8 0.5 collective-permute-start.2
  12.2 2.0 %collective-permute-done.3.refs_4_ = bf16[256,256]{1,0:T(8,128)(2,1)S(1)} collective-permute-done((bf16[256,256]{1,0:T(8,128)(2,1)S(1)}, bf16[256,256]{1,0:T(8,128)(2,1)S(1)}, u32[]{:S(2)}, u32[]{:S(2)}) %collective-permute-start.3) | collective-permute-done | bytes 131104 | tf_op jit(solution)/shard_map/ppermute | solution.py:500
  14.3 1.4 collective-permute-done.5.refs_6_
  15.7 1.5 pad_maximum_fusion.refs_4_.refs_2_
  17.2 0.6 copy-done.4
  17.9 0.6 copy-done.6
  18.5 0.6 copy-done.8
  19.2 0.6 copy-done.10
  19.8 0.5 collective-permute-start.7
  20.3 5.8 %collective-permute-start.17 = (bf16[1024,768]{1,0:T(8,128)(2,1)S(1)}, bf16[1024,768]{1,0:T(8,128)(2,1)}, u32[]{:S(2)}, u32[]{:S(2)}) collective-permute-start(bf16[1024,768]{1,0:T(8,128)(2,1)S(1)} %pad_maximum_fusion.refs_4_.refs_2_), channel_id=1, source_target_pairs={{0,24},{4,28},{8,16},{12,20},{16,8},{20,12},{24,0},{28,4},{1,25},{... | collective-permute-start | bytes 4718600 | tf_op jit(solution)/shard_map/ppermute | solution.py:195
  26.2 0.9 copy-done.3
  27.1 0.9 copy-done.5
  28.0 0.9 copy-done.7
  28.9 0.9 copy-done.9
  29.8 0.9 copy-done.11
  30.7 14.7 %attention.1 = (bf16[64,4096]{1,0:T(8,128)(2,1)S(1)}, bf16[64,4096]{1,0:T(8,128)(2,1)}, bf16[64,4096]{1,0:T(8,128)(2,1)}, bf16[64,4096]{1,0:T(8,128)(2,1)}) custom-call(s32[2]{0:T(128)S(1)} %pad_add_fusion.index, bf16[256,2048]{1,0:T(8,128)(2,1)} %q_hbm.1, bf16[256,256]{1,0:T(8,128)(2,1)S(1)} %pad_maximum_fusion.1.refs_0_, bf16[256,256]{1,0:T(8,128)(2,1)S(1)} %copy-done.5, ...), custom_call_target="tpu_custom_call" | custom-call | flops 1000 | bytes 1000 | tf_op jit(solution)/shard_map/attention/pallas_call | solution.py:296
  45.5 1.6 collective-permute-start.8
  47.0 1.5 collective-permute-start.9
  48.6 0.5 collective-permute-start.10
  49.1 11.5 %collective-permute-done.8.r1 = bf16[64,4096]{1,0:T(8,128)(2,1)S(1)} collective-permute-done((bf16[64,4096]{1,0:T(8,128)(2,1)}, bf16[64,4096]{1,0:T(8,128)(2,1)S(1)}, u32[]{:S(2)}, u32[]{:S(2)}) %collective-permute-start.8) | collective-permute-done | bytes 524320 | tf_op jit(solution)/shard_map/ppermute | solution.py:195
  60.5 11.7 %collective-permute-done.9.r2 = bf16[64,4096]{1,0:T(8,128)(2,1)S(1)} collective-permute-done((bf16[64,4096]{1,0:T(8,128)(2,1)}, bf16[64,4096]{1,0:T(8,128)(2,1)S(1)}, u32[]{:S(2)}, u32[]{:S(2)}) %collective-permute-start.9) | collective-permute-done | bytes 524320 | tf_op jit(solution)/shard_map/ppermute | solution.py:195
  72.2 1.2 norm.1
  73.4 1.3 collective-permute-start.12
  74.7 0.8 collective-permute-start.13
  75.6 1.4 collective-permute-start.14
  77.0 3.8 %collective-permute-done.11.refs_0_ = bf16[64,2048]{1,0:T(8,128)(2,1)S(1)} collective-permute-done((bf16[64,2048]{1,0:T(8,128)(2,1)S(1)}, bf16[64,2048]{1,0:T(8,128)(2,1)S(1)}, u32[]{:S(2)}, u32[]{:S(2)}) %collective-permute-start.11) | collective-permute-done | bytes 262176 | tf_op jit(solution)/shard_map/ppermute | solution.py:195
  80.8 2.0 %collective-permute-done.12.refs_1_ = bf16[64,2048]{1,0:T(8,128)(2,1)S(1)} collective-permute-done((bf16[64,2048]{1,0:T(8,128)(2,1)S(1)}, bf16[64,2048]{1,0:T(8,128)(2,1)S(1)}, u32[]{:S(2)}, u32[]{:S(2)}) %collective-permute-start.12) | collective-permute-done | bytes 262176 | tf_op jit(solution)/shard_map/ppermute | solution.py:195
  82.8 4.2 %collective-permute-done.13.refs_2_ = bf16[64,2048]{1,0:T(8,128)(2,1)S(1)} collective-permute-done((bf16[64,2048]{1,0:T(8,128)(2,1)S(1)}, bf16[64,2048]{1,0:T(8,128)(2,1)S(1)}, u32[]{:S(2)}, u32[]{:S(2)}) %collective-permute-start.13) | collective-permute-done | bytes 262176 | tf_op jit(solution)/shard_map/ppermute | solution.py:195
  87.0 1.8 %collective-permute-start.16 = (bf16[64,2048]{1,0:T(8,128)(2,1)S(1)}, bf16[64,2048]{1,0:T(8,128)(2,1)S(1)}, u32[]{:S(2)}, u32[]{:S(2)}) collective-permute-start(bf16[64,2048]{1,0:T(8,128)(2,1)S(1)} %collective-permute-done.11.refs_0_), channel_id=1, source_target_pairs={{0,2},{1,3},{2,0},{3,1},{4,6},{5,7},{6,4},{7,5},{8,10},{9,11},{10,... | collective-permute-start | bytes 786440 | tf_op jit(solution)/shard_map/ppermute | solution.py:195
  89.0 0.4 collective-permute-done.14.refs_3_
  89.4 4.0 %collective-permute-done.15.refs_1_ = bf16[64,2048]{1,0:T(8,128)(2,1)S(1)} collective-permute-done((bf16[64,2048]{1,0:T(8,128)(2,1)S(1)}, bf16[64,2048]{1,0:T(8,128)(2,1)S(1)}, u32[]{:S(2)}, u32[]{:S(2)}) %collective-permute-start.15) | collective-permute-done | bytes 262176 | tf_op jit(solution)/shard_map/ppermute | solution.py:195
  93.4 1.5 collective-permute-start.19
  94.8 7.5 %collective-permute-start.23 = (bf16[768,512]{1,0:T(8,128)(2,1)S(1)}, bf16[768,512]{1,0:T(8,128)(2,1)S(1)}, u32[]{:S(2)}, u32[]{:S(2)}) collective-permute-start(bf16[768,512]{1,0:T(8,128)(2,1)S(1)} %bitcast.13), channel_id=1, source_target_pairs={{0,24},{4,28},{8,16},{12,20},{16,8},{20,12},{24,0},{28,4},{1,25},{... | collective-permute-start | bytes 2359304 | tf_op jit(solution)/shard_map/ppermute | solution.py:195
  102.3 3.8 %enter.3.own = f32[256,1536]{1,0:T(8,128)S(1)} custom-call(bf16[64,2048]{1,0:T(8,128)(2,1)S(1)} %get-tuple-element.88.refs_0_, bf16[64,2048]{1,0:T(8,128)(2,1)S(1)} %collective-permute-done.12.refs_1_, bf16[64,2048]{1,0:T(8,128)(2,1)S(1)} %collective-permute-done.13.refs_2_, bf16[64,2048]{1,0:T(8,128)(2,1)S(1)} %collective-permute-done.14.refs_3_, ...), custom_call_target="tpu_custom_call" | custom-call | flops 1000 | bytes 1000 | tf_op jit(solution)/shard_map/enter/pallas_call | solution.py:377
  106.1 2.8 %enter.4 = bf16[128,1536]{1,0:T(8,128)(2,1)S(1)} custom-call(bf16[64,2048]{1,0:T(8,128)(2,1)S(1)} %collective-permute-done.11.refs_0_, bf16[64,2048]{1,0:T(8,128)(2,1)S(1)} %collective-permute-done.15.refs_1_, bf16[1024,768]{1,0:T(8,128)(2,1)S(1)} %pad_maximum_fusion.refs_4_.refs_2_, bf16[1024,768]{1,0:T(8,128)(2,1)S(1)} %collective-permute-done.7.refs_5_.refs_3_, ...), custom_call_target="tpu_custom_call" | custom-call | flops 1000 | bytes 1000 | tf_op jit(solution)/shard_map/enter/pallas_call | solution.py:377
  108.9 0.8 collective-permute-start.20
  109.6 2.7 %enter.5 = bf16[128,1536]{1,0:T(8,128)(2,1)S(1)} custom-call(bf16[64,2048]{1,0:T(8,128)(2,1)S(1)} %collective-permute-done.16.refs_0_, bf16[64,2048]{1,0:T(8,128)(2,1)S(1)} %collective-permute-done.19.refs_1_, bf16[1024,768]{1,0:T(8,128)(2,1)S(1)} %pad_maximum_fusion.refs_4_.refs_2_, bf16[1024,768]{1,0:T(8,128)(2,1)S(1)} %collective-permute-done.7.refs_5_.refs_3_, ...), custom_call_target="tpu_custom_call" | custom-call | flops 1000 | bytes 1000 | tf_op jit(solution)/shard_map/enter/pallas_call | solution.py:377
  112.4 1.4 collective-permute-start.21
  113.8 15.0 %collective-permute-done.20.other = bf16[128,1536]{1,0:T(8,128)(2,1)S(1)} collective-permute-done((bf16[128,1536]{1,0:T(8,128)(2,1)S(1)}, bf16[128,1536]{1,0:T(8,128)(2,1)S(1)}, u32[]{:S(2)}, u32[]{:S(2)}) %collective-permute-start.20) | collective-permute-done | bytes 393248 | tf_op jit(solution)/shard_map/ppermute | solution.py:195
  128.8 0.2 silu.2.refs_0_
  129.0 2.5 %collective-permute-start.22 = (bf16[128,768]{1,0:T(8,128)(2,1)S(1)}, bf16[128,768]{1,0:T(8,128)(2,1)S(1)}, u32[]{:S(2)}, u32[]{:S(2)}) collective-permute-start(bf16[128,768]{1,0:T(8,128)(2,1)S(1)} %silu.2.refs_0_), channel_id=1, source_target_pairs={{0,8},{4,12},{8,0},{12,4},{16,24},{20,28},{24,16},{28,20},{1,9},{5... | collective-permute-start | bytes 589832 | tf_op jit(solution)/shard_map/ppermute | solution.py:195
  131.5 10.6 %collective-permute-done.25 = f32[64,128]{1,0:T(8,128)S(1)} collective-permute-done((f32[64,128]{1,0:T(8,128)S(1)}, f32[64,128]{1,0:T(8,128)S(1)}, u32[]{:S(2)}, u32[]{:S(2)}) %collective-permute-start.25) | collective-permute-done | bytes 32800 | tf_op jit(solution)/shard_map/ppermute | solution.py:195
  142.4 1.7 collective-permute-start.26
  144.2 5.6 %collective-permute-done.26.refs_3_ = bf16[128,768]{1,0:T(8,128)(2,1)S(1)} collective-permute-done((bf16[128,768]{1,0:T(8,128)(2,1)S(1)}, bf16[128,768]{1,0:T(8,128)(2,1)S(1)}, u32[]{:S(2)}, u32[]{:S(2)}) %collective-permute-start.26) | collective-permute-done | bytes 196640 | tf_op jit(solution)/shard_map/ppermute | solution.py:195
  149.8 2.6 %leave.1 = (bf16[64,2048]{1,0:T(8,128)(2,1)S(1)}, bf16[64,2048]{1,0:T(8,128)(2,1)S(1)}, bf16[64,2048]{1,0:T(8,128)(2,1)S(1)}, bf16[64,2048]{1,0:T(8,128)(2,1)S(1...) custom-call(bf16[128,768]{1,0:T(8,128)(2,1)S(1)} %silu.2.refs_0_, ...), custom_call_target="tpu_custom_call" | custom-call | flops 1000 | bytes 1000 | tf_op jit(solution)/shard_map/leave/pallas_call | solution.py:432
  152.4 1.7 collective-permute-start.33
  154.0 1.6 collective-permute-start.32
  155.6 0.3 collective-permute-start.31
  155.9 0.2 slice_reduce_fusion.3
  156.1 1.8 %collective-permute-start.28 = (bf16[64,2048]{1,0:T(8,128)(2,1)S(1)}, bf16[64,2048]{1,0:T(8,128)(2,1)S(1)}, u32[]{:S(2)}, u32[]{:S(2)}) collective-permute-start(bf16[64,2048]{1,0:T(8,128)(2,1)S(1)} %get-tuple-element.107), channel_id=1, source_target_pairs={{0,1},{1,0},{2,3},{3,2},{4,5},{5,4},{6,7},{7,6},{8,9},{9,8},{10,11... | collective-permute-start | bytes 786440 | tf_op jit(solution)/shard_map/ppermute | solution.py:195
  157.9 0.4 collective-permute-start.29
  158.4 4.2 %collective-permute-done.33 = bf16[64,2048]{1,0:T(8,128)(2,1)S(1)} collective-permute-done((bf16[64,2048]{1,0:T(8,128)(2,1)S(1)}, bf16[64,2048]{1,0:T(8,128)(2,1)S(1)}, u32[]{:S(2)}, u32[]{:S(2)}) %collective-permute-start.33) | collective-permute-done | bytes 262176 | tf_op jit(solution)/shard_map/ppermute | solution.py:195
  162.6 1.6 collective-permute-start.30
  164.2 2.7 %collective-permute-done.32 = bf16[64,2048]{1,0:T(8,128)(2,1)S(1)} collective-permute-done((bf16[64,2048]{1,0:T(8,128)(2,1)S(1)}, bf16[64,2048]{1,0:T(8,128)(2,1)S(1)}, u32[]{:S(2)}, u32[]{:S(2)}) %collective-permute-start.32) | collective-permute-done | bytes 262176 | tf_op jit(solution)/shard_map/ppermute | solution.py:195
  166.9 1.6 collective-permute-done.31
  168.5 0.3 add_convert_fusion
  168.8 1.8 collective-permute-start.34
  170.6 3.5 %collective-permute-done.28.r1 = bf16[64,2048]{1,0:T(8,128)(2,1)S(1)} collective-permute-done((bf16[64,2048]{1,0:T(8,128)(2,1)S(1)}, bf16[64,2048]{1,0:T(8,128)(2,1)S(1)}, u32[]{:S(2)}, u32[]{:S(2)}) %collective-permute-start.28) | collective-permute-done | bytes 262176 | tf_op jit(solution)/shard_map/ppermute | solution.py:195
  174.1 4.0 %collective-permute-done.30.r3 = bf16[64,2048]{1,0:T(8,128)(2,1)S(1)} collective-permute-done((bf16[64,2048]{1,0:T(8,128)(2,1)S(1)}, bf16[64,2048]{1,0:T(8,128)(2,1)S(1)}, u32[]{:S(2)}, u32[]{:S(2)}) %collective-permute-start.30) | collective-permute-done | bytes 262176 | tf_op jit(solution)/shard_map/ppermute | solution.py:195
  178.1 1.7 final.1
  (55 shorter events, 0.8 us)
Async XLA Ops:
  0.9 10.8 %collective-permute-start.1 = (bf16[256,256]{1,0:T(8,128)(2,1)S(1)}, bf16[256,256]{1,0:T(8,128)(2,1)S(1)}, u32[]{:S(2)}, u32[]{:S(2)}) collective-permute-start(bf16[256,256]{1,0:T(8,128)(2,1)S(1)} %pad_maximum_fusion.1.refs_0_), channel_id=1, source_target_pairs={{0,8},{4,12},{8,16},{12,20},{16,24},{20,28},{1,9},{5,13},{9,17},{1... | collective-permute-start | bytes 393224 | tf_op jit(solution)/shard_map/ppermute | solution.py:500
  5.9 8.4 %collective-permute-start.3 = (bf16[256,256]{1,0:T(8,128)(2,1)S(1)}, bf16[256,256]{1,0:T(8,128)(2,1)S(1)}, u32[]{:S(2)}, u32[]{:S(2)}) collective-permute-start(bf16[256,256]{1,0:T(8,128)(2,1)S(1)} %pad_maximum_fusion.1.refs_0_), channel_id=1, source_target_pairs={{0,16},{4,20},{8,24},{12,28},{1,17},{5,21},{9,25},{13,29},{2,18},{... | collective-permute-start | bytes 393224 | tf_op jit(solution)/shard_map/ppermute | solution.py:500
  10.4 5.3 %collective-permute-start.5 = (bf16[256,256]{1,0:T(8,128)(2,1)S(1)}, bf16[256,256]{1,0:T(8,128)(2,1)S(1)}, u32[]{:S(2)}, u32[]{:S(2)}) collective-permute-start(bf16[256,256]{1,0:T(8,128)(2,1)S(1)} %pad_maximum_fusion.1.refs_0_), channel_id=1, source_target_pairs={{0,24},{4,28},{1,25},{5,29},{2,26},{6,30},{3,27},{7,31}} | collective-permute-start | bytes 393224 | tf_op jit(solution)/shard_map/ppermute | solution.py:500
  11.7 5.5 %collective-permute-start = (bf16[256,256]{1,0:T(8,128)(2,1)S(1)}, bf16[256,256]{1,0:T(8,128)(2,1)S(1)}, u32[]{:S(2)}, u32[]{:S(2)}) collective-permute-start(bf16[256,256]{1,0:T(8,128)(2,1)S(1)} %pad_maximum_fusion.1.refs_0_), channel_id=1, source_target_pairs={{0,4},{4,0},{8,12},{12,8},{16,20},{20,16},{24,28},{28,24},{1,5},{5... | collective-permute-start | bytes 393224 | tf_op jit(solution)/shard_map/ppermute | solution.py:195
  11.8 6.1 %collective-permute-start.2 = (bf16[256,256]{1,0:T(8,128)(2,1)S(1)}, bf16[256,256]{1,0:T(8,128)(2,1)S(1)}, u32[]{:S(2)}, u32[]{:S(2)}) collective-permute-start(bf16[256,256]{1,0:T(8,128)(2,1)S(1)} %collective-permute-done.1.refs_2_), channel_id=1, source_target_pairs={{0,4},{4,0},{8,12},{12,8},{16,20},{20,16},{24,28},{28,24},{1,5},{5... | collective-permute-start | bytes 393224 | tf_op jit(solution)/shard_map/ppermute | solution.py:195
  14.3 4.2 %collective-permute-start.4 = (bf16[256,256]{1,0:T(8,128)(2,1)S(1)}, bf16[256,256]{1,0:T(8,128)(2,1)S(1)}, u32[]{:S(2)}, u32[]{:S(2)}) collective-permute-start(bf16[256,256]{1,0:T(8,128)(2,1)S(1)} %collective-permute-done.3.refs_4_), channel_id=1, source_target_pairs={{0,4},{4,0},{8,12},{12,8},{16,20},{20,16},{24,28},{28,24},{1,5},{5... | collective-permute-start | bytes 393224 | tf_op jit(solution)/shard_map/ppermute | solution.py:195
  15.7 1.5 copy-start.2
  15.7 3.5 %collective-permute-start.6 = (bf16[256,256]{1,0:T(8,128)(2,1)S(1)}, bf16[256,256]{1,0:T(8,128)(2,1)S(1)}, u32[]{:S(2)}, u32[]{:S(2)}) collective-permute-start(bf16[256,256]{1,0:T(8,128)(2,1)S(1)} %collective-permute-done.5.refs_6_), channel_id=1, source_target_pairs={{0,4},{4,0},{8,12},{12,8},{16,20},{20,16},{24,28},{28,24},{1,5},{5... | collective-permute-start | bytes 393224 | tf_op jit(solution)/shard_map/ppermute | solution.py:195
  17.2 0.7 copy-start.4
  17.9 0.6 copy-start.6
  18.5 0.6 copy-start.8
  19.2 0.7 copy-start.10
  19.8 25.7 %collective-permute-start.7 = (bf16[1024,768]{1,0:T(8,128)(2,1)S(1)}, bf16[1024,768]{1,0:T(8,128)(2,1)S(1)}, u32[]{:S(2)}, u32[]{:S(2)}) collective-permute-start(bf16[1024,768]{1,0:T(8,128)(2,1)S(1)} %pad_maximum_fusion.refs_4_.refs_2_), channel_id=1, source_target_pairs={{0,4},{4,0},{8,12},{12,8},{16,20},{20,16},{24,28},{28,24},{1,5},{5... | collective-permute-start | bytes 4718600 | tf_op jit(solution)/shard_map/ppermute | solution.py:195
  20.3 68.7 %collective-permute-start.17 = (bf16[1024,768]{1,0:T(8,128)(2,1)S(1)}, bf16[1024,768]{1,0:T(8,128)(2,1)}, u32[]{:S(2)}, u32[]{:S(2)}) collective-permute-start(bf16[1024,768]{1,0:T(8,128)(2,1)S(1)} %pad_maximum_fusion.refs_4_.refs_2_), channel_id=1, source_target_pairs={{0,24},{4,28},{8,16},{12,20},{16,8},{20,12},{24,0},{28,4},{1,25},{... | collective-permute-start | bytes 4718600 | tf_op jit(solution)/shard_map/ppermute | solution.py:195
  26.2 0.9 copy-start.3
  27.1 0.9 copy-start.5
  28.0 0.9 copy-start.7
  28.9 0.9 copy-start.9
  29.8 0.9 copy-start.11
  30.7 18.3 %copy-start.12 = (bf16[4096]{0:T(1024)(128)(2,1)S(1)}, bf16[4096]{0:T(1024)(128)(2,1)}, u32[]{:S(2)}) copy-start(bf16[4096]{0:T(1024)(128)(2,1)} %param.16) | copy-start | bytes 24580
  30.7 41.5 %copy-start.1 = (bf16[64,4096]{1,0:T(8,128)(2,1)S(1)}, bf16[64,4096]{1,0:T(8,128)(2,1)}, u32[]{:S(2)}) copy-start(bf16[64,4096]{1,0:T(8,128)(2,1)} %residual.1) | copy-start | bytes 1572868
  45.4 30.1 %copy-start.13 = (f32[64,2]{0,1:T(2,128)S(1)}, f32[64,2]{0,1:T(2,128)}, u32[]{:S(2)}) copy-start(f32[64,2]{0,1:T(2,128)} %param.18) | copy-start | bytes 1540
  45.4 43.4 %copy-start.14 = (s32[64,2]{0,1:T(2,128)S(1)}, s32[64,2]{0,1:T(2,128)}, u32[]{:S(2)}) copy-start(s32[64,2]{0,1:T(2,128)} %param.17) | copy-start | bytes 1540
  45.5 49.4 %copy-start = (bf16[1,768,512]{2,1,0:T(8,128)(2,1)S(1)}, bf16[1,768,512]{2,1,0:T(8,128)(2,1)}, u32[]{:S(2)}) copy-start(bf16[1,768,512]{2,1,0:T(8,128)(2,1)} %param.21) | copy-start | bytes 2359300
  45.5 15.0 %collective-permute-start.8 = (bf16[64,4096]{1,0:T(8,128)(2,1)}, bf16[64,4096]{1,0:T(8,128)(2,1)S(1)}, u32[]{:S(2)}, u32[]{:S(2)}) collective-permute-start(bf16[64,4096]{1,0:T(8,128)(2,1)} %get-tuple-element.77), channel_id=1, source_target_pairs={{0,1},{1,0},{2,3},{3,2},{4,5},{5,4},{6,7},{7,6},{8,9},{9,8},{10,11... | collective-permute-start | bytes 1572872 | tf_op jit(solution)/shard_map/ppermute | solution.py:195
  47.0 25.2 %collective-permute-start.9 = (bf16[64,4096]{1,0:T(8,128)(2,1)}, bf16[64,4096]{1,0:T(8,128)(2,1)S(1)}, u32[]{:S(2)}, u32[]{:S(2)}) collective-permute-start(bf16[64,4096]{1,0:T(8,128)(2,1)} %get-tuple-element.78), channel_id=1, source_target_pairs={{0,2},{1,3},{2,0},{3,1},{4,6},{5,7},{6,4},{7,5},{8,10},{9,11},{10,... | collective-permute-start | bytes 1572872 | tf_op jit(solution)/shard_map/ppermute | solution.py:195
  48.6 23.6 %collective-permute-start.10 = (bf16[64,4096]{1,0:T(8,128)(2,1)}, bf16[64,4096]{1,0:T(8,128)(2,1)S(1)}, u32[]{:S(2)}, u32[]{:S(2)}) collective-permute-start(bf16[64,4096]{1,0:T(8,128)(2,1)} %get-tuple-element.79), channel_id=1, source_target_pairs={{0,3},{1,2},{2,1},{3,0},{4,7},{5,6},{6,5},{7,4},{8,11},{9,10},{10,... | collective-permute-start | bytes 1572872 | tf_op jit(solution)/shard_map/ppermute | solution.py:195
  73.4 7.4 %collective-permute-start.11 = (bf16[64,2048]{1,0:T(8,128)(2,1)S(1)}, bf16[64,2048]{1,0:T(8,128)(2,1)S(1)}, u32[]{:S(2)}, u32[]{:S(2)}) collective-permute-start(bf16[64,2048]{1,0:T(8,128)(2,1)S(1)} %get-tuple-element.82), channel_id=1, source_target_pairs={{0,8},{4,12},{8,0},{12,4},{16,24},{20,28},{24,16},{28,20},{1,9},{5... | collective-permute-start | bytes 786440 | tf_op jit(solution)/shard_map/ppermute | solution.py:195
  73.4 9.3 %collective-permute-start.12 = (bf16[64,2048]{1,0:T(8,128)(2,1)S(1)}, bf16[64,2048]{1,0:T(8,128)(2,1)S(1)}, u32[]{:S(2)}, u32[]{:S(2)}) collective-permute-start(bf16[64,2048]{1,0:T(8,128)(2,1)S(1)} %get-tuple-element.88.refs_0_), channel_id=1, source_target_pairs={{0,1},{1,0},{2,3},{3,2},{4,5},{5,4},{6,7},{7,6},{8,9},{9,8},{10,11... | collective-permute-start | bytes 786440 | tf_op jit(solution)/shard_map/ppermute | solution.py:195
  74.7 12.3 %collective-permute-start.13 = (bf16[64,2048]{1,0:T(8,128)(2,1)S(1)}, bf16[64,2048]{1,0:T(8,128)(2,1)S(1)}, u32[]{:S(2)}, u32[]{:S(2)}) collective-permute-start(bf16[64,2048]{1,0:T(8,128)(2,1)S(1)} %get-tuple-element.88.refs_0_), channel_id=1, source_target_pairs={{0,2},{1,3},{2,0},{3,1},{4,6},{5,7},{6,4},{7,5},{8,10},{9,11},{10,... | collective-permute-start | bytes 786440 | tf_op jit(solution)/shard_map/ppermute | solution.py:195
  75.6 13.8 %collective-permute-start.14 = (bf16[64,2048]{1,0:T(8,128)(2,1)S(1)}, bf16[64,2048]{1,0:T(8,128)(2,1)S(1)}, u32[]{:S(2)}, u32[]{:S(2)}) collective-permute-start(bf16[64,2048]{1,0:T(8,128)(2,1)S(1)} %get-tuple-element.88.refs_0_), channel_id=1, source_target_pairs={{0,3},{1,2},{2,1},{3,0},{4,7},{5,6},{6,5},{7,4},{8,11},{9,10},{10,... | collective-permute-start | bytes 786440 | tf_op jit(solution)/shard_map/ppermute | solution.py:195
  87.0 6.4 %collective-permute-start.15 = (bf16[64,2048]{1,0:T(8,128)(2,1)S(1)}, bf16[64,2048]{1,0:T(8,128)(2,1)S(1)}, u32[]{:S(2)}, u32[]{:S(2)}) collective-permute-start(bf16[64,2048]{1,0:T(8,128)(2,1)S(1)} %collective-permute-done.11.refs_0_), channel_id=1, source_target_pairs={{0,1},{1,0},{2,3},{3,2},{4,5},{5,4},{6,7},{7,6},{8,9},{9,8},{10,11... | collective-permute-start | bytes 786440 | tf_op jit(solution)/shard_map/ppermute | solution.py:195
  87.0 6.4 %collective-permute-start.16 = (bf16[64,2048]{1,0:T(8,128)(2,1)S(1)}, bf16[64,2048]{1,0:T(8,128)(2,1)S(1)}, u32[]{:S(2)}, u32[]{:S(2)}) collective-permute-start(bf16[64,2048]{1,0:T(8,128)(2,1)S(1)} %collective-permute-done.11.refs_0_), channel_id=1, source_target_pairs={{0,2},{1,3},{2,0},{3,1},{4,6},{5,7},{6,4},{7,5},{8,10},{9,11},{10,... | collective-permute-start | bytes 786440 | tf_op jit(solution)/shard_map/ppermute | solution.py:195
  93.4 9.0 %collective-permute-start.18 = (bf16[1024,768]{1,0:T(8,128)(2,1)}, bf16[1024,768]{1,0:T(8,128)(2,1)S(1)}, u32[]{:S(2)}, u32[]{:S(2)}) collective-permute-start(bf16[1024,768]{1,0:T(8,128)(2,1)} %collective-permute-done.17.refs_6_.refs_4_), channel_id=1, source_target_pairs={{0,4},{4,0},{8,12},{12,8},{16,20},{20,16},{24,28},{28,24},{1,5},{5... | collective-permute-start | bytes 4718600 | tf_op jit(solution)/shard_map/ppermute | solution.py:195
  93.4 15.5 %collective-permute-start.19 = (bf16[64,2048]{1,0:T(8,128)(2,1)S(1)}, bf16[64,2048]{1,0:T(8,128)(2,1)S(1)}, u32[]{:S(2)}, u32[]{:S(2)}) collective-permute-start(bf16[64,2048]{1,0:T(8,128)(2,1)S(1)} %collective-permute-done.11.refs_0_), channel_id=1, source_target_pairs={{0,3},{1,2},{2,1},{3,0},{4,7},{5,6},{6,5},{7,4},{8,11},{9,10},{10,... | collective-permute-start | bytes 786440 | tf_op jit(solution)/shard_map/ppermute | solution.py:195
  94.8 47.3 %collective-permute-start.23 = (bf16[768,512]{1,0:T(8,128)(2,1)S(1)}, bf16[768,512]{1,0:T(8,128)(2,1)S(1)}, u32[]{:S(2)}, u32[]{:S(2)}) collective-permute-start(bf16[768,512]{1,0:T(8,128)(2,1)S(1)} %bitcast.13), channel_id=1, source_target_pairs={{0,24},{4,28},{8,16},{12,20},{16,8},{20,12},{24,0},{28,4},{1,25},{... | collective-permute-start | bytes 2359304 | tf_op jit(solution)/shard_map/ppermute | solution.py:195
  102.3 39.8 %collective-permute-start.24 = (bf16[768,512]{1,0:T(8,128)(2,1)S(1)}, bf16[768,512]{1,0:T(8,128)(2,1)S(1)}, u32[]{:S(2)}, u32[]{:S(2)}) collective-permute-start(bf16[768,512]{1,0:T(8,128)(2,1)S(1)} %bitcast.14), channel_id=1, source_target_pairs={{0,4},{4,0},{8,12},{12,8},{16,20},{20,16},{24,28},{28,24},{1,5},{5... | collective-permute-start | bytes 2359304 | tf_op jit(solution)/shard_map/ppermute | solution.py:195
  108.9 19.9 %collective-permute-start.20 = (bf16[128,1536]{1,0:T(8,128)(2,1)S(1)}, bf16[128,1536]{1,0:T(8,128)(2,1)S(1)}, u32[]{:S(2)}, u32[]{:S(2)}) collective-permute-start(bf16[128,1536]{1,0:T(8,128)(2,1)S(1)} %enter.4), channel_id=1, source_target_pairs={{0,8},{4,12},{8,0},{12,4},{16,24},{20,28},{24,16},{28,20},{1,9},{5... | collective-permute-start | bytes 1179656 | tf_op jit(solution)/shard_map/ppermute | solution.py:195
  112.4 29.7 %collective-permute-start.21 = (bf16[128,1536]{1,0:T(8,128)(2,1)S(1)}, bf16[128,1536]{1,0:T(8,128)(2,1)S(1)}, u32[]{:S(2)}, u32[]{:S(2)}) collective-permute-start(bf16[128,1536]{1,0:T(8,128)(2,1)S(1)} %enter.5), channel_id=1, source_target_pairs={{0,8},{4,12},{8,0},{12,4},{16,24},{20,28},{24,16},{28,20},{1,9},{5... | collective-permute-start | bytes 1179656 | tf_op jit(solution)/shard_map/ppermute | solution.py:195
  129.0 13.2 %collective-permute-start.22 = (bf16[128,768]{1,0:T(8,128)(2,1)S(1)}, bf16[128,768]{1,0:T(8,128)(2,1)S(1)}, u32[]{:S(2)}, u32[]{:S(2)}) collective-permute-start(bf16[128,768]{1,0:T(8,128)(2,1)S(1)} %silu.2.refs_0_), channel_id=1, source_target_pairs={{0,8},{4,12},{8,0},{12,4},{16,24},{20,28},{24,16},{28,20},{1,9},{5... | collective-permute-start | bytes 589832 | tf_op jit(solution)/shard_map/ppermute | solution.py:195
  131.4 10.7 %collective-permute-start.25 = (f32[64,128]{1,0:T(8,128)S(1)}, f32[64,128]{1,0:T(8,128)S(1)}, u32[]{:S(2)}, u32[]{:S(2)}) collective-permute-start(f32[64,128]{1,0:T(8,128)S(1)} %select_add_fusion.shares), channel_id=1, source_target_pairs={{0,8},{4,12},{8,0},{12,4},{16,24},{20,28},{24,16},{28,20},{1,9},{5... | collective-permute-start | bytes 98312 | tf_op jit(solution)/shard_map/ppermute | solution.py:195
  142.1 7.6 %collective-permute-start.27 = (bf16[768,512]{1,0:T(8,128)(2,1)S(1)}, bf16[768,512]{1,0:T(8,128)(2,1)S(1)}, u32[]{:S(2)}, u32[]{:S(2)}) collective-permute-start(bf16[768,512]{1,0:T(8,128)(2,1)S(1)} %collective-permute-done.23.refs_6_), channel_id=1, source_target_pairs={{0,4},{4,0},{8,12},{12,8},{16,20},{20,16},{24,28},{28,24},{1,5},{5... | collective-permute-start | bytes 2359304 | tf_op jit(solution)/shard_map/ppermute | solution.py:195
  142.4 7.3 %collective-permute-start.26 = (bf16[128,768]{1,0:T(8,128)(2,1)S(1)}, bf16[128,768]{1,0:T(8,128)(2,1)S(1)}, u32[]{:S(2)}, u32[]{:S(2)}) collective-permute-start(bf16[128,768]{1,0:T(8,128)(2,1)S(1)} %silu.3.refs_1_), channel_id=1, source_target_pairs={{0,8},{4,12},{8,0},{12,4},{16,24},{20,28},{24,16},{28,20},{1,9},{5... | collective-permute-start | bytes 589832 | tf_op jit(solution)/shard_map/ppermute | solution.py:195
  152.4 10.2 %collective-permute-start.33 = (bf16[64,2048]{1,0:T(8,128)(2,1)S(1)}, bf16[64,2048]{1,0:T(8,128)(2,1)S(1)}, u32[]{:S(2)}, u32[]{:S(2)}) collective-permute-start(bf16[64,2048]{1,0:T(8,128)(2,1)S(1)} %get-tuple-element.114), channel_id=1, source_target_pairs={{0,3},{1,2},{2,1},{3,0},{4,7},{5,6},{6,5},{7,4},{8,11},{9,10},{10,... | collective-permute-start | bytes 786440 | tf_op jit(solution)/shard_map/ppermute | solution.py:195
  154.0 12.9 %collective-permute-start.32 = (bf16[64,2048]{1,0:T(8,128)(2,1)S(1)}, bf16[64,2048]{1,0:T(8,128)(2,1)S(1)}, u32[]{:S(2)}, u32[]{:S(2)}) collective-permute-start(bf16[64,2048]{1,0:T(8,128)(2,1)S(1)} %get-tuple-element.113), channel_id=1, source_target_pairs={{0,2},{1,3},{2,0},{3,1},{4,6},{5,7},{6,4},{7,5},{8,10},{9,11},{10,... | collective-permute-start | bytes 786440 | tf_op jit(solution)/shard_map/ppermute | solution.py:195
  155.6 12.8 %collective-permute-start.31 = (bf16[64,2048]{1,0:T(8,128)(2,1)S(1)}, bf16[64,2048]{1,0:T(8,128)(2,1)S(1)}, u32[]{:S(2)}, u32[]{:S(2)}) collective-permute-start(bf16[64,2048]{1,0:T(8,128)(2,1)S(1)} %get-tuple-element.112), channel_id=1, source_target_pairs={{0,1},{1,0},{2,3},{3,2},{4,5},{5,4},{6,7},{7,6},{8,9},{9,8},{10,11... | collective-permute-start | bytes 786440 | tf_op jit(solution)/shard_map/ppermute | solution.py:195
  156.1 18.0 %collective-permute-start.28 = (bf16[64,2048]{1,0:T(8,128)(2,1)S(1)}, bf16[64,2048]{1,0:T(8,128)(2,1)S(1)}, u32[]{:S(2)}, u32[]{:S(2)}) collective-permute-start(bf16[64,2048]{1,0:T(8,128)(2,1)S(1)} %get-tuple-element.107), channel_id=1, source_target_pairs={{0,1},{1,0},{2,3},{3,2},{4,5},{5,4},{6,7},{7,6},{8,9},{9,8},{10,11... | collective-permute-start | bytes 786440 | tf_op jit(solution)/shard_map/ppermute | solution.py:195
  157.9 16.1 %collective-permute-start.29 = (bf16[64,2048]{1,0:T(8,128)(2,1)S(1)}, bf16[64,2048]{1,0:T(8,128)(2,1)S(1)}, u32[]{:S(2)}, u32[]{:S(2)}) collective-permute-start(bf16[64,2048]{1,0:T(8,128)(2,1)S(1)} %get-tuple-element.108), channel_id=1, source_target_pairs={{0,2},{1,3},{2,0},{3,1},{4,6},{5,7},{6,4},{7,5},{8,10},{9,11},{10,... | collective-permute-start | bytes 786440 | tf_op jit(solution)/shard_map/ppermute | solution.py:195
  162.6 15.5 %collective-permute-start.30 = (bf16[64,2048]{1,0:T(8,128)(2,1)S(1)}, bf16[64,2048]{1,0:T(8,128)(2,1)S(1)}, u32[]{:S(2)}, u32[]{:S(2)}) collective-permute-start(bf16[64,2048]{1,0:T(8,128)(2,1)S(1)} %get-tuple-element.109), channel_id=1, source_target_pairs={{0,3},{1,2},{2,1},{3,0},{4,7},{5,6},{6,5},{7,4},{8,11},{9,10},{10,... | collective-permute-start | bytes 786440 | tf_op jit(solution)/shard_map/ppermute | solution.py:195
  168.8 9.3 %collective-permute-start.34 = (bf16[64,2048]{1,0:T(8,128)(2,1)S(1)}, bf16[64,2048]{1,0:T(8,128)(2,1)S(1)}, u32[]{:S(2)}, u32[]{:S(2)}) collective-permute-start(bf16[64,2048]{1,0:T(8,128)(2,1)S(1)} %add_convert_fusion), channel_id=1, source_target_pairs={{0,8},{4,12},{8,0},{12,4},{16,24},{20,28},{24,16},{28,20},{1,9},{5... | collective-permute-start | bytes 786440 | tf_op jit(solution)/shard_map/ppermute | solution.py:195

commit v6 on v3

--- a/solution.py
+++ b/solution.py
@@ -223,8 +223,6 @@
         )
         for i in range(steps)
     ]
-    for fetch in fetches:
-        fetch.start()
     factor = math.log2(math.e) / math.sqrt(HD)
     heads = q.shape[1] // HD
     ones_values[:, HD:] = jnp.ones((ones_values.shape[0], HD), BF16)
@@ -246,6 +244,8 @@
                 ones_values[here, :HD] = piece[:, HD:]
 
     q_fetch.wait()
+    for fetch in fetches:
+        fetch.start()
     part = QB // 4
 
     def run(length):
@@ -297,7 +297,7 @@
         attention_kernel,
         out_shape=[jax.ShapeDtypeStruct((rows, D), BF16)] * 4,
         in_specs=[pl.BlockSpec(memory_space=pltpu.SMEM)]
-        + [pl.BlockSpec(memory_space=pl.ANY)] * 10,
+        + [pl.BlockSpec(memory_space=pltpu.HBM)] * 10,
         out_specs=vmem_specs(4),
         scratch_shapes=[
             VMEM(w_out.shape, BF16),
@@ -442,21 +442,6 @@
     for b in range(1, 4):
         total = total + shares[:, b : b + 1] * parts[b][...].astype(F32)
     return total
-
-
-def total_kernel(shares, y0, r1, r2, r3, out):
-    out[...] = mixed(shares, (y0, r1, r2, r3)).astype(BF16)
-
-
-def total_of(shares, y0, r1, r2, r3):
-    return pl.pallas_call(
-        total_kernel,
-        out_shape=jax.ShapeDtypeStruct(y0.shape, BF16),
-        in_specs=vmem_specs(5),
-        out_specs=pl.BlockSpec(memory_space=VMEM),
-        cost_estimate=CHEAP,
-        name="total",
-    )(shares, y0, r1, r2, r3)
 
 
 def final_kernel(index, state, shares, y0, r1, r2, r3, other, out):
@@ -531,9 +516,10 @@
     state, mine, theirs = norm(index, p[0], *r, residual, norm_gain.reshape(1, D))
     others = swap(theirs, "ctx", 2)
     own_rows = [mine] + [swap(mine, "exp", b) for b in (1, 2, 3)]
+    others, own_rows[1:3] = lax.optimization_barrier((others, own_rows[1:3]))
     other_rows = [others] + [swap(others, "exp", b) for b in (1, 2, 3)]
-    own_rows, others, pair_far, down_here = lax.optimization_barrier(
-        (own_rows, others, pair_far, down_here)
+    own_rows, other_rows, pair_far, down_here = lax.optimization_barrier(
+        (own_rows, other_rows, pair_far, down_here)
     )
     down_far = swap(down_here, "ctx", 6)
     pairs = (pair_here, pair_near, pair_far, swap(pair_far, "ctx", 1))
@@ -549,7 +535,7 @@
     other_hidden, *own_parts[1:3] = lax.optimization_barrier((other_hidden, *own_parts[1:3]))
     z = leave(other_hidden, downs)
     other_parts = [z[0]] + [swap(z[b], "exp", b) for b in (1, 2, 3)]
-    back = swap(total_of(other_shares, *other_parts), "ctx", 2)
+    back = swap(mixed(other_shares, other_parts).astype(BF16), "ctx", 2)
     return final(index, state, shares, *own_parts, back)
 
 

time: 175 us -> 178 us (1.017)
  waiting for transfers between devices: 91.1 us -> 97.5 us
  Pallas kernels: 33.1 us -> 27.5 us
  starting transfers between devices: 46.3 us -> 49.1 us
    ppermute x30, waiting for transfers between devices: 87.7 us -> 94.9 us  [swap(): return lax.ppermute(array, axis, [(i, i ^ mask) for i in range(size)])]
    pallas_call x1, Pallas kernels: 18.2 us -> 14.7 us  [attention(): pl.pallas_call(attention_kernel, out_shape=[jax.ShapeDtypeStruct((rows, D...]
    ppermute x30, starting transfers between devices: 35.6 us -> 38.3 us  [swap(): return lax.ppermute(array, axis, [(i, i ^ mask) for i in range(size)])]
    pallas_call x1 -> x0, Pallas kernels: 2.17 us -> none  [total_of(): pl.pallas_call(total_kernel, out_shape=jax.ShapeDtypeStruct(y0.shape, BF1...]
  transfers between devices with their start and end apart: 33 -> 33, of which waited for: 15 -> 17; matrix products, arithmetic and copies ran while one was open for 1% -> 2% of each run, Pallas kernels for 17% -> 13%
where the time goes in v6:
time: 178 us
  waiting for transfers between devices  97.5 us (55%)
  starting transfers between devices  49.1 us (28%)
  Pallas kernels  27.5 us (15%)
  other arithmetic  2.71 us (2%)
    ppermute x30, waiting for transfers between devices, swap(): return lax.ppermute(array, axis, [(i, i ^ mask) for i in range(size)])  94.9 us
    ppermute x30, starting transfers between devices, swap(): return lax.ppermute(array, axis, [(i, i ^ mask) for i in range(size)])  38.3 us
    pallas_call x1, Pallas kernels, attention(): pl.pallas_call(attention_kernel, out_shape=[jax.ShapeDtypeStruct((rows, D...  14.7 us
    ppermute x3, starting transfers between devices, later(): lax.ppermute(array, 'ctx', [(i, i + 2 * chips) for i in range(8 - 2 * chi...  10.7 us
    pallas_call x2, Pallas kernels, enter(): pl.pallas_call(enter_kernel, out_shape=jax.ShapeDtypeStruct((count, 2 * w...  6.11 us
  transfers between devices with their start and end apart: 33, of which 17 were waited for; matrix products, arithmetic and copies ran while one was open for 2% of the time, Pallas kernels for 13%

profile of v6, /device:TPU:0, one launch (start us, length us, event | category | flops | bytes accessed | tf_op | source)
XLA Modules:
  0.0 178.2 jit_solution(15482242652917323877)
XLA Ops:
  0.0 0.9 constant_dynamic-slice_fusion
  0.9 4.9 %collective-permute-start.1 = (bf16[256,256]{1,0:T(8,128)(2,1)S(1)}, bf16[256,256]{1,0:T(8,128)(2,1)S(1)}, u32[]{:S(2)}, u32[]{:S(2)}) collective-permute-start(bf16[256,256]{1,0:T(8,128)(2,1)S(1)} %pad_maximum_fusion.1.refs_0_), channel_id=1, source_target_pairs={{0,8},{4,12},{8,16},{12,20},{16,24},{20,28},{1,9},{5,13},{9,17},{1... | collective-permute-start | bytes 393224 | tf_op jit(solution)/shard_map/ppermute | solution.py:496
  5.9 4.5 %collective-permute-start.3 = (bf16[256,256]{1,0:T(8,128)(2,1)S(1)}, bf16[256,256]{1,0:T(8,128)(2,1)S(1)}, u32[]{:S(2)}, u32[]{:S(2)}) collective-permute-start(bf16[256,256]{1,0:T(8,128)(2,1)S(1)} %pad_maximum_fusion.1.refs_0_), channel_id=1, source_target_pairs={{0,16},{4,20},{8,24},{12,28},{1,17},{5,21},{9,25},{13,29},{2,18},{... | collective-permute-start | bytes 393224 | tf_op jit(solution)/shard_map/ppermute | solution.py:496
  10.4 1.3 collective-permute-start.5
  11.7 0.1 collective-permute-start
  11.7 0.8 xor_bitcast_fusion.1
  12.5 0.6 collective-permute-start.2
  13.1 1.2 collective-permute-done.3.refs_4_
  14.3 0.0 collective-permute-start.4
  14.3 1.4 collective-permute-done.5.refs_6_
  15.7 0.0 collective-permute-start.6
  15.7 1.5 pad_maximum_fusion.refs_0_
  17.2 0.0 collective-permute-done.4.refs_5_
  17.2 6.3 %collective-permute-start.17 = (bf16[1024,768]{1,0:T(8,128)(2,1)S(1)}, bf16[1024,768]{1,0:T(8,128)(2,1)S(1)}, u32[]{:S(2)}, u32[]{:S(2)}) collective-permute-start(bf16[1024,768]{1,0:T(8,128)(2,1)S(1)} %pad_maximum_fusion.refs_0_), channel_id=1, source_target_pairs={{0,24},{4,28},{8,16},{12,20},{16,8},{20,12},{24,0},{28,4},{1,25},{... | collective-permute-start | bytes 4718600 | tf_op jit(solution)/shard_map/ppermute | solution.py:195
  23.5 0.1 pad_add_fusion.index
  23.6 0.1 select_add_fusion.shares
  23.7 0.0 copy-start.2
  23.7 0.0 copy-start.1
  23.7 14.7 %attention.1 = (bf16[64,4096]{1,0:T(8,128)(2,1)S(1)}, bf16[64,4096]{1,0:T(8,128)(2,1)}, bf16[64,4096]{1,0:T(8,128)(2,1)}, bf16[64,4096]{1,0:T(8,128)(2,1)}) custom-call(s32[2]{0:T(128)S(1)} %pad_add_fusion.index, bf16[256,2048]{1,0:T(8,128)(2,1)} %q_hbm.1, bf16[256,256]{1,0:T(8,128)(2,1)S(1)} %pad_maximum_fusion.1.refs_0_, ...), custom_call_target="tpu_custom_call" | custom-call | flops 1000 | bytes 1000 | tf_op jit(solution)/shard_map/attention/pallas_call | solution.py:296
  38.5 0.0 copy-start
  38.5 1.6 collective-permute-start.7
  40.0 1.5 collective-permute-start.8
  41.5 0.5 collective-permute-start.9
  42.0 11.5 %collective-permute-done.7.r1 = bf16[64,4096]{1,0:T(8,128)(2,1)S(1)} collective-permute-done((bf16[64,4096]{1,0:T(8,128)(2,1)}, bf16[64,4096]{1,0:T(8,128)(2,1)S(1)}, u32[]{:S(2)}, u32[]{:S(2)}) %collective-permute-start.7) | collective-permute-done | bytes 524320 | tf_op jit(solution)/shard_map/ppermute | solution.py:195
  53.6 11.2 %collective-permute-done.8.r2 = bf16[64,4096]{1,0:T(8,128)(2,1)S(1)} collective-permute-done((bf16[64,4096]{1,0:T(8,128)(2,1)}, bf16[64,4096]{1,0:T(8,128)(2,1)S(1)}, u32[]{:S(2)}, u32[]{:S(2)}) %collective-permute-start.8) | collective-permute-done | bytes 524320 | tf_op jit(solution)/shard_map/ppermute | solution.py:195
  64.7 1.2 norm.1
  65.9 0.1 collective-permute-start.10
  66.0 1.3 collective-permute-start.11
  67.3 0.8 collective-permute-start.12
  68.1 1.4 collective-permute-start.13
  69.5 3.3 %collective-permute-done.10.x0 = bf16[64,2048]{1,0:T(8,128)(2,1)S(1)} collective-permute-done((bf16[64,2048]{1,0:T(8,128)(2,1)S(1)}, bf16[64,2048]{1,0:T(8,128)(2,1)S(1)}, u32[]{:S(2)}, u32[]{:S(2)}) %collective-permute-start.10) | collective-permute-done | bytes 262176 | tf_op jit(solution)/shard_map/ppermute | solution.py:195
  72.8 2.5 %collective-permute-done.11.x1 = bf16[64,2048]{1,0:T(8,128)(2,1)S(1)} collective-permute-done((bf16[64,2048]{1,0:T(8,128)(2,1)S(1)}, bf16[64,2048]{1,0:T(8,128)(2,1)S(1)}, u32[]{:S(2)}, u32[]{:S(2)}) %collective-permute-start.11) | collective-permute-done | bytes 262176 | tf_op jit(solution)/shard_map/ppermute | solution.py:195
  75.3 4.6 %collective-permute-done.12.x2 = bf16[64,2048]{1,0:T(8,128)(2,1)S(1)} collective-permute-done((bf16[64,2048]{1,0:T(8,128)(2,1)S(1)}, bf16[64,2048]{1,0:T(8,128)(2,1)S(1)}, u32[]{:S(2)}, u32[]{:S(2)}) %collective-permute-start.12) | collective-permute-done | bytes 262176 | tf_op jit(solution)/shard_map/ppermute | solution.py:195
  79.9 0.1 collective-permute-start.15
  80.0 3.4 %collective-permute-start.16 = (bf16[64,2048]{1,0:T(8,128)(2,1)S(1)}, bf16[64,2048]{1,0:T(8,128)(2,1)S(1)}, u32[]{:S(2)}, u32[]{:S(2)}) collective-permute-start(bf16[64,2048]{1,0:T(8,128)(2,1)S(1)} %collective-permute-done.10.x0), channel_id=1, source_target_pairs={{0,3},{1,2},{2,1},{3,0},{4,7},{5,6},{6,5},{7,4},{8,11},{9,10},{10,... | collective-permute-start | bytes 786440 | tf_op jit(solution)/shard_map/ppermute | solution.py:195
  83.4 3.6 %collective-permute-done.14.x1 = bf16[64,2048]{1,0:T(8,128)(2,1)S(1)} collective-permute-done((bf16[64,2048]{1,0:T(8,128)(2,1)S(1)}, bf16[64,2048]{1,0:T(8,128)(2,1)S(1)}, u32[]{:S(2)}, u32[]{:S(2)}) %collective-permute-start.14) | collective-permute-done | bytes 262176 | tf_op jit(solution)/shard_map/ppermute | solution.py:195
  87.0 3.9 %collective-permute-done.15.x2 = bf16[64,2048]{1,0:T(8,128)(2,1)S(1)} collective-permute-done((bf16[64,2048]{1,0:T(8,128)(2,1)S(1)}, bf16[64,2048]{1,0:T(8,128)(2,1)S(1)}, u32[]{:S(2)}, u32[]{:S(2)}) %collective-permute-start.15) | collective-permute-done | bytes 262176 | tf_op jit(solution)/shard_map/ppermute | solution.py:195
  90.9 7.8 %collective-permute-start.18 = (bf16[768,512]{1,0:T(8,128)(2,1)S(1)}, bf16[768,512]{1,0:T(8,128)(2,1)S(1)}, u32[]{:S(2)}, u32[]{:S(2)}) collective-permute-start(bf16[768,512]{1,0:T(8,128)(2,1)S(1)} %bitcast.13), channel_id=1, source_target_pairs={{0,24},{4,28},{8,16},{12,20},{16,8},{20,12},{24,0},{28,4},{1,25},{... | collective-permute-start | bytes 2359304 | tf_op jit(solution)/shard_map/ppermute | solution.py:195
  98.7 3.1 %enter.3 = bf16[256,1536]{1,0:T(8,128)(2,1)S(1)} custom-call(bf16[64,2048]{1,0:T(8,128)(2,1)S(1)} %collective-permute-done.10.x0, bf16[64,2048]{1,0:T(8,128)(2,1)S(1)} %collective-permute-done.14.x1, bf16[64,2048]{1,0:T(8,128)(2,1)S(1)} %collective-permute-done.15.x2, bf16[64,2048]{1,0:T(8,128)(2,1)S(1)} %collective-permute-done.16.x3, ...), custom_call_target="tpu_custom_call" | custom-call | flops 1000 | bytes 1000 | tf_op jit(solution)/shard_map/enter/pallas_call | solution.py:377
  101.8 0.8 collective-permute-start.21
  102.6 14.6 %collective-permute-done.18.d2 = bf16[768,512]{1,0:T(8,128)(2,1)S(1)} collective-permute-done((bf16[768,512]{1,0:T(8,128)(2,1)S(1)}, bf16[768,512]{1,0:T(8,128)(2,1)S(1)}, u32[]{:S(2)}, u32[]{:S(2)}) %collective-permute-start.18) | collective-permute-done | bytes 786464 | tf_op jit(solution)/shard_map/ppermute | solution.py:195
  117.2 3.1 %enter.2.own = f32[256,1536]{1,0:T(8,128)S(1)} custom-call(bf16[64,2048]{1,0:T(8,128)(2,1)S(1)} %get-tuple-element.93.x0, bf16[64,2048]{1,0:T(8,128)(2,1)S(1)} %collective-permute-done.11.x1, bf16[64,2048]{1,0:T(8,128)(2,1)S(1)} %collective-permute-done.12.x2, bf16[64,2048]{1,0:T(8,128)(2,1)S(1)} %collective-permute-done.13.x3, ...), custom_call_target="tpu_custom_call" | custom-call | flops 1000 | bytes 1000 | tf_op jit(solution)/shard_map/enter/pallas_call | solution.py:377
  120.3 13.5 %collective-permute-done.21.other = bf16[256,1536]{1,0:T(8,128)(2,1)S(1)} collective-permute-done((bf16[256,1536]{1,0:T(8,128)(2,1)S(1)}, bf16[256,1536]{1,0:T(8,128)(2,1)S(1)}, u32[]{:S(2)}, u32[]{:S(2)}) %collective-permute-start.21) | collective-permute-done | bytes 786464 | tf_op jit(solution)/shard_map/ppermute | solution.py:195
  133.8 0.3 silu.1.hidden
  134.1 3.7 %collective-permute-start.24 = (bf16[256,768]{1,0:T(8,128)(2,1)S(1)}, bf16[256,768]{1,0:T(8,128)(2,1)S(1)}, u32[]{:S(2)}, u32[]{:S(2)}) collective-permute-start(bf16[256,768]{1,0:T(8,128)(2,1)S(1)} %silu.1.hidden), channel_id=1, source_target_pairs={{0,8},{4,12},{8,0},{12,4},{16,24},{20,28},{24,16},{28,20},{1,9},{5... | collective-permute-start | bytes 1179656 | tf_op jit(solution)/shard_map/ppermute | solution.py:195
  137.8 1.7 leave.2
  139.5 1.4 collective-permute-start.25
  141.0 0.8 collective-permute-start.26
  141.8 6.2 %collective-permute-done.25.r1 = bf16[64,2048]{1,0:T(8,128)(2,1)S(1)} collective-permute-done((bf16[64,2048]{1,0:T(8,128)(2,1)S(1)}, bf16[64,2048]{1,0:T(8,128)(2,1)S(1)}, u32[]{:S(2)}, u32[]{:S(2)}) %collective-permute-start.25) | collective-permute-done | bytes 262176 | tf_op jit(solution)/shard_map/ppermute | solution.py:195
  148.0 1.1 collective-permute-done.26.r2
  149.1 1.7 leave.3
  150.8 0.7 collective-permute-start.29
  151.5 0.6 collective-permute-start.30
  152.1 2.3 %collective-permute-start.31 = (bf16[64,2048]{1,0:T(8,128)(2,1)S(1)}, bf16[64,2048]{1,0:T(8,128)(2,1)S(1)}, u32[]{:S(2)}, u32[]{:S(2)}) collective-permute-start(bf16[64,2048]{1,0:T(8,128)(2,1)S(1)} %get-tuple-element.114), channel_id=1, source_target_pairs={{0,3},{1,2},{2,1},{3,0},{4,7},{5,6},{6,5},{7,4},{8,11},{9,10},{10,... | collective-permute-start | bytes 786440 | tf_op jit(solution)/shard_map/ppermute | solution.py:195
  154.4 0.3 collective-permute-start.28
  154.7 3.6 %collective-permute-done.28 = f32[64,128]{1,0:T(8,128)S(1)} collective-permute-done((f32[64,128]{1,0:T(8,128)S(1)}, f32[64,128]{1,0:T(8,128)S(1)}, u32[]{:S(2)}, u32[]{:S(2)}) %collective-permute-start.28) | collective-permute-done | bytes 32800 | tf_op jit(solution)/shard_map/ppermute | solution.py:195
  158.3 0.2 slice_reduce_fusion.3
  158.5 0.7 collective-permute-start.27
  159.2 0.9 collective-permute-done.29
  160.1 9.6 %collective-permute-done.30 = bf16[64,2048]{1,0:T(8,128)(2,1)S(1)} collective-permute-done((bf16[64,2048]{1,0:T(8,128)(2,1)S(1)}, bf16[64,2048]{1,0:T(8,128)(2,1)S(1)}, u32[]{:S(2)}, u32[]{:S(2)}) %collective-permute-start.30) | collective-permute-done | bytes 262176 | tf_op jit(solution)/shard_map/ppermute | solution.py:195
  169.7 0.3 add_convert_fusion
  170.0 1.6 collective-permute-start.32
  171.6 4.8 %collective-permute-done.32.other = bf16[64,2048]{1,0:T(8,128)(2,1)S(1)} collective-permute-done((bf16[64,2048]{1,0:T(8,128)(2,1)S(1)}, bf16[64,2048]{1,0:T(8,128)(2,1)S(1)}, u32[]{:S(2)}, u32[]{:S(2)}) %collective-permute-start.32) | collective-permute-done | bytes 262176 | tf_op jit(solution)/shard_map/ppermute | solution.py:195
  176.4 1.7 final.1
  (28 shorter events, 0.1 us)
Async XLA Ops:
  0.9 11.6 %collective-permute-start.1 = (bf16[256,256]{1,0:T(8,128)(2,1)S(1)}, bf16[256,256]{1,0:T(8,128)(2,1)S(1)}, u32[]{:S(2)}, u32[]{:S(2)}) collective-permute-start(bf16[256,256]{1,0:T(8,128)(2,1)S(1)} %pad_maximum_fusion.1.refs_0_), channel_id=1, source_target_pairs={{0,8},{4,12},{8,16},{12,20},{16,24},{20,28},{1,9},{5,13},{9,17},{1... | collective-permute-start | bytes 393224 | tf_op jit(solution)/shard_map/ppermute | solution.py:496
  5.9 8.4 %collective-permute-start.3 = (bf16[256,256]{1,0:T(8,128)(2,1)S(1)}, bf16[256,256]{1,0:T(8,128)(2,1)S(1)}, u32[]{:S(2)}, u32[]{:S(2)}) collective-permute-start(bf16[256,256]{1,0:T(8,128)(2,1)S(1)} %pad_maximum_fusion.1.refs_0_), channel_id=1, source_target_pairs={{0,16},{4,20},{8,24},{12,28},{1,17},{5,21},{9,25},{13,29},{2,18},{... | collective-permute-start | bytes 393224 | tf_op jit(solution)/shard_map/ppermute | solution.py:496
  10.4 5.3 %collective-permute-start.5 = (bf16[256,256]{1,0:T(8,128)(2,1)S(1)}, bf16[256,256]{1,0:T(8,128)(2,1)S(1)}, u32[]{:S(2)}, u32[]{:S(2)}) collective-permute-start(bf16[256,256]{1,0:T(8,128)(2,1)S(1)} %pad_maximum_fusion.1.refs_0_), channel_id=1, source_target_pairs={{0,24},{4,28},{1,25},{5,29},{2,26},{6,30},{3,27},{7,31}} | collective-permute-start | bytes 393224 | tf_op jit(solution)/shard_map/ppermute | solution.py:496
  11.7 5.5 %collective-permute-start = (bf16[256,256]{1,0:T(8,128)(2,1)S(1)}, bf16[256,256]{1,0:T(8,128)(2,1)S(1)}, u32[]{:S(2)}, u32[]{:S(2)}) collective-permute-start(bf16[256,256]{1,0:T(8,128)(2,1)S(1)} %pad_maximum_fusion.1.refs_0_), channel_id=1, source_target_pairs={{0,4},{4,0},{8,12},{12,8},{16,20},{20,16},{24,28},{28,24},{1,5},{5... | collective-permute-start | bytes 393224 | tf_op jit(solution)/shard_map/ppermute | solution.py:195
  12.5 11.1 %copy-start.3 = (f32[64,2]{0,1:T(2,128)S(1)}, f32[64,2]{0,1:T(2,128)}, u32[]{:S(2)}) copy-start(f32[64,2]{0,1:T(2,128)} %param.18) | copy-start | bytes 1540
  12.5 4.6 %collective-permute-start.2 = (bf16[256,256]{1,0:T(8,128)(2,1)S(1)}, bf16[256,256]{1,0:T(8,128)(2,1)S(1)}, u32[]{:S(2)}, u32[]{:S(2)}) collective-permute-start(bf16[256,256]{1,0:T(8,128)(2,1)S(1)} %collective-permute-done.1.refs_2_), channel_id=1, source_target_pairs={{0,4},{4,0},{8,12},{12,8},{16,20},{20,16},{24,28},{28,24},{1,5},{5... | collective-permute-start | bytes 393224 | tf_op jit(solution)/shard_map/ppermute | solution.py:195
  14.3 2.9 %collective-permute-start.4 = (bf16[256,256]{1,0:T(8,128)(2,1)S(1)}, bf16[256,256]{1,0:T(8,128)(2,1)S(1)}, u32[]{:S(2)}, u32[]{:S(2)}) collective-permute-start(bf16[256,256]{1,0:T(8,128)(2,1)S(1)} %collective-permute-done.3.refs_4_), channel_id=1, source_target_pairs={{0,4},{4,0},{8,12},{12,8},{16,20},{20,16},{24,28},{28,24},{1,5},{5... | collective-permute-start | bytes 393224 | tf_op jit(solution)/shard_map/ppermute | solution.py:195
  15.7 1.5 collective-permute-start.6
  17.2 73.7 %collective-permute-start.17 = (bf16[1024,768]{1,0:T(8,128)(2,1)S(1)}, bf16[1024,768]{1,0:T(8,128)(2,1)S(1)}, u32[]{:S(2)}, u32[]{:S(2)}) collective-permute-start(bf16[1024,768]{1,0:T(8,128)(2,1)S(1)} %pad_maximum_fusion.refs_0_), channel_id=1, source_target_pairs={{0,24},{4,28},{8,16},{12,20},{16,8},{20,12},{24,0},{28,4},{1,25},{... | collective-permute-start | bytes 4718600 | tf_op jit(solution)/shard_map/ppermute | solution.py:195
  23.7 18.3 %copy-start.2 = (bf16[4096]{0:T(1024)(128)(2,1)S(1)}, bf16[4096]{0:T(1024)(128)(2,1)}, u32[]{:S(2)}) copy-start(bf16[4096]{0:T(1024)(128)(2,1)} %param.16) | copy-start | bytes 24580
  23.7 41.0 %copy-start.1 = (bf16[64,4096]{1,0:T(8,128)(2,1)S(1)}, bf16[64,4096]{1,0:T(8,128)(2,1)}, u32[]{:S(2)}) copy-start(bf16[64,4096]{1,0:T(8,128)(2,1)} %residual.1) | copy-start | bytes 1572868
  38.5 52.5 %copy-start = (bf16[1,768,512]{2,1,0:T(8,128)(2,1)S(1)}, bf16[1,768,512]{2,1,0:T(8,128)(2,1)}, u32[]{:S(2)}) copy-start(bf16[1,768,512]{2,1,0:T(8,128)(2,1)} %param.21) | copy-start | bytes 2359300
  38.5 15.1 %collective-permute-start.7 = (bf16[64,4096]{1,0:T(8,128)(2,1)}, bf16[64,4096]{1,0:T(8,128)(2,1)S(1)}, u32[]{:S(2)}, u32[]{:S(2)}) collective-permute-start(bf16[64,4096]{1,0:T(8,128)(2,1)} %get-tuple-element.77), channel_id=1, source_target_pairs={{0,1},{1,0},{2,3},{3,2},{4,5},{5,4},{6,7},{7,6},{8,9},{9,8},{10,11... | collective-permute-start | bytes 1572872 | tf_op jit(solution)/shard_map/ppermute | solution.py:195
  40.0 24.7 %collective-permute-start.8 = (bf16[64,4096]{1,0:T(8,128)(2,1)}, bf16[64,4096]{1,0:T(8,128)(2,1)S(1)}, u32[]{:S(2)}, u32[]{:S(2)}) collective-permute-start(bf16[64,4096]{1,0:T(8,128)(2,1)} %get-tuple-element.78), channel_id=1, source_target_pairs={{0,2},{1,3},{2,0},{3,1},{4,6},{5,7},{6,4},{7,5},{8,10},{9,11},{10,... | collective-permute-start | bytes 1572872 | tf_op jit(solution)/shard_map/ppermute | solution.py:195
  41.5 23.2 %collective-permute-start.9 = (bf16[64,4096]{1,0:T(8,128)(2,1)}, bf16[64,4096]{1,0:T(8,128)(2,1)S(1)}, u32[]{:S(2)}, u32[]{:S(2)}) collective-permute-start(bf16[64,4096]{1,0:T(8,128)(2,1)} %get-tuple-element.79), channel_id=1, source_target_pairs={{0,3},{1,2},{2,1},{3,0},{4,7},{5,6},{6,5},{7,4},{8,11},{9,10},{10,... | collective-permute-start | bytes 1572872 | tf_op jit(solution)/shard_map/ppermute | solution.py:195
  65.9 6.9 %collective-permute-start.10 = (bf16[64,2048]{1,0:T(8,128)(2,1)S(1)}, bf16[64,2048]{1,0:T(8,128)(2,1)S(1)}, u32[]{:S(2)}, u32[]{:S(2)}) collective-permute-start(bf16[64,2048]{1,0:T(8,128)(2,1)S(1)} %get-tuple-element.83), channel_id=1, source_target_pairs={{0,8},{4,12},{8,0},{12,4},{16,24},{20,28},{24,16},{28,20},{1,9},{5... | collective-permute-start | bytes 786440 | tf_op jit(solution)/shard_map/ppermute | solution.py:195
  66.0 9.3 %collective-permute-start.11 = (bf16[64,2048]{1,0:T(8,128)(2,1)S(1)}, bf16[64,2048]{1,0:T(8,128)(2,1)S(1)}, u32[]{:S(2)}, u32[]{:S(2)}) collective-permute-start(bf16[64,2048]{1,0:T(8,128)(2,1)S(1)} %get-tuple-element.93.x0), channel_id=1, source_target_pairs={{0,1},{1,0},{2,3},{3,2},{4,5},{5,4},{6,7},{7,6},{8,9},{9,8},{10,11... | collective-permute-start | bytes 786440 | tf_op jit(solution)/shard_map/ppermute | solution.py:195
  67.3 12.6 %collective-permute-start.12 = (bf16[64,2048]{1,0:T(8,128)(2,1)S(1)}, bf16[64,2048]{1,0:T(8,128)(2,1)S(1)}, u32[]{:S(2)}, u32[]{:S(2)}) collective-permute-start(bf16[64,2048]{1,0:T(8,128)(2,1)S(1)} %get-tuple-element.93.x0), channel_id=1, source_target_pairs={{0,2},{1,3},{2,0},{3,1},{4,6},{5,7},{6,4},{7,5},{8,10},{9,11},{10,... | collective-permute-start | bytes 786440 | tf_op jit(solution)/shard_map/ppermute | solution.py:195
  68.1 15.3 %collective-permute-start.13 = (bf16[64,2048]{1,0:T(8,128)(2,1)S(1)}, bf16[64,2048]{1,0:T(8,128)(2,1)S(1)}, u32[]{:S(2)}, u32[]{:S(2)}) collective-permute-start(bf16[64,2048]{1,0:T(8,128)(2,1)S(1)} %get-tuple-element.93.x0), channel_id=1, source_target_pairs={{0,3},{1,2},{2,1},{3,0},{4,7},{5,6},{6,5},{7,4},{8,11},{9,10},{10,... | collective-permute-start | bytes 786440 | tf_op jit(solution)/shard_map/ppermute | solution.py:195
  79.9 7.1 %collective-permute-start.14 = (bf16[64,2048]{1,0:T(8,128)(2,1)S(1)}, bf16[64,2048]{1,0:T(8,128)(2,1)S(1)}, u32[]{:S(2)}, u32[]{:S(2)}) collective-permute-start(bf16[64,2048]{1,0:T(8,128)(2,1)S(1)} %collective-permute-done.10.x0), channel_id=1, source_target_pairs={{0,1},{1,0},{2,3},{3,2},{4,5},{5,4},{6,7},{7,6},{8,9},{9,8},{10,11... | collective-permute-start | bytes 786440 | tf_op jit(solution)/shard_map/ppermute | solution.py:195
  79.9 11.0 %collective-permute-start.15 = (bf16[64,2048]{1,0:T(8,128)(2,1)S(1)}, bf16[64,2048]{1,0:T(8,128)(2,1)S(1)}, u32[]{:S(2)}, u32[]{:S(2)}) collective-permute-start(bf16[64,2048]{1,0:T(8,128)(2,1)S(1)} %collective-permute-done.10.x0), channel_id=1, source_target_pairs={{0,2},{1,3},{2,0},{3,1},{4,6},{5,7},{6,4},{7,5},{8,10},{9,11},{10,... | collective-permute-start | bytes 786440 | tf_op jit(solution)/shard_map/ppermute | solution.py:195
  80.0 10.9 %collective-permute-start.16 = (bf16[64,2048]{1,0:T(8,128)(2,1)S(1)}, bf16[64,2048]{1,0:T(8,128)(2,1)S(1)}, u32[]{:S(2)}, u32[]{:S(2)}) collective-permute-start(bf16[64,2048]{1,0:T(8,128)(2,1)S(1)} %collective-permute-done.10.x0), channel_id=1, source_target_pairs={{0,3},{1,2},{2,1},{3,0},{4,7},{5,6},{6,5},{7,4},{8,11},{9,10},{10,... | collective-permute-start | bytes 786440 | tf_op jit(solution)/shard_map/ppermute | solution.py:195
  83.4 15.3 %collective-permute-start.19 = (bf16[1024,768]{1,0:T(8,128)(2,1)S(1)}, bf16[1024,768]{1,0:T(8,128)(2,1)S(1)}, u32[]{:S(2)}, u32[]{:S(2)}) collective-permute-start(bf16[1024,768]{1,0:T(8,128)(2,1)S(1)} %pad_maximum_fusion.refs_0_), channel_id=1, source_target_pairs={{0,4},{4,0},{8,12},{12,8},{16,20},{20,16},{24,28},{28,24},{1,5},{5... | collective-permute-start | bytes 4718600 | tf_op jit(solution)/shard_map/ppermute | solution.py:195
  90.9 7.8 %collective-permute-start.20 = (bf16[1024,768]{1,0:T(8,128)(2,1)S(1)}, bf16[1024,768]{1,0:T(8,128)(2,1)S(1)}, u32[]{:S(2)}, u32[]{:S(2)}) collective-permute-start(bf16[1024,768]{1,0:T(8,128)(2,1)S(1)} %collective-permute-done.17.refs_2_), channel_id=1, source_target_pairs={{0,4},{4,0},{8,12},{12,8},{16,20},{20,16},{24,28},{28,24},{1,5},{5... | collective-permute-start | bytes 4718600 | tf_op jit(solution)/shard_map/ppermute | solution.py:195
  90.9 26.3 %collective-permute-start.18 = (bf16[768,512]{1,0:T(8,128)(2,1)S(1)}, bf16[768,512]{1,0:T(8,128)(2,1)S(1)}, u32[]{:S(2)}, u32[]{:S(2)}) collective-permute-start(bf16[768,512]{1,0:T(8,128)(2,1)S(1)} %bitcast.13), channel_id=1, source_target_pairs={{0,24},{4,28},{8,16},{12,20},{16,8},{20,12},{24,0},{28,4},{1,25},{... | collective-permute-start | bytes 2359304 | tf_op jit(solution)/shard_map/ppermute | solution.py:195
  101.8 32.0 %collective-permute-start.21 = (bf16[256,1536]{1,0:T(8,128)(2,1)S(1)}, bf16[256,1536]{1,0:T(8,128)(2,1)S(1)}, u32[]{:S(2)}, u32[]{:S(2)}) collective-permute-start(bf16[256,1536]{1,0:T(8,128)(2,1)S(1)} %enter.3), channel_id=1, source_target_pairs={{0,8},{4,12},{8,0},{12,4},{16,24},{20,28},{24,16},{28,20},{1,9},{5... | collective-permute-start | bytes 2359304 | tf_op jit(solution)/shard_map/ppermute | solution.py:195
  102.6 35.2 %collective-permute-start.22 = (bf16[768,512]{1,0:T(8,128)(2,1)S(1)}, bf16[768,512]{1,0:T(8,128)(2,1)S(1)}, u32[]{:S(2)}, u32[]{:S(2)}) collective-permute-start(bf16[768,512]{1,0:T(8,128)(2,1)S(1)} %bitcast.14), channel_id=1, source_target_pairs={{0,4},{4,0},{8,12},{12,8},{16,20},{20,16},{24,28},{28,24},{1,5},{5... | collective-permute-start | bytes 2359304 | tf_op jit(solution)/shard_map/ppermute | solution.py:195
  117.2 20.6 %collective-permute-start.23 = (bf16[768,512]{1,0:T(8,128)(2,1)S(1)}, bf16[768,512]{1,0:T(8,128)(2,1)S(1)}, u32[]{:S(2)}, u32[]{:S(2)}) collective-permute-start(bf16[768,512]{1,0:T(8,128)(2,1)S(1)} %collective-permute-done.18.d2), channel_id=1, source_target_pairs={{0,4},{4,0},{8,12},{12,8},{16,20},{20,16},{24,28},{28,24},{1,5},{5... | collective-permute-start | bytes 2359304 | tf_op jit(solution)/shard_map/ppermute | solution.py:195
  134.1 15.0 %collective-permute-start.24 = (bf16[256,768]{1,0:T(8,128)(2,1)S(1)}, bf16[256,768]{1,0:T(8,128)(2,1)S(1)}, u32[]{:S(2)}, u32[]{:S(2)}) collective-permute-start(bf16[256,768]{1,0:T(8,128)(2,1)S(1)} %silu.1.hidden), channel_id=1, source_target_pairs={{0,8},{4,12},{8,0},{12,4},{16,24},{20,28},{24,16},{28,20},{1,9},{5... | collective-permute-start | bytes 1179656 | tf_op jit(solution)/shard_map/ppermute | solution.py:195
  139.5 8.4 %collective-permute-start.25 = (bf16[64,2048]{1,0:T(8,128)(2,1)S(1)}, bf16[64,2048]{1,0:T(8,128)(2,1)S(1)}, u32[]{:S(2)}, u32[]{:S(2)}) collective-permute-start(bf16[64,2048]{1,0:T(8,128)(2,1)S(1)} %get-tuple-element.105), channel_id=1, source_target_pairs={{0,1},{1,0},{2,3},{3,2},{4,5},{5,4},{6,7},{7,6},{8,9},{9,8},{10,11... | collective-permute-start | bytes 786440 | tf_op jit(solution)/shard_map/ppermute | solution.py:195
  141.0 8.1 %collective-permute-start.26 = (bf16[64,2048]{1,0:T(8,128)(2,1)S(1)}, bf16[64,2048]{1,0:T(8,128)(2,1)S(1)}, u32[]{:S(2)}, u32[]{:S(2)}) collective-permute-start(bf16[64,2048]{1,0:T(8,128)(2,1)S(1)} %get-tuple-element.106), channel_id=1, source_target_pairs={{0,2},{1,3},{2,0},{3,1},{4,6},{5,7},{6,4},{7,5},{8,10},{9,11},{10,... | collective-permute-start | bytes 786440 | tf_op jit(solution)/shard_map/ppermute | solution.py:195
  150.8 9.3 %collective-permute-start.29 = (bf16[64,2048]{1,0:T(8,128)(2,1)S(1)}, bf16[64,2048]{1,0:T(8,128)(2,1)S(1)}, u32[]{:S(2)}, u32[]{:S(2)}) collective-permute-start(bf16[64,2048]{1,0:T(8,128)(2,1)S(1)} %get-tuple-element.112), channel_id=1, source_target_pairs={{0,1},{1,0},{2,3},{3,2},{4,5},{5,4},{6,7},{7,6},{8,9},{9,8},{10,11... | collective-permute-start | bytes 786440 | tf_op jit(solution)/shard_map/ppermute | solution.py:195
  151.5 18.2 %collective-permute-start.30 = (bf16[64,2048]{1,0:T(8,128)(2,1)S(1)}, bf16[64,2048]{1,0:T(8,128)(2,1)S(1)}, u32[]{:S(2)}, u32[]{:S(2)}) collective-permute-start(bf16[64,2048]{1,0:T(8,128)(2,1)S(1)} %get-tuple-element.113), channel_id=1, source_target_pairs={{0,2},{1,3},{2,0},{3,1},{4,6},{5,7},{6,4},{7,5},{8,10},{9,11},{10,... | collective-permute-start | bytes 786440 | tf_op jit(solution)/shard_map/ppermute | solution.py:195
  152.1 17.6 %collective-permute-start.31 = (bf16[64,2048]{1,0:T(8,128)(2,1)S(1)}, bf16[64,2048]{1,0:T(8,128)(2,1)S(1)}, u32[]{:S(2)}, u32[]{:S(2)}) collective-permute-start(bf16[64,2048]{1,0:T(8,128)(2,1)S(1)} %get-tuple-element.114), channel_id=1, source_target_pairs={{0,3},{1,2},{2,1},{3,0},{4,7},{5,6},{6,5},{7,4},{8,11},{9,10},{10,... | collective-permute-start | bytes 786440 | tf_op jit(solution)/shard_map/ppermute | solution.py:195
  154.4 3.9 %collective-permute-start.28 = (f32[64,128]{1,0:T(8,128)S(1)}, f32[64,128]{1,0:T(8,128)S(1)}, u32[]{:S(2)}, u32[]{:S(2)}) collective-permute-start(f32[64,128]{1,0:T(8,128)S(1)} %select_add_fusion.shares), channel_id=1, source_target_pairs={{0,8},{4,12},{8,0},{12,4},{16,24},{20,28},{24,16},{28,20},{1,9},{5... | collective-permute-start | bytes 98312 | tf_op jit(solution)/shard_map/ppermute | solution.py:195
  158.5 13.1 %collective-permute-start.27 = (bf16[64,2048]{1,0:T(8,128)(2,1)S(1)}, bf16[64,2048]{1,0:T(8,128)(2,1)S(1)}, u32[]{:S(2)}, u32[]{:S(2)}) collective-permute-start(bf16[64,2048]{1,0:T(8,128)(2,1)S(1)} %get-tuple-element.109), channel_id=1, source_target_pairs={{0,3},{1,2},{2,1},{3,0},{4,7},{5,6},{6,5},{7,4},{8,11},{9,10},{10,... | collective-permute-start | bytes 786440 | tf_op jit(solution)/shard_map/ppermute | solution.py:195
  170.0 6.4 %collective-permute-start.32 = (bf16[64,2048]{1,0:T(8,128)(2,1)S(1)}, bf16[64,2048]{1,0:T(8,128)(2,1)S(1)}, u32[]{:S(2)}, u32[]{:S(2)}) collective-permute-start(bf16[64,2048]{1,0:T(8,128)(2,1)S(1)} %add_convert_fusion), channel_id=1, source_target_pairs={{0,8},{4,12},{8,0},{12,4},{16,24},{20,28},{24,16},{28,20},{1,9},{5... | collective-permute-start | bytes 786440 | tf_op jit(solution)/shard_map/ppermute | solution.py:195

commit v7 on v6

--- a/solution.py
+++ b/solution.py
@@ -499,7 +499,6 @@
     moved = [later(kv_here, d) for d in (3, 2, 1)][::-1]
     pair_here, down_here = jnp.concatenate([gate_here, up_here], axis=0), w_down[0]
     pieces = [part for piece in [kv_here] + moved for part in (piece, swap(piece, "ctx", 1))]
-    pieces, pair_here = lax.optimization_barrier((pieces, pair_here))
     pair_far = swap(pair_here, "ctx", 6)
 
     lane = lax.broadcasted_iota(jnp.int32, (expert_ids.shape[0], HD), 1)
@@ -516,10 +515,9 @@
     state, mine, theirs = norm(index, p[0], *r, residual, norm_gain.reshape(1, D))
     others = swap(theirs, "ctx", 2)
     own_rows = [mine] + [swap(mine, "exp", b) for b in (1, 2, 3)]
-    others, own_rows[1:3] = lax.optimization_barrier((others, own_rows[1:3]))
     other_rows = [others] + [swap(others, "exp", b) for b in (1, 2, 3)]
-    own_rows, other_rows, pair_far, down_here = lax.optimization_barrier(
-        (own_rows, other_rows, pair_far, down_here)
+    own_rows, others, pair_far, down_here = lax.optimization_barrier(
+        (own_rows, others, pair_far, down_here)
     )
     down_far = swap(down_here, "ctx", 6)
     pairs = (pair_here, pair_near, pair_far, swap(pair_far, "ctx", 1))

time: 178 us -> 194 us (1.090)
  starting transfers between devices: 49.1 us -> 87.5 us
  waiting for transfers between devices: 97.5 us -> 75.5 us
    ppermute x30, starting transfers between devices: 38.3 us -> 75.9 us  [swap(): return lax.ppermute(array, axis, [(i, i ^ mask) for i in range(size)])]
    ppermute x30, waiting for transfers between devices: 94.9 us -> 73.3 us  [swap(): return lax.ppermute(array, axis, [(i, i ^ mask) for i in range(size)])]
  transfers between devices with their start and end apart: 33 -> 33, of which waited for: 17 -> 15; matrix products, arithmetic and copies ran while one was open for 2% -> 1% of each run, Pallas kernels for 13% -> 12%
where the time goes in v7:
time: 194 us
  starting transfers between devices  87.5 us (45%)
  waiting for transfers between devices  75.5 us (39%)
  Pallas kernels  27 us (14%)
  local copies, waits for them, and re-layouts  2.47 us (1%)
    ppermute x30, starting transfers between devices, swap(): return lax.ppermute(array, axis, [(i, i ^ mask) for i in range(size)])  75.9 us
    ppermute x30, waiting for transfers between devices, swap(): return lax.ppermute(array, axis, [(i, i ^ mask) for i in range(size)])  73.3 us
    pallas_call x1, Pallas kernels, attention(): pl.pallas_call(attention_kernel, out_shape=[jax.ShapeDtypeStruct((rows, D...  14.2 us
    ppermute x3, starting transfers between devices, later(): lax.ppermute(array, 'ctx', [(i, i + 2 * chips) for i in range(8 - 2 * chi...  11.6 us
    pallas_call x2, Pallas kernels, enter(): pl.pallas_call(enter_kernel, out_shape=jax.ShapeDtypeStruct((count, 2 * w...  6.1 us
  transfers between devices with their start and end apart: 33, of which 15 were waited for; matrix products, arithmetic and copies ran while one was open for 1% of the time, Pallas kernels for 12%

profile of v7, /device:TPU:0, one launch (start us, length us, event | category | flops | bytes accessed | tf_op | source)
XLA Modules:
  0.0 193.7 jit_solution(1083989966463604089)
XLA Ops:
  0.0 1.0 constant_dynamic-slice_fusion
  1.0 0.0 copy-start.5
  1.0 0.0 copy-start.6
  1.0 0.5 collective-permute-start
  1.5 4.5 %collective-permute-start.1 = (bf16[256,256]{1,0:T(8,128)(2,1)S(1)}, bf16[256,256]{1,0:T(8,128)(2,1)S(1)}, u32[]{:S(2)}, u32[]{:S(2)}) collective-permute-start(bf16[256,256]{1,0:T(8,128)(2,1)S(1)} %pad_maximum_fusion.refs_0_), channel_id=1, source_target_pairs={{0,8},{4,12},{8,16},{12,20},{16,24},{20,28},{1,9},{5,13},{9,17},{1... | collective-permute-start | bytes 393224 | tf_op jit(solution)/shard_map/ppermute | solution.py:496
  6.0 5.1 %collective-permute-start.3 = (bf16[256,256]{1,0:T(8,128)(2,1)S(1)}, bf16[256,256]{1,0:T(8,128)(2,1)}, u32[]{:S(2)}, u32[]{:S(2)}) collective-permute-start(bf16[256,256]{1,0:T(8,128)(2,1)S(1)} %pad_maximum_fusion.refs_0_), channel_id=1, source_target_pairs={{0,16},{4,20},{8,24},{12,28},{1,17},{5,21},{9,25},{13,29},{2,18},{... | collective-permute-start | bytes 393224 | tf_op jit(solution)/shard_map/ppermute | solution.py:496
  11.2 1.9 %collective-permute-start.5 = (bf16[256,256]{1,0:T(8,128)(2,1)S(1)}, bf16[256,256]{1,0:T(8,128)(2,1)}, u32[]{:S(2)}, u32[]{:S(2)}) collective-permute-start(bf16[256,256]{1,0:T(8,128)(2,1)S(1)} %pad_maximum_fusion.refs_0_), channel_id=1, source_target_pairs={{0,24},{4,28},{1,25},{5,29},{2,26},{6,30},{3,27},{7,31}} | collective-permute-start | bytes 393224 | tf_op jit(solution)/shard_map/ppermute | solution.py:496
  13.1 1.2 constant_dynamic-update-slice_fusion.1
  14.3 0.1 constant_dynamic-update-slice_fusion.refs_0_
  14.4 0.1 collective-permute-start.14
  14.5 0.1 collective-permute-start.2
  14.6 0.5 collective-permute-start.4
  15.1 2.1 %collective-permute-done.5.refs_6_ = bf16[256,256]{1,0:T(8,128)(2,1)} collective-permute-done((bf16[256,256]{1,0:T(8,128)(2,1)S(1)}, bf16[256,256]{1,0:T(8,128)(2,1)}, u32[]{:S(2)}, u32[]{:S(2)}) %collective-permute-start.5) | collective-permute-done | bytes 131104 | tf_op jit(solution)/shard_map/ppermute | solution.py:496
  17.2 0.7 select_add_fusion.shares
  17.9 0.1 pad_add_fusion.index
  18.0 0.9 collective-permute-done.6.refs_7_
  18.9 14.2 %attention.1 = (bf16[64,4096]{1,0:T(8,128)(2,1)S(1)}, bf16[64,4096]{1,0:T(8,128)(2,1)}, bf16[64,4096]{1,0:T(8,128)(2,1)}, bf16[64,4096]{1,0:T(8,128)(2,1)}) custom-call(s32[2]{0:T(128)S(1)} %pad_add_fusion.index, bf16[256,2048]{1,0:T(8,128)(2,1)} %q_hbm.1, bf16[256,256]{1,0:T(8,128)(2,1)S(1)} %pad_maximum_fusion.refs_0_, ...), custom_call_target="tpu_custom_call" | custom-call | flops 1000 | bytes 1000 | tf_op jit(solution)/shard_map/attention/pallas_call | solution.py:296
  33.1 0.0 copy-start
  33.1 1.6 collective-permute-start.7
  34.7 1.5 collective-permute-start.8
  36.2 0.5 collective-permute-start.9
  36.7 11.5 %collective-permute-done.7.r1 = bf16[64,4096]{1,0:T(8,128)(2,1)S(1)} collective-permute-done((bf16[64,4096]{1,0:T(8,128)(2,1)}, bf16[64,4096]{1,0:T(8,128)(2,1)S(1)}, u32[]{:S(2)}, u32[]{:S(2)}) %collective-permute-start.7) | collective-permute-done | bytes 524320 | tf_op jit(solution)/shard_map/ppermute | solution.py:195
  48.2 11.7 %collective-permute-done.8.r2 = bf16[64,4096]{1,0:T(8,128)(2,1)S(1)} collective-permute-done((bf16[64,4096]{1,0:T(8,128)(2,1)}, bf16[64,4096]{1,0:T(8,128)(2,1)S(1)}, u32[]{:S(2)}, u32[]{:S(2)}) %collective-permute-start.8) | collective-permute-done | bytes 524320 | tf_op jit(solution)/shard_map/ppermute | solution.py:195
  59.8 1.2 norm.1
  61.0 1.3 collective-permute-start.10
  62.3 0.8 collective-permute-start.11
  63.1 1.4 collective-permute-start.12
  64.6 38.4 %collective-permute-start.13 = (bf16[64,2048]{1,0:T(8,128)(2,1)S(1)}, bf16[64,2048]{1,0:T(8,128)(2,1)S(1)}, u32[]{:S(2)}, u32[]{:S(2)}) collective-permute-start(bf16[64,2048]{1,0:T(8,128)(2,1)S(1)} %get-tuple-element.58), channel_id=1, source_target_pairs={{0,8},{4,12},{8,0},{12,4},{16,24},{20,28},{24,16},{28,20},{1,9},{5... | collective-permute-start | bytes 786440 | tf_op jit(solution)/shard_map/ppermute | solution.py:195
  103.0 4.9 %collective-permute-done.13.x0 = bf16[64,2048]{1,0:T(8,128)(2,1)S(1)} collective-permute-done((bf16[64,2048]{1,0:T(8,128)(2,1)S(1)}, bf16[64,2048]{1,0:T(8,128)(2,1)S(1)}, u32[]{:S(2)}, u32[]{:S(2)}) %collective-permute-start.13) | collective-permute-done | bytes 262176 | tf_op jit(solution)/shard_map/ppermute | solution.py:195
  107.9 14.4 %collective-permute-start.15 = (bf16[768,512]{1,0:T(8,128)(2,1)S(1)}, bf16[768,512]{1,0:T(8,128)(2,1)S(1)}, u32[]{:S(2)}, u32[]{:S(2)}) collective-permute-start(bf16[768,512]{1,0:T(8,128)(2,1)S(1)} %bitcast.13), channel_id=1, source_target_pairs={{0,24},{4,28},{8,16},{12,20},{16,8},{20,12},{24,0},{28,4},{1,25},{... | collective-permute-start | bytes 2359304 | tf_op jit(solution)/shard_map/ppermute | solution.py:195
  122.3 0.6 collective-permute-start.18
  122.9 1.4 collective-permute-start.19
  124.3 6.4 %collective-permute-done.18.x1 = bf16[64,2048]{1,0:T(8,128)(2,1)S(1)} collective-permute-done((bf16[64,2048]{1,0:T(8,128)(2,1)S(1)}, bf16[64,2048]{1,0:T(8,128)(2,1)S(1)}, u32[]{:S(2)}, u32[]{:S(2)}) %collective-permute-start.18) | collective-permute-done | bytes 262176 | tf_op jit(solution)/shard_map/ppermute | solution.py:195
  130.7 1.4 collective-permute-start.20
  132.1 7.0 %collective-permute-done.20.x3 = bf16[64,2048]{1,0:T(8,128)(2,1)S(1)} collective-permute-done((bf16[64,2048]{1,0:T(8,128)(2,1)S(1)}, bf16[64,2048]{1,0:T(8,128)(2,1)S(1)}, u32[]{:S(2)}, u32[]{:S(2)}) %collective-permute-start.20) | collective-permute-done | bytes 262176 | tf_op jit(solution)/shard_map/ppermute | solution.py:195
  139.1 3.1 %enter.3 = bf16[256,1536]{1,0:T(8,128)(2,1)S(1)} custom-call(bf16[64,2048]{1,0:T(8,128)(2,1)S(1)} %collective-permute-done.13.x0, bf16[64,2048]{1,0:T(8,128)(2,1)S(1)} %collective-permute-done.18.x1, bf16[64,2048]{1,0:T(8,128)(2,1)S(1)} %collective-permute-done.19.x2, bf16[64,2048]{1,0:T(8,128)(2,1)S(1)} %collective-permute-done.20.x3, ...), custom_call_target="tpu_custom_call" | custom-call | flops 1000 | bytes 1000 | tf_op jit(solution)/shard_map/enter/pallas_call | solution.py:377
  142.2 0.1 collective-permute-start.21
  142.3 0.1 collective-permute-start.22
  142.4 0.5 collective-permute-start.23
  142.9 3.0 %enter.2.own = f32[256,1536]{1,0:T(8,128)S(1)} custom-call(bf16[64,2048]{1,0:T(8,128)(2,1)S(1)} %get-tuple-element.65.x0, bf16[64,2048]{1,0:T(8,128)(2,1)S(1)} %collective-permute-done.10.x1, bf16[64,2048]{1,0:T(8,128)(2,1)S(1)} %collective-permute-done.11.x2, bf16[64,2048]{1,0:T(8,128)(2,1)S(1)} %collective-permute-done.12.x3, ...), custom_call_target="tpu_custom_call" | custom-call | flops 1000 | bytes 1000 | tf_op jit(solution)/shard_map/enter/pallas_call | solution.py:377
  145.9 14.2 %collective-permute-done.21.other = bf16[256,1536]{1,0:T(8,128)(2,1)S(1)} collective-permute-done((bf16[256,1536]{1,0:T(8,128)(2,1)S(1)}, bf16[256,1536]{1,0:T(8,128)(2,1)S(1)}, u32[]{:S(2)}, u32[]{:S(2)}) %collective-permute-start.21) | collective-permute-done | bytes 786464 | tf_op jit(solution)/shard_map/ppermute | solution.py:195
  160.1 0.3 silu.1.hidden
  160.4 0.4 collective-permute-start.24
  160.8 1.7 leave.2
  162.5 0.6 collective-permute-start.25
  163.2 1.4 collective-permute-start.26
  164.6 4.4 %collective-permute-done.25.r1 = bf16[64,2048]{1,0:T(8,128)(2,1)S(1)} collective-permute-done((bf16[64,2048]{1,0:T(8,128)(2,1)S(1)}, bf16[64,2048]{1,0:T(8,128)(2,1)S(1)}, u32[]{:S(2)}, u32[]{:S(2)}) %collective-permute-start.25) | collective-permute-done | bytes 262176 | tf_op jit(solution)/shard_map/ppermute | solution.py:195
  169.0 0.6 collective-permute-done.26.r2
  169.5 1.7 leave.3
  171.3 1.5 collective-permute-start.31
  172.8 1.5 collective-permute-start.30
  174.3 0.6 collective-permute-start.29
  174.8 1.7 collective-permute-start.28
  176.6 2.2 %collective-permute-done.28 = f32[64,128]{1,0:T(8,128)S(1)} collective-permute-done((f32[64,128]{1,0:T(8,128)S(1)}, f32[64,128]{1,0:T(8,128)S(1)}, u32[]{:S(2)}, u32[]{:S(2)}) %collective-permute-start.28) | collective-permute-done | bytes 32800 | tf_op jit(solution)/shard_map/ppermute | solution.py:195
  178.7 0.2 slice_reduce_fusion.3
  179.0 1.5 collective-permute-start.27
  180.5 1.1 collective-permute-done.31
  181.6 3.6 %collective-permute-done.30 = bf16[64,2048]{1,0:T(8,128)(2,1)S(1)} collective-permute-done((bf16[64,2048]{1,0:T(8,128)(2,1)S(1)}, bf16[64,2048]{1,0:T(8,128)(2,1)S(1)}, u32[]{:S(2)}, u32[]{:S(2)}) %collective-permute-start.30) | collective-permute-done | bytes 262176 | tf_op jit(solution)/shard_map/ppermute | solution.py:195
  185.2 0.1 collective-permute-done.29
  185.3 0.3 add_convert_fusion
  185.6 1.5 collective-permute-start.32
  187.1 1.0 collective-permute-done.27.r3
  188.1 3.9 %collective-permute-done.32.other = bf16[64,2048]{1,0:T(8,128)(2,1)S(1)} collective-permute-done((bf16[64,2048]{1,0:T(8,128)(2,1)S(1)}, bf16[64,2048]{1,0:T(8,128)(2,1)S(1)}, u32[]{:S(2)}, u32[]{:S(2)}) %collective-permute-start.32) | collective-permute-done | bytes 262176 | tf_op jit(solution)/shard_map/ppermute | solution.py:195
  192.0 1.7 final.1
  (35 shorter events, 0.1 us)
Async XLA Ops:
  0.0 14.3 %copy-start.3 = (bf16[1,512,768]{2,1,0:T(8,128)(2,1)S(1)}, bf16[1,512,768]{2,1,0:T(8,128)(2,1)}, u32[]{:S(2)}) copy-start(bf16[1,512,768]{2,1,0:T(8,128)(2,1)} %param.20) | copy-start | bytes 2359300
  1.0 13.5 %copy-start.5 = (f32[64,2]{0,1:T(2,128)S(1)}, f32[64,2]{0,1:T(2,128)}, u32[]{:S(2)}) copy-start(f32[64,2]{0,1:T(2,128)} %param.18) | copy-start | bytes 1540
  1.0 13.5 %copy-start.6 = (s32[64,2]{0,1:T(2,128)S(1)}, s32[64,2]{0,1:T(2,128)}, u32[]{:S(2)}) copy-start(s32[64,2]{0,1:T(2,128)} %param.17) | copy-start | bytes 1540
  1.0 17.0 %collective-permute-start = (bf16[256,256]{1,0:T(8,128)(2,1)S(1)}, bf16[256,256]{1,0:T(8,128)(2,1)S(1)}, u32[]{:S(2)}, u32[]{:S(2)}) collective-permute-start(bf16[256,256]{1,0:T(8,128)(2,1)S(1)} %pad_maximum_fusion.refs_0_), channel_id=1, source_target_pairs={{0,4},{4,0},{8,12},{12,8},{16,20},{20,16},{24,28},{28,24},{1,5},{5... | collective-permute-start | bytes 393224 | tf_op jit(solution)/shard_map/ppermute | solution.py:195
  1.5 13.0 %collective-permute-start.1 = (bf16[256,256]{1,0:T(8,128)(2,1)S(1)}, bf16[256,256]{1,0:T(8,128)(2,1)S(1)}, u32[]{:S(2)}, u32[]{:S(2)}) collective-permute-start(bf16[256,256]{1,0:T(8,128)(2,1)S(1)} %pad_maximum_fusion.refs_0_), channel_id=1, source_target_pairs={{0,8},{4,12},{8,16},{12,20},{16,24},{20,28},{1,9},{5,13},{9,17},{1... | collective-permute-start | bytes 393224 | tf_op jit(solution)/shard_map/ppermute | solution.py:496
  6.0 8.6 %collective-permute-start.3 = (bf16[256,256]{1,0:T(8,128)(2,1)S(1)}, bf16[256,256]{1,0:T(8,128)(2,1)}, u32[]{:S(2)}, u32[]{:S(2)}) collective-permute-start(bf16[256,256]{1,0:T(8,128)(2,1)S(1)} %pad_maximum_fusion.refs_0_), channel_id=1, source_target_pairs={{0,16},{4,20},{8,24},{12,28},{1,17},{5,21},{9,25},{13,29},{2,18},{... | collective-permute-start | bytes 393224 | tf_op jit(solution)/shard_map/ppermute | solution.py:496
  11.2 6.0 %collective-permute-start.5 = (bf16[256,256]{1,0:T(8,128)(2,1)S(1)}, bf16[256,256]{1,0:T(8,128)(2,1)}, u32[]{:S(2)}, u32[]{:S(2)}) collective-permute-start(bf16[256,256]{1,0:T(8,128)(2,1)S(1)} %pad_maximum_fusion.refs_0_), channel_id=1, source_target_pairs={{0,24},{4,28},{1,25},{5,29},{2,26},{6,30},{3,27},{7,31}} | collective-permute-start | bytes 393224 | tf_op jit(solution)/shard_map/ppermute | solution.py:496
  14.4 93.5 %collective-permute-start.14 = (bf16[1024,768]{1,0:T(8,128)(2,1)S(1)}, bf16[1024,768]{1,0:T(8,128)(2,1)S(1)}, u32[]{:S(2)}, u32[]{:S(2)}) collective-permute-start(bf16[1024,768]{1,0:T(8,128)(2,1)S(1)} %constant_dynamic-update-slice_fusion.refs_0_), channel_id=1, source_target_pairs={{0,24},{4,28},{8,16},{12,20},{16,8},{20,12},{24,0},{28,4},{1,25},{... | collective-permute-start | bytes 4718600 | tf_op jit(solution)/shard_map/ppermute | solution.py:195
  14.5 3.5 %collective-permute-start.2 = (bf16[256,256]{1,0:T(8,128)(2,1)S(1)}, bf16[256,256]{1,0:T(8,128)(2,1)}, u32[]{:S(2)}, u32[]{:S(2)}) collective-permute-start(bf16[256,256]{1,0:T(8,128)(2,1)S(1)} %collective-permute-done.1.refs_2_), channel_id=1, source_target_pairs={{0,4},{4,0},{8,12},{12,8},{16,20},{20,16},{24,28},{28,24},{1,5},{5... | collective-permute-start | bytes 393224 | tf_op jit(solution)/shard_map/ppermute | solution.py:195
  14.6 3.4 %collective-permute-start.4 = (bf16[256,256]{1,0:T(8,128)(2,1)}, bf16[256,256]{1,0:T(8,128)(2,1)}, u32[]{:S(2)}, u32[]{:S(2)}) collective-permute-start(bf16[256,256]{1,0:T(8,128)(2,1)} %collective-permute-done.3.refs_4_), channel_id=1, source_target_pairs={{0,4},{4,0},{8,12},{12,8},{16,20},{20,16},{24,28},{28,24},{1,5},{5... | collective-permute-start | bytes 393224 | tf_op jit(solution)/shard_map/ppermute | solution.py:195
  17.2 1.7 collective-permute-start.6
  18.0 18.7 %copy-start.4 = (bf16[4096]{0:T(1024)(128)(2,1)S(1)}, bf16[4096]{0:T(1024)(128)(2,1)}, u32[]{:S(2)}) copy-start(bf16[4096]{0:T(1024)(128)(2,1)} %param.16) | copy-start | bytes 24580
  18.0 41.8 %copy-start.1 = (bf16[64,4096]{1,0:T(8,128)(2,1)S(1)}, bf16[64,4096]{1,0:T(8,128)(2,1)}, u32[]{:S(2)}) copy-start(bf16[64,4096]{1,0:T(8,128)(2,1)} %residual.1) | copy-start | bytes 1572868
  33.1 74.8 %copy-start = (bf16[1,768,512]{2,1,0:T(8,128)(2,1)S(1)}, bf16[1,768,512]{2,1,0:T(8,128)(2,1)}, u32[]{:S(2)}) copy-start(bf16[1,768,512]{2,1,0:T(8,128)(2,1)} %param.21) | copy-start | bytes 2359300
  33.1 15.0 %collective-permute-start.7 = (bf16[64,4096]{1,0:T(8,128)(2,1)}, bf16[64,4096]{1,0:T(8,128)(2,1)S(1)}, u32[]{:S(2)}, u32[]{:S(2)}) collective-permute-start(bf16[64,4096]{1,0:T(8,128)(2,1)} %get-tuple-element.52), channel_id=1, source_target_pairs={{0,1},{1,0},{2,3},{3,2},{4,5},{5,4},{6,7},{7,6},{8,9},{9,8},{10,11... | collective-permute-start | bytes 1572872 | tf_op jit(solution)/shard_map/ppermute | solution.py:195
  34.7 25.1 %collective-permute-start.8 = (bf16[64,4096]{1,0:T(8,128)(2,1)}, bf16[64,4096]{1,0:T(8,128)(2,1)S(1)}, u32[]{:S(2)}, u32[]{:S(2)}) collective-permute-start(bf16[64,4096]{1,0:T(8,128)(2,1)} %get-tuple-element.53), channel_id=1, source_target_pairs={{0,2},{1,3},{2,0},{3,1},{4,6},{5,7},{6,4},{7,5},{8,10},{9,11},{10,... | collective-permute-start | bytes 1572872 | tf_op jit(solution)/shard_map/ppermute | solution.py:195
  36.2 23.6 %collective-permute-start.9 = (bf16[64,4096]{1,0:T(8,128)(2,1)}, bf16[64,4096]{1,0:T(8,128)(2,1)S(1)}, u32[]{:S(2)}, u32[]{:S(2)}) collective-permute-start(bf16[64,4096]{1,0:T(8,128)(2,1)} %get-tuple-element.54), channel_id=1, source_target_pairs={{0,3},{1,2},{2,1},{3,0},{4,7},{5,6},{6,5},{7,4},{8,11},{9,10},{10,... | collective-permute-start | bytes 1572872 | tf_op jit(solution)/shard_map/ppermute | solution.py:195
  61.0 41.9 %collective-permute-start.10 = (bf16[64,2048]{1,0:T(8,128)(2,1)S(1)}, bf16[64,2048]{1,0:T(8,128)(2,1)S(1)}, u32[]{:S(2)}, u32[]{:S(2)}) collective-permute-start(bf16[64,2048]{1,0:T(8,128)(2,1)S(1)} %get-tuple-element.65.x0), channel_id=1, source_target_pairs={{0,1},{1,0},{2,3},{3,2},{4,5},{5,4},{6,7},{7,6},{8,9},{9,8},{10,11... | collective-permute-start | bytes 786440 | tf_op jit(solution)/shard_map/ppermute | solution.py:195
  62.3 40.7 %collective-permute-start.11 = (bf16[64,2048]{1,0:T(8,128)(2,1)S(1)}, bf16[64,2048]{1,0:T(8,128)(2,1)S(1)}, u32[]{:S(2)}, u32[]{:S(2)}) collective-permute-start(bf16[64,2048]{1,0:T(8,128)(2,1)S(1)} %get-tuple-element.65.x0), channel_id=1, source_target_pairs={{0,2},{1,3},{2,0},{3,1},{4,6},{5,7},{6,4},{7,5},{8,10},{9,11},{10,... | collective-permute-start | bytes 786440 | tf_op jit(solution)/shard_map/ppermute | solution.py:195
  63.1 39.8 %collective-permute-start.12 = (bf16[64,2048]{1,0:T(8,128)(2,1)S(1)}, bf16[64,2048]{1,0:T(8,128)(2,1)S(1)}, u32[]{:S(2)}, u32[]{:S(2)}) collective-permute-start(bf16[64,2048]{1,0:T(8,128)(2,1)S(1)} %get-tuple-element.65.x0), channel_id=1, source_target_pairs={{0,3},{1,2},{2,1},{3,0},{4,7},{5,6},{6,5},{7,4},{8,11},{9,10},{10,... | collective-permute-start | bytes 786440 | tf_op jit(solution)/shard_map/ppermute | solution.py:195
  64.6 43.3 %collective-permute-start.13 = (bf16[64,2048]{1,0:T(8,128)(2,1)S(1)}, bf16[64,2048]{1,0:T(8,128)(2,1)S(1)}, u32[]{:S(2)}, u32[]{:S(2)}) collective-permute-start(bf16[64,2048]{1,0:T(8,128)(2,1)S(1)} %get-tuple-element.58), channel_id=1, source_target_pairs={{0,8},{4,12},{8,0},{12,4},{16,24},{20,28},{24,16},{28,20},{1,9},{5... | collective-permute-start | bytes 786440 | tf_op jit(solution)/shard_map/ppermute | solution.py:195
  102.9 36.2 %collective-permute-start.16 = (bf16[1024,768]{1,0:T(8,128)(2,1)S(1)}, bf16[1024,768]{1,0:T(8,128)(2,1)S(1)}, u32[]{:S(2)}, u32[]{:S(2)}) collective-permute-start(bf16[1024,768]{1,0:T(8,128)(2,1)S(1)} %constant_dynamic-update-slice_fusion.refs_0_), channel_id=1, source_target_pairs={{0,4},{4,0},{8,12},{12,8},{16,20},{20,16},{24,28},{28,24},{1,5},{5... | collective-permute-start | bytes 4718600 | tf_op jit(solution)/shard_map/ppermute | solution.py:195
  107.9 31.3 %collective-permute-start.17 = (bf16[1024,768]{1,0:T(8,128)(2,1)S(1)}, bf16[1024,768]{1,0:T(8,128)(2,1)S(1)}, u32[]{:S(2)}, u32[]{:S(2)}) collective-permute-start(bf16[1024,768]{1,0:T(8,128)(2,1)S(1)} %collective-permute-done.14.refs_2_), channel_id=1, source_target_pairs={{0,4},{4,0},{8,12},{12,8},{16,20},{20,16},{24,28},{28,24},{1,5},{5... | collective-permute-start | bytes 4718600 | tf_op jit(solution)/shard_map/ppermute | solution.py:195
  107.9 34.5 %collective-permute-start.15 = (bf16[768,512]{1,0:T(8,128)(2,1)S(1)}, bf16[768,512]{1,0:T(8,128)(2,1)S(1)}, u32[]{:S(2)}, u32[]{:S(2)}) collective-permute-start(bf16[768,512]{1,0:T(8,128)(2,1)S(1)} %bitcast.13), channel_id=1, source_target_pairs={{0,24},{4,28},{8,16},{12,20},{16,8},{20,12},{24,0},{28,4},{1,25},{... | collective-permute-start | bytes 2359304 | tf_op jit(solution)/shard_map/ppermute | solution.py:195
  122.3 8.4 %collective-permute-start.18 = (bf16[64,2048]{1,0:T(8,128)(2,1)S(1)}, bf16[64,2048]{1,0:T(8,128)(2,1)S(1)}, u32[]{:S(2)}, u32[]{:S(2)}) collective-permute-start(bf16[64,2048]{1,0:T(8,128)(2,1)S(1)} %collective-permute-done.13.x0), channel_id=1, source_target_pairs={{0,1},{1,0},{2,3},{3,2},{4,5},{5,4},{6,7},{7,6},{8,9},{9,8},{10,11... | collective-permute-start | bytes 786440 | tf_op jit(solution)/shard_map/ppermute | solution.py:195
  122.9 9.2 %collective-permute-start.19 = (bf16[64,2048]{1,0:T(8,128)(2,1)S(1)}, bf16[64,2048]{1,0:T(8,128)(2,1)S(1)}, u32[]{:S(2)}, u32[]{:S(2)}) collective-permute-start(bf16[64,2048]{1,0:T(8,128)(2,1)S(1)} %collective-permute-done.13.x0), channel_id=1, source_target_pairs={{0,2},{1,3},{2,0},{3,1},{4,6},{5,7},{6,4},{7,5},{8,10},{9,11},{10,... | collective-permute-start | bytes 786440 | tf_op jit(solution)/shard_map/ppermute | solution.py:195
  130.7 8.4 %collective-permute-start.20 = (bf16[64,2048]{1,0:T(8,128)(2,1)S(1)}, bf16[64,2048]{1,0:T(8,128)(2,1)S(1)}, u32[]{:S(2)}, u32[]{:S(2)}) collective-permute-start(bf16[64,2048]{1,0:T(8,128)(2,1)S(1)} %collective-permute-done.13.x0), channel_id=1, source_target_pairs={{0,3},{1,2},{2,1},{3,0},{4,7},{5,6},{6,5},{7,4},{8,11},{9,10},{10,... | collective-permute-start | bytes 786440 | tf_op jit(solution)/shard_map/ppermute | solution.py:195
  142.2 17.9 %collective-permute-start.21 = (bf16[256,1536]{1,0:T(8,128)(2,1)S(1)}, bf16[256,1536]{1,0:T(8,128)(2,1)S(1)}, u32[]{:S(2)}, u32[]{:S(2)}) collective-permute-start(bf16[256,1536]{1,0:T(8,128)(2,1)S(1)} %enter.3), channel_id=1, source_target_pairs={{0,8},{4,12},{8,0},{12,4},{16,24},{20,28},{24,16},{28,20},{1,9},{5... | collective-permute-start | bytes 2359304 | tf_op jit(solution)/shard_map/ppermute | solution.py:195
  142.3 18.5 %collective-permute-start.22 = (bf16[768,512]{1,0:T(8,128)(2,1)S(1)}, bf16[768,512]{1,0:T(8,128)(2,1)S(1)}, u32[]{:S(2)}, u32[]{:S(2)}) collective-permute-start(bf16[768,512]{1,0:T(8,128)(2,1)S(1)} %bitcast.14), channel_id=1, source_target_pairs={{0,4},{4,0},{8,12},{12,8},{16,20},{20,16},{24,28},{28,24},{1,5},{5... | collective-permute-start | bytes 2359304 | tf_op jit(solution)/shard_map/ppermute | solution.py:195
  142.4 18.4 %collective-permute-start.23 = (bf16[768,512]{1,0:T(8,128)(2,1)S(1)}, bf16[768,512]{1,0:T(8,128)(2,1)S(1)}, u32[]{:S(2)}, u32[]{:S(2)}) collective-permute-start(bf16[768,512]{1,0:T(8,128)(2,1)S(1)} %collective-permute-done.15.d2), channel_id=1, source_target_pairs={{0,4},{4,0},{8,12},{12,8},{16,20},{20,16},{24,28},{28,24},{1,5},{5... | collective-permute-start | bytes 2359304 | tf_op jit(solution)/shard_map/ppermute | solution.py:195
  160.4 9.1 %collective-permute-start.24 = (bf16[256,768]{1,0:T(8,128)(2,1)S(1)}, bf16[256,768]{1,0:T(8,128)(2,1)S(1)}, u32[]{:S(2)}, u32[]{:S(2)}) collective-permute-start(bf16[256,768]{1,0:T(8,128)(2,1)S(1)} %silu.1.hidden), channel_id=1, source_target_pairs={{0,8},{4,12},{8,0},{12,4},{16,24},{20,28},{24,16},{28,20},{1,9},{5... | collective-permute-start | bytes 1179656 | tf_op jit(solution)/shard_map/ppermute | solution.py:195
  162.5 6.4 %collective-permute-start.25 = (bf16[64,2048]{1,0:T(8,128)(2,1)S(1)}, bf16[64,2048]{1,0:T(8,128)(2,1)S(1)}, u32[]{:S(2)}, u32[]{:S(2)}) collective-permute-start(bf16[64,2048]{1,0:T(8,128)(2,1)S(1)} %get-tuple-element.73), channel_id=1, source_target_pairs={{0,1},{1,0},{2,3},{3,2},{4,5},{5,4},{6,7},{7,6},{8,9},{9,8},{10,11... | collective-permute-start | bytes 786440 | tf_op jit(solution)/shard_map/ppermute | solution.py:195
  163.1 11.7 %copy-start.2 = (f32[64,128]{1,0:T(8,128)S(1)}, f32[64,128]{1,0:T(8,128)}, u32[]{:S(2)}) copy-start(f32[64,128]{1,0:T(8,128)} %select_add_fusion.shares) | copy-start | bytes 98308
  163.2 6.4 %collective-permute-start.26 = (bf16[64,2048]{1,0:T(8,128)(2,1)S(1)}, bf16[64,2048]{1,0:T(8,128)(2,1)S(1)}, u32[]{:S(2)}, u32[]{:S(2)}) collective-permute-start(bf16[64,2048]{1,0:T(8,128)(2,1)S(1)} %get-tuple-element.74), channel_id=1, source_target_pairs={{0,2},{1,3},{2,0},{3,1},{4,6},{5,7},{6,4},{7,5},{8,10},{9,11},{10,... | collective-permute-start | bytes 786440 | tf_op jit(solution)/shard_map/ppermute | solution.py:195
  171.3 10.3 %collective-permute-start.31 = (bf16[64,2048]{1,0:T(8,128)(2,1)S(1)}, bf16[64,2048]{1,0:T(8,128)(2,1)S(1)}, u32[]{:S(2)}, u32[]{:S(2)}) collective-permute-start(bf16[64,2048]{1,0:T(8,128)(2,1)S(1)} %get-tuple-element.82), channel_id=1, source_target_pairs={{0,3},{1,2},{2,1},{3,0},{4,7},{5,6},{6,5},{7,4},{8,11},{9,10},{10,... | collective-permute-start | bytes 786440 | tf_op jit(solution)/shard_map/ppermute | solution.py:195
  172.8 12.4 %collective-permute-start.30 = (bf16[64,2048]{1,0:T(8,128)(2,1)S(1)}, bf16[64,2048]{1,0:T(8,128)(2,1)S(1)}, u32[]{:S(2)}, u32[]{:S(2)}) collective-permute-start(bf16[64,2048]{1,0:T(8,128)(2,1)S(1)} %get-tuple-element.81), channel_id=1, source_target_pairs={{0,2},{1,3},{2,0},{3,1},{4,6},{5,7},{6,4},{7,5},{8,10},{9,11},{10,... | collective-permute-start | bytes 786440 | tf_op jit(solution)/shard_map/ppermute | solution.py:195
  174.3 11.0 %collective-permute-start.29 = (bf16[64,2048]{1,0:T(8,128)(2,1)S(1)}, bf16[64,2048]{1,0:T(8,128)(2,1)S(1)}, u32[]{:S(2)}, u32[]{:S(2)}) collective-permute-start(bf16[64,2048]{1,0:T(8,128)(2,1)S(1)} %get-tuple-element.80), channel_id=1, source_target_pairs={{0,1},{1,0},{2,3},{3,2},{4,5},{5,4},{6,7},{7,6},{8,9},{9,8},{10,11... | collective-permute-start | bytes 786440 | tf_op jit(solution)/shard_map/ppermute | solution.py:195
  174.8 3.9 %collective-permute-start.28 = (f32[64,128]{1,0:T(8,128)S(1)}, f32[64,128]{1,0:T(8,128)S(1)}, u32[]{:S(2)}, u32[]{:S(2)}) collective-permute-start(f32[64,128]{1,0:T(8,128)S(1)} %copy-done.2), channel_id=1, source_target_pairs={{0,8},{4,12},{8,0},{12,4},{16,24},{20,28},{24,16},{28,20},{1,9},{5... | collective-permute-start | bytes 98312 | tf_op jit(solution)/shard_map/ppermute | solution.py:195
  179.0 9.2 %collective-permute-start.27 = (bf16[64,2048]{1,0:T(8,128)(2,1)S(1)}, bf16[64,2048]{1,0:T(8,128)(2,1)S(1)}, u32[]{:S(2)}, u32[]{:S(2)}) collective-permute-start(bf16[64,2048]{1,0:T(8,128)(2,1)S(1)} %get-tuple-element.77), channel_id=1, source_target_pairs={{0,3},{1,2},{2,1},{3,0},{4,7},{5,6},{6,5},{7,4},{8,11},{9,10},{10,... | collective-permute-start | bytes 786440 | tf_op jit(solution)/shard_map/ppermute | solution.py:195
  185.6 6.4 %collective-permute-start.32 = (bf16[64,2048]{1,0:T(8,128)(2,1)S(1)}, bf16[64,2048]{1,0:T(8,128)(2,1)S(1)}, u32[]{:S(2)}, u32[]{:S(2)}) collective-permute-start(bf16[64,2048]{1,0:T(8,128)(2,1)S(1)} %add_convert_fusion), channel_id=1, source_target_pairs={{0,8},{4,12},{8,0},{12,4},{16,24},{20,28},{24,16},{28,20},{1,9},{5... | collective-permute-start | bytes 786440 | tf_op jit(solution)/shard_map/ppermute | solution.py:195

commit v8 on v6

--- a/solution.py
+++ b/solution.py
@@ -509,24 +509,26 @@
         shares = shares + jnp.where(lane == named, gate_weights[:, k : k + 1], 0.0)
 
     p = attention(index, queries, pieces, w_out)
-    p, shares, pair_here, down_here = lax.optimization_barrier((p, shares, pair_here, down_here))
+    p, shares, pair_near, down_here = lax.optimization_barrier(
+        (p, shares, swap(pair_here, "ctx", 1), down_here)
+    )
     r = [swap(p[b], "exp", b) for b in (1, 2, 3)]
-    pair_near, down_near = swap(pair_here, "ctx", 1), swap(down_here, "ctx", 1)
+    down_near = swap(down_here, "ctx", 1)
     other_shares = swap(shares, "ctx", 2)
     state, mine, theirs = norm(index, p[0], *r, residual, norm_gain.reshape(1, D))
     others = swap(theirs, "ctx", 2)
     own_rows = [mine] + [swap(mine, "exp", b) for b in (1, 2, 3)]
     others, own_rows[1:3] = lax.optimization_barrier((others, own_rows[1:3]))
     other_rows = [others] + [swap(others, "exp", b) for b in (1, 2, 3)]
-    own_rows, other_rows, pair_far, down_here = lax.optimization_barrier(
-        (own_rows, other_rows, pair_far, down_here)
+    own_rows, other_rows[1:3], pair_far, down_here = lax.optimization_barrier(
+        (own_rows, other_rows[1:3], pair_far, down_here)
     )
     down_far = swap(down_here, "ctx", 6)
     pairs = (pair_here, pair_near, pair_far, swap(pair_far, "ctx", 1))
     other_pre = enter(other_rows, pairs, BF16)
     from_other = swap(other_pre, "ctx", 2)
-    own_rows, down_far = lax.optimization_barrier((own_rows, down_far))
     own_pre = enter(own_rows, pairs, F32)
+    own_pre, down_far = lax.optimization_barrier((own_pre, down_far))
     own_hidden = silu(own_pre, from_other)
     other_hidden = swap(own_hidden, "ctx", 2)
     downs = (down_here, down_near, down_far, swap(down_far, "ctx", 1))

time: 178 us -> 180 us (1.011)
  waiting for transfers between devices: 97.5 us -> 88.4 us
  local copies, waits for them, and re-layouts: 1.14 us -> 8.26 us
  starting transfers between devices: 49.1 us -> 53.1 us
    ppermute x30, waiting for transfers between devices: 94.9 us -> 85 us  [swap(): return lax.ppermute(array, axis, [(i, i ^ mask) for i in range(size)])]
    unnamed x8 -> x30, local copies, waits for them, and re-layouts: 0.02 us -> 7.14 us
    ppermute x30, starting transfers between devices: 38.3 us -> 42.4 us  [swap(): return lax.ppermute(array, axis, [(i, i ^ mask) for i in range(size)])]
  transfers between devices with their start and end apart: 33 -> 33, of which waited for: 17 -> 17; matrix products, arithmetic and copies ran while one was open for 2% -> 1% of each run, Pallas kernels for 13% -> 13%
where the time goes in v8:
time: 180 us
  waiting for transfers between devices  88.4 us (49%)
  starting transfers between devices  53.1 us (30%)
  Pallas kernels  27.5 us (15%)
  local copies, waits for them, and re-layouts  8.26 us (5%)
  other arithmetic  2 us (1%)
    ppermute x30, waiting for transfers between devices, swap(): return lax.ppermute(array, axis, [(i, i ^ mask) for i in range(size)])  85 us
    ppermute x30, starting transfers between devices, swap(): return lax.ppermute(array, axis, [(i, i ^ mask) for i in range(size)])  42.4 us
    pallas_call x1, Pallas kernels, attention(): pl.pallas_call(attention_kernel, out_shape=[jax.ShapeDtypeStruct((rows, D...  14.7 us
    ppermute x3, starting transfers between devices, later(): lax.ppermute(array, 'ctx', [(i, i + 2 * chips) for i in range(8 - 2 * chi...  10.7 us
    unnamed x30, local copies, waits for them, and re-layouts  7.14 us
    pallas_call x2, Pallas kernels, enter(): pl.pallas_call(enter_kernel, out_shape=jax.ShapeDtypeStruct((count, 2 * w...  6.1 us
  transfers between devices with their start and end apart: 33, of which 17 were waited for; matrix products, arithmetic and copies ran while one was open for 1% of the time, Pallas kernels for 13%

profile of v8, /device:TPU:0, one launch (start us, length us, event | category | flops | bytes accessed | tf_op | source)
XLA Modules:
  0.0 179.5 jit_solution(16669110371881329413)
XLA Ops:
  0.0 0.9 constant_dynamic-slice_fusion
  0.9 4.9 %collective-permute-start.1 = (bf16[256,256]{1,0:T(8,128)(2,1)S(1)}, bf16[256,256]{1,0:T(8,128)(2,1)S(1)}, u32[]{:S(2)}, u32[]{:S(2)}) collective-permute-start(bf16[256,256]{1,0:T(8,128)(2,1)S(1)} %pad_maximum_fusion.1.refs_0_), channel_id=1, source_target_pairs={{0,8},{4,12},{8,16},{12,20},{16,24},{20,28},{1,9},{5,13},{9,17},{1... | collective-permute-start | bytes 393224 | tf_op jit(solution)/shard_map/ppermute | solution.py:496
  5.9 4.5 %collective-permute-start.3 = (bf16[256,256]{1,0:T(8,128)(2,1)S(1)}, bf16[256,256]{1,0:T(8,128)(2,1)S(1)}, u32[]{:S(2)}, u32[]{:S(2)}) collective-permute-start(bf16[256,256]{1,0:T(8,128)(2,1)S(1)} %pad_maximum_fusion.1.refs_0_), channel_id=1, source_target_pairs={{0,16},{4,20},{8,24},{12,28},{1,17},{5,21},{9,25},{13,29},{2,18},{... | collective-permute-start | bytes 393224 | tf_op jit(solution)/shard_map/ppermute | solution.py:496
  10.4 1.3 collective-permute-start.5
  11.8 0.5 collective-permute-start.2
  12.3 2.0 %collective-permute-done.3.refs_4_ = bf16[256,256]{1,0:T(8,128)(2,1)S(1)} collective-permute-done((bf16[256,256]{1,0:T(8,128)(2,1)S(1)}, bf16[256,256]{1,0:T(8,128)(2,1)S(1)}, u32[]{:S(2)}, u32[]{:S(2)}) %collective-permute-start.3) | collective-permute-done | bytes 131104 | tf_op jit(solution)/shard_map/ppermute | solution.py:496
  14.3 1.4 collective-permute-done.5.refs_6_
  15.7 1.5 pad_maximum_fusion.refs_0_
  17.3 0.6 copy-done.4
  17.9 0.7 copy-done.6
  18.6 0.6 copy-done.8
  19.2 0.6 copy-done.10
  19.9 0.5 collective-permute-start.7
  20.3 5.9 %collective-permute-start.17 = (bf16[1024,768]{1,0:T(8,128)(2,1)S(1)}, bf16[1024,768]{1,0:T(8,128)(2,1)S(1)}, u32[]{:S(2)}, u32[]{:S(2)}) collective-permute-start(bf16[1024,768]{1,0:T(8,128)(2,1)S(1)} %pad_maximum_fusion.refs_0_), channel_id=1, source_target_pairs={{0,24},{4,28},{8,16},{12,20},{16,8},{20,12},{24,0},{28,4},{1,25},{... | collective-permute-start | bytes 4718600 | tf_op jit(solution)/shard_map/ppermute | solution.py:195
  26.3 0.1 select_add_fusion.shares
  26.4 0.9 copy-done.3
  27.3 0.9 copy-done.5
  28.2 0.9 copy-done.7
  29.1 0.9 copy-done.9
  30.0 0.9 copy-done.11
  30.9 14.7 %attention.1 = (bf16[64,4096]{1,0:T(8,128)(2,1)S(1)}, bf16[64,4096]{1,0:T(8,128)(2,1)}, bf16[64,4096]{1,0:T(8,128)(2,1)}, bf16[64,4096]{1,0:T(8,128)(2,1)}) custom-call(s32[2]{0:T(128)S(1)} %pad_add_fusion.index, bf16[256,2048]{1,0:T(8,128)(2,1)} %q_hbm.1, bf16[256,256]{1,0:T(8,128)(2,1)S(1)} %pad_maximum_fusion.1.refs_0_, bf16[256,256]{1,0:T(8,128)(2,1)S(1)} %copy-done.5, ...), custom_call_target="tpu_custom_call" | custom-call | flops 1000 | bytes 1000 | tf_op jit(solution)/shard_map/attention/pallas_call | solution.py:296
  45.7 2.5 %collective-permute-start.10 = (bf16[64,4096]{1,0:T(8,128)(2,1)}, bf16[64,4096]{1,0:T(8,128)(2,1)S(1)}, u32[]{:S(2)}, u32[]{:S(2)}) collective-permute-start(bf16[64,4096]{1,0:T(8,128)(2,1)} %get-tuple-element.74), channel_id=1, source_target_pairs={{0,3},{1,2},{2,1},{3,0},{4,7},{5,6},{6,5},{7,4},{8,11},{9,10},{10,... | collective-permute-start | bytes 1572872 | tf_op jit(solution)/shard_map/ppermute | solution.py:195
  48.2 0.5 collective-permute-start.8
  48.7 0.5 collective-permute-start.9
  49.2 12.4 %collective-permute-done.10.r3 = bf16[64,4096]{1,0:T(8,128)(2,1)S(1)} collective-permute-done((bf16[64,4096]{1,0:T(8,128)(2,1)}, bf16[64,4096]{1,0:T(8,128)(2,1)S(1)}, u32[]{:S(2)}, u32[]{:S(2)}) %collective-permute-start.10) | collective-permute-done | bytes 524320 | tf_op jit(solution)/shard_map/ppermute | solution.py:195
  61.7 10.5 %collective-permute-done.8.r1 = bf16[64,4096]{1,0:T(8,128)(2,1)S(1)} collective-permute-done((bf16[64,4096]{1,0:T(8,128)(2,1)}, bf16[64,4096]{1,0:T(8,128)(2,1)S(1)}, u32[]{:S(2)}, u32[]{:S(2)}) %collective-permute-start.8) | collective-permute-done | bytes 524320 | tf_op jit(solution)/shard_map/ppermute | solution.py:195
  72.2 1.2 norm.1
  73.4 1.6 collective-permute-start.12
  75.0 1.4 collective-permute-start.13
  76.4 0.6 collective-permute-start.14
  77.0 4.6 %collective-permute-done.11.x0 = bf16[64,2048]{1,0:T(8,128)(2,1)S(1)} collective-permute-done((bf16[64,2048]{1,0:T(8,128)(2,1)S(1)}, bf16[64,2048]{1,0:T(8,128)(2,1)S(1)}, u32[]{:S(2)}, u32[]{:S(2)}) %collective-permute-start.11) | collective-permute-done | bytes 262176 | tf_op jit(solution)/shard_map/ppermute | solution.py:195
  81.5 1.1 collective-permute-done.12.x1
  82.7 5.9 %collective-permute-done.13.x2 = bf16[64,2048]{1,0:T(8,128)(2,1)S(1)} collective-permute-done((bf16[64,2048]{1,0:T(8,128)(2,1)S(1)}, bf16[64,2048]{1,0:T(8,128)(2,1)S(1)}, u32[]{:S(2)}, u32[]{:S(2)}) %collective-permute-start.13) | collective-permute-done | bytes 262176 | tf_op jit(solution)/shard_map/ppermute | solution.py:195
  88.6 2.5 %collective-permute-start.16 = (bf16[64,2048]{1,0:T(8,128)(2,1)S(1)}, bf16[64,2048]{1,0:T(8,128)(2,1)S(1)}, u32[]{:S(2)}, u32[]{:S(2)}) collective-permute-start(bf16[64,2048]{1,0:T(8,128)(2,1)S(1)} %collective-permute-done.11.x0), channel_id=1, source_target_pairs={{0,2},{1,3},{2,0},{3,1},{4,6},{5,7},{6,4},{7,5},{8,10},{9,11},{10,... | collective-permute-start | bytes 786440 | tf_op jit(solution)/shard_map/ppermute | solution.py:195
  91.0 3.9 %collective-permute-done.15.x1 = bf16[64,2048]{1,0:T(8,128)(2,1)S(1)} collective-permute-done((bf16[64,2048]{1,0:T(8,128)(2,1)S(1)}, bf16[64,2048]{1,0:T(8,128)(2,1)S(1)}, u32[]{:S(2)}, u32[]{:S(2)}) %collective-permute-start.15) | collective-permute-done | bytes 262176 | tf_op jit(solution)/shard_map/ppermute | solution.py:195
  94.9 0.5 collective-permute-done.16.x2
  95.4 7.4 %collective-permute-start.19 = (bf16[768,512]{1,0:T(8,128)(2,1)S(1)}, bf16[768,512]{1,0:T(8,128)(2,1)S(1)}, u32[]{:S(2)}, u32[]{:S(2)}) collective-permute-start(bf16[768,512]{1,0:T(8,128)(2,1)S(1)} %bitcast.13), channel_id=1, source_target_pairs={{0,24},{4,28},{8,16},{12,20},{16,8},{20,12},{24,0},{28,4},{1,25},{... | collective-permute-start | bytes 2359304 | tf_op jit(solution)/shard_map/ppermute | solution.py:195
  102.8 3.5 %collective-permute-start.20 = (bf16[64,2048]{1,0:T(8,128)(2,1)S(1)}, bf16[64,2048]{1,0:T(8,128)(2,1)S(1)}, u32[]{:S(2)}, u32[]{:S(2)}) collective-permute-start(bf16[64,2048]{1,0:T(8,128)(2,1)S(1)} %collective-permute-done.11.x0), channel_id=1, source_target_pairs={{0,3},{1,2},{2,1},{3,0},{4,7},{5,6},{6,5},{7,4},{8,11},{9,10},{10,... | collective-permute-start | bytes 786440 | tf_op jit(solution)/shard_map/ppermute | solution.py:195
  106.2 6.7 %collective-permute-done.20.x3 = bf16[64,2048]{1,0:T(8,128)(2,1)S(1)} collective-permute-done((bf16[64,2048]{1,0:T(8,128)(2,1)S(1)}, bf16[64,2048]{1,0:T(8,128)(2,1)S(1)}, u32[]{:S(2)}, u32[]{:S(2)}) %collective-permute-start.20) | collective-permute-done | bytes 262176 | tf_op jit(solution)/shard_map/ppermute | solution.py:195
  112.9 3.1 %enter.3 = bf16[256,1536]{1,0:T(8,128)(2,1)S(1)} custom-call(bf16[64,2048]{1,0:T(8,128)(2,1)S(1)} %collective-permute-done.11.x0, bf16[64,2048]{1,0:T(8,128)(2,1)S(1)} %collective-permute-done.15.x1, bf16[64,2048]{1,0:T(8,128)(2,1)S(1)} %collective-permute-done.16.x2, bf16[64,2048]{1,0:T(8,128)(2,1)S(1)} %collective-permute-done.20.x3, ...), custom_call_target="tpu_custom_call" | custom-call | flops 1000 | bytes 1000 | tf_op jit(solution)/shard_map/enter/pallas_call | solution.py:377
  116.0 0.8 collective-permute-start.21
  116.8 3.0 %enter.2.own = f32[256,1536]{1,0:T(8,128)S(1)} custom-call(bf16[64,2048]{1,0:T(8,128)(2,1)S(1)} %get-tuple-element.83.x0, bf16[64,2048]{1,0:T(8,128)(2,1)S(1)} %collective-permute-done.12.x1, bf16[64,2048]{1,0:T(8,128)(2,1)S(1)} %collective-permute-done.13.x2, bf16[64,2048]{1,0:T(8,128)(2,1)S(1)} %collective-permute-done.14.x3, ...), custom_call_target="tpu_custom_call" | custom-call | flops 1000 | bytes 1000 | tf_op jit(solution)/shard_map/enter/pallas_call | solution.py:377
  119.9 1.3 collective-permute-done.19.d2
  121.2 16.7 %collective-permute-done.21.other = bf16[256,1536]{1,0:T(8,128)(2,1)S(1)} collective-permute-done((bf16[256,1536]{1,0:T(8,128)(2,1)S(1)}, bf16[256,1536]{1,0:T(8,128)(2,1)S(1)}, u32[]{:S(2)}, u32[]{:S(2)}) %collective-permute-start.21) | collective-permute-done | bytes 786464 | tf_op jit(solution)/shard_map/ppermute | solution.py:195
  137.9 0.3 silu.1.hidden
  138.2 1.8 %collective-permute-start.24 = (bf16[256,768]{1,0:T(8,128)(2,1)S(1)}, bf16[256,768]{1,0:T(8,128)(2,1)S(1)}, u32[]{:S(2)}, u32[]{:S(2)}) collective-permute-start(bf16[256,768]{1,0:T(8,128)(2,1)S(1)} %silu.1.hidden), channel_id=1, source_target_pairs={{0,8},{4,12},{8,0},{12,4},{16,24},{20,28},{24,16},{28,20},{1,9},{5... | collective-permute-start | bytes 1179656 | tf_op jit(solution)/shard_map/ppermute | solution.py:195
  140.1 1.7 leave.2
  141.8 2.1 %collective-permute-start.25 = (bf16[64,2048]{1,0:T(8,128)(2,1)S(1)}, bf16[64,2048]{1,0:T(8,128)(2,1)S(1)}, u32[]{:S(2)}, u32[]{:S(2)}) collective-permute-start(bf16[64,2048]{1,0:T(8,128)(2,1)S(1)} %get-tuple-element.95), channel_id=1, source_target_pairs={{0,1},{1,0},{2,3},{3,2},{4,5},{5,4},{6,7},{7,6},{8,9},{9,8},{10,11... | collective-permute-start | bytes 786440 | tf_op jit(solution)/shard_map/ppermute | solution.py:195
  143.9 2.0 %collective-permute-start.26 = (bf16[64,2048]{1,0:T(8,128)(2,1)S(1)}, bf16[64,2048]{1,0:T(8,128)(2,1)S(1)}, u32[]{:S(2)}, u32[]{:S(2)}) collective-permute-start(bf16[64,2048]{1,0:T(8,128)(2,1)S(1)} %get-tuple-element.96), channel_id=1, source_target_pairs={{0,2},{1,3},{2,0},{3,1},{4,6},{5,7},{6,4},{7,5},{8,10},{9,11},{10,... | collective-permute-start | bytes 786440 | tf_op jit(solution)/shard_map/ppermute | solution.py:195
  145.9 3.9 %collective-permute-done.25.r1 = bf16[64,2048]{1,0:T(8,128)(2,1)S(1)} collective-permute-done((bf16[64,2048]{1,0:T(8,128)(2,1)S(1)}, bf16[64,2048]{1,0:T(8,128)(2,1)S(1)}, u32[]{:S(2)}, u32[]{:S(2)}) %collective-permute-start.25) | collective-permute-done | bytes 262176 | tf_op jit(solution)/shard_map/ppermute | solution.py:195
  149.8 1.7 collective-permute-done.26.r2
  151.5 1.7 leave.3
  153.3 0.4 collective-permute-start.29
  153.7 1.7 collective-permute-start.30
  155.4 1.4 collective-permute-start.31
  156.8 1.3 collective-permute-start.28
  158.1 2.6 %collective-permute-done.28 = f32[64,128]{1,0:T(8,128)S(1)} collective-permute-done((f32[64,128]{1,0:T(8,128)S(1)}, f32[64,128]{1,0:T(8,128)S(1)}, u32[]{:S(2)}, u32[]{:S(2)}) %collective-permute-start.28) | collective-permute-done | bytes 32800 | tf_op jit(solution)/shard_map/ppermute | solution.py:195
  160.7 0.2 slice_reduce_fusion.3
  161.0 1.6 collective-permute-start.27
  162.6 8.5 %collective-permute-done.30 = bf16[64,2048]{1,0:T(8,128)(2,1)S(1)} collective-permute-done((bf16[64,2048]{1,0:T(8,128)(2,1)S(1)}, bf16[64,2048]{1,0:T(8,128)(2,1)S(1)}, u32[]{:S(2)}, u32[]{:S(2)}) %collective-permute-start.30) | collective-permute-done | bytes 262176 | tf_op jit(solution)/shard_map/ppermute | solution.py:195
  171.1 0.3 add_convert_fusion
  171.3 1.8 %collective-permute-start.32 = (bf16[64,2048]{1,0:T(8,128)(2,1)S(1)}, bf16[64,2048]{1,0:T(8,128)(2,1)S(1)}, u32[]{:S(2)}, u32[]{:S(2)}) collective-permute-start(bf16[64,2048]{1,0:T(8,128)(2,1)S(1)} %add_convert_fusion), channel_id=1, source_target_pairs={{0,8},{4,12},{8,0},{12,4},{16,24},{20,28},{24,16},{28,20},{1,9},{5... | collective-permute-start | bytes 786440 | tf_op jit(solution)/shard_map/ppermute | solution.py:195
  173.1 4.6 %collective-permute-done.32.other = bf16[64,2048]{1,0:T(8,128)(2,1)S(1)} collective-permute-done((bf16[64,2048]{1,0:T(8,128)(2,1)S(1)}, bf16[64,2048]{1,0:T(8,128)(2,1)S(1)}, u32[]{:S(2)}, u32[]{:S(2)}) %collective-permute-start.32) | collective-permute-done | bytes 262176 | tf_op jit(solution)/shard_map/ppermute | solution.py:195
  177.8 1.7 final.1
  (50 shorter events, 0.4 us)
Async XLA Ops:
  0.9 19.4 %copy-start.13 = (s32[64,2]{0,1:T(2,128)S(1)}, s32[64,2]{0,1:T(2,128)}, u32[]{:S(2)}) copy-start(s32[64,2]{0,1:T(2,128)} %param.17) | copy-start | bytes 1540
  0.9 25.3 %copy-start.14 = (f32[64,2]{0,1:T(2,128)S(1)}, f32[64,2]{0,1:T(2,128)}, u32[]{:S(2)}) copy-start(f32[64,2]{0,1:T(2,128)} %param.18) | copy-start | bytes 1540
  0.9 10.8 %collective-permute-start.1 = (bf16[256,256]{1,0:T(8,128)(2,1)S(1)}, bf16[256,256]{1,0:T(8,128)(2,1)S(1)}, u32[]{:S(2)}, u32[]{:S(2)}) collective-permute-start(bf16[256,256]{1,0:T(8,128)(2,1)S(1)} %pad_maximum_fusion.1.refs_0_), channel_id=1, source_target_pairs={{0,8},{4,12},{8,16},{12,20},{16,24},{20,28},{1,9},{5,13},{9,17},{1... | collective-permute-start | bytes 393224 | tf_op jit(solution)/shard_map/ppermute | solution.py:496
  5.9 8.4 %collective-permute-start.3 = (bf16[256,256]{1,0:T(8,128)(2,1)S(1)}, bf16[256,256]{1,0:T(8,128)(2,1)S(1)}, u32[]{:S(2)}, u32[]{:S(2)}) collective-permute-start(bf16[256,256]{1,0:T(8,128)(2,1)S(1)} %pad_maximum_fusion.1.refs_0_), channel_id=1, source_target_pairs={{0,16},{4,20},{8,24},{12,28},{1,17},{5,21},{9,25},{13,29},{2,18},{... | collective-permute-start | bytes 393224 | tf_op jit(solution)/shard_map/ppermute | solution.py:496
  10.4 5.3 %collective-permute-start.5 = (bf16[256,256]{1,0:T(8,128)(2,1)S(1)}, bf16[256,256]{1,0:T(8,128)(2,1)S(1)}, u32[]{:S(2)}, u32[]{:S(2)}) collective-permute-start(bf16[256,256]{1,0:T(8,128)(2,1)S(1)} %pad_maximum_fusion.1.refs_0_), channel_id=1, source_target_pairs={{0,24},{4,28},{1,25},{5,29},{2,26},{6,30},{3,27},{7,31}} | collective-permute-start | bytes 393224 | tf_op jit(solution)/shard_map/ppermute | solution.py:496
  11.7 5.5 %collective-permute-start = (bf16[256,256]{1,0:T(8,128)(2,1)S(1)}, bf16[256,256]{1,0:T(8,128)(2,1)S(1)}, u32[]{:S(2)}, u32[]{:S(2)}) collective-permute-start(bf16[256,256]{1,0:T(8,128)(2,1)S(1)} %pad_maximum_fusion.1.refs_0_), channel_id=1, source_target_pairs={{0,4},{4,0},{8,12},{12,8},{16,20},{20,16},{24,28},{28,24},{1,5},{5... | collective-permute-start | bytes 393224 | tf_op jit(solution)/shard_map/ppermute | solution.py:195
  11.8 6.1 %collective-permute-start.2 = (bf16[256,256]{1,0:T(8,128)(2,1)S(1)}, bf16[256,256]{1,0:T(8,128)(2,1)S(1)}, u32[]{:S(2)}, u32[]{:S(2)}) collective-permute-start(bf16[256,256]{1,0:T(8,128)(2,1)S(1)} %collective-permute-done.1.refs_2_), channel_id=1, source_target_pairs={{0,4},{4,0},{8,12},{12,8},{16,20},{20,16},{24,28},{28,24},{1,5},{5... | collective-permute-start | bytes 393224 | tf_op jit(solution)/shard_map/ppermute | solution.py:195
  14.3 4.3 %collective-permute-start.4 = (bf16[256,256]{1,0:T(8,128)(2,1)S(1)}, bf16[256,256]{1,0:T(8,128)(2,1)S(1)}, u32[]{:S(2)}, u32[]{:S(2)}) collective-permute-start(bf16[256,256]{1,0:T(8,128)(2,1)S(1)} %collective-permute-done.3.refs_4_), channel_id=1, source_target_pairs={{0,4},{4,0},{8,12},{12,8},{16,20},{20,16},{24,28},{28,24},{1,5},{5... | collective-permute-start | bytes 393224 | tf_op jit(solution)/shard_map/ppermute | solution.py:195
  15.7 1.5 copy-start.2
  15.7 3.5 %collective-permute-start.6 = (bf16[256,256]{1,0:T(8,128)(2,1)S(1)}, bf16[256,256]{1,0:T(8,128)(2,1)S(1)}, u32[]{:S(2)}, u32[]{:S(2)}) collective-permute-start(bf16[256,256]{1,0:T(8,128)(2,1)S(1)} %collective-permute-done.5.refs_6_), channel_id=1, source_target_pairs={{0,4},{4,0},{8,12},{12,8},{16,20},{20,16},{24,28},{28,24},{1,5},{5... | collective-permute-start | bytes 393224 | tf_op jit(solution)/shard_map/ppermute | solution.py:195
  17.2 0.7 copy-start.4
  17.9 0.7 copy-start.6
  18.6 0.7 copy-start.8
  19.2 0.6 copy-start.10
  19.9 25.8 %collective-permute-start.7 = (bf16[1024,768]{1,0:T(8,128)(2,1)S(1)}, bf16[1024,768]{1,0:T(8,128)(2,1)S(1)}, u32[]{:S(2)}, u32[]{:S(2)}) collective-permute-start(bf16[1024,768]{1,0:T(8,128)(2,1)S(1)} %pad_maximum_fusion.refs_0_), channel_id=1, source_target_pairs={{0,4},{4,0},{8,12},{12,8},{16,20},{20,16},{24,28},{28,24},{1,5},{5... | collective-permute-start | bytes 4718600 | tf_op jit(solution)/shard_map/ppermute | solution.py:195
  20.3 70.7 %collective-permute-start.17 = (bf16[1024,768]{1,0:T(8,128)(2,1)S(1)}, bf16[1024,768]{1,0:T(8,128)(2,1)S(1)}, u32[]{:S(2)}, u32[]{:S(2)}) collective-permute-start(bf16[1024,768]{1,0:T(8,128)(2,1)S(1)} %pad_maximum_fusion.refs_0_), channel_id=1, source_target_pairs={{0,24},{4,28},{8,16},{12,20},{16,8},{20,12},{24,0},{28,4},{1,25},{... | collective-permute-start | bytes 4718600 | tf_op jit(solution)/shard_map/ppermute | solution.py:195
  26.4 0.9 copy-start.3
  27.3 0.9 copy-start.5
  28.2 0.9 copy-start.7
  29.1 0.9 copy-start.9
  30.0 0.9 copy-start.11
  30.9 18.3 %copy-start.12 = (bf16[4096]{0:T(1024)(128)(2,1)S(1)}, bf16[4096]{0:T(1024)(128)(2,1)}, u32[]{:S(2)}) copy-start(bf16[4096]{0:T(1024)(128)(2,1)} %param.16) | copy-start | bytes 24580
  30.9 41.3 %copy-start.1 = (bf16[64,4096]{1,0:T(8,128)(2,1)S(1)}, bf16[64,4096]{1,0:T(8,128)(2,1)}, u32[]{:S(2)}) copy-start(bf16[64,4096]{1,0:T(8,128)(2,1)} %residual.1) | copy-start | bytes 1572868
  45.6 49.8 %copy-start = (bf16[1,768,512]{2,1,0:T(8,128)(2,1)S(1)}, bf16[1,768,512]{2,1,0:T(8,128)(2,1)}, u32[]{:S(2)}) copy-start(bf16[1,768,512]{2,1,0:T(8,128)(2,1)} %param.21) | copy-start | bytes 2359300
  45.7 16.0 %collective-permute-start.10 = (bf16[64,4096]{1,0:T(8,128)(2,1)}, bf16[64,4096]{1,0:T(8,128)(2,1)S(1)}, u32[]{:S(2)}, u32[]{:S(2)}) collective-permute-start(bf16[64,4096]{1,0:T(8,128)(2,1)} %get-tuple-element.74), channel_id=1, source_target_pairs={{0,3},{1,2},{2,1},{3,0},{4,7},{5,6},{6,5},{7,4},{8,11},{9,10},{10,... | collective-permute-start | bytes 1572872 | tf_op jit(solution)/shard_map/ppermute | solution.py:195
  48.2 24.0 %collective-permute-start.8 = (bf16[64,4096]{1,0:T(8,128)(2,1)}, bf16[64,4096]{1,0:T(8,128)(2,1)S(1)}, u32[]{:S(2)}, u32[]{:S(2)}) collective-permute-start(bf16[64,4096]{1,0:T(8,128)(2,1)} %get-tuple-element.72), channel_id=1, source_target_pairs={{0,1},{1,0},{2,3},{3,2},{4,5},{5,4},{6,7},{7,6},{8,9},{9,8},{10,11... | collective-permute-start | bytes 1572872 | tf_op jit(solution)/shard_map/ppermute | solution.py:195
  48.7 23.4 %collective-permute-start.9 = (bf16[64,4096]{1,0:T(8,128)(2,1)}, bf16[64,4096]{1,0:T(8,128)(2,1)S(1)}, u32[]{:S(2)}, u32[]{:S(2)}) collective-permute-start(bf16[64,4096]{1,0:T(8,128)(2,1)} %get-tuple-element.73), channel_id=1, source_target_pairs={{0,2},{1,3},{2,0},{3,1},{4,6},{5,7},{6,4},{7,5},{8,10},{9,11},{10,... | collective-permute-start | bytes 1572872 | tf_op jit(solution)/shard_map/ppermute | solution.py:195
  73.3 8.2 %collective-permute-start.11 = (bf16[64,2048]{1,0:T(8,128)(2,1)S(1)}, bf16[64,2048]{1,0:T(8,128)(2,1)S(1)}, u32[]{:S(2)}, u32[]{:S(2)}) collective-permute-start(bf16[64,2048]{1,0:T(8,128)(2,1)S(1)} %get-tuple-element.78), channel_id=1, source_target_pairs={{0,8},{4,12},{8,0},{12,4},{16,24},{20,28},{24,16},{28,20},{1,9},{5... | collective-permute-start | bytes 786440 | tf_op jit(solution)/shard_map/ppermute | solution.py:195
  73.4 9.3 %collective-permute-start.12 = (bf16[64,2048]{1,0:T(8,128)(2,1)S(1)}, bf16[64,2048]{1,0:T(8,128)(2,1)S(1)}, u32[]{:S(2)}, u32[]{:S(2)}) collective-permute-start(bf16[64,2048]{1,0:T(8,128)(2,1)S(1)} %get-tuple-element.83.x0), channel_id=1, source_target_pairs={{0,1},{1,0},{2,3},{3,2},{4,5},{5,4},{6,7},{7,6},{8,9},{9,8},{10,11... | collective-permute-start | bytes 786440 | tf_op jit(solution)/shard_map/ppermute | solution.py:195
  75.0 13.6 %collective-permute-start.13 = (bf16[64,2048]{1,0:T(8,128)(2,1)S(1)}, bf16[64,2048]{1,0:T(8,128)(2,1)S(1)}, u32[]{:S(2)}, u32[]{:S(2)}) collective-permute-start(bf16[64,2048]{1,0:T(8,128)(2,1)S(1)} %get-tuple-element.83.x0), channel_id=1, source_target_pairs={{0,2},{1,3},{2,0},{3,1},{4,6},{5,7},{6,4},{7,5},{8,10},{9,11},{10,... | collective-permute-start | bytes 786440 | tf_op jit(solution)/shard_map/ppermute | solution.py:195
  76.4 14.7 %collective-permute-start.14 = (bf16[64,2048]{1,0:T(8,128)(2,1)S(1)}, bf16[64,2048]{1,0:T(8,128)(2,1)S(1)}, u32[]{:S(2)}, u32[]{:S(2)}) collective-permute-start(bf16[64,2048]{1,0:T(8,128)(2,1)S(1)} %get-tuple-element.83.x0), channel_id=1, source_target_pairs={{0,3},{1,2},{2,1},{3,0},{4,7},{5,6},{6,5},{7,4},{8,11},{9,10},{10,... | collective-permute-start | bytes 786440 | tf_op jit(solution)/shard_map/ppermute | solution.py:195
  88.6 6.4 %collective-permute-start.15 = (bf16[64,2048]{1,0:T(8,128)(2,1)S(1)}, bf16[64,2048]{1,0:T(8,128)(2,1)S(1)}, u32[]{:S(2)}, u32[]{:S(2)}) collective-permute-start(bf16[64,2048]{1,0:T(8,128)(2,1)S(1)} %collective-permute-done.11.x0), channel_id=1, source_target_pairs={{0,1},{1,0},{2,3},{3,2},{4,5},{5,4},{6,7},{7,6},{8,9},{9,8},{10,11... | collective-permute-start | bytes 786440 | tf_op jit(solution)/shard_map/ppermute | solution.py:195
  88.6 6.8 %collective-permute-start.16 = (bf16[64,2048]{1,0:T(8,128)(2,1)S(1)}, bf16[64,2048]{1,0:T(8,128)(2,1)S(1)}, u32[]{:S(2)}, u32[]{:S(2)}) collective-permute-start(bf16[64,2048]{1,0:T(8,128)(2,1)S(1)} %collective-permute-done.11.x0), channel_id=1, source_target_pairs={{0,2},{1,3},{2,0},{3,1},{4,6},{5,7},{6,4},{7,5},{8,10},{9,11},{10,... | collective-permute-start | bytes 786440 | tf_op jit(solution)/shard_map/ppermute | solution.py:195
  95.4 17.5 %collective-permute-start.18 = (bf16[1024,768]{1,0:T(8,128)(2,1)S(1)}, bf16[1024,768]{1,0:T(8,128)(2,1)S(1)}, u32[]{:S(2)}, u32[]{:S(2)}) collective-permute-start(bf16[1024,768]{1,0:T(8,128)(2,1)S(1)} %collective-permute-done.17.refs_2_), channel_id=1, source_target_pairs={{0,4},{4,0},{8,12},{12,8},{16,20},{20,16},{24,28},{28,24},{1,5},{5... | collective-permute-start | bytes 4718600 | tf_op jit(solution)/shard_map/ppermute | solution.py:195
  95.4 25.8 %collective-permute-start.19 = (bf16[768,512]{1,0:T(8,128)(2,1)S(1)}, bf16[768,512]{1,0:T(8,128)(2,1)S(1)}, u32[]{:S(2)}, u32[]{:S(2)}) collective-permute-start(bf16[768,512]{1,0:T(8,128)(2,1)S(1)} %bitcast.13), channel_id=1, source_target_pairs={{0,24},{4,28},{8,16},{12,20},{16,8},{20,12},{24,0},{28,4},{1,25},{... | collective-permute-start | bytes 2359304 | tf_op jit(solution)/shard_map/ppermute | solution.py:195
  102.8 10.2 %collective-permute-start.20 = (bf16[64,2048]{1,0:T(8,128)(2,1)S(1)}, bf16[64,2048]{1,0:T(8,128)(2,1)S(1)}, u32[]{:S(2)}, u32[]{:S(2)}) collective-permute-start(bf16[64,2048]{1,0:T(8,128)(2,1)S(1)} %collective-permute-done.11.x0), channel_id=1, source_target_pairs={{0,3},{1,2},{2,1},{3,0},{4,7},{5,6},{6,5},{7,4},{8,11},{9,10},{10,... | collective-permute-start | bytes 786440 | tf_op jit(solution)/shard_map/ppermute | solution.py:195
  116.0 21.9 %collective-permute-start.21 = (bf16[256,1536]{1,0:T(8,128)(2,1)S(1)}, bf16[256,1536]{1,0:T(8,128)(2,1)S(1)}, u32[]{:S(2)}, u32[]{:S(2)}) collective-permute-start(bf16[256,1536]{1,0:T(8,128)(2,1)S(1)} %enter.3), channel_id=1, source_target_pairs={{0,8},{4,12},{8,0},{12,4},{16,24},{20,28},{24,16},{28,20},{1,9},{5... | collective-permute-start | bytes 2359304 | tf_op jit(solution)/shard_map/ppermute | solution.py:195
  116.8 23.2 %collective-permute-start.22 = (bf16[768,512]{1,0:T(8,128)(2,1)S(1)}, bf16[768,512]{1,0:T(8,128)(2,1)S(1)}, u32[]{:S(2)}, u32[]{:S(2)}) collective-permute-start(bf16[768,512]{1,0:T(8,128)(2,1)S(1)} %bitcast.14), channel_id=1, source_target_pairs={{0,4},{4,0},{8,12},{12,8},{16,20},{20,16},{24,28},{28,24},{1,5},{5... | collective-permute-start | bytes 2359304 | tf_op jit(solution)/shard_map/ppermute | solution.py:195
  121.2 18.8 %collective-permute-start.23 = (bf16[768,512]{1,0:T(8,128)(2,1)S(1)}, bf16[768,512]{1,0:T(8,128)(2,1)S(1)}, u32[]{:S(2)}, u32[]{:S(2)}) collective-permute-start(bf16[768,512]{1,0:T(8,128)(2,1)S(1)} %collective-permute-done.19.d2), channel_id=1, source_target_pairs={{0,4},{4,0},{8,12},{12,8},{16,20},{20,16},{24,28},{28,24},{1,5},{5... | collective-permute-start | bytes 2359304 | tf_op jit(solution)/shard_map/ppermute | solution.py:195
  138.2 13.3 %collective-permute-start.24 = (bf16[256,768]{1,0:T(8,128)(2,1)S(1)}, bf16[256,768]{1,0:T(8,128)(2,1)S(1)}, u32[]{:S(2)}, u32[]{:S(2)}) collective-permute-start(bf16[256,768]{1,0:T(8,128)(2,1)S(1)} %silu.1.hidden), channel_id=1, source_target_pairs={{0,8},{4,12},{8,0},{12,4},{16,24},{20,28},{24,16},{28,20},{1,9},{5... | collective-permute-start | bytes 1179656 | tf_op jit(solution)/shard_map/ppermute | solution.py:195
  141.8 8.0 %collective-permute-start.25 = (bf16[64,2048]{1,0:T(8,128)(2,1)S(1)}, bf16[64,2048]{1,0:T(8,128)(2,1)S(1)}, u32[]{:S(2)}, u32[]{:S(2)}) collective-permute-start(bf16[64,2048]{1,0:T(8,128)(2,1)S(1)} %get-tuple-element.95), channel_id=1, source_target_pairs={{0,1},{1,0},{2,3},{3,2},{4,5},{5,4},{6,7},{7,6},{8,9},{9,8},{10,11... | collective-permute-start | bytes 786440 | tf_op jit(solution)/shard_map/ppermute | solution.py:195
  143.9 7.7 %collective-permute-start.26 = (bf16[64,2048]{1,0:T(8,128)(2,1)S(1)}, bf16[64,2048]{1,0:T(8,128)(2,1)S(1)}, u32[]{:S(2)}, u32[]{:S(2)}) collective-permute-start(bf16[64,2048]{1,0:T(8,128)(2,1)S(1)} %get-tuple-element.96), channel_id=1, source_target_pairs={{0,2},{1,3},{2,0},{3,1},{4,6},{5,7},{6,4},{7,5},{8,10},{9,11},{10,... | collective-permute-start | bytes 786440 | tf_op jit(solution)/shard_map/ppermute | solution.py:195
  153.3 9.3 %collective-permute-start.29 = (bf16[64,2048]{1,0:T(8,128)(2,1)S(1)}, bf16[64,2048]{1,0:T(8,128)(2,1)S(1)}, u32[]{:S(2)}, u32[]{:S(2)}) collective-permute-start(bf16[64,2048]{1,0:T(8,128)(2,1)S(1)} %get-tuple-element.102), channel_id=1, source_target_pairs={{0,1},{1,0},{2,3},{3,2},{4,5},{5,4},{6,7},{7,6},{8,9},{9,8},{10,11... | collective-permute-start | bytes 786440 | tf_op jit(solution)/shard_map/ppermute | solution.py:195
  153.7 17.3 %collective-permute-start.30 = (bf16[64,2048]{1,0:T(8,128)(2,1)S(1)}, bf16[64,2048]{1,0:T(8,128)(2,1)S(1)}, u32[]{:S(2)}, u32[]{:S(2)}) collective-permute-start(bf16[64,2048]{1,0:T(8,128)(2,1)S(1)} %get-tuple-element.103), channel_id=1, source_target_pairs={{0,2},{1,3},{2,0},{3,1},{4,6},{5,7},{6,4},{7,5},{8,10},{9,11},{10,... | collective-permute-start | bytes 786440 | tf_op jit(solution)/shard_map/ppermute | solution.py:195
  155.4 15.6 %collective-permute-start.31 = (bf16[64,2048]{1,0:T(8,128)(2,1)S(1)}, bf16[64,2048]{1,0:T(8,128)(2,1)S(1)}, u32[]{:S(2)}, u32[]{:S(2)}) collective-permute-start(bf16[64,2048]{1,0:T(8,128)(2,1)S(1)} %get-tuple-element.104), channel_id=1, source_target_pairs={{0,3},{1,2},{2,1},{3,0},{4,7},{5,6},{6,5},{7,4},{8,11},{9,10},{10,... | collective-permute-start | bytes 786440 | tf_op jit(solution)/shard_map/ppermute | solution.py:195
  156.8 3.9 %collective-permute-start.28 = (f32[64,128]{1,0:T(8,128)S(1)}, f32[64,128]{1,0:T(8,128)S(1)}, u32[]{:S(2)}, u32[]{:S(2)}) collective-permute-start(f32[64,128]{1,0:T(8,128)S(1)} %select_add_fusion.shares), channel_id=1, source_target_pairs={{0,8},{4,12},{8,0},{12,4},{16,24},{20,28},{24,16},{28,20},{1,9},{5... | collective-permute-start | bytes 98312 | tf_op jit(solution)/shard_map/ppermute | solution.py:195
  161.0 12.2 %collective-permute-start.27 = (bf16[64,2048]{1,0:T(8,128)(2,1)S(1)}, bf16[64,2048]{1,0:T(8,128)(2,1)S(1)}, u32[]{:S(2)}, u32[]{:S(2)}) collective-permute-start(bf16[64,2048]{1,0:T(8,128)(2,1)S(1)} %get-tuple-element.99), channel_id=1, source_target_pairs={{0,3},{1,2},{2,1},{3,0},{4,7},{5,6},{6,5},{7,4},{8,11},{9,10},{10,... | collective-permute-start | bytes 786440 | tf_op jit(solution)/shard_map/ppermute | solution.py:195
  171.3 6.4 %collective-permute-start.32 = (bf16[64,2048]{1,0:T(8,128)(2,1)S(1)}, bf16[64,2048]{1,0:T(8,128)(2,1)S(1)}, u32[]{:S(2)}, u32[]{:S(2)}) collective-permute-start(bf16[64,2048]{1,0:T(8,128)(2,1)S(1)} %add_convert_fusion), channel_id=1, source_target_pairs={{0,8},{4,12},{8,0},{12,4},{16,24},{20,28},{24,16},{28,20},{1,9},{5... | collective-permute-start | bytes 786440 | tf_op jit(solution)/shard_map/ppermute | solution.py:195

commit v9 on v7

--- a/solution.py
+++ b/solution.py
@@ -499,6 +499,7 @@
     moved = [later(kv_here, d) for d in (3, 2, 1)][::-1]
     pair_here, down_here = jnp.concatenate([gate_here, up_here], axis=0), w_down[0]
     pieces = [part for piece in [kv_here] + moved for part in (piece, swap(piece, "ctx", 1))]
+    pieces, pair_here = lax.optimization_barrier((pieces, pair_here))
     pair_far = swap(pair_here, "ctx", 6)
 
     lane = lax.broadcasted_iota(jnp.int32, (expert_ids.shape[0], HD), 1)
@@ -523,8 +524,8 @@
     pairs = (pair_here, pair_near, pair_far, swap(pair_far, "ctx", 1))
     other_pre = enter(other_rows, pairs, BF16)
     from_other = swap(other_pre, "ctx", 2)
-    own_rows, down_far = lax.optimization_barrier((own_rows, down_far))
     own_pre = enter(own_rows, pairs, F32)
+    own_pre, down_far = lax.optimization_barrier((own_pre, down_far))
     own_hidden = silu(own_pre, from_other)
     other_hidden = swap(own_hidden, "ctx", 2)
     downs = (down_here, down_near, down_far, swap(down_far, "ctx", 1))

time: 194 us -> 182 us (0.938)
  starting transfers between devices: 87.5 us -> 68.1 us
  waiting for transfers between devices: 75.5 us -> 82.9 us
    ppermute x30, starting transfers between devices: 75.9 us -> 57.4 us  [swap(): return lax.ppermute(array, axis, [(i, i ^ mask) for i in range(size)])]
    ppermute x30, waiting for transfers between devices: 73.3 us -> 79.5 us  [swap(): return lax.ppermute(array, axis, [(i, i ^ mask) for i in range(size)])]
  transfers between devices with their start and end apart: 33 -> 33, of which waited for: 15 -> 15; matrix products, arithmetic and copies ran while one was open for 1% -> 1% of each run, Pallas kernels for 12% -> 13%
where the time goes in v9:
time: 182 us
  waiting for transfers between devices  82.9 us (46%)
  starting transfers between devices  68.1 us (37%)
  Pallas kernels  27.5 us (15%)
  other arithmetic  1.95 us (1%)
    ppermute x30, waiting for transfers between devices, swap(): return lax.ppermute(array, axis, [(i, i ^ mask) for i in range(size)])  79.5 us
    ppermute x30, starting transfers between devices, swap(): return lax.ppermute(array, axis, [(i, i ^ mask) for i in range(size)])  57.4 us
    pallas_call x1, Pallas kernels, attention(): pl.pallas_call(attention_kernel, out_shape=[jax.ShapeDtypeStruct((rows, D...  14.7 us
    ppermute x3, starting transfers between devices, later(): lax.ppermute(array, 'ctx', [(i, i + 2 * chips) for i in range(8 - 2 * chi...  10.7 us
    pallas_call x2, Pallas kernels, enter(): pl.pallas_call(enter_kernel, out_shape=jax.ShapeDtypeStruct((count, 2 * w...  6.11 us
  transfers between devices with their start and end apart: 33, of which 15 were waited for; matrix products, arithmetic and copies ran while one was open for 1% of the time, Pallas kernels for 13%

profile of v9, /device:TPU:0, one launch (start us, length us, event | category | flops | bytes accessed | tf_op | source)
XLA Modules:
  0.0 181.8 jit_solution(9217657919847712466)
XLA Ops:
  0.0 0.9 constant_dynamic-slice_fusion
  0.9 4.9 %collective-permute-start.1 = (bf16[256,256]{1,0:T(8,128)(2,1)S(1)}, bf16[256,256]{1,0:T(8,128)(2,1)S(1)}, u32[]{:S(2)}, u32[]{:S(2)}) collective-permute-start(bf16[256,256]{1,0:T(8,128)(2,1)S(1)} %pad_maximum_fusion.1.refs_0_), channel_id=1, source_target_pairs={{0,8},{4,12},{8,16},{12,20},{16,24},{20,28},{1,9},{5,13},{9,17},{1... | collective-permute-start | bytes 393224 | tf_op jit(solution)/shard_map/ppermute | solution.py:496
  5.9 4.5 %collective-permute-start.3 = (bf16[256,256]{1,0:T(8,128)(2,1)S(1)}, bf16[256,256]{1,0:T(8,128)(2,1)S(1)}, u32[]{:S(2)}, u32[]{:S(2)}) collective-permute-start(bf16[256,256]{1,0:T(8,128)(2,1)S(1)} %pad_maximum_fusion.1.refs_0_), channel_id=1, source_target_pairs={{0,16},{4,20},{8,24},{12,28},{1,17},{5,21},{9,25},{13,29},{2,18},{... | collective-permute-start | bytes 393224 | tf_op jit(solution)/shard_map/ppermute | solution.py:496
  10.4 1.3 collective-permute-start.5
  11.7 0.1 collective-permute-start
  11.7 0.0 copy-start.3
  11.8 0.0 copy-start.4
  11.8 0.5 collective-permute-start.2
  12.2 2.0 %collective-permute-done.3.refs_4_ = bf16[256,256]{1,0:T(8,128)(2,1)S(1)} collective-permute-done((bf16[256,256]{1,0:T(8,128)(2,1)S(1)}, bf16[256,256]{1,0:T(8,128)(2,1)S(1)}, u32[]{:S(2)}, u32[]{:S(2)}) %collective-permute-start.3) | collective-permute-done | bytes 131104 | tf_op jit(solution)/shard_map/ppermute | solution.py:496
  14.3 0.0 collective-permute-start.4
  14.3 1.4 collective-permute-done.5.refs_6_
  15.7 0.0 collective-permute-start.6
  15.7 1.5 pad_maximum_fusion.refs_0_
  17.2 6.3 %collective-permute-start.14 = (bf16[1024,768]{1,0:T(8,128)(2,1)S(1)}, bf16[1024,768]{1,0:T(8,128)(2,1)S(1)}, u32[]{:S(2)}, u32[]{:S(2)}) collective-permute-start(bf16[1024,768]{1,0:T(8,128)(2,1)S(1)} %pad_maximum_fusion.refs_0_), channel_id=1, source_target_pairs={{0,24},{4,28},{8,16},{12,20},{16,8},{20,12},{24,0},{28,4},{1,25},{... | collective-permute-start | bytes 4718600 | tf_op jit(solution)/shard_map/ppermute | solution.py:195
  23.5 0.1 pad_add_fusion.index
  23.6 0.1 select_add_fusion.shares
  23.7 0.0 copy-start.2
  23.7 0.0 copy-start.1
  23.7 14.7 %attention.1 = (bf16[64,4096]{1,0:T(8,128)(2,1)S(1)}, bf16[64,4096]{1,0:T(8,128)(2,1)}, bf16[64,4096]{1,0:T(8,128)(2,1)}, bf16[64,4096]{1,0:T(8,128)(2,1)}) custom-call(s32[2]{0:T(128)S(1)} %pad_add_fusion.index, bf16[256,2048]{1,0:T(8,128)(2,1)} %q_hbm.1, bf16[256,256]{1,0:T(8,128)(2,1)S(1)} %pad_maximum_fusion.1.refs_0_, ...), custom_call_target="tpu_custom_call" | custom-call | flops 1000 | bytes 1000 | tf_op jit(solution)/shard_map/attention/pallas_call | solution.py:296
  38.5 0.0 copy-start
  38.5 1.5 collective-permute-start.7
  40.0 1.5 collective-permute-start.8
  41.6 0.5 collective-permute-start.9
  42.1 11.5 %collective-permute-done.7.r1 = bf16[64,4096]{1,0:T(8,128)(2,1)S(1)} collective-permute-done((bf16[64,4096]{1,0:T(8,128)(2,1)}, bf16[64,4096]{1,0:T(8,128)(2,1)S(1)}, u32[]{:S(2)}, u32[]{:S(2)}) %collective-permute-start.7) | collective-permute-done | bytes 524320 | tf_op jit(solution)/shard_map/ppermute | solution.py:195
  53.6 11.2 %collective-permute-done.8.r2 = bf16[64,4096]{1,0:T(8,128)(2,1)S(1)} collective-permute-done((bf16[64,4096]{1,0:T(8,128)(2,1)}, bf16[64,4096]{1,0:T(8,128)(2,1)S(1)}, u32[]{:S(2)}, u32[]{:S(2)}) %collective-permute-start.8) | collective-permute-done | bytes 524320 | tf_op jit(solution)/shard_map/ppermute | solution.py:195
  64.8 1.2 norm.1
  65.9 1.3 collective-permute-start.10
  67.2 0.8 collective-permute-start.11
  68.0 1.4 collective-permute-start.12
  69.5 5.8 %collective-permute-done.10.x1 = bf16[64,2048]{1,0:T(8,128)(2,1)S(1)} collective-permute-done((bf16[64,2048]{1,0:T(8,128)(2,1)S(1)}, bf16[64,2048]{1,0:T(8,128)(2,1)S(1)}, u32[]{:S(2)}, u32[]{:S(2)}) %collective-permute-start.10) | collective-permute-done | bytes 262176 | tf_op jit(solution)/shard_map/ppermute | solution.py:195
  75.2 4.4 %collective-permute-done.11.x2 = bf16[64,2048]{1,0:T(8,128)(2,1)S(1)} collective-permute-done((bf16[64,2048]{1,0:T(8,128)(2,1)S(1)}, bf16[64,2048]{1,0:T(8,128)(2,1)S(1)}, u32[]{:S(2)}, u32[]{:S(2)}) %collective-permute-start.11) | collective-permute-done | bytes 262176 | tf_op jit(solution)/shard_map/ppermute | solution.py:195
  79.6 0.1 collective-permute-start.16
  79.7 7.8 %collective-permute-start.17 = (bf16[768,512]{1,0:T(8,128)(2,1)S(1)}, bf16[768,512]{1,0:T(8,128)(2,1)S(1)}, u32[]{:S(2)}, u32[]{:S(2)}) collective-permute-start(bf16[768,512]{1,0:T(8,128)(2,1)S(1)} %bitcast.13), channel_id=1, source_target_pairs={{0,24},{4,28},{8,16},{12,20},{16,8},{20,12},{24,0},{28,4},{1,25},{... | collective-permute-start | bytes 2359304 | tf_op jit(solution)/shard_map/ppermute | solution.py:195
  87.5 0.6 collective-permute-start.18
  88.1 1.1 collective-permute-start.19
  89.1 6.7 %collective-permute-done.18.x1 = bf16[64,2048]{1,0:T(8,128)(2,1)S(1)} collective-permute-done((bf16[64,2048]{1,0:T(8,128)(2,1)S(1)}, bf16[64,2048]{1,0:T(8,128)(2,1)S(1)}, u32[]{:S(2)}, u32[]{:S(2)}) %collective-permute-start.18) | collective-permute-done | bytes 262176 | tf_op jit(solution)/shard_map/ppermute | solution.py:195
  95.8 1.1 collective-permute-start.20
  97.0 7.3 %collective-permute-done.20.x3 = bf16[64,2048]{1,0:T(8,128)(2,1)S(1)} collective-permute-done((bf16[64,2048]{1,0:T(8,128)(2,1)S(1)}, bf16[64,2048]{1,0:T(8,128)(2,1)S(1)}, u32[]{:S(2)}, u32[]{:S(2)}) %collective-permute-start.20) | collective-permute-done | bytes 262176 | tf_op jit(solution)/shard_map/ppermute | solution.py:195
  104.3 3.1 %enter.3 = bf16[256,1536]{1,0:T(8,128)(2,1)S(1)} custom-call(bf16[64,2048]{1,0:T(8,128)(2,1)S(1)} %collective-permute-done.13.x0, bf16[64,2048]{1,0:T(8,128)(2,1)S(1)} %collective-permute-done.18.x1, bf16[64,2048]{1,0:T(8,128)(2,1)S(1)} %collective-permute-done.19.x2, bf16[64,2048]{1,0:T(8,128)(2,1)S(1)} %collective-permute-done.20.x3, ...), custom_call_target="tpu_custom_call" | custom-call | flops 1000 | bytes 1000 | tf_op jit(solution)/shard_map/enter/pallas_call | solution.py:377
  107.4 20.8 %collective-permute-start.21 = (bf16[256,1536]{1,0:T(8,128)(2,1)S(1)}, bf16[256,1536]{1,0:T(8,128)(2,1)S(1)}, u32[]{:S(2)}, u32[]{:S(2)}) collective-permute-start(bf16[256,1536]{1,0:T(8,128)(2,1)S(1)} %enter.3), channel_id=1, source_target_pairs={{0,8},{4,12},{8,0},{12,4},{16,24},{20,28},{24,16},{28,20},{1,9},{5... | collective-permute-start | bytes 2359304 | tf_op jit(solution)/shard_map/ppermute | solution.py:195
  128.2 3.1 %enter.2.own = f32[256,1536]{1,0:T(8,128)S(1)} custom-call(bf16[64,2048]{1,0:T(8,128)(2,1)S(1)} %get-tuple-element.75.x0, bf16[64,2048]{1,0:T(8,128)(2,1)S(1)} %collective-permute-done.10.x1, bf16[64,2048]{1,0:T(8,128)(2,1)S(1)} %collective-permute-done.11.x2, bf16[64,2048]{1,0:T(8,128)(2,1)S(1)} %collective-permute-done.12.x3, ...), custom_call_target="tpu_custom_call" | custom-call | flops 1000 | bytes 1000 | tf_op jit(solution)/shard_map/enter/pallas_call | solution.py:377
  131.2 0.6 collective-permute-start.23
  131.8 12.8 %collective-permute-done.21.other = bf16[256,1536]{1,0:T(8,128)(2,1)S(1)} collective-permute-done((bf16[256,1536]{1,0:T(8,128)(2,1)S(1)}, bf16[256,1536]{1,0:T(8,128)(2,1)S(1)}, u32[]{:S(2)}, u32[]{:S(2)}) %collective-permute-start.21) | collective-permute-done | bytes 786464 | tf_op jit(solution)/shard_map/ppermute | solution.py:195
  144.6 0.3 silu.1.hidden
  144.9 1.8 collective-permute-start.24
  146.7 1.7 leave.2
  148.5 1.6 collective-permute-start.25
  150.0 1.0 collective-permute-start.26
  151.1 3.9 %collective-permute-done.25.r1 = bf16[64,2048]{1,0:T(8,128)(2,1)S(1)} collective-permute-done((bf16[64,2048]{1,0:T(8,128)(2,1)S(1)}, bf16[64,2048]{1,0:T(8,128)(2,1)S(1)}, u32[]{:S(2)}, u32[]{:S(2)}) %collective-permute-start.25) | collective-permute-done | bytes 262176 | tf_op jit(solution)/shard_map/ppermute | solution.py:195
  154.9 1.5 collective-permute-done.26.r2
  156.4 1.7 leave.3
  158.1 0.6 collective-permute-start.29
  158.8 1.5 collective-permute-start.30
  160.3 1.4 collective-permute-start.31
  161.7 0.3 collective-permute-start.28
  162.0 3.6 %collective-permute-done.28 = f32[64,128]{1,0:T(8,128)S(1)} collective-permute-done((f32[64,128]{1,0:T(8,128)S(1)}, f32[64,128]{1,0:T(8,128)S(1)}, u32[]{:S(2)}, u32[]{:S(2)}) %collective-permute-start.28) | collective-permute-done | bytes 32800 | tf_op jit(solution)/shard_map/ppermute | solution.py:195
  165.6 0.2 slice_reduce_fusion.3
  165.8 1.6 collective-permute-start.27
  167.4 0.1 collective-permute-done.29
  167.5 5.9 %collective-permute-done.30 = bf16[64,2048]{1,0:T(8,128)(2,1)S(1)} collective-permute-done((bf16[64,2048]{1,0:T(8,128)(2,1)S(1)}, bf16[64,2048]{1,0:T(8,128)(2,1)S(1)}, u32[]{:S(2)}, u32[]{:S(2)}) %collective-permute-start.30) | collective-permute-done | bytes 262176 | tf_op jit(solution)/shard_map/ppermute | solution.py:195
  173.4 0.3 add_convert_fusion
  173.7 1.6 collective-permute-start.32
  175.3 4.8 %collective-permute-done.32.other = bf16[64,2048]{1,0:T(8,128)(2,1)S(1)} collective-permute-done((bf16[64,2048]{1,0:T(8,128)(2,1)S(1)}, bf16[64,2048]{1,0:T(8,128)(2,1)S(1)}, u32[]{:S(2)}, u32[]{:S(2)}) %collective-permute-start.32) | collective-permute-done | bytes 262176 | tf_op jit(solution)/shard_map/ppermute | solution.py:195
  180.1 1.7 final.1
  (30 shorter events, 0.1 us)
Async XLA Ops:
  0.9 10.9 %collective-permute-start.1 = (bf16[256,256]{1,0:T(8,128)(2,1)S(1)}, bf16[256,256]{1,0:T(8,128)(2,1)S(1)}, u32[]{:S(2)}, u32[]{:S(2)}) collective-permute-start(bf16[256,256]{1,0:T(8,128)(2,1)S(1)} %pad_maximum_fusion.1.refs_0_), channel_id=1, source_target_pairs={{0,8},{4,12},{8,16},{12,20},{16,24},{20,28},{1,9},{5,13},{9,17},{1... | collective-permute-start | bytes 393224 | tf_op jit(solution)/shard_map/ppermute | solution.py:496
  5.9 8.4 %collective-permute-start.3 = (bf16[256,256]{1,0:T(8,128)(2,1)S(1)}, bf16[256,256]{1,0:T(8,128)(2,1)S(1)}, u32[]{:S(2)}, u32[]{:S(2)}) collective-permute-start(bf16[256,256]{1,0:T(8,128)(2,1)S(1)} %pad_maximum_fusion.1.refs_0_), channel_id=1, source_target_pairs={{0,16},{4,20},{8,24},{12,28},{1,17},{5,21},{9,25},{13,29},{2,18},{... | collective-permute-start | bytes 393224 | tf_op jit(solution)/shard_map/ppermute | solution.py:496
  10.4 5.3 %collective-permute-start.5 = (bf16[256,256]{1,0:T(8,128)(2,1)S(1)}, bf16[256,256]{1,0:T(8,128)(2,1)S(1)}, u32[]{:S(2)}, u32[]{:S(2)}) collective-permute-start(bf16[256,256]{1,0:T(8,128)(2,1)S(1)} %pad_maximum_fusion.1.refs_0_), channel_id=1, source_target_pairs={{0,24},{4,28},{1,25},{5,29},{2,26},{6,30},{3,27},{7,31}} | collective-permute-start | bytes 393224 | tf_op jit(solution)/shard_map/ppermute | solution.py:496
  11.7 5.5 %collective-permute-start = (bf16[256,256]{1,0:T(8,128)(2,1)S(1)}, bf16[256,256]{1,0:T(8,128)(2,1)S(1)}, u32[]{:S(2)}, u32[]{:S(2)}) collective-permute-start(bf16[256,256]{1,0:T(8,128)(2,1)S(1)} %pad_maximum_fusion.1.refs_0_), channel_id=1, source_target_pairs={{0,4},{4,0},{8,12},{12,8},{16,20},{20,16},{24,28},{28,24},{1,5},{5... | collective-permute-start | bytes 393224 | tf_op jit(solution)/shard_map/ppermute | solution.py:195
  11.7 11.8 %copy-start.3 = (s32[64,2]{0,1:T(2,128)S(1)}, s32[64,2]{0,1:T(2,128)}, u32[]{:S(2)}) copy-start(s32[64,2]{0,1:T(2,128)} %param.17) | copy-start | bytes 1540
  11.8 11.8 %copy-start.4 = (f32[64,2]{0,1:T(2,128)S(1)}, f32[64,2]{0,1:T(2,128)}, u32[]{:S(2)}) copy-start(f32[64,2]{0,1:T(2,128)} %param.18) | copy-start | bytes 1540
  11.8 5.4 %collective-permute-start.2 = (bf16[256,256]{1,0:T(8,128)(2,1)S(1)}, bf16[256,256]{1,0:T(8,128)(2,1)S(1)}, u32[]{:S(2)}, u32[]{:S(2)}) collective-permute-start(bf16[256,256]{1,0:T(8,128)(2,1)S(1)} %collective-permute-done.1.refs_2_), channel_id=1, source_target_pairs={{0,4},{4,0},{8,12},{12,8},{16,20},{20,16},{24,28},{28,24},{1,5},{5... | collective-permute-start | bytes 393224 | tf_op jit(solution)/shard_map/ppermute | solution.py:195
  14.3 2.9 %collective-permute-start.4 = (bf16[256,256]{1,0:T(8,128)(2,1)S(1)}, bf16[256,256]{1,0:T(8,128)(2,1)S(1)}, u32[]{:S(2)}, u32[]{:S(2)}) collective-permute-start(bf16[256,256]{1,0:T(8,128)(2,1)S(1)} %collective-permute-done.3.refs_4_), channel_id=1, source_target_pairs={{0,4},{4,0},{8,12},{12,8},{16,20},{20,16},{24,28},{28,24},{1,5},{5... | collective-permute-start | bytes 393224 | tf_op jit(solution)/shard_map/ppermute | solution.py:195
  15.7 1.5 collective-permute-start.6
  17.2 62.4 %collective-permute-start.14 = (bf16[1024,768]{1,0:T(8,128)(2,1)S(1)}, bf16[1024,768]{1,0:T(8,128)(2,1)S(1)}, u32[]{:S(2)}, u32[]{:S(2)}) collective-permute-start(bf16[1024,768]{1,0:T(8,128)(2,1)S(1)} %pad_maximum_fusion.refs_0_), channel_id=1, source_target_pairs={{0,24},{4,28},{8,16},{12,20},{16,8},{20,12},{24,0},{28,4},{1,25},{... | collective-permute-start | bytes 4718600 | tf_op jit(solution)/shard_map/ppermute | solution.py:195
  23.7 18.3 %copy-start.2 = (bf16[4096]{0:T(1024)(128)(2,1)S(1)}, bf16[4096]{0:T(1024)(128)(2,1)}, u32[]{:S(2)}) copy-start(bf16[4096]{0:T(1024)(128)(2,1)} %param.16) | copy-start | bytes 24580
  23.7 41.0 %copy-start.1 = (bf16[64,4096]{1,0:T(8,128)(2,1)S(1)}, bf16[64,4096]{1,0:T(8,128)(2,1)}, u32[]{:S(2)}) copy-start(bf16[64,4096]{1,0:T(8,128)(2,1)} %residual.1) | copy-start | bytes 1572868
  38.5 41.2 %copy-start = (bf16[1,768,512]{2,1,0:T(8,128)(2,1)S(1)}, bf16[1,768,512]{2,1,0:T(8,128)(2,1)}, u32[]{:S(2)}) copy-start(bf16[1,768,512]{2,1,0:T(8,128)(2,1)} %param.21) | copy-start | bytes 2359300
  38.5 15.1 %collective-permute-start.7 = (bf16[64,4096]{1,0:T(8,128)(2,1)}, bf16[64,4096]{1,0:T(8,128)(2,1)S(1)}, u32[]{:S(2)}, u32[]{:S(2)}) collective-permute-start(bf16[64,4096]{1,0:T(8,128)(2,1)} %get-tuple-element.67), channel_id=1, source_target_pairs={{0,1},{1,0},{2,3},{3,2},{4,5},{5,4},{6,7},{7,6},{8,9},{9,8},{10,11... | collective-permute-start | bytes 1572872 | tf_op jit(solution)/shard_map/ppermute | solution.py:195
  40.0 24.7 %collective-permute-start.8 = (bf16[64,4096]{1,0:T(8,128)(2,1)}, bf16[64,4096]{1,0:T(8,128)(2,1)S(1)}, u32[]{:S(2)}, u32[]{:S(2)}) collective-permute-start(bf16[64,4096]{1,0:T(8,128)(2,1)} %get-tuple-element.68), channel_id=1, source_target_pairs={{0,2},{1,3},{2,0},{3,1},{4,6},{5,7},{6,4},{7,5},{8,10},{9,11},{10,... | collective-permute-start | bytes 1572872 | tf_op jit(solution)/shard_map/ppermute | solution.py:195
  41.6 23.2 %collective-permute-start.9 = (bf16[64,4096]{1,0:T(8,128)(2,1)}, bf16[64,4096]{1,0:T(8,128)(2,1)S(1)}, u32[]{:S(2)}, u32[]{:S(2)}) collective-permute-start(bf16[64,4096]{1,0:T(8,128)(2,1)} %get-tuple-element.69), channel_id=1, source_target_pairs={{0,3},{1,2},{2,1},{3,0},{4,7},{5,6},{6,5},{7,4},{8,11},{9,10},{10,... | collective-permute-start | bytes 1572872 | tf_op jit(solution)/shard_map/ppermute | solution.py:195
  65.9 9.3 %collective-permute-start.10 = (bf16[64,2048]{1,0:T(8,128)(2,1)S(1)}, bf16[64,2048]{1,0:T(8,128)(2,1)S(1)}, u32[]{:S(2)}, u32[]{:S(2)}) collective-permute-start(bf16[64,2048]{1,0:T(8,128)(2,1)S(1)} %get-tuple-element.75.x0), channel_id=1, source_target_pairs={{0,1},{1,0},{2,3},{3,2},{4,5},{5,4},{6,7},{7,6},{8,9},{9,8},{10,11... | collective-permute-start | bytes 786440 | tf_op jit(solution)/shard_map/ppermute | solution.py:195
  67.2 12.4 %collective-permute-start.11 = (bf16[64,2048]{1,0:T(8,128)(2,1)S(1)}, bf16[64,2048]{1,0:T(8,128)(2,1)S(1)}, u32[]{:S(2)}, u32[]{:S(2)}) collective-permute-start(bf16[64,2048]{1,0:T(8,128)(2,1)S(1)} %get-tuple-element.75.x0), channel_id=1, source_target_pairs={{0,2},{1,3},{2,0},{3,1},{4,6},{5,7},{6,4},{7,5},{8,10},{9,11},{10,... | collective-permute-start | bytes 786440 | tf_op jit(solution)/shard_map/ppermute | solution.py:195
  68.0 11.6 %collective-permute-start.12 = (bf16[64,2048]{1,0:T(8,128)(2,1)S(1)}, bf16[64,2048]{1,0:T(8,128)(2,1)S(1)}, u32[]{:S(2)}, u32[]{:S(2)}) collective-permute-start(bf16[64,2048]{1,0:T(8,128)(2,1)S(1)} %get-tuple-element.75.x0), channel_id=1, source_target_pairs={{0,3},{1,2},{2,1},{3,0},{4,7},{5,6},{6,5},{7,4},{8,11},{9,10},{10,... | collective-permute-start | bytes 786440 | tf_op jit(solution)/shard_map/ppermute | solution.py:195
  69.5 10.1 %collective-permute-start.13 = (bf16[64,2048]{1,0:T(8,128)(2,1)S(1)}, bf16[64,2048]{1,0:T(8,128)(2,1)S(1)}, u32[]{:S(2)}, u32[]{:S(2)}) collective-permute-start(bf16[64,2048]{1,0:T(8,128)(2,1)S(1)} %get-tuple-element.73), channel_id=1, source_target_pairs={{0,8},{4,12},{8,0},{12,4},{16,24},{20,28},{24,16},{28,20},{1,9},{5... | collective-permute-start | bytes 786440 | tf_op jit(solution)/shard_map/ppermute | solution.py:195
  75.2 29.0 %collective-permute-start.15 = (bf16[1024,768]{1,0:T(8,128)(2,1)S(1)}, bf16[1024,768]{1,0:T(8,128)(2,1)S(1)}, u32[]{:S(2)}, u32[]{:S(2)}) collective-permute-start(bf16[1024,768]{1,0:T(8,128)(2,1)S(1)} %pad_maximum_fusion.refs_0_), channel_id=1, source_target_pairs={{0,4},{4,0},{8,12},{12,8},{16,20},{20,16},{24,28},{28,24},{1,5},{5... | collective-permute-start | bytes 4718600 | tf_op jit(solution)/shard_map/ppermute | solution.py:195
  79.6 24.7 %collective-permute-start.16 = (bf16[1024,768]{1,0:T(8,128)(2,1)S(1)}, bf16[1024,768]{1,0:T(8,128)(2,1)S(1)}, u32[]{:S(2)}, u32[]{:S(2)}) collective-permute-start(bf16[1024,768]{1,0:T(8,128)(2,1)S(1)} %collective-permute-done.14.refs_2_), channel_id=1, source_target_pairs={{0,4},{4,0},{8,12},{12,8},{16,20},{20,16},{24,28},{28,24},{1,5},{5... | collective-permute-start | bytes 4718600 | tf_op jit(solution)/shard_map/ppermute | solution.py:195
  79.7 51.5 %collective-permute-start.17 = (bf16[768,512]{1,0:T(8,128)(2,1)S(1)}, bf16[768,512]{1,0:T(8,128)(2,1)S(1)}, u32[]{:S(2)}, u32[]{:S(2)}) collective-permute-start(bf16[768,512]{1,0:T(8,128)(2,1)S(1)} %bitcast.13), channel_id=1, source_target_pairs={{0,24},{4,28},{8,16},{12,20},{16,8},{20,12},{24,0},{28,4},{1,25},{... | collective-permute-start | bytes 2359304 | tf_op jit(solution)/shard_map/ppermute | solution.py:195
  87.5 8.4 %collective-permute-start.18 = (bf16[64,2048]{1,0:T(8,128)(2,1)S(1)}, bf16[64,2048]{1,0:T(8,128)(2,1)S(1)}, u32[]{:S(2)}, u32[]{:S(2)}) collective-permute-start(bf16[64,2048]{1,0:T(8,128)(2,1)S(1)} %collective-permute-done.13.x0), channel_id=1, source_target_pairs={{0,1},{1,0},{2,3},{3,2},{4,5},{5,4},{6,7},{7,6},{8,9},{9,8},{10,11... | collective-permute-start | bytes 786440 | tf_op jit(solution)/shard_map/ppermute | solution.py:195
  88.1 8.9 %collective-permute-start.19 = (bf16[64,2048]{1,0:T(8,128)(2,1)S(1)}, bf16[64,2048]{1,0:T(8,128)(2,1)S(1)}, u32[]{:S(2)}, u32[]{:S(2)}) collective-permute-start(bf16[64,2048]{1,0:T(8,128)(2,1)S(1)} %collective-permute-done.13.x0), channel_id=1, source_target_pairs={{0,2},{1,3},{2,0},{3,1},{4,6},{5,7},{6,4},{7,5},{8,10},{9,11},{10,... | collective-permute-start | bytes 786440 | tf_op jit(solution)/shard_map/ppermute | solution.py:195
  95.8 8.4 %collective-permute-start.20 = (bf16[64,2048]{1,0:T(8,128)(2,1)S(1)}, bf16[64,2048]{1,0:T(8,128)(2,1)S(1)}, u32[]{:S(2)}, u32[]{:S(2)}) collective-permute-start(bf16[64,2048]{1,0:T(8,128)(2,1)S(1)} %collective-permute-done.13.x0), channel_id=1, source_target_pairs={{0,3},{1,2},{2,1},{3,0},{4,7},{5,6},{6,5},{7,4},{8,11},{9,10},{10,... | collective-permute-start | bytes 786440 | tf_op jit(solution)/shard_map/ppermute | solution.py:195
  107.4 37.3 %collective-permute-start.21 = (bf16[256,1536]{1,0:T(8,128)(2,1)S(1)}, bf16[256,1536]{1,0:T(8,128)(2,1)S(1)}, u32[]{:S(2)}, u32[]{:S(2)}) collective-permute-start(bf16[256,1536]{1,0:T(8,128)(2,1)S(1)} %enter.3), channel_id=1, source_target_pairs={{0,8},{4,12},{8,0},{12,4},{16,24},{20,28},{24,16},{28,20},{1,9},{5... | collective-permute-start | bytes 2359304 | tf_op jit(solution)/shard_map/ppermute | solution.py:195
  128.2 18.6 %collective-permute-start.22 = (bf16[768,512]{1,0:T(8,128)(2,1)S(1)}, bf16[768,512]{1,0:T(8,128)(2,1)S(1)}, u32[]{:S(2)}, u32[]{:S(2)}) collective-permute-start(bf16[768,512]{1,0:T(8,128)(2,1)S(1)} %bitcast.14), channel_id=1, source_target_pairs={{0,4},{4,0},{8,12},{12,8},{16,20},{20,16},{24,28},{28,24},{1,5},{5... | collective-permute-start | bytes 2359304 | tf_op jit(solution)/shard_map/ppermute | solution.py:195
  131.2 15.5 %collective-permute-start.23 = (bf16[768,512]{1,0:T(8,128)(2,1)S(1)}, bf16[768,512]{1,0:T(8,128)(2,1)S(1)}, u32[]{:S(2)}, u32[]{:S(2)}) collective-permute-start(bf16[768,512]{1,0:T(8,128)(2,1)S(1)} %collective-permute-done.17.d2), channel_id=1, source_target_pairs={{0,4},{4,0},{8,12},{12,8},{16,20},{20,16},{24,28},{28,24},{1,5},{5... | collective-permute-start | bytes 2359304 | tf_op jit(solution)/shard_map/ppermute | solution.py:195
  144.9 11.5 %collective-permute-start.24 = (bf16[256,768]{1,0:T(8,128)(2,1)S(1)}, bf16[256,768]{1,0:T(8,128)(2,1)S(1)}, u32[]{:S(2)}, u32[]{:S(2)}) collective-permute-start(bf16[256,768]{1,0:T(8,128)(2,1)S(1)} %silu.1.hidden), channel_id=1, source_target_pairs={{0,8},{4,12},{8,0},{12,4},{16,24},{20,28},{24,16},{28,20},{1,9},{5... | collective-permute-start | bytes 1179656 | tf_op jit(solution)/shard_map/ppermute | solution.py:195
  148.5 6.4 %collective-permute-start.25 = (bf16[64,2048]{1,0:T(8,128)(2,1)S(1)}, bf16[64,2048]{1,0:T(8,128)(2,1)S(1)}, u32[]{:S(2)}, u32[]{:S(2)}) collective-permute-start(bf16[64,2048]{1,0:T(8,128)(2,1)S(1)} %get-tuple-element.85), channel_id=1, source_target_pairs={{0,1},{1,0},{2,3},{3,2},{4,5},{5,4},{6,7},{7,6},{8,9},{9,8},{10,11... | collective-permute-start | bytes 786440 | tf_op jit(solution)/shard_map/ppermute | solution.py:195
  150.0 6.4 %collective-permute-start.26 = (bf16[64,2048]{1,0:T(8,128)(2,1)S(1)}, bf16[64,2048]{1,0:T(8,128)(2,1)S(1)}, u32[]{:S(2)}, u32[]{:S(2)}) collective-permute-start(bf16[64,2048]{1,0:T(8,128)(2,1)S(1)} %get-tuple-element.86), channel_id=1, source_target_pairs={{0,2},{1,3},{2,0},{3,1},{4,6},{5,7},{6,4},{7,5},{8,10},{9,11},{10,... | collective-permute-start | bytes 786440 | tf_op jit(solution)/shard_map/ppermute | solution.py:195
  158.1 9.3 %collective-permute-start.29 = (bf16[64,2048]{1,0:T(8,128)(2,1)S(1)}, bf16[64,2048]{1,0:T(8,128)(2,1)S(1)}, u32[]{:S(2)}, u32[]{:S(2)}) collective-permute-start(bf16[64,2048]{1,0:T(8,128)(2,1)S(1)} %get-tuple-element.92), channel_id=1, source_target_pairs={{0,1},{1,0},{2,3},{3,2},{4,5},{5,4},{6,7},{7,6},{8,9},{9,8},{10,11... | collective-permute-start | bytes 786440 | tf_op jit(solution)/shard_map/ppermute | solution.py:195
  158.8 14.6 %collective-permute-start.30 = (bf16[64,2048]{1,0:T(8,128)(2,1)S(1)}, bf16[64,2048]{1,0:T(8,128)(2,1)S(1)}, u32[]{:S(2)}, u32[]{:S(2)}) collective-permute-start(bf16[64,2048]{1,0:T(8,128)(2,1)S(1)} %get-tuple-element.93), channel_id=1, source_target_pairs={{0,2},{1,3},{2,0},{3,1},{4,6},{5,7},{6,4},{7,5},{8,10},{9,11},{10,... | collective-permute-start | bytes 786440 | tf_op jit(solution)/shard_map/ppermute | solution.py:195
  160.3 13.1 %collective-permute-start.31 = (bf16[64,2048]{1,0:T(8,128)(2,1)S(1)}, bf16[64,2048]{1,0:T(8,128)(2,1)S(1)}, u32[]{:S(2)}, u32[]{:S(2)}) collective-permute-start(bf16[64,2048]{1,0:T(8,128)(2,1)S(1)} %get-tuple-element.94), channel_id=1, source_target_pairs={{0,3},{1,2},{2,1},{3,0},{4,7},{5,6},{6,5},{7,4},{8,11},{9,10},{10,... | collective-permute-start | bytes 786440 | tf_op jit(solution)/shard_map/ppermute | solution.py:195
  161.7 3.9 %collective-permute-start.28 = (f32[64,128]{1,0:T(8,128)S(1)}, f32[64,128]{1,0:T(8,128)S(1)}, u32[]{:S(2)}, u32[]{:S(2)}) collective-permute-start(f32[64,128]{1,0:T(8,128)S(1)} %select_add_fusion.shares), channel_id=1, source_target_pairs={{0,8},{4,12},{8,0},{12,4},{16,24},{20,28},{24,16},{28,20},{1,9},{5... | collective-permute-start | bytes 98312 | tf_op jit(solution)/shard_map/ppermute | solution.py:195
  165.8 9.4 %collective-permute-start.27 = (bf16[64,2048]{1,0:T(8,128)(2,1)S(1)}, bf16[64,2048]{1,0:T(8,128)(2,1)S(1)}, u32[]{:S(2)}, u32[]{:S(2)}) collective-permute-start(bf16[64,2048]{1,0:T(8,128)(2,1)S(1)} %get-tuple-element.89), channel_id=1, source_target_pairs={{0,3},{1,2},{2,1},{3,0},{4,7},{5,6},{6,5},{7,4},{8,11},{9,10},{10,... | collective-permute-start | bytes 786440 | tf_op jit(solution)/shard_map/ppermute | solution.py:195
  173.7 6.4 %collective-permute-start.32 = (bf16[64,2048]{1,0:T(8,128)(2,1)S(1)}, bf16[64,2048]{1,0:T(8,128)(2,1)S(1)}, u32[]{:S(2)}, u32[]{:S(2)}) collective-permute-start(bf16[64,2048]{1,0:T(8,128)(2,1)S(1)} %add_convert_fusion), channel_id=1, source_target_pairs={{0,8},{4,12},{8,0},{12,4},{16,24},{20,28},{24,16},{28,20},{1,9},{5... | collective-permute-start | bytes 786440 | tf_op jit(solution)/shard_map/ppermute | solution.py:195

commit v10 on v9

--- a/solution.py
+++ b/solution.py
@@ -223,6 +223,8 @@
         )
         for i in range(steps)
     ]
+    for fetch in fetches:
+        fetch.start()
     factor = math.log2(math.e) / math.sqrt(HD)
     heads = q.shape[1] // HD
     ones_values[:, HD:] = jnp.ones((ones_values.shape[0], HD), BF16)
@@ -244,8 +246,6 @@
                 ones_values[here, :HD] = piece[:, HD:]
 
     q_fetch.wait()
-    for fetch in fetches:
-        fetch.start()
     part = QB // 4
 
     def run(length):
@@ -297,7 +297,7 @@
         attention_kernel,
         out_shape=[jax.ShapeDtypeStruct((rows, D), BF16)] * 4,
         in_specs=[pl.BlockSpec(memory_space=pltpu.SMEM)]
-        + [pl.BlockSpec(memory_space=pltpu.HBM)] * 10,
+        + [pl.BlockSpec(memory_space=pl.ANY)] * 10,
         out_specs=vmem_specs(4),
         scratch_shapes=[
             VMEM(w_out.shape, BF16),

time: 182 us -> 167 us (0.918)
  starting transfers between devices: 68.1 us -> 48.4 us
  Pallas kernels: 27.5 us -> 30.9 us
    ppermute x30, starting transfers between devices: 57.4 us -> 37.7 us  [swap(): return lax.ppermute(array, axis, [(i, i ^ mask) for i in range(size)])]
    pallas_call x1, Pallas kernels: 14.7 us -> 18.2 us  [attention(): pl.pallas_call(attention_kernel, out_shape=[jax.ShapeDtypeStruct((rows, D...]
  transfers between devices with their start and end apart: 33 -> 33, of which waited for: 15 -> 15; matrix products, arithmetic and copies ran while one was open for 1% -> 1% of each run, Pallas kernels for 13% -> 16%
where the time goes in v10:
time: 167 us
  waiting for transfers between devices  83.9 us (50%)
  starting transfers between devices  48.4 us (29%)
  Pallas kernels  30.9 us (19%)
  other arithmetic  1.95 us (1%)
    ppermute x30, waiting for transfers between devices, swap(): return lax.ppermute(array, axis, [(i, i ^ mask) for i in range(size)])  80.5 us
    ppermute x30, starting transfers between devices, swap(): return lax.ppermute(array, axis, [(i, i ^ mask) for i in range(size)])  37.7 us
    pallas_call x1, Pallas kernels, attention(): pl.pallas_call(attention_kernel, out_shape=[jax.ShapeDtypeStruct((rows, D...  18.2 us
    ppermute x3, starting transfers between devices, later(): lax.ppermute(array, 'ctx', [(i, i + 2 * chips) for i in range(8 - 2 * chi...  10.7 us
    pallas_call x2, Pallas kernels, enter(): pl.pallas_call(enter_kernel, out_shape=jax.ShapeDtypeStruct((count, 2 * w...  6.11 us
    pallas_call x2, Pallas kernels, leave(): pl.pallas_call(leave_kernel, out_shape=[part] * 4, in_specs=vmem_specs(1)...  3.46 us
    ppermute x3, waiting for transfers between devices, later(): lax.ppermute(array, 'ctx', [(i, i + 2 * chips) for i in range(8 - 2 * chi...  3.41 us
  transfers between devices with their start and end apart: 33, of which 15 were waited for; matrix products, arithmetic and copies ran while one was open for 1% of the time, Pallas kernels for 16%

profile of v10, /device:TPU:0, one launch (start us, length us, event | category | flops | bytes accessed | tf_op | source)
XLA Modules:
  0.0 166.6 jit_solution(10858248549202472177)
XLA Ops:
  0.0 0.9 constant_dynamic-slice_fusion
  0.9 4.9 %collective-permute-start.1 = (bf16[256,256]{1,0:T(8,128)(2,1)S(1)}, bf16[256,256]{1,0:T(8,128)(2,1)S(1)}, u32[]{:S(2)}, u32[]{:S(2)}) collective-permute-start(bf16[256,256]{1,0:T(8,128)(2,1)S(1)} %pad_maximum_fusion.1.refs_0_), channel_id=1, source_target_pairs={{0,8},{4,12},{8,16},{12,20},{16,24},{20,28},{1,9},{5,13},{9,17},{1... | collective-permute-start | bytes 393224 | tf_op jit(solution)/shard_map/ppermute | solution.py:496
  5.9 4.5 %collective-permute-start.3 = (bf16[256,256]{1,0:T(8,128)(2,1)S(1)}, bf16[256,256]{1,0:T(8,128)(2,1)S(1)}, u32[]{:S(2)}, u32[]{:S(2)}) collective-permute-start(bf16[256,256]{1,0:T(8,128)(2,1)S(1)} %pad_maximum_fusion.1.refs_0_), channel_id=1, source_target_pairs={{0,16},{4,20},{8,24},{12,28},{1,17},{5,21},{9,25},{13,29},{2,18},{... | collective-permute-start | bytes 393224 | tf_op jit(solution)/shard_map/ppermute | solution.py:496
  10.4 1.3 collective-permute-start.5
  11.7 0.1 collective-permute-start
  11.7 0.0 copy-start.3
  11.8 0.0 copy-start.4
  11.8 0.5 collective-permute-start.2
  12.2 2.0 %collective-permute-done.3.refs_4_ = bf16[256,256]{1,0:T(8,128)(2,1)S(1)} collective-permute-done((bf16[256,256]{1,0:T(8,128)(2,1)S(1)}, bf16[256,256]{1,0:T(8,128)(2,1)S(1)}, u32[]{:S(2)}, u32[]{:S(2)}) %collective-permute-start.3) | collective-permute-done | bytes 131104 | tf_op jit(solution)/shard_map/ppermute | solution.py:496
  14.3 1.4 collective-permute-done.5.refs_6_
  15.7 1.5 pad_maximum_fusion.refs_0_
  17.2 6.3 %collective-permute-start.14 = (bf16[1024,768]{1,0:T(8,128)(2,1)S(1)}, bf16[1024,768]{1,0:T(8,128)(2,1)S(1)}, u32[]{:S(2)}, u32[]{:S(2)}) collective-permute-start(bf16[1024,768]{1,0:T(8,128)(2,1)S(1)} %pad_maximum_fusion.refs_0_), channel_id=1, source_target_pairs={{0,24},{4,28},{8,16},{12,20},{16,8},{20,12},{24,0},{28,4},{1,25},{... | collective-permute-start | bytes 4718600 | tf_op jit(solution)/shard_map/ppermute | solution.py:195
  23.5 0.1 pad_add_fusion.index
  23.6 0.1 select_add_fusion.shares
  23.7 0.0 copy-start.2
  23.7 0.0 copy-start.1
  23.7 18.2 %attention.1 = (bf16[64,4096]{1,0:T(8,128)(2,1)S(1)}, bf16[64,4096]{1,0:T(8,128)(2,1)}, bf16[64,4096]{1,0:T(8,128)(2,1)}, bf16[64,4096]{1,0:T(8,128)(2,1)}) custom-call(s32[2]{0:T(128)S(1)} %pad_add_fusion.index, bf16[256,2048]{1,0:T(8,128)(2,1)} %q_hbm.1, bf16[256,256]{1,0:T(8,128)(2,1)S(1)} %pad_maximum_fusion.1.refs_0_, ...), custom_call_target="tpu_custom_call" | custom-call | flops 1000 | bytes 1000 | tf_op jit(solution)/shard_map/attention/pallas_call | solution.py:296
  41.9 0.0 copy-start
  41.9 1.6 collective-permute-start.7
  43.5 1.5 collective-permute-start.8
  45.0 0.5 collective-permute-start.9
  45.5 11.5 %collective-permute-done.7.r1 = bf16[64,4096]{1,0:T(8,128)(2,1)S(1)} collective-permute-done((bf16[64,4096]{1,0:T(8,128)(2,1)}, bf16[64,4096]{1,0:T(8,128)(2,1)S(1)}, u32[]{:S(2)}, u32[]{:S(2)}) %collective-permute-start.7) | collective-permute-done | bytes 524320 | tf_op jit(solution)/shard_map/ppermute | solution.py:195
  57.0 11.2 %collective-permute-done.8.r2 = bf16[64,4096]{1,0:T(8,128)(2,1)S(1)} collective-permute-done((bf16[64,4096]{1,0:T(8,128)(2,1)}, bf16[64,4096]{1,0:T(8,128)(2,1)S(1)}, u32[]{:S(2)}, u32[]{:S(2)}) %collective-permute-start.8) | collective-permute-done | bytes 524320 | tf_op jit(solution)/shard_map/ppermute | solution.py:195
  68.2 1.2 norm.1
  69.4 1.3 collective-permute-start.10
  70.7 0.8 collective-permute-start.11
  71.5 1.4 collective-permute-start.12
  72.9 0.3 collective-permute-start.13
  73.2 5.5 %collective-permute-done.10.x1 = bf16[64,2048]{1,0:T(8,128)(2,1)S(1)} collective-permute-done((bf16[64,2048]{1,0:T(8,128)(2,1)S(1)}, bf16[64,2048]{1,0:T(8,128)(2,1)S(1)}, u32[]{:S(2)}, u32[]{:S(2)}) %collective-permute-start.10) | collective-permute-done | bytes 262176 | tf_op jit(solution)/shard_map/ppermute | solution.py:195
  78.7 4.4 %collective-permute-done.11.x2 = bf16[64,2048]{1,0:T(8,128)(2,1)S(1)} collective-permute-done((bf16[64,2048]{1,0:T(8,128)(2,1)S(1)}, bf16[64,2048]{1,0:T(8,128)(2,1)S(1)}, u32[]{:S(2)}, u32[]{:S(2)}) %collective-permute-start.11) | collective-permute-done | bytes 262176 | tf_op jit(solution)/shard_map/ppermute | solution.py:195
  83.1 0.1 collective-permute-start.16
  83.1 8.9 %collective-permute-start.17 = (bf16[768,512]{1,0:T(8,128)(2,1)S(1)}, bf16[768,512]{1,0:T(8,128)(2,1)S(1)}, u32[]{:S(2)}, u32[]{:S(2)}) collective-permute-start(bf16[768,512]{1,0:T(8,128)(2,1)S(1)} %bitcast.13), channel_id=1, source_target_pairs={{0,24},{4,28},{8,16},{12,20},{16,8},{20,12},{24,0},{28,4},{1,25},{... | collective-permute-start | bytes 2359304 | tf_op jit(solution)/shard_map/ppermute | solution.py:195
  92.0 0.6 collective-permute-start.18
  92.6 1.1 collective-permute-start.19
  93.7 6.7 %collective-permute-done.18.x1 = bf16[64,2048]{1,0:T(8,128)(2,1)S(1)} collective-permute-done((bf16[64,2048]{1,0:T(8,128)(2,1)S(1)}, bf16[64,2048]{1,0:T(8,128)(2,1)S(1)}, u32[]{:S(2)}, u32[]{:S(2)}) %collective-permute-start.18) | collective-permute-done | bytes 262176 | tf_op jit(solution)/shard_map/ppermute | solution.py:195
  100.4 1.1 collective-permute-start.20
  101.5 7.3 %collective-permute-done.20.x3 = bf16[64,2048]{1,0:T(8,128)(2,1)S(1)} collective-permute-done((bf16[64,2048]{1,0:T(8,128)(2,1)S(1)}, bf16[64,2048]{1,0:T(8,128)(2,1)S(1)}, u32[]{:S(2)}, u32[]{:S(2)}) %collective-permute-start.20) | collective-permute-done | bytes 262176 | tf_op jit(solution)/shard_map/ppermute | solution.py:195
  108.9 3.1 %enter.3 = bf16[256,1536]{1,0:T(8,128)(2,1)S(1)} custom-call(bf16[64,2048]{1,0:T(8,128)(2,1)S(1)} %collective-permute-done.13.x0, bf16[64,2048]{1,0:T(8,128)(2,1)S(1)} %collective-permute-done.18.x1, bf16[64,2048]{1,0:T(8,128)(2,1)S(1)} %collective-permute-done.19.x2, bf16[64,2048]{1,0:T(8,128)(2,1)S(1)} %collective-permute-done.20.x3, ...), custom_call_target="tpu_custom_call" | custom-call | flops 1000 | bytes 1000 | tf_op jit(solution)/shard_map/enter/pallas_call | solution.py:377
  111.9 0.1 collective-permute-start.21
  112.0 0.1 collective-permute-start.22
  112.1 3.1 %enter.2.own = f32[256,1536]{1,0:T(8,128)S(1)} custom-call(bf16[64,2048]{1,0:T(8,128)(2,1)S(1)} %get-tuple-element.75.x0, bf16[64,2048]{1,0:T(8,128)(2,1)S(1)} %collective-permute-done.10.x1, bf16[64,2048]{1,0:T(8,128)(2,1)S(1)} %collective-permute-done.11.x2, bf16[64,2048]{1,0:T(8,128)(2,1)S(1)} %collective-permute-done.12.x3, ...), custom_call_target="tpu_custom_call" | custom-call | flops 1000 | bytes 1000 | tf_op jit(solution)/shard_map/enter/pallas_call | solution.py:377
  115.2 0.6 collective-permute-start.23
  115.7 14.1 %collective-permute-done.21.other = bf16[256,1536]{1,0:T(8,128)(2,1)S(1)} collective-permute-done((bf16[256,1536]{1,0:T(8,128)(2,1)S(1)}, bf16[256,1536]{1,0:T(8,128)(2,1)S(1)}, u32[]{:S(2)}, u32[]{:S(2)}) %collective-permute-start.21) | collective-permute-done | bytes 786464 | tf_op jit(solution)/shard_map/ppermute | solution.py:195
  129.8 0.3 silu.1.hidden
  130.1 0.4 collective-permute-start.24
  130.5 1.7 %leave.2 = (bf16[64,2048]{1,0:T(8,128)(2,1)S(1)}, bf16[64,2048]{1,0:T(8,128)(2,1)S(1)}, bf16[64,2048]{1,0:T(8,128)(2,1)S(1)}, bf16[64,2048]{1,0:T(8,128)(2,1)S(1)}) custom-call(bf16[256,768]{1,0:T(8,128)(2,1)S(1)} %silu.1.hidden, bf16[768,512]{1,0:T(8,128)(2,1)S(1)} %bitcast.15, bf16[768,512]{1,0:T(8,128)(2,1)S(1)} %collective-permute-done.22.d1, ...), custom_call_target="tpu_custom_call" | custom-call | flops 1000 | bytes 1000 | tf_op jit(solution)/shard_map/leave/pallas_call | solution.py:428
  132.2 0.7 collective-permute-start.25
  132.9 1.3 collective-permute-start.26
  134.2 4.5 %collective-permute-done.25.r1 = bf16[64,2048]{1,0:T(8,128)(2,1)S(1)} collective-permute-done((bf16[64,2048]{1,0:T(8,128)(2,1)S(1)}, bf16[64,2048]{1,0:T(8,128)(2,1)S(1)}, u32[]{:S(2)}, u32[]{:S(2)}) %collective-permute-start.25) | collective-permute-done | bytes 262176 | tf_op jit(solution)/shard_map/ppermute | solution.py:195
  138.7 0.6 collective-permute-done.26.r2
  139.3 1.7 %leave.3 = (bf16[64,2048]{1,0:T(8,128)(2,1)S(1)}, bf16[64,2048]{1,0:T(8,128)(2,1)S(1)}, bf16[64,2048]{1,0:T(8,128)(2,1)S(1)}, bf16[64,2048]{1,0:T(8,128)(2,1)S(1)}) custom-call(bf16[256,768]{1,0:T(8,128)(2,1)S(1)} %collective-permute-done.24.hidden, bf16[768,512]{1,0:T(8,128)(2,1)S(1)} %bitcast.16, bf16[768,512]{1,0:T(8,128)(2,1)S(1)} %collective-permute-done.22.d1, ...), custom_call_target="tpu_custom_call" | custom-call | flops 1000 | bytes 1000 | tf_op jit(solution)/shard_map/leave/pallas_call | solution.py:428
  141.0 1.5 collective-permute-start.29
  142.5 0.6 collective-permute-start.30
  143.1 1.5 collective-permute-start.31
  144.6 1.7 %collective-permute-start.28 = (f32[64,128]{1,0:T(8,128)S(1)}, f32[64,128]{1,0:T(8,128)S(1)}, u32[]{:S(2)}, u32[]{:S(2)}) collective-permute-start(f32[64,128]{1,0:T(8,128)S(1)} %select_add_fusion.shares), channel_id=1, source_target_pairs={{0,8},{4,12},{8,0},{12,4},{16,24},{20,28},{24,16},{28,20},{1,9},{5... | collective-permute-start | bytes 98312 | tf_op jit(solution)/shard_map/ppermute | solution.py:195
  146.3 2.2 %collective-permute-done.28 = f32[64,128]{1,0:T(8,128)S(1)} collective-permute-done((f32[64,128]{1,0:T(8,128)S(1)}, f32[64,128]{1,0:T(8,128)S(1)}, u32[]{:S(2)}, u32[]{:S(2)}) %collective-permute-start.28) | collective-permute-done | bytes 32800 | tf_op jit(solution)/shard_map/ppermute | solution.py:195
  148.5 0.2 slice_reduce_fusion.3
  148.7 1.5 collective-permute-start.27
  150.2 0.1 collective-permute-done.29
  150.3 7.8 %collective-permute-done.30 = bf16[64,2048]{1,0:T(8,128)(2,1)S(1)} collective-permute-done((bf16[64,2048]{1,0:T(8,128)(2,1)S(1)}, bf16[64,2048]{1,0:T(8,128)(2,1)S(1)}, u32[]{:S(2)}, u32[]{:S(2)}) %collective-permute-start.30) | collective-permute-done | bytes 262176 | tf_op jit(solution)/shard_map/ppermute | solution.py:195
  158.2 0.3 add_convert_fusion
  158.5 1.9 %collective-permute-start.32 = (bf16[64,2048]{1,0:T(8,128)(2,1)S(1)}, bf16[64,2048]{1,0:T(8,128)(2,1)S(1)}, u32[]{:S(2)}, u32[]{:S(2)}) collective-permute-start(bf16[64,2048]{1,0:T(8,128)(2,1)S(1)} %add_convert_fusion), channel_id=1, source_target_pairs={{0,8},{4,12},{8,0},{12,4},{16,24},{20,28},{24,16},{28,20},{1,9},{5... | collective-permute-start | bytes 786440 | tf_op jit(solution)/shard_map/ppermute | solution.py:195
  160.3 4.6 %collective-permute-done.32.other = bf16[64,2048]{1,0:T(8,128)(2,1)S(1)} collective-permute-done((bf16[64,2048]{1,0:T(8,128)(2,1)S(1)}, bf16[64,2048]{1,0:T(8,128)(2,1)S(1)}, u32[]{:S(2)}, u32[]{:S(2)}) %collective-permute-start.32) | collective-permute-done | bytes 262176 | tf_op jit(solution)/shard_map/ppermute | solution.py:195
  164.9 1.7 %final.1 = bf16[64,4096]{1,0:T(8,128)(2,1)} custom-call(s32[2]{0:T(128)S(1)} %pad_add_fusion.index, bf16[64,4096]{1,0:T(8,128)(2,1)S(1)} %get-tuple-element.70.state, f32[64,128]{1,0:T(8,128)S(1)} %select_add_fusion.shares, bf16[64,2048]{1,0:T(8,128)(2,1)S(1)} %get-tuple-element.84.y0, bf16[64,2048]{1,0:T(8,128)(2,1)S(1)} %collective-permute-done.25.r1, ...), custom_call_target="tpu_custom_call" | custom-call | flops 1000 | bytes 1000 | tf_op jit(solution)/shard_map/final/pallas_call | solution.py:460
  (30 shorter events, 0.1 us)
Async XLA Ops:
  0.9 10.9 %collective-permute-start.1 = (bf16[256,256]{1,0:T(8,128)(2,1)S(1)}, bf16[256,256]{1,0:T(8,128)(2,1)S(1)}, u32[]{:S(2)}, u32[]{:S(2)}) collective-permute-start(bf16[256,256]{1,0:T(8,128)(2,1)S(1)} %pad_maximum_fusion.1.refs_0_), channel_id=1, source_target_pairs={{0,8},{4,12},{8,16},{12,20},{16,24},{20,28},{1,9},{5,13},{9,17},{1... | collective-permute-start | bytes 393224 | tf_op jit(solution)/shard_map/ppermute | solution.py:496
  5.9 8.4 %collective-permute-start.3 = (bf16[256,256]{1,0:T(8,128)(2,1)S(1)}, bf16[256,256]{1,0:T(8,128)(2,1)S(1)}, u32[]{:S(2)}, u32[]{:S(2)}) collective-permute-start(bf16[256,256]{1,0:T(8,128)(2,1)S(1)} %pad_maximum_fusion.1.refs_0_), channel_id=1, source_target_pairs={{0,16},{4,20},{8,24},{12,28},{1,17},{5,21},{9,25},{13,29},{2,18},{... | collective-permute-start | bytes 393224 | tf_op jit(solution)/shard_map/ppermute | solution.py:496
  10.4 5.3 %collective-permute-start.5 = (bf16[256,256]{1,0:T(8,128)(2,1)S(1)}, bf16[256,256]{1,0:T(8,128)(2,1)S(1)}, u32[]{:S(2)}, u32[]{:S(2)}) collective-permute-start(bf16[256,256]{1,0:T(8,128)(2,1)S(1)} %pad_maximum_fusion.1.refs_0_), channel_id=1, source_target_pairs={{0,24},{4,28},{1,25},{5,29},{2,26},{6,30},{3,27},{7,31}} | collective-permute-start | bytes 393224 | tf_op jit(solution)/shard_map/ppermute | solution.py:496
  11.7 5.5 %collective-permute-start = (bf16[256,256]{1,0:T(8,128)(2,1)S(1)}, bf16[256,256]{1,0:T(8,128)(2,1)S(1)}, u32[]{:S(2)}, u32[]{:S(2)}) collective-permute-start(bf16[256,256]{1,0:T(8,128)(2,1)S(1)} %pad_maximum_fusion.1.refs_0_), channel_id=1, source_target_pairs={{0,4},{4,0},{8,12},{12,8},{16,20},{20,16},{24,28},{28,24},{1,5},{5... | collective-permute-start | bytes 393224 | tf_op jit(solution)/shard_map/ppermute | solution.py:195
  11.7 11.8 %copy-start.3 = (s32[64,2]{0,1:T(2,128)S(1)}, s32[64,2]{0,1:T(2,128)}, u32[]{:S(2)}) copy-start(s32[64,2]{0,1:T(2,128)} %param.17) | copy-start | bytes 1540
  11.8 11.8 %copy-start.4 = (f32[64,2]{0,1:T(2,128)S(1)}, f32[64,2]{0,1:T(2,128)}, u32[]{:S(2)}) copy-start(f32[64,2]{0,1:T(2,128)} %param.18) | copy-start | bytes 1540
  11.8 5.4 %collective-permute-start.2 = (bf16[256,256]{1,0:T(8,128)(2,1)S(1)}, bf16[256,256]{1,0:T(8,128)(2,1)S(1)}, u32[]{:S(2)}, u32[]{:S(2)}) collective-permute-start(bf16[256,256]{1,0:T(8,128)(2,1)S(1)} %collective-permute-done.1.refs_2_), channel_id=1, source_target_pairs={{0,4},{4,0},{8,12},{12,8},{16,20},{20,16},{24,28},{28,24},{1,5},{5... | collective-permute-start | bytes 393224 | tf_op jit(solution)/shard_map/ppermute | solution.py:195
  14.3 2.9 %collective-permute-start.4 = (bf16[256,256]{1,0:T(8,128)(2,1)S(1)}, bf16[256,256]{1,0:T(8,128)(2,1)S(1)}, u32[]{:S(2)}, u32[]{:S(2)}) collective-permute-start(bf16[256,256]{1,0:T(8,128)(2,1)S(1)} %collective-permute-done.3.refs_4_), channel_id=1, source_target_pairs={{0,4},{4,0},{8,12},{12,8},{16,20},{20,16},{24,28},{28,24},{1,5},{5... | collective-permute-start | bytes 393224 | tf_op jit(solution)/shard_map/ppermute | solution.py:195
  15.7 1.5 collective-permute-start.6
  17.2 65.9 %collective-permute-start.14 = (bf16[1024,768]{1,0:T(8,128)(2,1)S(1)}, bf16[1024,768]{1,0:T(8,128)(2,1)S(1)}, u32[]{:S(2)}, u32[]{:S(2)}) collective-permute-start(bf16[1024,768]{1,0:T(8,128)(2,1)S(1)} %pad_maximum_fusion.refs_0_), channel_id=1, source_target_pairs={{0,24},{4,28},{8,16},{12,20},{16,8},{20,12},{24,0},{28,4},{1,25},{... | collective-permute-start | bytes 4718600 | tf_op jit(solution)/shard_map/ppermute | solution.py:195
  23.7 21.8 %copy-start.2 = (bf16[4096]{0:T(1024)(128)(2,1)S(1)}, bf16[4096]{0:T(1024)(128)(2,1)}, u32[]{:S(2)}) copy-start(bf16[4096]{0:T(1024)(128)(2,1)} %param.16) | copy-start | bytes 24580
  23.7 44.5 %copy-start.1 = (bf16[64,4096]{1,0:T(8,128)(2,1)S(1)}, bf16[64,4096]{1,0:T(8,128)(2,1)}, u32[]{:S(2)}) copy-start(bf16[64,4096]{1,0:T(8,128)(2,1)} %residual.1) | copy-start | bytes 1572868
  41.9 41.2 %copy-start = (bf16[1,768,512]{2,1,0:T(8,128)(2,1)S(1)}, bf16[1,768,512]{2,1,0:T(8,128)(2,1)}, u32[]{:S(2)}) copy-start(bf16[1,768,512]{2,1,0:T(8,128)(2,1)} %param.21) | copy-start | bytes 2359300
  41.9 15.1 %collective-permute-start.7 = (bf16[64,4096]{1,0:T(8,128)(2,1)}, bf16[64,4096]{1,0:T(8,128)(2,1)S(1)}, u32[]{:S(2)}, u32[]{:S(2)}) collective-permute-start(bf16[64,4096]{1,0:T(8,128)(2,1)} %get-tuple-element.67), channel_id=1, source_target_pairs={{0,1},{1,0},{2,3},{3,2},{4,5},{5,4},{6,7},{7,6},{8,9},{9,8},{10,11... | collective-permute-start | bytes 1572872 | tf_op jit(solution)/shard_map/ppermute | solution.py:195
  43.5 24.7 %collective-permute-start.8 = (bf16[64,4096]{1,0:T(8,128)(2,1)}, bf16[64,4096]{1,0:T(8,128)(2,1)S(1)}, u32[]{:S(2)}, u32[]{:S(2)}) collective-permute-start(bf16[64,4096]{1,0:T(8,128)(2,1)} %get-tuple-element.68), channel_id=1, source_target_pairs={{0,2},{1,3},{2,0},{3,1},{4,6},{5,7},{6,4},{7,5},{8,10},{9,11},{10,... | collective-permute-start | bytes 1572872 | tf_op jit(solution)/shard_map/ppermute | solution.py:195
  45.0 23.2 %collective-permute-start.9 = (bf16[64,4096]{1,0:T(8,128)(2,1)}, bf16[64,4096]{1,0:T(8,128)(2,1)S(1)}, u32[]{:S(2)}, u32[]{:S(2)}) collective-permute-start(bf16[64,4096]{1,0:T(8,128)(2,1)} %get-tuple-element.69), channel_id=1, source_target_pairs={{0,3},{1,2},{2,1},{3,0},{4,7},{5,6},{6,5},{7,4},{8,11},{9,10},{10,... | collective-permute-start | bytes 1572872 | tf_op jit(solution)/shard_map/ppermute | solution.py:195
  69.4 9.3 %collective-permute-start.10 = (bf16[64,2048]{1,0:T(8,128)(2,1)S(1)}, bf16[64,2048]{1,0:T(8,128)(2,1)S(1)}, u32[]{:S(2)}, u32[]{:S(2)}) collective-permute-start(bf16[64,2048]{1,0:T(8,128)(2,1)S(1)} %get-tuple-element.75.x0), channel_id=1, source_target_pairs={{0,1},{1,0},{2,3},{3,2},{4,5},{5,4},{6,7},{7,6},{8,9},{9,8},{10,11... | collective-permute-start | bytes 786440 | tf_op jit(solution)/shard_map/ppermute | solution.py:195
  70.7 12.4 %collective-permute-start.11 = (bf16[64,2048]{1,0:T(8,128)(2,1)S(1)}, bf16[64,2048]{1,0:T(8,128)(2,1)S(1)}, u32[]{:S(2)}, u32[]{:S(2)}) collective-permute-start(bf16[64,2048]{1,0:T(8,128)(2,1)S(1)} %get-tuple-element.75.x0), channel_id=1, source_target_pairs={{0,2},{1,3},{2,0},{3,1},{4,6},{5,7},{6,4},{7,5},{8,10},{9,11},{10,... | collective-permute-start | bytes 786440 | tf_op jit(solution)/shard_map/ppermute | solution.py:195
  71.5 11.5 %collective-permute-start.12 = (bf16[64,2048]{1,0:T(8,128)(2,1)S(1)}, bf16[64,2048]{1,0:T(8,128)(2,1)S(1)}, u32[]{:S(2)}, u32[]{:S(2)}) collective-permute-start(bf16[64,2048]{1,0:T(8,128)(2,1)S(1)} %get-tuple-element.75.x0), channel_id=1, source_target_pairs={{0,3},{1,2},{2,1},{3,0},{4,7},{5,6},{6,5},{7,4},{8,11},{9,10},{10,... | collective-permute-start | bytes 786440 | tf_op jit(solution)/shard_map/ppermute | solution.py:195
  72.9 10.1 %collective-permute-start.13 = (bf16[64,2048]{1,0:T(8,128)(2,1)S(1)}, bf16[64,2048]{1,0:T(8,128)(2,1)S(1)}, u32[]{:S(2)}, u32[]{:S(2)}) collective-permute-start(bf16[64,2048]{1,0:T(8,128)(2,1)S(1)} %get-tuple-element.73), channel_id=1, source_target_pairs={{0,8},{4,12},{8,0},{12,4},{16,24},{20,28},{24,16},{28,20},{1,9},{5... | collective-permute-start | bytes 786440 | tf_op jit(solution)/shard_map/ppermute | solution.py:195
  78.7 30.2 %collective-permute-start.15 = (bf16[1024,768]{1,0:T(8,128)(2,1)S(1)}, bf16[1024,768]{1,0:T(8,128)(2,1)S(1)}, u32[]{:S(2)}, u32[]{:S(2)}) collective-permute-start(bf16[1024,768]{1,0:T(8,128)(2,1)S(1)} %pad_maximum_fusion.refs_0_), channel_id=1, source_target_pairs={{0,4},{4,0},{8,12},{12,8},{16,20},{20,16},{24,28},{28,24},{1,5},{5... | collective-permute-start | bytes 4718600 | tf_op jit(solution)/shard_map/ppermute | solution.py:195
  83.1 25.8 %collective-permute-start.16 = (bf16[1024,768]{1,0:T(8,128)(2,1)S(1)}, bf16[1024,768]{1,0:T(8,128)(2,1)S(1)}, u32[]{:S(2)}, u32[]{:S(2)}) collective-permute-start(bf16[1024,768]{1,0:T(8,128)(2,1)S(1)} %collective-permute-done.14.refs_2_), channel_id=1, source_target_pairs={{0,4},{4,0},{8,12},{12,8},{16,20},{20,16},{24,28},{28,24},{1,5},{5... | collective-permute-start | bytes 4718600 | tf_op jit(solution)/shard_map/ppermute | solution.py:195
  83.1 32.0 %collective-permute-start.17 = (bf16[768,512]{1,0:T(8,128)(2,1)S(1)}, bf16[768,512]{1,0:T(8,128)(2,1)S(1)}, u32[]{:S(2)}, u32[]{:S(2)}) collective-permute-start(bf16[768,512]{1,0:T(8,128)(2,1)S(1)} %bitcast.13), channel_id=1, source_target_pairs={{0,24},{4,28},{8,16},{12,20},{16,8},{20,12},{24,0},{28,4},{1,25},{... | collective-permute-start | bytes 2359304 | tf_op jit(solution)/shard_map/ppermute | solution.py:195
  92.0 8.4 %collective-permute-start.18 = (bf16[64,2048]{1,0:T(8,128)(2,1)S(1)}, bf16[64,2048]{1,0:T(8,128)(2,1)S(1)}, u32[]{:S(2)}, u32[]{:S(2)}) collective-permute-start(bf16[64,2048]{1,0:T(8,128)(2,1)S(1)} %collective-permute-done.13.x0), channel_id=1, source_target_pairs={{0,1},{1,0},{2,3},{3,2},{4,5},{5,4},{6,7},{7,6},{8,9},{9,8},{10,11... | collective-permute-start | bytes 786440 | tf_op jit(solution)/shard_map/ppermute | solution.py:195
  92.6 8.9 %collective-permute-start.19 = (bf16[64,2048]{1,0:T(8,128)(2,1)S(1)}, bf16[64,2048]{1,0:T(8,128)(2,1)S(1)}, u32[]{:S(2)}, u32[]{:S(2)}) collective-permute-start(bf16[64,2048]{1,0:T(8,128)(2,1)S(1)} %collective-permute-done.13.x0), channel_id=1, source_target_pairs={{0,2},{1,3},{2,0},{3,1},{4,6},{5,7},{6,4},{7,5},{8,10},{9,11},{10,... | collective-permute-start | bytes 786440 | tf_op jit(solution)/shard_map/ppermute | solution.py:195
  100.4 8.4 %collective-permute-start.20 = (bf16[64,2048]{1,0:T(8,128)(2,1)S(1)}, bf16[64,2048]{1,0:T(8,128)(2,1)S(1)}, u32[]{:S(2)}, u32[]{:S(2)}) collective-permute-start(bf16[64,2048]{1,0:T(8,128)(2,1)S(1)} %collective-permute-done.13.x0), channel_id=1, source_target_pairs={{0,3},{1,2},{2,1},{3,0},{4,7},{5,6},{6,5},{7,4},{8,11},{9,10},{10,... | collective-permute-start | bytes 786440 | tf_op jit(solution)/shard_map/ppermute | solution.py:195
  111.9 17.9 %collective-permute-start.21 = (bf16[256,1536]{1,0:T(8,128)(2,1)S(1)}, bf16[256,1536]{1,0:T(8,128)(2,1)S(1)}, u32[]{:S(2)}, u32[]{:S(2)}) collective-permute-start(bf16[256,1536]{1,0:T(8,128)(2,1)S(1)} %enter.3), channel_id=1, source_target_pairs={{0,8},{4,12},{8,0},{12,4},{16,24},{20,28},{24,16},{28,20},{1,9},{5... | collective-permute-start | bytes 2359304 | tf_op jit(solution)/shard_map/ppermute | solution.py:195
  112.0 18.5 %collective-permute-start.22 = (bf16[768,512]{1,0:T(8,128)(2,1)S(1)}, bf16[768,512]{1,0:T(8,128)(2,1)S(1)}, u32[]{:S(2)}, u32[]{:S(2)}) collective-permute-start(bf16[768,512]{1,0:T(8,128)(2,1)S(1)} %bitcast.14), channel_id=1, source_target_pairs={{0,4},{4,0},{8,12},{12,8},{16,20},{20,16},{24,28},{28,24},{1,5},{5... | collective-permute-start | bytes 2359304 | tf_op jit(solution)/shard_map/ppermute | solution.py:195
  115.2 15.4 %collective-permute-start.23 = (bf16[768,512]{1,0:T(8,128)(2,1)S(1)}, bf16[768,512]{1,0:T(8,128)(2,1)S(1)}, u32[]{:S(2)}, u32[]{:S(2)}) collective-permute-start(bf16[768,512]{1,0:T(8,128)(2,1)S(1)} %collective-permute-done.17.d2), channel_id=1, source_target_pairs={{0,4},{4,0},{8,12},{12,8},{16,20},{20,16},{24,28},{28,24},{1,5},{5... | collective-permute-start | bytes 2359304 | tf_op jit(solution)/shard_map/ppermute | solution.py:195
  130.1 9.1 %collective-permute-start.24 = (bf16[256,768]{1,0:T(8,128)(2,1)S(1)}, bf16[256,768]{1,0:T(8,128)(2,1)S(1)}, u32[]{:S(2)}, u32[]{:S(2)}) collective-permute-start(bf16[256,768]{1,0:T(8,128)(2,1)S(1)} %silu.1.hidden), channel_id=1, source_target_pairs={{0,8},{4,12},{8,0},{12,4},{16,24},{20,28},{24,16},{28,20},{1,9},{5... | collective-permute-start | bytes 1179656 | tf_op jit(solution)/shard_map/ppermute | solution.py:195
  132.2 6.4 %collective-permute-start.25 = (bf16[64,2048]{1,0:T(8,128)(2,1)S(1)}, bf16[64,2048]{1,0:T(8,128)(2,1)S(1)}, u32[]{:S(2)}, u32[]{:S(2)}) collective-permute-start(bf16[64,2048]{1,0:T(8,128)(2,1)S(1)} %get-tuple-element.85), channel_id=1, source_target_pairs={{0,1},{1,0},{2,3},{3,2},{4,5},{5,4},{6,7},{7,6},{8,9},{9,8},{10,11... | collective-permute-start | bytes 786440 | tf_op jit(solution)/shard_map/ppermute | solution.py:195
  132.9 6.4 %collective-permute-start.26 = (bf16[64,2048]{1,0:T(8,128)(2,1)S(1)}, bf16[64,2048]{1,0:T(8,128)(2,1)S(1)}, u32[]{:S(2)}, u32[]{:S(2)}) collective-permute-start(bf16[64,2048]{1,0:T(8,128)(2,1)S(1)} %get-tuple-element.86), channel_id=1, source_target_pairs={{0,2},{1,3},{2,0},{3,1},{4,6},{5,7},{6,4},{7,5},{8,10},{9,11},{10,... | collective-permute-start | bytes 786440 | tf_op jit(solution)/shard_map/ppermute | solution.py:195
  141.0 9.3 %collective-permute-start.29 = (bf16[64,2048]{1,0:T(8,128)(2,1)S(1)}, bf16[64,2048]{1,0:T(8,128)(2,1)S(1)}, u32[]{:S(2)}, u32[]{:S(2)}) collective-permute-start(bf16[64,2048]{1,0:T(8,128)(2,1)S(1)} %get-tuple-element.92), channel_id=1, source_target_pairs={{0,1},{1,0},{2,3},{3,2},{4,5},{5,4},{6,7},{7,6},{8,9},{9,8},{10,11... | collective-permute-start | bytes 786440 | tf_op jit(solution)/shard_map/ppermute | solution.py:195
  142.5 15.6 %collective-permute-start.30 = (bf16[64,2048]{1,0:T(8,128)(2,1)S(1)}, bf16[64,2048]{1,0:T(8,128)(2,1)S(1)}, u32[]{:S(2)}, u32[]{:S(2)}) collective-permute-start(bf16[64,2048]{1,0:T(8,128)(2,1)S(1)} %get-tuple-element.93), channel_id=1, source_target_pairs={{0,2},{1,3},{2,0},{3,1},{4,6},{5,7},{6,4},{7,5},{8,10},{9,11},{10,... | collective-permute-start | bytes 786440 | tf_op jit(solution)/shard_map/ppermute | solution.py:195
  143.1 15.1 %collective-permute-start.31 = (bf16[64,2048]{1,0:T(8,128)(2,1)S(1)}, bf16[64,2048]{1,0:T(8,128)(2,1)S(1)}, u32[]{:S(2)}, u32[]{:S(2)}) collective-permute-start(bf16[64,2048]{1,0:T(8,128)(2,1)S(1)} %get-tuple-element.94), channel_id=1, source_target_pairs={{0,3},{1,2},{2,1},{3,0},{4,7},{5,6},{6,5},{7,4},{8,11},{9,10},{10,... | collective-permute-start | bytes 786440 | tf_op jit(solution)/shard_map/ppermute | solution.py:195
  144.6 3.9 %collective-permute-start.28 = (f32[64,128]{1,0:T(8,128)S(1)}, f32[64,128]{1,0:T(8,128)S(1)}, u32[]{:S(2)}, u32[]{:S(2)}) collective-permute-start(f32[64,128]{1,0:T(8,128)S(1)} %select_add_fusion.shares), channel_id=1, source_target_pairs={{0,8},{4,12},{8,0},{12,4},{16,24},{20,28},{24,16},{28,20},{1,9},{5... | collective-permute-start | bytes 98312 | tf_op jit(solution)/shard_map/ppermute | solution.py:195
  148.7 11.6 %collective-permute-start.27 = (bf16[64,2048]{1,0:T(8,128)(2,1)S(1)}, bf16[64,2048]{1,0:T(8,128)(2,1)S(1)}, u32[]{:S(2)}, u32[]{:S(2)}) collective-permute-start(bf16[64,2048]{1,0:T(8,128)(2,1)S(1)} %get-tuple-element.89), channel_id=1, source_target_pairs={{0,3},{1,2},{2,1},{3,0},{4,7},{5,6},{6,5},{7,4},{8,11},{9,10},{10,... | collective-permute-start | bytes 786440 | tf_op jit(solution)/shard_map/ppermute | solution.py:195
  158.5 6.4 %collective-permute-start.32 = (bf16[64,2048]{1,0:T(8,128)(2,1)S(1)}, bf16[64,2048]{1,0:T(8,128)(2,1)S(1)}, u32[]{:S(2)}, u32[]{:S(2)}) collective-permute-start(bf16[64,2048]{1,0:T(8,128)(2,1)S(1)} %add_convert_fusion), channel_id=1, source_target_pairs={{0,8},{4,12},{8,0},{12,4},{16,24},{20,28},{24,16},{28,20},{1,9},{5... | collective-permute-start | bytes 786440 | tf_op jit(solution)/shard_map/ppermute | solution.py:195

commit v11 on v10

--- a/solution.py
+++ b/solution.py
@@ -525,7 +525,7 @@
     other_pre = enter(other_rows, pairs, BF16)
     from_other = swap(other_pre, "ctx", 2)
     own_pre = enter(own_rows, pairs, F32)
-    own_pre, down_far = lax.optimization_barrier((own_pre, down_far))
+    own_pre, down_far, other_shares = lax.optimization_barrier((own_pre, down_far, other_shares))
     own_hidden = silu(own_pre, from_other)
     other_hidden = swap(own_hidden, "ctx", 2)
     downs = (down_here, down_near, down_far, swap(down_far, "ctx", 1))

time: 167 us -> 173 us (1.036)
  waiting for transfers between devices: 83.9 us -> 92.5 us
  starting transfers between devices: 48.4 us -> 46.3 us
    ppermute x30, waiting for transfers between devices: 80.5 us -> 89.1 us  [swap(): return lax.ppermute(array, axis, [(i, i ^ mask) for i in range(size)])]
    ppermute x30, starting transfers between devices: 37.7 us -> 35.6 us  [swap(): return lax.ppermute(array, axis, [(i, i ^ mask) for i in range(size)])]
where the time goes in v11:
time: 173 us
  waiting for transfers between devices  92.5 us (53%)
  starting transfers between devices  46.3 us (27%)
  Pallas kernels  30.9 us (18%)
  other arithmetic  1.95 us (1%)
    ppermute x30, waiting for transfers between devices, swap(): return lax.ppermute(array, axis, [(i, i ^ mask) for i in range(size)])  89.1 us
    ppermute x30, starting transfers between devices, swap(): return lax.ppermute(array, axis, [(i, i ^ mask) for i in range(size)])  35.6 us
    pallas_call x1, Pallas kernels, attention(): pl.pallas_call(attention_kernel, out_shape=[jax.ShapeDtypeStruct((rows, D...  18.2 us
    ppermute x3, starting transfers between devices, later(): lax.ppermute(array, 'ctx', [(i, i + 2 * chips) for i in range(8 - 2 * chi...  10.7 us
    pallas_call x2, Pallas kernels, enter(): pl.pallas_call(enter_kernel, out_shape=jax.ShapeDtypeStruct((count, 2 * w...  6.1 us
    pallas_call x2, Pallas kernels, leave(): pl.pallas_call(leave_kernel, out_shape=[part] * 4, in_specs=vmem_specs(1)...  3.46 us
  transfers between devices with their start and end apart: 33, of which 15 were waited for; matrix products, arithmetic and copies ran while one was open for 1% of the time, Pallas kernels for 16%

profile of v11, /device:TPU:0, one launch (start us, length us, event | category | flops | bytes accessed | tf_op | source)
XLA Modules:
  0.0 173.2 jit_solution(11659308063617105946)
XLA Ops:
  0.0 0.9 constant_dynamic-slice_fusion
  0.9 4.9 %collective-permute-start.1 = (bf16[256,256]{1,0:T(8,128)(2,1)S(1)}, bf16[256,256]{1,0:T(8,128)(2,1)S(1)}, u32[]{:S(2)}, u32[]{:S(2)}) collective-permute-start(bf16[256,256]{1,0:T(8,128)(2,1)S(1)} %pad_maximum_fusion.1.refs_0_), channel_id=1, source_target_pairs={{0,8},{4,12},{8,16},{12,20},{16,24},{20,28},{1,9},{5,13},{9,17},{1... | collective-permute-start | bytes 393224 | tf_op jit(solution)/shard_map/ppermute | solution.py:496
  5.9 4.5 %collective-permute-start.3 = (bf16[256,256]{1,0:T(8,128)(2,1)S(1)}, bf16[256,256]{1,0:T(8,128)(2,1)S(1)}, u32[]{:S(2)}, u32[]{:S(2)}) collective-permute-start(bf16[256,256]{1,0:T(8,128)(2,1)S(1)} %pad_maximum_fusion.1.refs_0_), channel_id=1, source_target_pairs={{0,16},{4,20},{8,24},{12,28},{1,17},{5,21},{9,25},{13,29},{2,18},{... | collective-permute-start | bytes 393224 | tf_op jit(solution)/shard_map/ppermute | solution.py:496
  10.4 1.3 collective-permute-start.5
  11.7 0.1 collective-permute-start
  11.7 0.0 copy-start.3
  11.8 0.0 copy-start.4
  11.8 0.0 collective-permute-done.1.refs_2_
  11.8 0.5 collective-permute-start.2
  12.2 2.0 %collective-permute-done.3.refs_4_ = bf16[256,256]{1,0:T(8,128)(2,1)S(1)} collective-permute-done((bf16[256,256]{1,0:T(8,128)(2,1)S(1)}, bf16[256,256]{1,0:T(8,128)(2,1)S(1)}, u32[]{:S(2)}, u32[]{:S(2)}) %collective-permute-start.3) | collective-permute-done | bytes 131104 | tf_op jit(solution)/shard_map/ppermute | solution.py:496
  14.3 1.4 collective-permute-done.5.refs_6_
  15.7 1.5 pad_maximum_fusion.refs_0_
  17.1 0.0 collective-permute-done.refs_1_
  17.2 6.3 %collective-permute-start.14 = (bf16[1024,768]{1,0:T(8,128)(2,1)S(1)}, bf16[1024,768]{1,0:T(8,128)(2,1)S(1)}, u32[]{:S(2)}, u32[]{:S(2)}) collective-permute-start(bf16[1024,768]{1,0:T(8,128)(2,1)S(1)} %pad_maximum_fusion.refs_0_), channel_id=1, source_target_pairs={{0,24},{4,28},{8,16},{12,20},{16,8},{20,12},{24,0},{28,4},{1,25},{... | collective-permute-start | bytes 4718600 | tf_op jit(solution)/shard_map/ppermute | solution.py:195
  23.5 0.1 pad_add_fusion.index
  23.6 0.1 select_add_fusion.shares
  23.7 0.0 copy-start.2
  23.7 0.0 copy-start.1
  23.7 18.2 %attention.1 = (bf16[64,4096]{1,0:T(8,128)(2,1)S(1)}, bf16[64,4096]{1,0:T(8,128)(2,1)}, bf16[64,4096]{1,0:T(8,128)(2,1)}, bf16[64,4096]{1,0:T(8,128)(2,1)}) custom-call(s32[2]{0:T(128)S(1)} %pad_add_fusion.index, bf16[256,2048]{1,0:T(8,128)(2,1)} %q_hbm.1, bf16[256,256]{1,0:T(8,128)(2,1)S(1)} %pad_maximum_fusion.1.refs_0_, ...), custom_call_target="tpu_custom_call" | custom-call | flops 1000 | bytes 1000 | tf_op jit(solution)/shard_map/attention/pallas_call | solution.py:296
  41.9 0.0 copy-start
  41.9 1.6 collective-permute-start.7
  43.5 1.5 collective-permute-start.8
  45.0 0.5 collective-permute-start.9
  45.5 11.5 %collective-permute-done.7.r1 = bf16[64,4096]{1,0:T(8,128)(2,1)S(1)} collective-permute-done((bf16[64,4096]{1,0:T(8,128)(2,1)}, bf16[64,4096]{1,0:T(8,128)(2,1)S(1)}, u32[]{:S(2)}, u32[]{:S(2)}) %collective-permute-start.7) | collective-permute-done | bytes 524320 | tf_op jit(solution)/shard_map/ppermute | solution.py:195
  57.0 11.2 %collective-permute-done.8.r2 = bf16[64,4096]{1,0:T(8,128)(2,1)S(1)} collective-permute-done((bf16[64,4096]{1,0:T(8,128)(2,1)}, bf16[64,4096]{1,0:T(8,128)(2,1)S(1)}, u32[]{:S(2)}, u32[]{:S(2)}) %collective-permute-start.8) | collective-permute-done | bytes 524320 | tf_op jit(solution)/shard_map/ppermute | solution.py:195
  68.2 1.2 norm.1
  69.4 1.3 collective-permute-start.10
  70.7 0.8 collective-permute-start.11
  71.5 1.4 collective-permute-start.12
  72.9 0.3 collective-permute-start.13
  73.2 5.5 %collective-permute-done.10.x1 = bf16[64,2048]{1,0:T(8,128)(2,1)S(1)} collective-permute-done((bf16[64,2048]{1,0:T(8,128)(2,1)S(1)}, bf16[64,2048]{1,0:T(8,128)(2,1)S(1)}, u32[]{:S(2)}, u32[]{:S(2)}) %collective-permute-start.10) | collective-permute-done | bytes 262176 | tf_op jit(solution)/shard_map/ppermute | solution.py:195
  78.7 4.4 %collective-permute-done.11.x2 = bf16[64,2048]{1,0:T(8,128)(2,1)S(1)} collective-permute-done((bf16[64,2048]{1,0:T(8,128)(2,1)S(1)}, bf16[64,2048]{1,0:T(8,128)(2,1)S(1)}, u32[]{:S(2)}, u32[]{:S(2)}) %collective-permute-start.11) | collective-permute-done | bytes 262176 | tf_op jit(solution)/shard_map/ppermute | solution.py:195
  83.1 0.1 collective-permute-start.16
  83.1 8.9 %collective-permute-start.17 = (bf16[768,512]{1,0:T(8,128)(2,1)S(1)}, bf16[768,512]{1,0:T(8,128)(2,1)S(1)}, u32[]{:S(2)}, u32[]{:S(2)}) collective-permute-start(bf16[768,512]{1,0:T(8,128)(2,1)S(1)} %bitcast.13), channel_id=1, source_target_pairs={{0,24},{4,28},{8,16},{12,20},{16,8},{20,12},{24,0},{28,4},{1,25},{... | collective-permute-start | bytes 2359304 | tf_op jit(solution)/shard_map/ppermute | solution.py:195
  92.0 0.6 collective-permute-start.19
  92.6 1.1 collective-permute-start.20
  93.7 6.7 %collective-permute-done.19.x1 = bf16[64,2048]{1,0:T(8,128)(2,1)S(1)} collective-permute-done((bf16[64,2048]{1,0:T(8,128)(2,1)S(1)}, bf16[64,2048]{1,0:T(8,128)(2,1)S(1)}, u32[]{:S(2)}, u32[]{:S(2)}) %collective-permute-start.19) | collective-permute-done | bytes 262176 | tf_op jit(solution)/shard_map/ppermute | solution.py:195
  100.4 1.1 collective-permute-start.21
  101.5 7.3 %collective-permute-done.21.x3 = bf16[64,2048]{1,0:T(8,128)(2,1)S(1)} collective-permute-done((bf16[64,2048]{1,0:T(8,128)(2,1)S(1)}, bf16[64,2048]{1,0:T(8,128)(2,1)S(1)}, u32[]{:S(2)}, u32[]{:S(2)}) %collective-permute-start.21) | collective-permute-done | bytes 262176 | tf_op jit(solution)/shard_map/ppermute | solution.py:195
  108.9 3.1 %enter.3 = bf16[256,1536]{1,0:T(8,128)(2,1)S(1)} custom-call(bf16[64,2048]{1,0:T(8,128)(2,1)S(1)} %collective-permute-done.13.x0, bf16[64,2048]{1,0:T(8,128)(2,1)S(1)} %collective-permute-done.19.x1, bf16[64,2048]{1,0:T(8,128)(2,1)S(1)} %collective-permute-done.20.x2, bf16[64,2048]{1,0:T(8,128)(2,1)S(1)} %collective-permute-done.21.x3, ...), custom_call_target="tpu_custom_call" | custom-call | flops 1000 | bytes 1000 | tf_op jit(solution)/shard_map/enter/pallas_call | solution.py:377
  111.9 0.1 collective-permute-start.22
  112.0 2.0 %collective-permute-start.18 = (f32[64,128]{1,0:T(8,128)S(1)}, f32[64,128]{1,0:T(8,128)S(1)}, u32[]{:S(2)}, u32[]{:S(2)}) collective-permute-start(f32[64,128]{1,0:T(8,128)S(1)} %select_add_fusion.shares), channel_id=1, source_target_pairs={{0,8},{4,12},{8,0},{12,4},{16,24},{20,28},{24,16},{28,20},{1,9},{5... | collective-permute-start | bytes 98312 | tf_op jit(solution)/shard_map/ppermute | solution.py:195
  114.0 3.0 %enter.2.own = f32[256,1536]{1,0:T(8,128)S(1)} custom-call(bf16[64,2048]{1,0:T(8,128)(2,1)S(1)} %get-tuple-element.76.x0, bf16[64,2048]{1,0:T(8,128)(2,1)S(1)} %collective-permute-done.10.x1, bf16[64,2048]{1,0:T(8,128)(2,1)S(1)} %collective-permute-done.11.x2, bf16[64,2048]{1,0:T(8,128)(2,1)S(1)} %collective-permute-done.12.x3, ...), custom_call_target="tpu_custom_call" | custom-call | flops 1000 | bytes 1000 | tf_op jit(solution)/shard_map/enter/pallas_call | solution.py:377
  117.1 13.5 %collective-permute-done.18 = f32[64,128]{1,0:T(8,128)S(1)} collective-permute-done((f32[64,128]{1,0:T(8,128)S(1)}, f32[64,128]{1,0:T(8,128)S(1)}, u32[]{:S(2)}, u32[]{:S(2)}) %collective-permute-start.18) | collective-permute-done | bytes 32800 | tf_op jit(solution)/shard_map/ppermute | solution.py:195
  130.6 0.3 silu.1.hidden
  130.9 0.4 collective-permute-start.25
  131.2 1.6 collective-permute-done.24.d3
  132.8 1.7 leave.2
  134.6 0.7 collective-permute-start.26
  135.2 1.1 collective-permute-start.27
  136.3 6.7 %collective-permute-done.26.r1 = bf16[64,2048]{1,0:T(8,128)(2,1)S(1)} collective-permute-done((bf16[64,2048]{1,0:T(8,128)(2,1)S(1)}, bf16[64,2048]{1,0:T(8,128)(2,1)S(1)}, u32[]{:S(2)}, u32[]{:S(2)}) %collective-permute-start.26) | collective-permute-done | bytes 262176 | tf_op jit(solution)/shard_map/ppermute | solution.py:195
  143.0 0.3 collective-permute-done.27.r2
  143.3 1.7 leave.3
  145.0 1.5 collective-permute-start.29
  146.5 0.6 collective-permute-start.30
  147.1 1.5 collective-permute-start.31
  148.6 0.2 slice_reduce_fusion.3
  148.8 1.5 collective-permute-start.28
  150.3 4.0 %collective-permute-done.29 = bf16[64,2048]{1,0:T(8,128)(2,1)S(1)} collective-permute-done((bf16[64,2048]{1,0:T(8,128)(2,1)S(1)}, bf16[64,2048]{1,0:T(8,128)(2,1)S(1)}, u32[]{:S(2)}, u32[]{:S(2)}) %collective-permute-start.29) | collective-permute-done | bytes 262176 | tf_op jit(solution)/shard_map/ppermute | solution.py:195
  154.3 10.4 %collective-permute-done.30 = bf16[64,2048]{1,0:T(8,128)(2,1)S(1)} collective-permute-done((bf16[64,2048]{1,0:T(8,128)(2,1)S(1)}, bf16[64,2048]{1,0:T(8,128)(2,1)S(1)}, u32[]{:S(2)}, u32[]{:S(2)}) %collective-permute-start.30) | collective-permute-done | bytes 262176 | tf_op jit(solution)/shard_map/ppermute | solution.py:195
  164.7 0.3 add_convert_fusion
  165.0 0.3 collective-permute-start.32
  165.3 6.1 %collective-permute-done.32.other = bf16[64,2048]{1,0:T(8,128)(2,1)S(1)} collective-permute-done((bf16[64,2048]{1,0:T(8,128)(2,1)S(1)}, bf16[64,2048]{1,0:T(8,128)(2,1)S(1)}, u32[]{:S(2)}, u32[]{:S(2)}) %collective-permute-start.32) | collective-permute-done | bytes 262176 | tf_op jit(solution)/shard_map/ppermute | solution.py:195
  171.4 1.7 final.1
  (30 shorter events, 0.1 us)
Async XLA Ops:
  0.9 10.9 %collective-permute-start.1 = (bf16[256,256]{1,0:T(8,128)(2,1)S(1)}, bf16[256,256]{1,0:T(8,128)(2,1)S(1)}, u32[]{:S(2)}, u32[]{:S(2)}) collective-permute-start(bf16[256,256]{1,0:T(8,128)(2,1)S(1)} %pad_maximum_fusion.1.refs_0_), channel_id=1, source_target_pairs={{0,8},{4,12},{8,16},{12,20},{16,24},{20,28},{1,9},{5,13},{9,17},{1... | collective-permute-start | bytes 393224 | tf_op jit(solution)/shard_map/ppermute | solution.py:496
  5.9 8.4 %collective-permute-start.3 = (bf16[256,256]{1,0:T(8,128)(2,1)S(1)}, bf16[256,256]{1,0:T(8,128)(2,1)S(1)}, u32[]{:S(2)}, u32[]{:S(2)}) collective-permute-start(bf16[256,256]{1,0:T(8,128)(2,1)S(1)} %pad_maximum_fusion.1.refs_0_), channel_id=1, source_target_pairs={{0,16},{4,20},{8,24},{12,28},{1,17},{5,21},{9,25},{13,29},{2,18},{... | collective-permute-start | bytes 393224 | tf_op jit(solution)/shard_map/ppermute | solution.py:496
  10.4 5.3 %collective-permute-start.5 = (bf16[256,256]{1,0:T(8,128)(2,1)S(1)}, bf16[256,256]{1,0:T(8,128)(2,1)S(1)}, u32[]{:S(2)}, u32[]{:S(2)}) collective-permute-start(bf16[256,256]{1,0:T(8,128)(2,1)S(1)} %pad_maximum_fusion.1.refs_0_), channel_id=1, source_target_pairs={{0,24},{4,28},{1,25},{5,29},{2,26},{6,30},{3,27},{7,31}} | collective-permute-start | bytes 393224 | tf_op jit(solution)/shard_map/ppermute | solution.py:496
  11.7 5.5 %collective-permute-start = (bf16[256,256]{1,0:T(8,128)(2,1)S(1)}, bf16[256,256]{1,0:T(8,128)(2,1)S(1)}, u32[]{:S(2)}, u32[]{:S(2)}) collective-permute-start(bf16[256,256]{1,0:T(8,128)(2,1)S(1)} %pad_maximum_fusion.1.refs_0_), channel_id=1, source_target_pairs={{0,4},{4,0},{8,12},{12,8},{16,20},{20,16},{24,28},{28,24},{1,5},{5... | collective-permute-start | bytes 393224 | tf_op jit(solution)/shard_map/ppermute | solution.py:195
  11.7 11.8 %copy-start.3 = (s32[64,2]{0,1:T(2,128)S(1)}, s32[64,2]{0,1:T(2,128)}, u32[]{:S(2)}) copy-start(s32[64,2]{0,1:T(2,128)} %param.17) | copy-start | bytes 1540
  11.8 11.8 %copy-start.4 = (f32[64,2]{0,1:T(2,128)S(1)}, f32[64,2]{0,1:T(2,128)}, u32[]{:S(2)}) copy-start(f32[64,2]{0,1:T(2,128)} %param.18) | copy-start | bytes 1540
  11.8 5.4 %collective-permute-start.2 = (bf16[256,256]{1,0:T(8,128)(2,1)S(1)}, bf16[256,256]{1,0:T(8,128)(2,1)S(1)}, u32[]{:S(2)}, u32[]{:S(2)}) collective-permute-start(bf16[256,256]{1,0:T(8,128)(2,1)S(1)} %collective-permute-done.1.refs_2_), channel_id=1, source_target_pairs={{0,4},{4,0},{8,12},{12,8},{16,20},{20,16},{24,28},{28,24},{1,5},{5... | collective-permute-start | bytes 393224 | tf_op jit(solution)/shard_map/ppermute | solution.py:195
  14.3 2.9 %collective-permute-start.4 = (bf16[256,256]{1,0:T(8,128)(2,1)S(1)}, bf16[256,256]{1,0:T(8,128)(2,1)S(1)}, u32[]{:S(2)}, u32[]{:S(2)}) collective-permute-start(bf16[256,256]{1,0:T(8,128)(2,1)S(1)} %collective-permute-done.3.refs_4_), channel_id=1, source_target_pairs={{0,4},{4,0},{8,12},{12,8},{16,20},{20,16},{24,28},{28,24},{1,5},{5... | collective-permute-start | bytes 393224 | tf_op jit(solution)/shard_map/ppermute | solution.py:195
  15.7 1.5 collective-permute-start.6
  17.2 65.9 %collective-permute-start.14 = (bf16[1024,768]{1,0:T(8,128)(2,1)S(1)}, bf16[1024,768]{1,0:T(8,128)(2,1)S(1)}, u32[]{:S(2)}, u32[]{:S(2)}) collective-permute-start(bf16[1024,768]{1,0:T(8,128)(2,1)S(1)} %pad_maximum_fusion.refs_0_), channel_id=1, source_target_pairs={{0,24},{4,28},{8,16},{12,20},{16,8},{20,12},{24,0},{28,4},{1,25},{... | collective-permute-start | bytes 4718600 | tf_op jit(solution)/shard_map/ppermute | solution.py:195
  23.7 21.8 %copy-start.2 = (bf16[4096]{0:T(1024)(128)(2,1)S(1)}, bf16[4096]{0:T(1024)(128)(2,1)}, u32[]{:S(2)}) copy-start(bf16[4096]{0:T(1024)(128)(2,1)} %param.16) | copy-start | bytes 24580
  23.7 44.5 %copy-start.1 = (bf16[64,4096]{1,0:T(8,128)(2,1)S(1)}, bf16[64,4096]{1,0:T(8,128)(2,1)}, u32[]{:S(2)}) copy-start(bf16[64,4096]{1,0:T(8,128)(2,1)} %residual.1) | copy-start | bytes 1572868
  41.9 41.2 %copy-start = (bf16[1,768,512]{2,1,0:T(8,128)(2,1)S(1)}, bf16[1,768,512]{2,1,0:T(8,128)(2,1)}, u32[]{:S(2)}) copy-start(bf16[1,768,512]{2,1,0:T(8,128)(2,1)} %param.21) | copy-start | bytes 2359300
  41.9 15.1 %collective-permute-start.7 = (bf16[64,4096]{1,0:T(8,128)(2,1)}, bf16[64,4096]{1,0:T(8,128)(2,1)S(1)}, u32[]{:S(2)}, u32[]{:S(2)}) collective-permute-start(bf16[64,4096]{1,0:T(8,128)(2,1)} %get-tuple-element.68), channel_id=1, source_target_pairs={{0,1},{1,0},{2,3},{3,2},{4,5},{5,4},{6,7},{7,6},{8,9},{9,8},{10,11... | collective-permute-start | bytes 1572872 | tf_op jit(solution)/shard_map/ppermute | solution.py:195
  43.5 24.7 %collective-permute-start.8 = (bf16[64,4096]{1,0:T(8,128)(2,1)}, bf16[64,4096]{1,0:T(8,128)(2,1)S(1)}, u32[]{:S(2)}, u32[]{:S(2)}) collective-permute-start(bf16[64,4096]{1,0:T(8,128)(2,1)} %get-tuple-element.69), channel_id=1, source_target_pairs={{0,2},{1,3},{2,0},{3,1},{4,6},{5,7},{6,4},{7,5},{8,10},{9,11},{10,... | collective-permute-start | bytes 1572872 | tf_op jit(solution)/shard_map/ppermute | solution.py:195
  45.0 23.2 %collective-permute-start.9 = (bf16[64,4096]{1,0:T(8,128)(2,1)}, bf16[64,4096]{1,0:T(8,128)(2,1)S(1)}, u32[]{:S(2)}, u32[]{:S(2)}) collective-permute-start(bf16[64,4096]{1,0:T(8,128)(2,1)} %get-tuple-element.70), channel_id=1, source_target_pairs={{0,3},{1,2},{2,1},{3,0},{4,7},{5,6},{6,5},{7,4},{8,11},{9,10},{10,... | collective-permute-start | bytes 1572872 | tf_op jit(solution)/shard_map/ppermute | solution.py:195
  69.4 9.3 %collective-permute-start.10 = (bf16[64,2048]{1,0:T(8,128)(2,1)S(1)}, bf16[64,2048]{1,0:T(8,128)(2,1)S(1)}, u32[]{:S(2)}, u32[]{:S(2)}) collective-permute-start(bf16[64,2048]{1,0:T(8,128)(2,1)S(1)} %get-tuple-element.76.x0), channel_id=1, source_target_pairs={{0,1},{1,0},{2,3},{3,2},{4,5},{5,4},{6,7},{7,6},{8,9},{9,8},{10,11... | collective-permute-start | bytes 786440 | tf_op jit(solution)/shard_map/ppermute | solution.py:195
  70.7 12.4 %collective-permute-start.11 = (bf16[64,2048]{1,0:T(8,128)(2,1)S(1)}, bf16[64,2048]{1,0:T(8,128)(2,1)S(1)}, u32[]{:S(2)}, u32[]{:S(2)}) collective-permute-start(bf16[64,2048]{1,0:T(8,128)(2,1)S(1)} %get-tuple-element.76.x0), channel_id=1, source_target_pairs={{0,2},{1,3},{2,0},{3,1},{4,6},{5,7},{6,4},{7,5},{8,10},{9,11},{10,... | collective-permute-start | bytes 786440 | tf_op jit(solution)/shard_map/ppermute | solution.py:195
  71.5 11.5 %collective-permute-start.12 = (bf16[64,2048]{1,0:T(8,128)(2,1)S(1)}, bf16[64,2048]{1,0:T(8,128)(2,1)S(1)}, u32[]{:S(2)}, u32[]{:S(2)}) collective-permute-start(bf16[64,2048]{1,0:T(8,128)(2,1)S(1)} %get-tuple-element.76.x0), channel_id=1, source_target_pairs={{0,3},{1,2},{2,1},{3,0},{4,7},{5,6},{6,5},{7,4},{8,11},{9,10},{10,... | collective-permute-start | bytes 786440 | tf_op jit(solution)/shard_map/ppermute | solution.py:195
  72.9 10.1 %collective-permute-start.13 = (bf16[64,2048]{1,0:T(8,128)(2,1)S(1)}, bf16[64,2048]{1,0:T(8,128)(2,1)S(1)}, u32[]{:S(2)}, u32[]{:S(2)}) collective-permute-start(bf16[64,2048]{1,0:T(8,128)(2,1)S(1)} %get-tuple-element.74), channel_id=1, source_target_pairs={{0,8},{4,12},{8,0},{12,4},{16,24},{20,28},{24,16},{28,20},{1,9},{5... | collective-permute-start | bytes 786440 | tf_op jit(solution)/shard_map/ppermute | solution.py:195
  78.7 30.2 %collective-permute-start.15 = (bf16[1024,768]{1,0:T(8,128)(2,1)S(1)}, bf16[1024,768]{1,0:T(8,128)(2,1)S(1)}, u32[]{:S(2)}, u32[]{:S(2)}) collective-permute-start(bf16[1024,768]{1,0:T(8,128)(2,1)S(1)} %pad_maximum_fusion.refs_0_), channel_id=1, source_target_pairs={{0,4},{4,0},{8,12},{12,8},{16,20},{20,16},{24,28},{28,24},{1,5},{5... | collective-permute-start | bytes 4718600 | tf_op jit(solution)/shard_map/ppermute | solution.py:195
  83.1 25.8 %collective-permute-start.16 = (bf16[1024,768]{1,0:T(8,128)(2,1)S(1)}, bf16[1024,768]{1,0:T(8,128)(2,1)S(1)}, u32[]{:S(2)}, u32[]{:S(2)}) collective-permute-start(bf16[1024,768]{1,0:T(8,128)(2,1)S(1)} %collective-permute-done.14.refs_2_), channel_id=1, source_target_pairs={{0,4},{4,0},{8,12},{12,8},{16,20},{20,16},{24,28},{28,24},{1,5},{5... | collective-permute-start | bytes 4718600 | tf_op jit(solution)/shard_map/ppermute | solution.py:195
  83.1 47.4 %collective-permute-start.17 = (bf16[768,512]{1,0:T(8,128)(2,1)S(1)}, bf16[768,512]{1,0:T(8,128)(2,1)S(1)}, u32[]{:S(2)}, u32[]{:S(2)}) collective-permute-start(bf16[768,512]{1,0:T(8,128)(2,1)S(1)} %bitcast.13), channel_id=1, source_target_pairs={{0,24},{4,28},{8,16},{12,20},{16,8},{20,12},{24,0},{28,4},{1,25},{... | collective-permute-start | bytes 2359304 | tf_op jit(solution)/shard_map/ppermute | solution.py:195
  92.0 8.4 %collective-permute-start.19 = (bf16[64,2048]{1,0:T(8,128)(2,1)S(1)}, bf16[64,2048]{1,0:T(8,128)(2,1)S(1)}, u32[]{:S(2)}, u32[]{:S(2)}) collective-permute-start(bf16[64,2048]{1,0:T(8,128)(2,1)S(1)} %collective-permute-done.13.x0), channel_id=1, source_target_pairs={{0,1},{1,0},{2,3},{3,2},{4,5},{5,4},{6,7},{7,6},{8,9},{9,8},{10,11... | collective-permute-start | bytes 786440 | tf_op jit(solution)/shard_map/ppermute | solution.py:195
  92.6 8.9 %collective-permute-start.20 = (bf16[64,2048]{1,0:T(8,128)(2,1)S(1)}, bf16[64,2048]{1,0:T(8,128)(2,1)S(1)}, u32[]{:S(2)}, u32[]{:S(2)}) collective-permute-start(bf16[64,2048]{1,0:T(8,128)(2,1)S(1)} %collective-permute-done.13.x0), channel_id=1, source_target_pairs={{0,2},{1,3},{2,0},{3,1},{4,6},{5,7},{6,4},{7,5},{8,10},{9,11},{10,... | collective-permute-start | bytes 786440 | tf_op jit(solution)/shard_map/ppermute | solution.py:195
  100.4 8.4 %collective-permute-start.21 = (bf16[64,2048]{1,0:T(8,128)(2,1)S(1)}, bf16[64,2048]{1,0:T(8,128)(2,1)S(1)}, u32[]{:S(2)}, u32[]{:S(2)}) collective-permute-start(bf16[64,2048]{1,0:T(8,128)(2,1)S(1)} %collective-permute-done.13.x0), channel_id=1, source_target_pairs={{0,3},{1,2},{2,1},{3,0},{4,7},{5,6},{6,5},{7,4},{8,11},{9,10},{10,... | collective-permute-start | bytes 786440 | tf_op jit(solution)/shard_map/ppermute | solution.py:195
  111.9 18.6 %collective-permute-start.22 = (bf16[256,1536]{1,0:T(8,128)(2,1)S(1)}, bf16[256,1536]{1,0:T(8,128)(2,1)S(1)}, u32[]{:S(2)}, u32[]{:S(2)}) collective-permute-start(bf16[256,1536]{1,0:T(8,128)(2,1)S(1)} %enter.3), channel_id=1, source_target_pairs={{0,8},{4,12},{8,0},{12,4},{16,24},{20,28},{24,16},{28,20},{1,9},{5... | collective-permute-start | bytes 2359304 | tf_op jit(solution)/shard_map/ppermute | solution.py:195
  112.0 18.5 %collective-permute-start.18 = (f32[64,128]{1,0:T(8,128)S(1)}, f32[64,128]{1,0:T(8,128)S(1)}, u32[]{:S(2)}, u32[]{:S(2)}) collective-permute-start(f32[64,128]{1,0:T(8,128)S(1)} %select_add_fusion.shares), channel_id=1, source_target_pairs={{0,8},{4,12},{8,0},{12,4},{16,24},{20,28},{24,16},{28,20},{1,9},{5... | collective-permute-start | bytes 98312 | tf_op jit(solution)/shard_map/ppermute | solution.py:195
  114.0 17.2 %collective-permute-start.23 = (bf16[768,512]{1,0:T(8,128)(2,1)S(1)}, bf16[768,512]{1,0:T(8,128)(2,1)S(1)}, u32[]{:S(2)}, u32[]{:S(2)}) collective-permute-start(bf16[768,512]{1,0:T(8,128)(2,1)S(1)} %bitcast.14), channel_id=1, source_target_pairs={{0,4},{4,0},{8,12},{12,8},{16,20},{20,16},{24,28},{28,24},{1,5},{5... | collective-permute-start | bytes 2359304 | tf_op jit(solution)/shard_map/ppermute | solution.py:195
  130.5 2.3 %collective-permute-start.24 = (bf16[768,512]{1,0:T(8,128)(2,1)S(1)}, bf16[768,512]{1,0:T(8,128)(2,1)S(1)}, u32[]{:S(2)}, u32[]{:S(2)}) collective-permute-start(bf16[768,512]{1,0:T(8,128)(2,1)S(1)} %collective-permute-done.17.d2), channel_id=1, source_target_pairs={{0,4},{4,0},{8,12},{12,8},{16,20},{20,16},{24,28},{28,24},{1,5},{5... | collective-permute-start | bytes 2359304 | tf_op jit(solution)/shard_map/ppermute | solution.py:195
  130.9 12.4 %collective-permute-start.25 = (bf16[256,768]{1,0:T(8,128)(2,1)S(1)}, bf16[256,768]{1,0:T(8,128)(2,1)S(1)}, u32[]{:S(2)}, u32[]{:S(2)}) collective-permute-start(bf16[256,768]{1,0:T(8,128)(2,1)S(1)} %silu.1.hidden), channel_id=1, source_target_pairs={{0,8},{4,12},{8,0},{12,4},{16,24},{20,28},{24,16},{28,20},{1,9},{5... | collective-permute-start | bytes 1179656 | tf_op jit(solution)/shard_map/ppermute | solution.py:195
  134.6 8.4 %collective-permute-start.26 = (bf16[64,2048]{1,0:T(8,128)(2,1)S(1)}, bf16[64,2048]{1,0:T(8,128)(2,1)S(1)}, u32[]{:S(2)}, u32[]{:S(2)}) collective-permute-start(bf16[64,2048]{1,0:T(8,128)(2,1)S(1)} %get-tuple-element.86), channel_id=1, source_target_pairs={{0,1},{1,0},{2,3},{3,2},{4,5},{5,4},{6,7},{7,6},{8,9},{9,8},{10,11... | collective-permute-start | bytes 786440 | tf_op jit(solution)/shard_map/ppermute | solution.py:195
  135.2 8.1 %collective-permute-start.27 = (bf16[64,2048]{1,0:T(8,128)(2,1)S(1)}, bf16[64,2048]{1,0:T(8,128)(2,1)S(1)}, u32[]{:S(2)}, u32[]{:S(2)}) collective-permute-start(bf16[64,2048]{1,0:T(8,128)(2,1)S(1)} %get-tuple-element.87), channel_id=1, source_target_pairs={{0,2},{1,3},{2,0},{3,1},{4,6},{5,7},{6,4},{7,5},{8,10},{9,11},{10,... | collective-permute-start | bytes 786440 | tf_op jit(solution)/shard_map/ppermute | solution.py:195
  145.0 9.3 %collective-permute-start.29 = (bf16[64,2048]{1,0:T(8,128)(2,1)S(1)}, bf16[64,2048]{1,0:T(8,128)(2,1)S(1)}, u32[]{:S(2)}, u32[]{:S(2)}) collective-permute-start(bf16[64,2048]{1,0:T(8,128)(2,1)S(1)} %get-tuple-element.94), channel_id=1, source_target_pairs={{0,1},{1,0},{2,3},{3,2},{4,5},{5,4},{6,7},{7,6},{8,9},{9,8},{10,11... | collective-permute-start | bytes 786440 | tf_op jit(solution)/shard_map/ppermute | solution.py:195
  146.5 18.2 %collective-permute-start.30 = (bf16[64,2048]{1,0:T(8,128)(2,1)S(1)}, bf16[64,2048]{1,0:T(8,128)(2,1)S(1)}, u32[]{:S(2)}, u32[]{:S(2)}) collective-permute-start(bf16[64,2048]{1,0:T(8,128)(2,1)S(1)} %get-tuple-element.95), channel_id=1, source_target_pairs={{0,2},{1,3},{2,0},{3,1},{4,6},{5,7},{6,4},{7,5},{8,10},{9,11},{10,... | collective-permute-start | bytes 786440 | tf_op jit(solution)/shard_map/ppermute | solution.py:195
  147.1 17.6 %collective-permute-start.31 = (bf16[64,2048]{1,0:T(8,128)(2,1)S(1)}, bf16[64,2048]{1,0:T(8,128)(2,1)S(1)}, u32[]{:S(2)}, u32[]{:S(2)}) collective-permute-start(bf16[64,2048]{1,0:T(8,128)(2,1)S(1)} %get-tuple-element.96), channel_id=1, source_target_pairs={{0,3},{1,2},{2,1},{3,0},{4,7},{5,6},{6,5},{7,4},{8,11},{9,10},{10,... | collective-permute-start | bytes 786440 | tf_op jit(solution)/shard_map/ppermute | solution.py:195
  148.8 16.5 %collective-permute-start.28 = (bf16[64,2048]{1,0:T(8,128)(2,1)S(1)}, bf16[64,2048]{1,0:T(8,128)(2,1)S(1)}, u32[]{:S(2)}, u32[]{:S(2)}) collective-permute-start(bf16[64,2048]{1,0:T(8,128)(2,1)S(1)} %get-tuple-element.90), channel_id=1, source_target_pairs={{0,3},{1,2},{2,1},{3,0},{4,7},{5,6},{6,5},{7,4},{8,11},{9,10},{10,... | collective-permute-start | bytes 786440 | tf_op jit(solution)/shard_map/ppermute | solution.py:195
  165.0 6.4 %collective-permute-start.32 = (bf16[64,2048]{1,0:T(8,128)(2,1)S(1)}, bf16[64,2048]{1,0:T(8,128)(2,1)S(1)}, u32[]{:S(2)}, u32[]{:S(2)}) collective-permute-start(bf16[64,2048]{1,0:T(8,128)(2,1)S(1)} %add_convert_fusion), channel_id=1, source_target_pairs={{0,8},{4,12},{8,0},{12,4},{16,24},{20,28},{24,16},{28,20},{1,9},{5... | collective-permute-start | bytes 786440 | tf_op jit(solution)/shard_map/ppermute | solution.py:195
